TPU v7x, 32 devices: a whole 2x2x4 slice. The times are simulated.
32 devices in a mesh: groups: 2 (over y), tm: 8 (over z, x), chan: 2 (over core).
Axes of the slice: x: 2, y: 2, z: 4, core: 2. Of those that a mesh axis runs over, the one named last changes fastest.
Arguments:
- strain: bfloat16 [32768, 2048], P(('groups', 'tm'), 'chan'), parts along dimension 0
Outputs:
- covariance: float32 [2048, 2048], P(('groups', 'tm'), 'chan'), parts along dimension 0
- segment_auto: float32 [256, 2048], P(('groups', 'tm'), 'chan'), parts along dimension 0
There are 2 independent parts, one for each index of `groups`. A program takes and returns all parts, laid end to end along the dimension named above; each array names one. Nothing has to cross between parts.
All inputs are finite; a program needn't handle non-finite values.
Results may differ from a plain program's by a relative error of at most 0.0003.
Values may be sent and summed in bfloat16 or wider, within the bound.
No kernel may reach another device: no remote copies, remote signals or barrier semaphores. Data moves between devices by JAX's collectives and lax.ppermute only.
A program may use at most 64 MiB of HBM per device.

v0:
```python
import jax
import jax.numpy as jnp
from jax import lax
from jax.sharding import PartitionSpec as P

LAGS = 16
REF = 64


def passed_along(value, axis, steps):
    count = lax.axis_size(axis)
    initial, last = (max(0, -steps), min(count, count - steps))
    return lax.ppermute(value, axis, [(source, source + steps) for source in range(initial, last)])


def swapped(block, axis, apart):
    count = lax.axis_size(axis)
    route = []
    for low in range(count):
        high = low | 1 << apart
        if high != low and high < count:
            route += [(low, high), (high, low)]
    return lax.ppermute(block, axis, route)


def stack_lags(ref_cols, lags):
    pieces = [jnp.pad(ref_cols, ((offset, lags - 1 - offset), (0, 0))) for offset in range(lags)]
    return jnp.concatenate(pieces, axis=1)


def auto_rows(extended, block_rows, lags, rows):
    block_wide = block_rows.astype(jnp.float32)
    return jnp.stack(
        [
            jnp.sum(extended[offset : offset + rows].astype(jnp.float32) * block_wide, axis=0)
            for offset in range(lags)
        ]
    )


def local(strain):
    seg_rows = strain.shape[0]
    width_dev = strain.shape[1]
    halfref = REF // 2
    chan_index = lax.axis_index("chan")
    time_index = lax.axis_index("tm")
    slab_rows = seg_rows * lax.axis_size("tm")
    wide = strain.astype(jnp.float32)
    local_power = jnp.sum(wide * wide, axis=0)
    blank = jnp.zeros_like(local_power)
    placed = jnp.where(
        chan_index == 0,
        jnp.concatenate([local_power, blank]),
        jnp.concatenate([blank, local_power]),
    )
    tail_rows = passed_along(strain[: LAGS - 1], "tm", -1)
    own_refs = strain[:, :halfref]
    other_refs = swapped(own_refs, "chan", 0)
    ref_cols = jnp.where(
        chan_index == 0,
        jnp.concatenate([own_refs, other_refs], axis=1),
        jnp.concatenate([other_refs, own_refs], axis=1),
    )
    extended = jnp.concatenate([strain, tail_rows], axis=0)
    power_sum = lax.psum(placed, ("tm", "chan"))
    inv_all = 1.0 / jnp.sqrt(power_sum / slab_rows + 1e-06)
    own_scale = lax.dynamic_slice_in_dim(inv_all, chan_index * width_dev, width_dev)
    ref_scale = jnp.concatenate([inv_all[:halfref], inv_all[width_dev : width_dev + halfref]])
    toeplitz = stack_lags(ref_cols, LAGS)
    total_rows = LAGS * REF
    rows_dev = total_rows // lax.axis_size("tm")
    summed = lax.psum(
        lax.dot_general(
            toeplitz, extended, (((0,), (0,)), ((), ())), preferred_element_type=jnp.float32
        ),
        "tm",
    )
    mine = lax.dynamic_slice_in_dim(summed, time_index * rows_dev, rows_dev, 0)
    auto_lags = auto_rows(extended, strain, LAGS, seg_rows)
    global_row = time_index * rows_dev + jnp.arange(rows_dev, dtype=jnp.int32)
    lag_index = global_row // REF
    denom = (slab_rows - lag_index).astype(jnp.float32)
    ref_slot = global_row % REF
    onehot = (ref_slot[:, None] == jnp.arange(REF, dtype=jnp.int32)[None, :]).astype(jnp.float32)
    row_scale = jnp.sum(onehot * ref_scale[None, :], axis=1)
    covariance = mine * own_scale[None, :] * (row_scale / denom)[:, None]
    segment_auto = auto_lags * (own_scale * own_scale)[None, :] / seg_rows
    return (covariance, segment_auto)


def solution(mesh):
    in_specs = (P(("groups", "tm"), "chan"),)
    out_specs = (P(("groups", "tm"), "chan"), P(("groups", "tm"), "chan"))
    return jax.shard_map(local, mesh=mesh, in_specs=in_specs, out_specs=out_specs, check_vma=False)
```

profile of v0, /device:TPU:0, one launch (start us, length us, event | category | flops | bytes accessed | tf_op | source)
XLA Modules:
  0.0 210.4 jit_solution(6749905641121418327)
XLA Ops:
  7.2 0.0 all-reduce.20.cloned.1.call-start
  7.2 1.1 slice.57
  8.3 0.5 collective-permute-start
  8.8 0.8 slice.58
  9.6 1.3 collective-permute-start.1
  10.9 4.6 %constant_dynamic-update-slice_fusion.1 = bf16[2063,1024]{1,0:T(8,128)(2,1)} fusion(bf16[2048,1024]{1,0:T(8,128)(2,1)} %param.1), kind=kLoop, calls=%fused_computation.40 | loop fusion | bytes 8388608
  15.5 0.5 collective-permute-done.1
  16.0 0.6 constant_dynamic-update-slice_fusion
  16.6 0.0 collective-permute-done
  16.6 0.6 maximum_select_fusion
  17.2 1.5 fusion.18
  18.8 2.6 %fusion.17 = (bf16[2063,64]{1,0:T(8,128)(2,1)}, bf16[2063,64]{1,0:T(8,128)(2,1)}, bf16[2063,64]{1,0:T(8,128)(2,1)}, bf16[2063,64]{1,0:T(8,128)(2,1)}, bf16[2063,...) fusion(bf16[2048,64]{1,0:T(8,128)(2,1)S(1)} %maximum_select_fusion), kind=kLoop, calls=%fused_computation.50 | loop fusion | bytes 2638720 | tf_op jit(solution)/shard_map/jit(_pad)/pad | solution.py:27
  21.3 10.8 %concatenate.23 = bf16[2063,1024]{1,0:T(8,128)(2,1)} concatenate(bf16[2063,64]{1,0:T(8,128)(2,1)} %get-tuple-element.35, bf16[2063,64]{1,0:T(8,128)(2,1)S(1)} %get-tuple-element.34, bf16[2063,64]{1,0:T(8,128)(2,1)S(1)} %get-tuple-element.33, bf16[2063,64]{1,0:T(8,128)(2,1)S(1)} %get-tuple-element.32, bf16[2063,64]{1,0:T(8,128)(2,1)S(1)} %get-tuple-element.31, ...), dimensions={1} | concatenate | bytes 8450048 | tf_op jit(solution)/shard_map/concatenate | solution.py:28
  32.1 9.5 %fusion.20 = f32[1024,1024]{1,0:T(8,128)} fusion(bf16[2063,1024]{1,0:T(8,128)(2,1)} %concatenate.23, bf16[2063,1024]{1,0:T(8,128)(2,1)} %constant_dynamic-update-slice_fusion), kind=kOutput, calls=%fused_computation.53 | convolution fusion | flops 4326424576 | bytes 12644352 | tf_op jit(solution)/shard_map/dot_general | solution.py:73
  41.6 0.0 all-reduce.20.cloned.1.call-update
  41.6 37.0 %fusion.15 = (f32[1024]{0:T(1024)S(1)}, f32[1024]{0:T(1024)S(1)}, f32[1024]{0:T(1024)S(1)}, f32[1024]{0:T(1024)S(1)}, f32[1024]{0:T(1024)S(1)}, /*index=5*/f32[1...) fusion(bf16[2048,1024]{1,0:T(8,128)(2,1)} %param.1, ...), kind=kLoop, calls=%fused_computation.31 | loop fusion | flops 100646912 | bytes 67174400 | tf_op jit(solution)/shard_map/reduce_sum | solution.py:35
  78.6 0.1 stack.67
  78.7 37.5 %psum.15 = f32[2048]{0:T(1024)S(1)} all-reduce(f32[2048]{0:T(1024)S(1)} %pad_select_fusion), channel_id=1, replica_groups=mesh['groups'=2,'tm'=8,'chan'=2] {'tm','chan'}, use_global_device_ids=true, to_apply=%region_2.3 | all-reduce | flops 2048 | bytes 16384 | tf_op jit(solution)/shard_map/psum | solution.py:65
  116.2 0.1 pad_maximum_fusion
  116.3 0.1 select_reduce_fusion
  116.4 0.6 multiply_multiply_fusion.1
  117.1 84.5 %all-reduce.20.cloned.1.call-done = f32[1024,1024]{1,0:T(8,128)} async-done(((f32[1024,1024]{1,0:T(8,128)}), f32[1024,1024]{1,0:T(8,128)}) %all-reduce.20.cloned.1.call-update) | async-done | bytes 4194320 | tf_op jit(solution)/shard_map/psum | solution.py:72
  201.6 1.9 multiply_multiply_fusion
  (6 shorter events, 0.0 us)
Async XLA Ops:
  7.2 194.4 %all-reduce.20.cloned.1.call-start = ((), (), s32[]{:S(2)}) async-start(), calls=%async_computation | async-start | bytes 8388608 | tf_op jit(solution)/shard_map/psum | solution.py:72
  8.3 8.3 %collective-permute-start = (bf16[2048,32]{1,0:T(8,128)(2,1)S(1)}, bf16[2048,32]{1,0:T(8,128)(2,1)S(1)}, u32[]{:S(2)}, u32[]{:S(2)}) collective-permute-start(bf16[2048,32]{1,0:T(8,128)(2,1)S(1)} %slice.57), channel_id=1, source_target_pairs={{0,1},{1,0},{2,3},{3,2},{4,5},{5,4},{6,7},{7,6},{8,9},{9,8},{10,11... | collective-permute-start | bytes 393224 | tf_op jit(solution)/shard_map/ppermute | solution.py:23
  9.6 6.4 %collective-permute-start.1 = (bf16[15,1024]{1,0:T(8,128)(2,1)S(1)}, bf16[15,1024]{1,0:T(8,128)(2,1)S(1)}, u32[]{:S(2)}, u32[]{:S(2)}) collective-permute-start(bf16[15,1024]{1,0:T(8,128)(2,1)S(1)} %slice.58), channel_id=1, source_target_pairs={{2,0},{4,2},{6,4},{8,6},{10,8},{12,10},{14,12},{3,1},{5,3},{7,5},{... | collective-permute-start | bytes 92168 | tf_op jit(solution)/shard_map/ppermute | solution.py:13
Sparse Core Ops, SparseCore 0:
  41.7 159.8 all-reduce.19
where the time goes:
time: 212 us; the launch traced here: 210 us
  waiting for transfers between devices  85.1 us (40%)
  other arithmetic  40.3 us (19%)
  blocking collectives  37.5 us (18%)
  local copies, waits for them, and re-layouts  22 us (10%)
  between operations  14.1 us (7%)
  matrix products  9.48 us (4%)
    psum x1, waiting for transfers between devices, local(): lax.psum(lax.dot_general(toeplitz, extended, (((0,), (0,)), ((), ())), pr...  84.5 us
    psum x1, blocking collectives, local(): power_sum = lax.psum(placed, ('tm', 'chan'))  37.5 us
    reduce_sum x1, other arithmetic, auto_rows(): jnp.sum(extended[offset:offset + rows].astype(jnp.float32) * block_wide,...  37 us
    concatenate x1, local copies, waits for them, and re-layouts, stack_lags(): return jnp.concatenate(pieces, axis=1)  10.8 us
    dot_general x1, matrix products, local(): lax.dot_general(toeplitz, extended, (((0,), (0,)), ((), ())), preferred_e...  9.48 us
    unnamed x1, local copies, waits for them, and re-layouts  4.59 us
  transfers between devices with their start and end apart: 3, of which 2 were waited for; matrix products, arithmetic and copies ran while one was open for 21% of the time, Pallas kernels for 0%

commit v1 on v0

v1 whole, which is shorter than its diff:
```python
import functools

import jax
import jax.numpy as jnp
import numpy as np
from jax import lax
from jax.experimental import pallas as pl
from jax.experimental.pallas import tpu as pltpu
from jax.sharding import PartitionSpec as P

LAGS = 16
REF = 64
HALF = REF // 2
HALO = 128
LANES = 128
VMEM_BYTES = 48 * 1024 * 1024


def passed_along(value, axis, steps):
    count = lax.axis_size(axis)
    initial, last = (max(0, -steps), min(count, count - steps))
    return lax.ppermute(value, axis, [(source, source + steps) for source in range(initial, last)])


def exchanged(value, axis, bit):
    count = lax.axis_size(axis)
    return lax.ppermute(value, axis, [(source, source ^ bit) for source in range(count)])


def summed_over(value, axis):
    bit = 1
    while bit < lax.axis_size(axis):
        value = value + exchanged(value, axis, bit)
        bit *= 2
    return value


def lag_products_kernel(place, order, strain, own, other, halo_own, halo_other, keep, send, shifted):
    chan, near = place[0], place[1]
    slot = pl.program_id(0)
    rows = strain.shape[0]
    chunk = keep.shape[1]

    @pl.when(slot == 0)
    def _():
        for refs, halo, half in ((own, halo_own, chan), (other, halo_other, 1 - chan)):
            long = jnp.concatenate([halo[...], refs[...]], axis=1).astype(jnp.float32)
            for lag in range(LAGS):
                start = pl.multiple_of(lag * REF + half * HALF, HALF)
                piece = long[:, HALO - lag : HALO - lag + rows]
                shifted[pl.ds(start, HALF), :] = piece.astype(jnp.bfloat16)

    start = pl.multiple_of(order[slot] * 2 * chunk, 2 * chunk)
    product = jnp.dot(
        shifted[pl.ds(start, 2 * chunk), :], strain[...], preferred_element_type=jnp.float32
    )
    keep[0] = jnp.where(near == 0, product[:chunk], product[chunk:])
    send[0] = jnp.where(near == 0, product[chunk:], product[:chunk])


def lag_products(place, order, strain, own, other, halo_own, halo_other, chunk):
    slots = order.shape[0]
    rows, width = strain.shape
    whole = lambda array: pl.BlockSpec(array.shape, lambda slot, *_: (0, 0))
    block = pl.BlockSpec((1, chunk, width), lambda slot, *_: (slot, 0, 0))
    shape = jax.ShapeDtypeStruct((slots, chunk, width), jnp.float32)
    return pl.pallas_call(
        lag_products_kernel,
        grid_spec=pltpu.PrefetchScalarGridSpec(
            num_scalar_prefetch=2,
            grid=(slots,),
            in_specs=[whole(array) for array in (strain, own, other, halo_own, halo_other)],
            out_specs=[block, block],
            scratch_shapes=[pltpu.VMEM((LAGS * REF, rows), jnp.bfloat16)],
        ),
        out_shape=[shape, shape],
        compiler_params=pltpu.CompilerParams(vmem_limit_bytes=VMEM_BYTES),
        cost_estimate=pl.CostEstimate(
            flops=2 * slots * 2 * chunk * rows * width,
            bytes_accessed=rows * width * 2 + slots * 2 * chunk * width * 4,
            transcendentals=0,
        ),
        name="lag_products",
    )(place, order, strain, own, other, halo_own, halo_other)


def segment_kernel(strain, tail, out, wide):
    rows, lanes = strain.shape
    pitch = rows // 8
    for lane in range(0, lanes, LANES):
        wide[:rows, :] = strain[:, lane : lane + LANES].astype(jnp.float32)
        wide[rows:, :] = tail[:, lane : lane + LANES].astype(jnp.float32)
        taken = lambda first: wide[pl.ds(first, 8, stride=pitch), :]

        def step(index, carry):
            window, sums = carry
            window = window + (taken(index + LAGS - 1),)
            sums = tuple(total + window[0] * window[lag] for lag, total in enumerate(sums))
            return window[1:], sums

        window = tuple(taken(first) for first in range(LAGS - 1))
        zero = jnp.zeros((8, LANES), jnp.float32)
        _, sums = lax.fori_loop(0, pitch, step, (window, (zero,) * LAGS), unroll=16)
        out[:, lane : lane + LANES] = jnp.concatenate(
            [jnp.sum(total, axis=0, keepdims=True) for total in sums], axis=0
        )


def segment_rows(strain, tail, block):
    rows, width = strain.shape
    return pl.pallas_call(
        segment_kernel,
        grid=(width // block,),
        in_specs=[
            pl.BlockSpec((rows, block), lambda index: (0, index)),
            pl.BlockSpec((LAGS, block), lambda index: (0, index)),
        ],
        out_specs=pl.BlockSpec((LAGS, block), lambda index: (0, index)),
        out_shape=jax.ShapeDtypeStruct((LAGS, width), jnp.float32),
        scratch_shapes=[pltpu.VMEM((rows + LAGS, LANES), jnp.float32)],
        compiler_params=pltpu.CompilerParams(vmem_limit_bytes=VMEM_BYTES),
        cost_estimate=pl.CostEstimate(
            flops=2 * LAGS * rows * width, bytes_accessed=rows * width * 2, transcendentals=0
        ),
        name="segment_rows",
    )(strain, tail)


def chosen(array, index):
    return lax.dynamic_index_in_dim(array, index, 0, keepdims=False)


def scattered_sums(keep, send, order):
    count = keep.shape[0]
    far = lax.axis_index("tm") // 2
    table = np.argsort(order, axis=1)
    arrived = []
    right = left = None
    for step in range(count):
        arrived.append(keep[step] + exchanged(send[step], "tm", 1))
        if step == count - 1:
            return arrived[step] + right + left
        stacked = jnp.stack(arrived)
        ahead = np.clip(count - 1 + np.arange(count) - step, 0, count - 1)
        back = np.clip(step + np.arange(count) - count + 1, 0, count - 1)
        slot_ahead = jnp.asarray(np.minimum(table[np.arange(count), ahead], step), jnp.int32)[far]
        slot_back = jnp.asarray(np.minimum(table[np.arange(count), back], step), jnp.int32)[far]
        to_right = chosen(stacked, slot_ahead)
        to_left = chosen(stacked, slot_back)
        if step:
            to_right = to_right + right
            to_left = to_left + left
        right = lax.ppermute(
            to_right, "tm", [(2 * z + x, 2 * z + 2 + x) for z in range(min(step + 1, count - 1)) for x in range(2)]
        )
        left = lax.ppermute(
            to_left, "tm", [(2 * z + x, 2 * z - 2 + x) for z in range(max(count - 1 - step, 1), count) for x in range(2)]
        )


def send_order(count):
    places = np.arange(count)
    return np.stack([np.argsort(-np.abs(places - place), kind="stable") for place in places]).astype(np.int32)


def local(strain):
    rows, width = strain.shape
    count = lax.axis_size("tm")
    chan = lax.axis_index("chan")
    time = lax.axis_index("tm")
    slab_rows = rows * count
    rows_dev = LAGS * REF // count
    pairs = count // 2

    own = strain[:, :HALF].T
    edge = own[:, rows - HALO :]
    other = exchanged(own, "chan", 1)
    halo_own = passed_along(edge, "tm", 1)
    halo_other = exchanged(halo_own, "chan", 1)
    tail = passed_along(strain[:LAGS], "tm", -1)

    place = jnp.stack([chan, time % 2]).astype(jnp.int32)
    products = functools.partial(
        lag_products,
        place,
        strain=strain,
        own=own,
        other=other,
        halo_own=halo_own,
        halo_other=halo_other,
        chunk=rows_dev,
    )

    wide = strain.astype(jnp.float32)
    power = jnp.sum(wide * wide, axis=0)
    power_other = jnp.sum(jnp.square(other.astype(jnp.float32)), axis=1)
    power = summed_over(jnp.concatenate([power, power_other]), "tm")
    inv = 1.0 / jnp.sqrt(power / slab_rows + 1e-06)
    own_scale = inv[:width]
    ref_scale = jnp.where(
        chan == 0,
        jnp.concatenate([inv[:HALF], inv[width:]]),
        jnp.concatenate([inv[width:], inv[:HALF]]),
    )

    if pairs <= 4:
        order = send_order(pairs)
        mine = jnp.asarray(order)[time // 2]
        first = products(order=mine[:1])
        rest = products(order=mine[1:])
        keep = [first[0][0]] + [rest[0][slot] for slot in range(pairs - 1)]
        send = [first[1][0]] + [rest[1][slot] for slot in range(pairs - 1)]
        summed = scattered_sums(jnp.stack(keep), send, order)
    else:
        keep, send = products(order=jnp.arange(pairs, dtype=jnp.int32))
        near = (time % 2)[None, None, None]
        blocks = jnp.stack([jnp.where(near == 0, keep, send), jnp.where(near == 0, send, keep)], axis=1)
        summed = lax.psum_scatter(
            blocks.reshape(LAGS * REF, width), "tm", scatter_dimension=0, tiled=True
        )

    row = time * rows_dev + jnp.arange(rows_dev, dtype=jnp.int32)
    denom = (slab_rows - row // REF).astype(jnp.float32)
    row_scale = ref_scale[row % REF] / denom
    covariance = summed * own_scale[None, :] * row_scale[:, None]

    auto = segment_rows(strain, tail, 256)
    segment_auto = auto * (own_scale * own_scale)[None, :] / rows
    return (covariance, segment_auto)


def solution(mesh):
    in_specs = (P(("groups", "tm"), "chan"),)
    out_specs = (P(("groups", "tm"), "chan"), P(("groups", "tm"), "chan"))
    return jax.shard_map(local, mesh=mesh, in_specs=in_specs, out_specs=out_specs, check_vma=False)
```

time: 212 us -> 103 us (0.49)
  waiting for transfers between devices: 85.1 us -> 15.6 us
  blocking collectives: 37.5 us -> 0 us
  starting transfers between devices: 1.84 us -> 34.4 us
  other arithmetic: 40.3 us -> 11 us
  Pallas kernels: 0 us -> 23.4 us
  local copies, waits for them, and re-layouts: 22 us -> 11.4 us
  matrix products: 9.48 us -> 0 us
  between operations: 14.1 us -> 6.63 us
    psum x1 -> x0, waiting for transfers between devices: 84.5 us -> none  [local(): lax.psum(lax.dot_general(toeplitz, extended, (((0,), (0,)), ((), ())), pr...]
    psum x1 -> x0, blocking collectives: 37.5 us -> none  [local(): power_sum = lax.psum(placed, ('tm', 'chan'))]
    reduce_sum x2, other arithmetic: 37.1 us -> 3.25 us  [the longest x1 3.11 us: local(): power = jnp.sum(wide * wide, axis=0)]
    ppermute x1 -> x15, starting transfers between devices: 0.52 us -> 28.8 us  [the longest x3 13.8 us: scattered_sums(): lax.ppermute(to_right, 'tm', [(2 * z + x, 2 * z + 2 + x) for z in range(m...]
    pallas_call x0 -> x3, Pallas kernels: none -> 23.4 us  [the longest x1 12.6 us: segment_rows(): pl.pallas_call(segment_kernel, grid=(width // block,), in_specs=[pl.Block...]
    ppermute x1 -> x15, waiting for transfers between devices: 0.01 us -> 15.6 us  [the longest x3 5.69 us: scattered_sums(): lax.ppermute(to_left, 'tm', [(2 * z + x, 2 * z - 2 + x) for z in range(ma...]
    concatenate x2 -> x0, local copies, waits for them, and re-layouts: 11.4 us -> none  [the longest x1 10.8 us: stack_lags(): return jnp.concatenate(pieces, axis=1)]
    dot_general x1 -> x0, matrix products: 9.48 us -> none  [local(): lax.dot_general(toeplitz, extended, (((0,), (0,)), ((), ())), preferred_e...]
  transfers between devices with their start and end apart: 3 -> 17, of which waited for: 2 -> 6; matrix products, arithmetic and copies ran while one was open for 21% -> 15% of each run, Pallas kernels for 0% -> 23%
where the time goes in v1:
time: 103 us
  starting transfers between devices  34.4 us (33%)
  Pallas kernels  23.4 us (23%)
  waiting for transfers between devices  15.6 us (15%)
  local copies, waits for them, and re-layouts  11.4 us (11%)
  other arithmetic  11 us (11%)
  between operations  6.63 us (6%)
    ppermute x3, starting transfers between devices, scattered_sums(): lax.ppermute(to_right, 'tm', [(2 * z + x, 2 * z + 2 + x) for z in range(m...  13.8 us
    pallas_call x1, Pallas kernels, segment_rows(): pl.pallas_call(segment_kernel, grid=(width // block,), in_specs=[pl.Block...  12.6 us
    pallas_call x2, Pallas kernels, lag_products(): pl.pallas_call(lag_products_kernel, grid_spec=pltpu.PrefetchScalarGridSpe...  10.8 us
    ppermute x9, starting transfers between devices, exchanged(): lax.ppermute(value, axis, [(source, source ^ bit) for source in range(cou...  10.8 us
    ppermute x2, starting transfers between devices, passed_along(): lax.ppermute(value, axis, [(source, source + steps) for source in range(i...  5.69 us
    ppermute x3, waiting for transfers between devices, scattered_sums(): lax.ppermute(to_left, 'tm', [(2 * z + x, 2 * z - 2 + x) for z in range(ma...  5.69 us
    ppermute x9, waiting for transfers between devices, exchanged(): lax.ppermute(value, axis, [(source, source ^ bit) for source in range(cou...  5.23 us
    ppermute x3, waiting for transfers between devices, scattered_sums(): lax.ppermute(to_right, 'tm', [(2 * z + x, 2 * z + 2 + x) for z in range(m...  4.64 us
  transfers between devices with their start and end apart: 17, of which 6 were waited for; matrix products, arithmetic and copies ran while one was open for 15% of the time, Pallas kernels for 23%

profile of v1, /device:TPU:0, one launch (start us, length us, event | category | flops | bytes accessed | tf_op | source)
XLA Modules:
  0.0 102.5 jit_solution(13677050230185616148)
XLA Ops:
  0.6 1.1 %slice.52 = bf16[2048,32]{1,0:T(8,128)(2,1)S(1)} slice(bf16[2048,1024]{1,0:T(8,128)(2,1)} %strain.5), slice={[0:2048], [0:32]} | slice | bytes 262144 | tf_op jit(solution)/shard_map/slice | solution.py:175
  1.7 0.2 copy.10
  1.9 0.5 collective-permute-start
  2.4 4.4 %collective-permute-start.1 = (bf16[32,128]{1,0:T(8,128)(2,1)S(1)}, bf16[32,128]{1,0:T(8,128)(2,1)S(1)}, u32[]{:S(2)}, u32[]{:S(2)}) collective-permute-start(bf16[32,128]{1,0:T(8,128)(2,1)S(1)} %slice.69), channel_id=1, source_target_pairs={{0,2},{2,4},{4,6},{6,8},{8,10},{10,12},{12,14},{1,3},{3,5},{5,7},{... | collective-permute-start | bytes 24584 | tf_op jit(solution)/shard_map/ppermute | solution.py:22
  6.8 0.8 slice.65
  7.6 1.3 %collective-permute-start.16 = (bf16[16,1024]{1,0:T(8,128)(2,1)S(1)}, bf16[16,1024]{1,0:T(8,128)(2,1)S(1)}, u32[]{:S(2)}, u32[]{:S(2)}) collective-permute-start(bf16[16,1024]{1,0:T(8,128)(2,1)S(1)} %slice.65), channel_id=1, source_target_pairs={{2,0},{4,2},{6,4},{8,6},{10,8},{12,10},{14,12},{3,1},{5,3},{7,5},{... | collective-permute-start | bytes 98312 | tf_op jit(solution)/shard_map/ppermute | solution.py:22
  8.9 3.1 %multiply_reduce_fusion = f32[1024]{0:T(1024)S(1)} fusion(bf16[2048,1024]{1,0:T(8,128)(2,1)} %strain.5), kind=kLoop, calls=%fused_computation.1 | loop fusion | flops 6290432 | bytes 4198400 | tf_op jit(solution)/shard_map/reduce_sum | solution.py:195
  12.0 0.7 constant_dynamic-slice_fusion
  12.7 0.1 slice_bitcast_fusion.3.order
  12.8 0.0 collective-permute-done.1.halo_own
  12.8 0.3 collective-permute-start.2
  13.1 0.1 pad_add_fusion.place
  13.2 0.9 collective-permute-done.2.halo_other
  14.1 0.0 collective-permute-done.other
  14.1 2.2 %copy-done = bf16[2048,1024]{1,0:T(8,128)(2,1)S(1)} copy-done((bf16[2048,1024]{1,0:T(8,128)(2,1)S(1)}, bf16[2048,1024]{1,0:T(8,128)(2,1)}, u32[]{:S(2)}) %copy-start) | copy-done | bytes 4194328
  16.3 3.0 %lag_products.3 = (f32[1,128,1024]{2,1,0:T(8,128)S(1)}, f32[1,128,1024]{2,1,0:T(8,128)S(1)}) custom-call(s32[2]{0:T(128)S(1)} %pad_add_fusion.place, s32[1]{0:T(128)S(1)} %bitcast.62, bf16[2048,1024]{1,0:T(8,128)(2,1)S(1)} %copy-done, bf16[32,2048]{1,0:T(8,128)(2,1)S(1)} %bitcast.60, bf16[32,2048]{1,0:T(8,128)(2,1)S(1)} %collective-permute-done.other, ...), custom_call_target="tpu_custom_call" | custom-call | flops 1073741824 | bytes 5242880 | tf_op jit(solution)/shard_map/lag_products/pallas_call | solution.py:67
  19.3 2.7 %collective-permute-start.4 = (f32[128,1024]{1,0:T(8,128)S(1)}, f32[128,1024]{1,0:T(8,128)S(1)}, u32[]{:S(2)}, u32[]{:S(2)}) collective-permute-start(f32[128,1024]{1,0:T(8,128)S(1)} %bitcast.63), channel_id=1, source_target_pairs={{0,2},{2,0},{4,6},{6,4},{8,10},{10,8},{12,14},{14,12},{1,3},{3,1},... | collective-permute-start | bytes 1572872 | tf_op jit(solution)/shard_map/ppermute | solution.py:27
  22.0 7.8 %lag_products.2 = (f32[3,128,1024]{2,1,0:T(8,128)S(1)}, f32[3,128,1024]{2,1,0:T(8,128)S(1)}) custom-call(s32[2]{0:T(128)S(1)} %pad_add_fusion.place, s32[3]{0:T(128)S(1)} %slice_bitcast_fusion.3.order, bf16[2048,1024]{1,0:T(8,128)(2,1)} %strain.5, bf16[32,2048]{1,0:T(8,128)(2,1)S(1)} %bitcast.61, bf16[32,2048]{1,0:T(8,128)(2,1)S(1)} %collective-permute-done.other, ...), custom_call_target="tpu_custom_call" | custom-call | flops 3221225472 | bytes 7340032 | tf_op jit(solution)/shard_map/lag_products/pallas_call | solution.py:67
  29.7 1.2 %slice_bitcast_fusion.2 = (f32[128,1024]{1,0:T(8,128)}, f32[128,1024]{1,0:T(8,128)}, f32[128,1024]{1,0:T(8,128)}) fusion(f32[3,128,1024]{2,1,0:T(8,128)S(1)} %get-tuple-element.7), kind=kLoop, calls=%fused_computation.30 | loop fusion | bytes 3145728 | tf_op jit(solution)/shard_map/squeeze | solution.py:212
  30.9 0.0 collective-permute-start.5
  30.9 0.1 multiply_reduce_fusion.1
  31.1 2.1 %collective-permute-start.13 = (f32[1056]{0:T(1024)S(1)}, f32[1056]{0:T(1024)S(1)}, u32[]{:S(2)}, u32[]{:S(2)}) collective-permute-start(f32[1056]{0:T(1024)S(1)} %pad_maximum_fusion), channel_id=1, source_target_pairs={{0,2},{2,0},{4,6},{6,4},{8,10},{10,8},{12,14},{14,12},{1,3},{3,1},... | collective-permute-start | bytes 12680 | tf_op jit(solution)/shard_map/ppermute | solution.py:27
  33.2 1.5 %collective-permute-done.4 = f32[128,1024]{1,0:T(8,128)S(1)} collective-permute-done((f32[128,1024]{1,0:T(8,128)S(1)}, f32[128,1024]{1,0:T(8,128)S(1)}, u32[]{:S(2)}, u32[]{:S(2)}) %collective-permute-start.4) | collective-permute-done | bytes 524320 | tf_op jit(solution)/shard_map/ppermute | solution.py:27
  34.7 0.1 bitcast_add_fusion.1
  34.7 1.5 %collective-permute-start.10 = (f32[128,1024]{1,0:T(8,128)S(1)}, f32[128,1024]{1,0:T(8,128)}, u32[]{:S(2)}, u32[]{:S(2)}) collective-permute-start(f32[128,1024]{1,0:T(8,128)S(1)} %bitcast_add_fusion.1), channel_id=1, source_target_pairs={{12,8},{14,10},{13,9},{15,11},{28,24},{30,26},{29,25},{31,27}} | collective-permute-start | bytes 1572872 | tf_op jit(solution)/shard_map/ppermute | solution.py:156
  36.2 5.7 %collective-permute-start.7 = (f32[128,1024]{1,0:T(8,128)S(1)}, f32[128,1024]{1,0:T(8,128)}, u32[]{:S(2)}, u32[]{:S(2)}) collective-permute-start(f32[128,1024]{1,0:T(8,128)S(1)} %bitcast_add_fusion.1), channel_id=1, source_target_pairs={{0,4},{2,6},{1,5},{3,7},{16,20},{18,22},{17,21},{19,23}} | collective-permute-start | bytes 1572872 | tf_op jit(solution)/shard_map/ppermute | solution.py:153
  42.0 0.0 copy-done.4
  42.0 0.6 dynamic_slice.37
  43.8 0.0 copy-done.3
  43.9 0.7 dynamic_slice.41
  45.8 0.0 copy-done.2
  45.8 0.6 dynamic_slice.39
  49.6 0.0 collective-permute-done.13
  49.6 0.1 collective-permute-start.14
  49.7 0.0 collective-permute-done.16.tail
  49.7 0.0 copy-start.1
  49.7 2.2 %copy-done.1 = bf16[2048,1024]{1,0:T(8,128)(2,1)S(1)} copy-done((bf16[2048,1024]{1,0:T(8,128)(2,1)S(1)}, bf16[2048,1024]{1,0:T(8,128)(2,1)}, u32[]{:S(2)}) %copy-start.1) | copy-done | bytes 4194328
  51.9 12.6 %segment_rows.1 = f32[16,1024]{1,0:T(8,128)S(1)} custom-call(bf16[2048,1024]{1,0:T(8,128)(2,1)S(1)} %copy-done.1, bf16[16,1024]{1,0:T(8,128)(2,1)S(1)} %collective-permute-done.16.tail), custom_call_target="tpu_custom_call" | custom-call | flops 67108864 | bytes 4194304 | tf_op jit(solution)/shard_map/segment_rows/pallas_call | solution.py:111
  64.5 0.7 collective-permute-start.6
  65.2 0.0 collective-permute-done.14
  65.2 1.4 %collective-permute-start.3 = (f32[128,1024]{1,0:T(8,128)}, f32[128,1024]{1,0:T(8,128)}, u32[]{:S(2)}, u32[]{:S(2)}) collective-permute-start(f32[128,1024]{1,0:T(8,128)} %get-tuple-element.12), channel_id=1, source_target_pairs={{0,2},{2,0},{4,6},{6,4},{8,10},{10,8},{12,14},{14,12},{1,3},{3,1},... | collective-permute-start | bytes 1572872 | tf_op jit(solution)/shard_map/ppermute | solution.py:27
  66.6 0.0 collective-permute-done.5
  66.6 3.0 %collective-permute-start.15 = (f32[1056]{0:T(1024)S(1)}, f32[1056]{0:T(1024)S(1)}, u32[]{:S(2)}, u32[]{:S(2)}) collective-permute-start(f32[1056]{0:T(1024)S(1)} %add.142), channel_id=1, source_target_pairs={{0,8},{2,10},{4,12},{6,14},{8,0},{10,2},{12,4},{14,6},{1,9},{3,11}... | collective-permute-start | bytes 12680 | tf_op jit(solution)/shard_map/ppermute | solution.py:27
  69.7 0.1 fusion.10
  69.7 0.0 collective-permute-done.10
  69.7 0.0 collective-permute-done.7
  69.7 2.5 %fusion.5 = (f32[128,1024]{1,0:T(8,128)}, f32[128,1024]{1,0:T(8,128)}) fusion(f32[128,1024]{1,0:T(8,128)} %collective-permute-done.7, s32[]{:T(128)S(6)} %select_n.82, f32[1,128,1024]{2,1,0:T(8,128)S(1)} %bitcast.64, f32[1,128,1024]{2,1,0:T(8,128)S(1)} %fusion.10, f32[128,1024]{1,0:T(8,128)} %collective-permute-done.10, s32[]{:T(128)S(6)} %select_n.84), kind=kLoop, calls=%fused_computation.14 | loop fusion | flops 524288 | bytes 3145736 | tf_op jit(solution)/shard_map/add | solution.py:151
  72.2 1.9 %collective-permute-start.8 = (f32[128,1024]{1,0:T(8,128)}, f32[128,1024]{1,0:T(8,128)S(1)}, u32[]{:S(2)}, u32[]{:S(2)}) collective-permute-start(f32[128,1024]{1,0:T(8,128)} %get-tuple-element.15), channel_id=1, source_target_pairs={{0,4},{2,6},{4,8},{6,10},{1,5},{3,7},{5,9},{7,11},{16,20},{18,22},... | collective-permute-start | bytes 1572872 | tf_op jit(solution)/shard_map/ppermute | solution.py:153
  74.2 0.0 collective-permute-done.15
  74.2 1.5 %collective-permute-start.11 = (f32[128,1024]{1,0:T(8,128)}, f32[128,1024]{1,0:T(8,128)}, u32[]{:S(2)}, u32[]{:S(2)}) collective-permute-start(f32[128,1024]{1,0:T(8,128)} %get-tuple-element.16), channel_id=1, source_target_pairs={{8,4},{10,6},{12,8},{14,10},{9,5},{11,7},{13,9},{15,11},{24,20},{2... | collective-permute-start | bytes 1572872 | tf_op jit(solution)/shard_map/ppermute | solution.py:156
  75.7 0.1 broadcast_select_fusion
  75.8 1.2 %gather_fusion = f32[128]{0:T(128)S(1)} fusion(f32[64]{0:T(128)S(1)} %broadcast_select_fusion, s32[1024]{0:T(1024)S(1)} %pad_clamp_fusion), kind=kCustom, calls=%fused_computation | custom fusion | bytes 1536 | tf_op jit(solution)/shard_map/gather | solution.py:224
  77.0 2.8 %collective-permute-done.6 = f32[128,1024]{1,0:T(8,128)} collective-permute-done((f32[128,1024]{1,0:T(8,128)}, f32[128,1024]{1,0:T(8,128)}, u32[]{:S(2)}, u32[]{:S(2)}) %collective-permute-start.6) | collective-permute-done | bytes 524320 | tf_op jit(solution)/shard_map/ppermute | solution.py:27
  79.8 3.5 %collective-permute-done.8 = f32[128,1024]{1,0:T(8,128)S(1)} collective-permute-done((f32[128,1024]{1,0:T(8,128)}, f32[128,1024]{1,0:T(8,128)S(1)}, u32[]{:S(2)}, u32[]{:S(2)}) %collective-permute-start.8) | collective-permute-done | bytes 524320 | tf_op jit(solution)/shard_map/ppermute | solution.py:153
  83.2 1.2 %fusion.15 = (f32[128,1024]{1,0:T(8,128)S(1)}, f32[1,128,1024]{2,1,0:T(8,128)S(1)}) fusion(f32[128,1024]{1,0:T(8,128)S(1)} %collective-permute-done.8, f32[128,1024]{1,0:T(8,128)} %collective-permute-done.6, f32[3,128,1024]{2,1,0:T(8,128)S(1)} %get-tuple-element.6), kind=kLoop, calls=%fused_computation.32 | loop fusion | flops 262144 | bytes 2621440 | tf_op jit(solution)/shard_map/add | solution.py:151
  84.4 0.0 collective-permute-done.11
  84.4 1.2 %fusion.9 = f32[128,1024]{1,0:T(8,128)S(1)} fusion(f32[128,1024]{1,0:T(8,128)} %collective-permute-done.11, s32[]{:T(128)S(6)} %select_n.83, f32[1,128,1024]{2,1,0:T(8,128)S(1)} %bitcast.65, f32[1,128,1024]{2,1,0:T(8,128)S(1)} %fusion.10, f32[1,128,1024]{2,1,0:T(8,128)S(1)} %get-tuple-element.11), kind=kLoop, calls=%fused_computation.18 | loop fusion | flops 393216 | bytes 2621444 | tf_op jit(solution)/shard_map/add | solution.py:152
  85.6 1.3 %collective-permute-start.12 = (f32[128,1024]{1,0:T(8,128)S(1)}, f32[128,1024]{1,0:T(8,128)S(1)}, u32[]{:S(2)}, u32[]{:S(2)}) collective-permute-start(f32[128,1024]{1,0:T(8,128)S(1)} %fusion.9), channel_id=1, source_target_pairs={{4,0},{6,2},{8,4},{10,6},{12,8},{14,10},{5,1},{7,3},{9,5},{11,7},{... | collective-permute-start | bytes 1572872 | tf_op jit(solution)/shard_map/ppermute | solution.py:156
  86.9 6.1 %collective-permute-start.9 = (f32[128,1024]{1,0:T(8,128)S(1)}, f32[128,1024]{1,0:T(8,128)S(1)}, u32[]{:S(2)}, u32[]{:S(2)}) collective-permute-start(f32[128,1024]{1,0:T(8,128)S(1)} %get-tuple-element.10), channel_id=1, source_target_pairs={{0,4},{2,6},{4,8},{6,10},{8,12},{10,14},{1,5},{3,7},{5,9},{7,11},{... | collective-permute-start | bytes 1572872 | tf_op jit(solution)/shard_map/ppermute | solution.py:153
  93.1 0.6 multiply_multiply_fusion
  93.7 0.0 collective-permute-done.3
  93.7 5.7 %collective-permute-done.12 = f32[128,1024]{1,0:T(8,128)S(1)} collective-permute-done((f32[128,1024]{1,0:T(8,128)S(1)}, f32[128,1024]{1,0:T(8,128)S(1)}, u32[]{:S(2)}, u32[]{:S(2)}) %collective-permute-start.12) | collective-permute-done | bytes 524320 | tf_op jit(solution)/shard_map/ppermute | solution.py:156
  99.4 1.2 %collective-permute-done.9 = f32[128,1024]{1,0:T(8,128)S(1)} collective-permute-done((f32[128,1024]{1,0:T(8,128)S(1)}, f32[128,1024]{1,0:T(8,128)S(1)}, u32[]{:S(2)}, u32[]{:S(2)}) %collective-permute-start.9) | collective-permute-done | bytes 524320 | tf_op jit(solution)/shard_map/ppermute | solution.py:153
  100.6 2.0 %fusion.14 = f32[128,1024]{1,0:T(8,128)} fusion(f32[128,1024]{1,0:T(8,128)S(1)} %collective-permute-done.12, f32[128,1024]{1,0:T(8,128)S(1)} %collective-permute-done.9, f32[128,1024]{1,0:T(8,128)} %collective-permute-done.3, f32[3,128,1024]{2,1,0:T(8,128)S(1)} %get-tuple-element.6, f32[128]{0:T(128)S(1)} %convert_divide_fusion, f32[1024]{0:T(1024)S(1)} %get-tuple-element.18), kind=kLoop, calls=%fused_computation.27 | loop fusion | flops 655360 | bytes 2626048 | tf_op jit(solution)/shard_map/mul | solution.py:225
  (14 shorter events, 0.1 us)
Async XLA Ops:
  1.9 12.2 %collective-permute-start = (bf16[32,2048]{1,0:T(8,128)(2,1)S(1)}, bf16[32,2048]{1,0:T(8,128)(2,1)S(1)}, u32[]{:S(2)}, u32[]{:S(2)}) collective-permute-start(bf16[32,2048]{1,0:T(8,128)(2,1)S(1)} %bitcast.58), channel_id=1, source_target_pairs={{0,1},{1,0},{2,3},{3,2},{4,5},{5,4},{6,7},{7,6},{8,9},{9,8},{10,11... | collective-permute-start | bytes 393224 | tf_op jit(solution)/shard_map/ppermute | solution.py:27
  2.4 10.4 %collective-permute-start.1 = (bf16[32,128]{1,0:T(8,128)(2,1)S(1)}, bf16[32,128]{1,0:T(8,128)(2,1)S(1)}, u32[]{:S(2)}, u32[]{:S(2)}) collective-permute-start(bf16[32,128]{1,0:T(8,128)(2,1)S(1)} %slice.69), channel_id=1, source_target_pairs={{0,2},{2,4},{4,6},{6,8},{8,10},{10,12},{12,14},{1,3},{3,5},{5,7},{... | collective-permute-start | bytes 24584 | tf_op jit(solution)/shard_map/ppermute | solution.py:22
  7.6 42.1 %collective-permute-start.16 = (bf16[16,1024]{1,0:T(8,128)(2,1)S(1)}, bf16[16,1024]{1,0:T(8,128)(2,1)S(1)}, u32[]{:S(2)}, u32[]{:S(2)}) collective-permute-start(bf16[16,1024]{1,0:T(8,128)(2,1)S(1)} %slice.65), channel_id=1, source_target_pairs={{2,0},{4,2},{6,4},{8,6},{10,8},{12,10},{14,12},{3,1},{5,3},{7,5},{... | collective-permute-start | bytes 98312 | tf_op jit(solution)/shard_map/ppermute | solution.py:22
  12.8 1.2 %collective-permute-start.2 = (bf16[32,128]{1,0:T(8,128)(2,1)S(1)}, bf16[32,128]{1,0:T(8,128)(2,1)S(1)}, u32[]{:S(2)}, u32[]{:S(2)}) collective-permute-start(bf16[32,128]{1,0:T(8,128)(2,1)S(1)} %collective-permute-done.1.halo_own), channel_id=1, source_target_pairs={{0,1},{1,0},{2,3},{3,2},{4,5},{5,4},{6,7},{7,6},{8,9},{9,8},{10,11... | collective-permute-start | bytes 24584 | tf_op jit(solution)/shard_map/ppermute | solution.py:27
  14.1 2.2 %copy-start = (bf16[2048,1024]{1,0:T(8,128)(2,1)S(1)}, bf16[2048,1024]{1,0:T(8,128)(2,1)}, u32[]{:S(2)}) copy-start(bf16[2048,1024]{1,0:T(8,128)(2,1)} %strain.5) | copy-start | bytes 12582916
  19.3 15.4 %collective-permute-start.4 = (f32[128,1024]{1,0:T(8,128)S(1)}, f32[128,1024]{1,0:T(8,128)S(1)}, u32[]{:S(2)}, u32[]{:S(2)}) collective-permute-start(f32[128,1024]{1,0:T(8,128)S(1)} %bitcast.63), channel_id=1, source_target_pairs={{0,2},{2,0},{4,6},{6,4},{8,10},{10,8},{12,14},{14,12},{1,3},{3,1},... | collective-permute-start | bytes 1572872 | tf_op jit(solution)/shard_map/ppermute | solution.py:27
  30.9 11.0 %copy-start.4 = (s32[4]{0:T(128)S(1)}, s32[4]{0:T(128)}, u32[]{:S(2)}) copy-start(s32[4]{0:T(128)} %constant.111.clone) | copy-start | bytes 52
  30.9 12.9 %copy-start.3 = (s32[4]{0:T(128)S(1)}, s32[4]{0:T(128)}, u32[]{:S(2)}) copy-start(s32[4]{0:T(128)} %constant.112.clone) | copy-start | bytes 52
  30.9 14.8 %copy-start.2 = (s32[4]{0:T(128)S(1)}, s32[4]{0:T(128)}, u32[]{:S(2)}) copy-start(s32[4]{0:T(128)} %constant.114.clone) | copy-start | bytes 52
  30.9 35.7 %collective-permute-start.5 = (f32[128,1024]{1,0:T(8,128)}, f32[128,1024]{1,0:T(8,128)S(1)}, u32[]{:S(2)}, u32[]{:S(2)}) collective-permute-start(f32[128,1024]{1,0:T(8,128)} %get-tuple-element.14), channel_id=1, source_target_pairs={{0,2},{2,0},{4,6},{6,4},{8,10},{10,8},{12,14},{14,12},{1,3},{3,1},... | collective-permute-start | bytes 1572872 | tf_op jit(solution)/shard_map/ppermute | solution.py:27
  31.1 18.5 %collective-permute-start.13 = (f32[1056]{0:T(1024)S(1)}, f32[1056]{0:T(1024)S(1)}, u32[]{:S(2)}, u32[]{:S(2)}) collective-permute-start(f32[1056]{0:T(1024)S(1)} %pad_maximum_fusion), channel_id=1, source_target_pairs={{0,2},{2,0},{4,6},{6,4},{8,10},{10,8},{12,14},{14,12},{1,3},{3,1},... | collective-permute-start | bytes 12680 | tf_op jit(solution)/shard_map/ppermute | solution.py:27
  34.7 35.0 %collective-permute-start.10 = (f32[128,1024]{1,0:T(8,128)S(1)}, f32[128,1024]{1,0:T(8,128)}, u32[]{:S(2)}, u32[]{:S(2)}) collective-permute-start(f32[128,1024]{1,0:T(8,128)S(1)} %bitcast_add_fusion.1), channel_id=1, source_target_pairs={{12,8},{14,10},{13,9},{15,11},{28,24},{30,26},{29,25},{31,27}} | collective-permute-start | bytes 1572872 | tf_op jit(solution)/shard_map/ppermute | solution.py:156
  36.2 33.5 %collective-permute-start.7 = (f32[128,1024]{1,0:T(8,128)S(1)}, f32[128,1024]{1,0:T(8,128)}, u32[]{:S(2)}, u32[]{:S(2)}) collective-permute-start(f32[128,1024]{1,0:T(8,128)S(1)} %bitcast_add_fusion.1), channel_id=1, source_target_pairs={{0,4},{2,6},{1,5},{3,7},{16,20},{18,22},{17,21},{19,23}} | collective-permute-start | bytes 1572872 | tf_op jit(solution)/shard_map/ppermute | solution.py:153
  49.6 15.6 %collective-permute-start.14 = (f32[1056]{0:T(1024)S(1)}, f32[1056]{0:T(1024)S(1)}, u32[]{:S(2)}, u32[]{:S(2)}) collective-permute-start(f32[1056]{0:T(1024)S(1)} %fusion.19), channel_id=1, source_target_pairs={{0,4},{2,6},{4,0},{6,2},{8,12},{10,14},{12,8},{14,10},{1,5},{3,7},... | collective-permute-start | bytes 12680 | tf_op jit(solution)/shard_map/ppermute | solution.py:27
  49.7 2.2 %copy-start.1 = (bf16[2048,1024]{1,0:T(8,128)(2,1)S(1)}, bf16[2048,1024]{1,0:T(8,128)(2,1)}, u32[]{:S(2)}) copy-start(bf16[2048,1024]{1,0:T(8,128)(2,1)} %strain.5) | copy-start | bytes 12582916
  64.5 15.2 %collective-permute-start.6 = (f32[128,1024]{1,0:T(8,128)}, f32[128,1024]{1,0:T(8,128)}, u32[]{:S(2)}, u32[]{:S(2)}) collective-permute-start(f32[128,1024]{1,0:T(8,128)} %get-tuple-element.13), channel_id=1, source_target_pairs={{0,2},{2,0},{4,6},{6,4},{8,10},{10,8},{12,14},{14,12},{1,3},{3,1},... | collective-permute-start | bytes 1572872 | tf_op jit(solution)/shard_map/ppermute | solution.py:27
  65.2 28.5 %collective-permute-start.3 = (f32[128,1024]{1,0:T(8,128)}, f32[128,1024]{1,0:T(8,128)}, u32[]{:S(2)}, u32[]{:S(2)}) collective-permute-start(f32[128,1024]{1,0:T(8,128)} %get-tuple-element.12), channel_id=1, source_target_pairs={{0,2},{2,0},{4,6},{6,4},{8,10},{10,8},{12,14},{14,12},{1,3},{3,1},... | collective-permute-start | bytes 1572872 | tf_op jit(solution)/shard_map/ppermute | solution.py:27
  66.6 7.5 %collective-permute-start.15 = (f32[1056]{0:T(1024)S(1)}, f32[1056]{0:T(1024)S(1)}, u32[]{:S(2)}, u32[]{:S(2)}) collective-permute-start(f32[1056]{0:T(1024)S(1)} %add.142), channel_id=1, source_target_pairs={{0,8},{2,10},{4,12},{6,14},{8,0},{10,2},{12,4},{14,6},{1,9},{3,11}... | collective-permute-start | bytes 12680 | tf_op jit(solution)/shard_map/ppermute | solution.py:27
  72.2 11.0 %collective-permute-start.8 = (f32[128,1024]{1,0:T(8,128)}, f32[128,1024]{1,0:T(8,128)S(1)}, u32[]{:S(2)}, u32[]{:S(2)}) collective-permute-start(f32[128,1024]{1,0:T(8,128)} %get-tuple-element.15), channel_id=1, source_target_pairs={{0,4},{2,6},{4,8},{6,10},{1,5},{3,7},{5,9},{7,11},{16,20},{18,22},... | collective-permute-start | bytes 1572872 | tf_op jit(solution)/shard_map/ppermute | solution.py:153
  74.2 10.2 %collective-permute-start.11 = (f32[128,1024]{1,0:T(8,128)}, f32[128,1024]{1,0:T(8,128)}, u32[]{:S(2)}, u32[]{:S(2)}) collective-permute-start(f32[128,1024]{1,0:T(8,128)} %get-tuple-element.16), channel_id=1, source_target_pairs={{8,4},{10,6},{12,8},{14,10},{9,5},{11,7},{13,9},{15,11},{24,20},{2... | collective-permute-start | bytes 1572872 | tf_op jit(solution)/shard_map/ppermute | solution.py:156
  85.6 13.7 %collective-permute-start.12 = (f32[128,1024]{1,0:T(8,128)S(1)}, f32[128,1024]{1,0:T(8,128)S(1)}, u32[]{:S(2)}, u32[]{:S(2)}) collective-permute-start(f32[128,1024]{1,0:T(8,128)S(1)} %fusion.9), channel_id=1, source_target_pairs={{4,0},{6,2},{8,4},{10,6},{12,8},{14,10},{5,1},{7,3},{9,5},{11,7},{... | collective-permute-start | bytes 1572872 | tf_op jit(solution)/shard_map/ppermute | solution.py:156
  86.9 13.6 %collective-permute-start.9 = (f32[128,1024]{1,0:T(8,128)S(1)}, f32[128,1024]{1,0:T(8,128)S(1)}, u32[]{:S(2)}, u32[]{:S(2)}) collective-permute-start(f32[128,1024]{1,0:T(8,128)S(1)} %get-tuple-element.10), channel_id=1, source_target_pairs={{0,4},{2,6},{4,8},{6,10},{8,12},{10,14},{1,5},{3,7},{5,9},{7,11},{... | collective-permute-start | bytes 1572872 | tf_op jit(solution)/shard_map/ppermute | solution.py:153

commit v2 on v0

v2 whole, which is shorter than its diff:
```python
import jax
import jax.numpy as jnp
from jax import lax
from jax.experimental import pallas as pl
from jax.experimental.pallas import tpu as pltpu
from jax.sharding import PartitionSpec as P

LAGS = 16
REF = 64
HALF = REF // 2
HALO = 128
LANES = 128
GROUP = 4
POWER = 16
CODE_SCALE = 2.0 ** (126 / POWER)
TINY = 1e-35
VMEM_BYTES = 48 * 1024 * 1024


def passed_along(value, axis, steps):
    count = lax.axis_size(axis)
    initial, last = (max(0, -steps), min(count, count - steps))
    return lax.ppermute(value, axis, [(source, source + steps) for source in range(initial, last)])


def exchanged(value, axis, bit):
    count = lax.axis_size(axis)
    return lax.ppermute(value, axis, [(source, source ^ bit) for source in range(count)])


def passed_across(value):
    count = lax.axis_size("tm")
    route = [(2 * t + c, 2 * t + 2 + (1 - c)) for t in range(count - 1) for c in range(2)]
    return lax.ppermute(value, ("tm", "chan"), route)


def as_column(row):
    size = row.shape[1]
    eye = lax.broadcasted_iota(jnp.int32, (size, size), 0) == lax.broadcasted_iota(jnp.int32, (size, size), 1)
    return jnp.sum(jnp.where(eye, row, 0.0), axis=1, keepdims=True)


def as_row(column):
    size = column.shape[0]
    eye = lax.broadcasted_iota(jnp.int32, (size, size), 0) == lax.broadcasted_iota(jnp.int32, (size, size), 1)
    return jnp.sum(jnp.where(eye, column, 0.0), axis=0, keepdims=True)


def for_chunk(ref_column, rows):
    return jnp.concatenate([ref_column] * (rows // REF), axis=0)


def bounds(powers):
    return (
        jnp.maximum(powers[0:1, :], TINY),
        jnp.maximum(as_column(powers[2:3, :LANES])[:REF], TINY),
    )


def coded(values, channel_bound, ref_bound):
    ref_column = for_chunk(lax.rsqrt(ref_bound) * CODE_SCALE, values.shape[0])
    power = values * lax.rsqrt(channel_bound) * ref_column
    for _ in range(4):
        power = power * jnp.abs(power)
    return power.astype(jnp.bfloat16)


def expanded(code, channel_bound, ref_bound):
    wide = code.astype(jnp.float32)
    root = jnp.exp2(jnp.log2(jnp.abs(wide)) * (1.0 / POWER))
    ref_column = for_chunk(jnp.sqrt(ref_bound) * (1.0 / CODE_SCALE), code.shape[0])
    return jnp.where(wide < 0.0, -root, root) * jnp.sqrt(channel_bound) * ref_column


def lag_rows(own, other, halo_own, halo_other, chan, first_lag, shifted):
    rows = own.shape[1]
    for refs, halo, half in ((own, halo_own, chan), (other, halo_other, 1 - chan)):
        long = jnp.concatenate([halo[...], refs[...]], axis=1).astype(jnp.float32)
        for index in range(GROUP):
            moved = pltpu.roll(long, first_lag + index, 1)[:, HALO:]
            start = pl.multiple_of(index * REF + half * HALF, HALF)
            shifted[pl.ds(start, HALF), :] = moved.astype(jnp.bfloat16)


def ref_powers(refs, halo):
    squares = jnp.square(refs[...].astype(jnp.float32))
    lane = lax.broadcasted_iota(jnp.int32, (1, HALO), 1)
    edge = jnp.where(lane > HALO - LAGS, jnp.square(halo[...].astype(jnp.float32)), 0.0)
    inside = jnp.sum(squares, axis=1, keepdims=True)
    return inside, inside + jnp.sum(edge, axis=1, keepdims=True)


def first_products_kernel(place, power, strain, own, other, halo_own, halo_other, keep, send, powers, shifted):
    chan, group, near = place[0], place[1], place[2]
    lag_rows(own, other, halo_own, halo_other, chan, group * GROUP, shifted)
    ours = ref_powers(own, halo_own)
    theirs = ref_powers(other, halo_other)
    columns = [
        jnp.where(chan == 0, jnp.concatenate([a, b], axis=0), jnp.concatenate([b, a], axis=0))
        for a, b in zip(ours, theirs)
    ]
    pad = jnp.zeros((1, power.shape[1] - REF), jnp.float32)
    rows = [jnp.concatenate([as_row(column), pad], axis=1) for column in columns]
    powers[...] = jnp.concatenate(
        [power[...]] + rows + [jnp.zeros((5, power.shape[1]), jnp.float32)], axis=0
    )
    product = jnp.dot(shifted[...], strain[...], preferred_element_type=jnp.float32)
    chunk = keep.shape[0]
    keep[...] = jnp.where(near == 0, product[:chunk], product[chunk:])
    other_half = jnp.where(near == 0, product[chunk:], product[:chunk])
    send[...] = coded(other_half, jnp.maximum(power[...], TINY), jnp.maximum(columns[1], TINY))


def first_products(place, power, strain, own, other, halo_own, halo_other, chunk):
    rows, width = strain.shape
    return pl.pallas_call(
        first_products_kernel,
        in_specs=[pl.BlockSpec(memory_space=pltpu.SMEM)] + [pl.BlockSpec(memory_space=pltpu.VMEM)] * 6,
        out_specs=[pl.BlockSpec(memory_space=pltpu.VMEM)] * 3,
        out_shape=[
            jax.ShapeDtypeStruct((chunk, width), jnp.float32),
            jax.ShapeDtypeStruct((chunk, width), jnp.bfloat16),
            jax.ShapeDtypeStruct((8, width), jnp.float32),
        ],
        scratch_shapes=[pltpu.VMEM((GROUP * REF, rows), jnp.bfloat16)],
        compiler_params=pltpu.CompilerParams(vmem_limit_bytes=VMEM_BYTES),
        cost_estimate=pl.CostEstimate(
            flops=2 * 2 * chunk * rows * width, bytes_accessed=rows * width * 2, transcendentals=0
        ),
        name="first_products",
    )(place, power, strain, own, other, halo_own, halo_other)


def later_products_kernel(place, powers, strain, own, other, halo_own, halo_other, *rest):
    chan, near = place[0], place[2]
    shifted = rest[-1]
    channel_bound, ref_bound = bounds(powers)
    for slot in range((len(rest) - 1) // 2):
        keep, send = rest[2 * slot], rest[2 * slot + 1]
        chunk = keep.shape[0]
        lag_rows(own, other, halo_own, halo_other, chan, place[3 + slot] * GROUP, shifted)
        product = jnp.dot(shifted[...], strain[...], preferred_element_type=jnp.float32)
        keep[...] = jnp.where(near == 0, product[:chunk], product[chunk:])
        other_half = jnp.where(near == 0, product[chunk:], product[:chunk])
        send[...] = coded(other_half, channel_bound, ref_bound)


def later_products(place, powers, strain, own, other, halo_own, halo_other, chunk, slots):
    rows, width = strain.shape
    return pl.pallas_call(
        later_products_kernel,
        in_specs=[pl.BlockSpec(memory_space=pltpu.SMEM)] + [pl.BlockSpec(memory_space=pltpu.VMEM)] * 6,
        out_specs=[pl.BlockSpec(memory_space=pltpu.VMEM)] * (2 * slots),
        out_shape=[
            jax.ShapeDtypeStruct((chunk, width), jnp.float32),
            jax.ShapeDtypeStruct((chunk, width), jnp.bfloat16),
        ]
        * slots,
        scratch_shapes=[pltpu.VMEM((GROUP * REF, rows), jnp.bfloat16)],
        compiler_params=pltpu.CompilerParams(vmem_limit_bytes=VMEM_BYTES),
        cost_estimate=pl.CostEstimate(
            flops=2 * 2 * chunk * slots * rows * width, bytes_accessed=rows * width * 2, transcendentals=0
        ),
        name="later_products",
    )(place, powers, strain, own, other, halo_own, halo_other)


def merge_kernel(powers, keep, *rest):
    total = keep[...]
    out = rest[-1]
    for code, sender in zip(rest[:-1:2], rest[1:-1:2]):
        total = total + expanded(code[...], *bounds(sender))
    out[...] = coded(total, *bounds(powers))


def merged(powers, keep, *received):
    return pl.pallas_call(
        merge_kernel,
        out_shape=jax.ShapeDtypeStruct(keep.shape, jnp.bfloat16),
        compiler_params=pltpu.CompilerParams(vmem_limit_bytes=VMEM_BYTES),
        cost_estimate=pl.CostEstimate(flops=0, bytes_accessed=keep.size * 8, transcendentals=0),
        name="merged",
    )(powers, keep, *received)


def finish_kernel(segment, slab_rows, place, powers, auto, keep, *rest):
    covariance, segment_auto = rest[-2:]
    total = keep[...]
    for code, sender in zip(rest[:-2:2], rest[1:-2:2]):
        total = total + expanded(code[...], *bounds(sender))
    chunk = total.shape[0]
    inverse = 1.0 / jnp.sqrt(powers[0:2, :] / slab_rows + 1e-06)
    scale = inverse[0:1]
    ref_scale = for_chunk(as_column(inverse[1:2, :LANES])[:REF], chunk)
    lag = lax.broadcasted_iota(jnp.int32, (chunk, 1), 0) // REF + place[4] * (chunk // REF)
    denom = (slab_rows - lag).astype(jnp.float32)
    covariance[...] = total * scale * (ref_scale / denom)
    segment_auto[...] = auto[...] * (scale * scale) / segment


def finished(segment, slab_rows, place, powers, auto, keep, *received):
    def kernel(*refs):
        finish_kernel(segment, slab_rows, *refs)

    vmem = pl.BlockSpec(memory_space=pltpu.VMEM)
    return pl.pallas_call(
        kernel,
        in_specs=[pl.BlockSpec(memory_space=pltpu.SMEM)] + [vmem] * (3 + len(received)),
        out_specs=[vmem, vmem],
        out_shape=[
            jax.ShapeDtypeStruct(keep.shape, jnp.float32),
            jax.ShapeDtypeStruct(auto.shape, jnp.float32),
        ],
        compiler_params=pltpu.CompilerParams(vmem_limit_bytes=VMEM_BYTES),
        cost_estimate=pl.CostEstimate(flops=0, bytes_accessed=keep.size * 8, transcendentals=0),
        name="finished",
    )(place, powers, auto, keep, *received)


def segment_kernel(strain, tail, out, wide):
    rows, lanes = strain.shape
    pitch = rows // 8
    for lane in range(0, lanes, LANES):
        wide[:rows, :] = strain[:, lane : lane + LANES].astype(jnp.float32)
        wide[rows:, :] = tail[:, lane : lane + LANES].astype(jnp.float32)
        taken = lambda first: wide[pl.ds(first, 8, stride=pitch), :]

        def step(index, carry):
            window, sums = carry
            window = window + (taken(index + LAGS - 1),)
            sums = tuple(total + window[0] * window[lag] for lag, total in enumerate(sums))
            return window[1:], sums

        window = tuple(taken(first) for first in range(LAGS - 1))
        zero = jnp.zeros((8, LANES), jnp.float32)
        _, sums = lax.fori_loop(0, pitch, step, (window, (zero,) * LAGS), unroll=16)
        out[:, lane : lane + LANES] = jnp.concatenate(
            [jnp.sum(total, axis=0, keepdims=True) for total in sums], axis=0
        )


def segment_rows(strain, tail, first, size):
    rows = strain.shape[0]
    return pl.pallas_call(
        segment_kernel,
        grid=(1,),
        in_specs=[
            pl.BlockSpec((rows, size), lambda index: (0, first)),
            pl.BlockSpec((LAGS, size), lambda index: (0, first)),
        ],
        out_specs=pl.BlockSpec((LAGS, size), lambda index: (0, 0)),
        out_shape=jax.ShapeDtypeStruct((LAGS, size), jnp.float32),
        scratch_shapes=[pltpu.VMEM((rows + LAGS, LANES), jnp.float32)],
        compiler_params=pltpu.CompilerParams(vmem_limit_bytes=VMEM_BYTES),
        cost_estimate=pl.CostEstimate(
            flops=64 * LAGS * rows * size, bytes_accessed=rows * size * 2, transcendentals=0
        ),
        name="segment_rows",
    )(strain, tail)


def all_products_kernel(place, strain, own, other, halo_own, halo_other, out, shifted):
    group = pl.program_id(0)
    lag_rows(own, other, halo_own, halo_other, place[0], group * GROUP, shifted)
    out[...] = jnp.dot(shifted[...], strain[...], preferred_element_type=jnp.float32)


def all_products(place, strain, *refs):
    rows, width = strain.shape
    whole = lambda array: pl.BlockSpec(array.shape, lambda group: (0, 0))
    return pl.pallas_call(
        all_products_kernel,
        grid=(LAGS // GROUP,),
        in_specs=[pl.BlockSpec(memory_space=pltpu.SMEM)] + [whole(array) for array in (strain, *refs)],
        out_specs=pl.BlockSpec((GROUP * REF, width), lambda group: (group, 0)),
        out_shape=jax.ShapeDtypeStruct((LAGS * REF, width), jnp.float32),
        scratch_shapes=[pltpu.VMEM((GROUP * REF, rows), jnp.bfloat16)],
        compiler_params=pltpu.CompilerParams(vmem_limit_bytes=VMEM_BYTES),
        name="all_products",
    )(place, strain, *refs)


def local(strain):
    rows, width = strain.shape
    count = lax.axis_size("tm")
    chan = lax.axis_index("chan").astype(jnp.int32)
    time = lax.axis_index("tm").astype(jnp.int32)
    slab_rows = rows * count
    chunk = LAGS * REF // count
    pair = lax.shift_right_logical(time, 1)

    own = strain[:, :HALF].T
    edge = own[:, rows - HALO :]
    other = exchanged(own, "chan", 1)
    halo_own = passed_along(edge, "tm", 1)
    halo_other = passed_across(edge)
    refs = (own, other, halo_own, halo_other)
    tail = passed_along(strain[:LAGS], "tm", -1)

    wide = strain.astype(jnp.float32)
    power = jnp.sum(wide * wide, axis=0, keepdims=True)

    size = 256
    pieces = [segment_rows(strain, tail, first, size) for first in range(width // size)]
    auto = jnp.concatenate(pieces, axis=1)

    if chunk * 2 == GROUP * REF:
        place = jnp.stack([chan, pair ^ 3, time & 1, pair ^ 2, pair ^ 1, pair])
        keep6, send7, powers0 = first_products(place, power, strain, *refs, chunk)
        got7 = exchanged(send7, "tm", 1)
        near0 = exchanged(powers0, "tm", 1)
        powers1 = powers0 + near0
        near1 = exchanged(powers1, "tm", 2)
        powers2 = powers1 + near1
        near2 = exchanged(powers2, "tm", 4)
        powers3 = powers2 + near2
        keep4, send5, keep2, send3, keep0, send1 = later_products(place, powers0, strain, *refs, chunk, 3)
        got5 = exchanged(send5, "tm", 1)
        got3 = exchanged(send3, "tm", 1)
        got1 = exchanged(send1, "tm", 1)
        got6 = exchanged(merged(powers1, keep6, got7, near0), "tm", 2)
        got4 = exchanged(merged(powers2, keep4, got5, near0, got6, near1), "tm", 4)
        got2 = exchanged(merged(powers1, keep2, got3, near0), "tm", 2)
        place = jnp.stack([chan, chan, chan, chan, time])
        covariance, segment_auto = finished(
            rows, slab_rows, place, powers3, auto, keep0, got1, near0, got2, near1, got4, near2
        )
        return (covariance, segment_auto)

    place = jnp.stack([chan, time])
    power_other = jnp.sum(jnp.square(other.astype(jnp.float32)), axis=1)
    power = lax.psum(jnp.concatenate([power[0], power_other]), "tm")
    inv = 1.0 / jnp.sqrt(power / slab_rows + 1e-06)
    scale = inv[:width]
    ref_scale = jnp.where(
        chan == 0,
        jnp.concatenate([inv[:HALF], inv[width:]]),
        jnp.concatenate([inv[width:], inv[:HALF]]),
    )
    products = all_products(place, strain, *refs)
    summed = lax.psum_scatter(products, "tm", scatter_dimension=0, tiled=True)
    row = time * chunk + jnp.arange(chunk, dtype=jnp.int32)
    row_scale = ref_scale[row % REF] / (slab_rows - row // REF).astype(jnp.float32)
    covariance = summed * scale[None, :] * row_scale[:, None]
    segment_auto = auto * (scale * scale)[None, :] / rows
    return (covariance, segment_auto)


def solution(mesh):
    in_specs = (P(("groups", "tm"), "chan"),)
    out_specs = (P(("groups", "tm"), "chan"), P(("groups", "tm"), "chan"))
    return jax.shard_map(local, mesh=mesh, in_specs=in_specs, out_specs=out_specs, check_vma=False)
```

time: 212 us -> 69.8 us (0.33)
  waiting for transfers between devices: 85.1 us -> 7.24 us
  blocking collectives: 37.5 us -> 0 us
  other arithmetic: 40.3 us -> 3.13 us
  Pallas kernels: 0 us -> 27.4 us
  starting transfers between devices: 1.84 us -> 24.1 us
  local copies, waits for them, and re-layouts: 22 us -> 6.58 us
  between operations: 14.1 us -> 0.82 us
  matrix products: 9.48 us -> 0 us
    psum x1 -> x0, waiting for transfers between devices: 84.5 us -> none  [local(): lax.psum(lax.dot_general(toeplitz, extended, (((0,), (0,)), ((), ())), pr...]
    psum x1 -> x0, blocking collectives: 37.5 us -> none  [local(): power_sum = lax.psum(placed, ('tm', 'chan'))]
    reduce_sum x2 -> x1, other arithmetic: 37.1 us -> 3.11 us  [local(): power = jnp.sum(wide * wide, axis=0, keepdims=True)]
    pallas_call x0 -> x10, Pallas kernels: none -> 27.4 us  [the longest x4 12.5 us: segment_rows(): pl.pallas_call(segment_kernel, grid=(1,), in_specs=[pl.BlockSpec((rows, s...]
    ppermute x1 -> x12, starting transfers between devices: 0.52 us -> 17.8 us  [the longest x11 15.2 us: exchanged(): lax.ppermute(value, axis, [(source, source ^ bit) for source in range(cou...]
    concatenate x2 -> x0, local copies, waits for them, and re-layouts: 11.4 us -> none  [the longest x1 10.8 us: stack_lags(): return jnp.concatenate(pieces, axis=1)]
    dot_general x1 -> x0, matrix products: 9.48 us -> none  [local(): lax.dot_general(toeplitz, extended, (((0,), (0,)), ((), ())), preferred_e...]
    ppermute x1 -> x2, starting transfers between devices: 1.28 us -> 6.3 us  [passed_along(): lax.ppermute(value, axis, [(source, source + steps) for source in range(i...]
  transfers between devices with their start and end apart: 3 -> 14, of which waited for: 2 -> 2; matrix products, arithmetic and copies ran while one was open for 21% -> 6% of each run, Pallas kernels for 0% -> 32%
where the time goes in v2:
time: 69.8 us; the launch traced here: 69.3 us
  Pallas kernels  27.4 us (39%)
  starting transfers between devices  24.1 us (35%)
  waiting for transfers between devices  7.24 us (10%)
  local copies, waits for them, and re-layouts  6.58 us (9%)
  other arithmetic  3.13 us (4%)
  between operations  0.82 us (1%)
    ppermute x11, starting transfers between devices, exchanged(): lax.ppermute(value, axis, [(source, source ^ bit) for source in range(cou...  15.2 us
    pallas_call x4, Pallas kernels, segment_rows(): pl.pallas_call(segment_kernel, grid=(1,), in_specs=[pl.BlockSpec((rows, s...  12.5 us
    pallas_call x1, Pallas kernels, later_products(): pl.pallas_call(later_products_kernel, in_specs=[pl.BlockSpec(memory_space...  8.19 us
    ppermute x2, starting transfers between devices, passed_along(): lax.ppermute(value, axis, [(source, source + steps) for source in range(i...  6.3 us
    unnamed x7, local copies, waits for them, and re-layouts  4.56 us
    ppermute x2, waiting for transfers between devices, passed_along(): lax.ppermute(value, axis, [(source, source + steps) for source in range(i...  3.9 us
    ppermute x11, waiting for transfers between devices, exchanged(): lax.ppermute(value, axis, [(source, source ^ bit) for source in range(cou...  3.34 us
    reduce_sum x1, other arithmetic, local(): power = jnp.sum(wide * wide, axis=0, keepdims=True)  3.11 us
  transfers between devices with their start and end apart: 14, of which 2 were waited for; matrix products, arithmetic and copies ran while one was open for 6% of the time, Pallas kernels for 32%

profile of v2, /device:TPU:0, one launch (start us, length us, event | category | flops | bytes accessed | tf_op | source)
XLA Modules:
  0.0 69.3 jit_solution(14725302833358193016)
XLA Ops:
  0.6 1.1 %slice.9 = bf16[2048,32]{1,0:T(8,128)(2,1)S(1)} slice(bf16[2048,1024]{1,0:T(8,128)(2,1)} %strain.11), slice={[0:2048], [0:32]} | slice | bytes 262144 | tf_op jit(solution)/shard_map/slice | solution.py:292
  1.7 0.2 copy.4
  1.9 4.8 %collective-permute-start.1 = (bf16[32,128]{1,0:T(8,128)(2,1)S(1)}, bf16[32,128]{1,0:T(8,128)(2,1)S(1)}, u32[]{:S(2)}, u32[]{:S(2)}) collective-permute-start(bf16[32,128]{1,0:T(8,128)(2,1)S(1)} %slice.12), channel_id=1, source_target_pairs={{0,2},{2,4},{4,6},{6,8},{8,10},{10,12},{12,14},{1,3},{3,5},{5,7},{... | collective-permute-start | bytes 24584 | tf_op jit(solution)/shard_map/ppermute | solution.py:23
  6.8 2.6 %collective-permute-start.2 = (bf16[32,128]{1,0:T(8,128)(2,1)S(1)}, bf16[32,128]{1,0:T(8,128)(2,1)S(1)}, u32[]{:S(2)}, u32[]{:S(2)}) collective-permute-start(bf16[32,128]{1,0:T(8,128)(2,1)S(1)} %slice.12), channel_id=1, source_target_pairs={{0,3},{1,2},{2,5},{3,4},{4,7},{5,6},{6,9},{7,8},{8,11},{9,10},{10,... | collective-permute-start | bytes 24584 | tf_op jit(solution)/shard_map/ppermute | solution.py:34
  9.4 1.0 %collective-permute-start = (bf16[32,2048]{1,0:T(8,128)(2,1)S(1)}, bf16[32,2048]{1,0:T(8,128)(2,1)S(1)}, u32[]{:S(2)}, u32[]{:S(2)}) collective-permute-start(bf16[32,2048]{1,0:T(8,128)(2,1)S(1)} %bitcast.10), channel_id=1, source_target_pairs={{0,1},{1,0},{2,3},{3,2},{4,5},{5,4},{6,7},{7,6},{8,9},{9,8},{10,11... | collective-permute-start | bytes 393224 | tf_op jit(solution)/shard_map/ppermute | solution.py:28
  10.4 3.1 %multiply_reduce_fusion = f32[1024]{0:T(1024)S(1)} fusion(bf16[2048,1024]{1,0:T(8,128)(2,1)} %strain.11), kind=kLoop, calls=%fused_computation | loop fusion | flops 6290432 | bytes 4198400 | tf_op jit(solution)/shard_map/reduce_sum | solution.py:301
  13.5 0.1 stack.39.place
  13.6 0.0 collective-permute-done.1.halo_own
  13.6 0.0 collective-permute-done.2.halo_other
  13.6 0.0 collective-permute-done.other
  13.6 0.0 copy-start
  13.6 2.2 %copy-done = bf16[2048,1024]{1,0:T(8,128)(2,1)S(1)} copy-done((bf16[2048,1024]{1,0:T(8,128)(2,1)S(1)}, bf16[2048,1024]{1,0:T(8,128)(2,1)}, u32[]{:S(2)}) %copy-start) | copy-done | bytes 4194328
  15.8 2.8 %first_products.1 = (f32[128,1024]{1,0:T(8,128)S(1)}, bf16[128,1024]{1,0:T(8,128)(2,1)S(1)}, f32[8,1024]{1,0:T(8,128)S(1)}) custom-call(s32[6]{0:T(128)S(1)} %stack.39.place, f32[1,1024]{1,0:T(1,128)S(1)} %bitcast.13, bf16[2048,1024]{1,0:T(8,128)(2,1)S(1)} %copy-done, bf16[32,2048]{1,0:T(8,128)(2,1)S(1)} %bitcast.11, ...), custom_call_target="tpu_custom_call" | custom-call | flops 1073741824 | bytes 4194304 | tf_op jit(solution)/shard_map/first_products/pallas_call | solution.py:116
  18.7 1.6 %collective-permute-start.3 = (f32[8,1024]{1,0:T(8,128)S(1)}, f32[8,1024]{1,0:T(8,128)S(1)}, u32[]{:S(2)}, u32[]{:S(2)}) collective-permute-start(f32[8,1024]{1,0:T(8,128)S(1)} %get-tuple-element.11.powers), channel_id=1, source_target_pairs={{0,2},{2,0},{4,6},{6,4},{8,10},{10,8},{12,14},{14,12},{1,3},{3,1},... | collective-permute-start | bytes 98312 | tf_op jit(solution)/shard_map/ppermute | solution.py:28
  20.2 0.5 collective-permute-start.11
  20.7 8.2 %later_products.1 = (f32[128,1024]{1,0:T(8,128)S(1)}, bf16[128,1024]{1,0:T(8,128)(2,1)S(1)}, f32[128,1024]{1,0:T(8,128)S(1)}, bf16[128,1024]{1,0:T(8,128)(2,1)},...) custom-call(s32[6]{0:T(128)S(1)} %stack.39.place, f32[8,1024]{1,0:T(8,128)S(1)} %get-tuple-element.11.powers, ...), custom_call_target="tpu_custom_call" | custom-call | flops 3221225472 | bytes 4194304 | tf_op jit(solution)/shard_map/later_products/pallas_call | solution.py:150
  28.9 1.6 %collective-permute-start.10 = (bf16[128,1024]{1,0:T(8,128)(2,1)S(1)}, bf16[128,1024]{1,0:T(8,128)(2,1)S(1)}, u32[]{:S(2)}, u32[]{:S(2)}) collective-permute-start(bf16[128,1024]{1,0:T(8,128)(2,1)S(1)} %get-tuple-element.17), channel_id=1, source_target_pairs={{0,2},{2,0},{4,6},{6,4},{8,10},{10,8},{12,14},{14,12},{1,3},{3,1},... | collective-permute-start | bytes 786440 | tf_op jit(solution)/shard_map/ppermute | solution.py:28
  30.5 0.5 collective-permute-start.8
  31.0 0.0 collective-permute-done.3.rest_1_.refs_5_
  31.0 0.0 collective-permute-done.11.rest_0_
  31.1 0.5 merged.4
  31.6 1.7 %collective-permute-start.12 = (bf16[128,1024]{1,0:T(8,128)(2,1)S(1)}, bf16[128,1024]{1,0:T(8,128)(2,1)S(1)}, u32[]{:S(2)}, u32[]{:S(2)}) collective-permute-start(bf16[128,1024]{1,0:T(8,128)(2,1)S(1)} %merged.4), channel_id=1, source_target_pairs={{0,4},{2,6},{4,0},{6,2},{8,12},{10,14},{12,8},{14,10},{1,5},{3,7},... | collective-permute-start | bytes 786440 | tf_op jit(solution)/shard_map/ppermute | solution.py:28
  33.2 0.8 %slice.11 = bf16[16,1024]{1,0:T(8,128)(2,1)S(1)} slice(bf16[2048,1024]{1,0:T(8,128)(2,1)} %strain.11), slice={[0:16], [0:1024]} | slice | bytes 65536 | tf_op jit(solution)/shard_map/slice | solution.py:298
  34.0 1.5 %collective-permute-start.6 = (bf16[16,1024]{1,0:T(8,128)(2,1)S(1)}, bf16[16,1024]{1,0:T(8,128)(2,1)S(1)}, u32[]{:S(2)}, u32[]{:S(2)}) collective-permute-start(bf16[16,1024]{1,0:T(8,128)(2,1)S(1)} %slice.11), channel_id=1, source_target_pairs={{2,0},{4,2},{6,4},{8,6},{10,8},{12,10},{14,12},{3,1},{5,3},{7,5},{... | collective-permute-start | bytes 98312 | tf_op jit(solution)/shard_map/ppermute | solution.py:23
  35.4 0.1 stack.33.refs_0_
  35.5 3.6 %collective-permute-start.4 = (f32[8,1024]{1,0:T(8,128)S(1)}, f32[8,1024]{1,0:T(8,128)S(1)}, u32[]{:S(2)}, u32[]{:S(2)}) collective-permute-start(f32[8,1024]{1,0:T(8,128)S(1)} %add.9.powers), channel_id=1, source_target_pairs={{0,4},{2,6},{4,0},{6,2},{8,12},{10,14},{12,8},{14,10},{1,5},{3,7},... | collective-permute-start | bytes 98312 | tf_op jit(solution)/shard_map/ppermute | solution.py:28
  39.1 3.9 %collective-permute-done.6.tail = bf16[16,1024]{1,0:T(8,128)(2,1)S(1)} collective-permute-done((bf16[16,1024]{1,0:T(8,128)(2,1)S(1)}, bf16[16,1024]{1,0:T(8,128)(2,1)S(1)}, u32[]{:S(2)}, u32[]{:S(2)}) %collective-permute-start.6) | collective-permute-done | bytes 32800 | tf_op jit(solution)/shard_map/ppermute | solution.py:23
  43.0 0.0 copy-start.1
  43.0 2.2 %copy-done.1 = bf16[2048,1024]{1,0:T(8,128)(2,1)S(1)} copy-done((bf16[2048,1024]{1,0:T(8,128)(2,1)S(1)}, bf16[2048,1024]{1,0:T(8,128)(2,1)}, u32[]{:S(2)}) %copy-start.1) | copy-done | bytes 4194328
  45.2 0.0 copy-start.2
  45.2 3.1 %segment_rows.4 = f32[16,256]{1,0:T(8,128)S(1)} custom-call(bf16[2048,1024]{1,0:T(8,128)(2,1)S(1)} %copy-done.1, bf16[16,1024]{1,0:T(8,128)(2,1)S(1)} %collective-permute-done.6.tail), custom_call_target="tpu_custom_call" | custom-call | flops 536870912 | bytes 1048576 | tf_op jit(solution)/shard_map/segment_rows/pallas_call | solution.py:244
  48.3 0.1 collective-permute-start.7
  48.4 0.0 collective-permute-done.4.rest_3_.refs_7_
  48.4 0.0 collective-permute-done.8.rest_0_
  48.4 0.5 merged.3
  48.9 1.6 %collective-permute-start.9 = (bf16[128,1024]{1,0:T(8,128)(2,1)S(1)}, bf16[128,1024]{1,0:T(8,128)(2,1)S(1)}, u32[]{:S(2)}, u32[]{:S(2)}) collective-permute-start(bf16[128,1024]{1,0:T(8,128)(2,1)S(1)} %merged.3), channel_id=1, source_target_pairs={{0,4},{2,6},{4,0},{6,2},{8,12},{10,14},{12,8},{14,10},{1,5},{3,7},... | collective-permute-start | bytes 786440 | tf_op jit(solution)/shard_map/ppermute | solution.py:28
  50.6 0.0 collective-permute-done.10.rest_0_
  50.6 0.0 collective-permute-done.12.rest_2_
  50.6 0.7 %merged.5 = bf16[128,1024]{1,0:T(8,128)(2,1)S(1)} custom-call(f32[8,1024]{1,0:T(8,128)S(1)} %add.10.powers, f32[128,1024]{1,0:T(8,128)S(1)} %get-tuple-element.16.keep, bf16[128,1024]{1,0:T(8,128)(2,1)S(1)} %collective-permute-done.10.rest_0_, f32[8,1024]{1,0:T(8,128)S(1)} %collective-permute-done.3.rest_1_.refs_5_, ...), custom_call_target="tpu_custom_call" | custom-call | bytes 1048576 | tf_op jit(solution)/shard_map/merged/pallas_call | solution.py:177
  51.3 1.5 %collective-permute-start.13 = (bf16[128,1024]{1,0:T(8,128)(2,1)S(1)}, bf16[128,1024]{1,0:T(8,128)(2,1)S(1)}, u32[]{:S(2)}, u32[]{:S(2)}) collective-permute-start(bf16[128,1024]{1,0:T(8,128)(2,1)S(1)} %merged.5), channel_id=1, source_target_pairs={{0,8},{2,10},{4,12},{6,14},{8,0},{10,2},{12,4},{14,6},{1,9},{3,11}... | collective-permute-start | bytes 786440 | tf_op jit(solution)/shard_map/ppermute | solution.py:28
  52.8 0.0 copy-done.2
  52.8 3.1 %segment_rows.5 = f32[16,256]{1,0:T(8,128)S(1)} custom-call(bf16[2048,1024]{1,0:T(8,128)(2,1)S(1)} %copy-done.2, bf16[16,1024]{1,0:T(8,128)(2,1)S(1)} %collective-permute-done.6.tail), custom_call_target="tpu_custom_call" | custom-call | flops 536870912 | bytes 1048576 | tf_op jit(solution)/shard_map/segment_rows/pallas_call | solution.py:244
  56.0 3.1 %segment_rows.6 = f32[16,256]{1,0:T(8,128)S(1)} custom-call(bf16[2048,1024]{1,0:T(8,128)(2,1)S(1)} %copy-done.2, bf16[16,1024]{1,0:T(8,128)(2,1)S(1)} %collective-permute-done.6.tail), custom_call_target="tpu_custom_call" | custom-call | flops 536870912 | bytes 1048576 | tf_op jit(solution)/shard_map/segment_rows/pallas_call | solution.py:244
  59.1 3.1 %segment_rows.7 = f32[16,256]{1,0:T(8,128)S(1)} custom-call(bf16[2048,1024]{1,0:T(8,128)(2,1)S(1)} %copy-done.2, bf16[16,1024]{1,0:T(8,128)(2,1)S(1)} %collective-permute-done.6.tail), custom_call_target="tpu_custom_call" | custom-call | flops 536870912 | bytes 1048576 | tf_op jit(solution)/shard_map/segment_rows/pallas_call | solution.py:244
  62.2 1.6 %collective-permute-start.5 = (f32[8,1024]{1,0:T(8,128)S(1)}, f32[8,1024]{1,0:T(8,128)S(1)}, u32[]{:S(2)}, u32[]{:S(2)}) collective-permute-start(f32[8,1024]{1,0:T(8,128)S(1)} %add.10.powers), channel_id=1, source_target_pairs={{0,8},{2,10},{4,12},{6,14},{8,0},{10,2},{12,4},{14,6},{1,9},{3,11}... | collective-permute-start | bytes 98312 | tf_op jit(solution)/shard_map/ppermute | solution.py:28
  63.8 3.3 %collective-permute-done.5.refs_9_ = f32[8,1024]{1,0:T(8,128)S(1)} collective-permute-done((f32[8,1024]{1,0:T(8,128)S(1)}, f32[8,1024]{1,0:T(8,128)S(1)}, u32[]{:S(2)}, u32[]{:S(2)}) %collective-permute-start.5) | collective-permute-done | bytes 32800 | tf_op jit(solution)/shard_map/ppermute | solution.py:28
  67.1 0.0 collective-permute-done.7.refs_4_
  67.1 0.0 collective-permute-done.9.refs_6_
  67.1 0.0 collective-permute-done.13.refs_8_
  67.2 2.2 %finished.1 = (f32[128,1024]{1,0:T(8,128)}, f32[16,1024]{1,0:T(8,128)}) custom-call(s32[5]{0:T(128)S(1)} %stack.33.refs_0_, f32[8,1024]{1,0:T(8,128)S(1)} %add.11.refs_1_, f32[16,1024]{1,0:T(8,128)S(1)} %pad_maximum_fusion.refs_2_, f32[128,1024]{1,0:T(8,128)S(1)} %get-tuple-element.12.refs_3_, bf16[128,1024]{1,0:T(8,128)(2,1)S(1)} %collective-permute-done.7.refs_4_, ...), custom_call_target="tpu_custom_call" | custom-call | bytes 1048576 | tf_op jit(solution)/shard_map/finished/pallas_call | solution.py:206
  (5 shorter events, 0.0 us)
Async XLA Ops:
  1.9 11.7 %collective-permute-start.1 = (bf16[32,128]{1,0:T(8,128)(2,1)S(1)}, bf16[32,128]{1,0:T(8,128)(2,1)S(1)}, u32[]{:S(2)}, u32[]{:S(2)}) collective-permute-start(bf16[32,128]{1,0:T(8,128)(2,1)S(1)} %slice.12), channel_id=1, source_target_pairs={{0,2},{2,4},{4,6},{6,8},{8,10},{10,12},{12,14},{1,3},{3,5},{5,7},{... | collective-permute-start | bytes 24584 | tf_op jit(solution)/shard_map/ppermute | solution.py:23
  6.8 6.8 %collective-permute-start.2 = (bf16[32,128]{1,0:T(8,128)(2,1)S(1)}, bf16[32,128]{1,0:T(8,128)(2,1)S(1)}, u32[]{:S(2)}, u32[]{:S(2)}) collective-permute-start(bf16[32,128]{1,0:T(8,128)(2,1)S(1)} %slice.12), channel_id=1, source_target_pairs={{0,3},{1,2},{2,5},{3,4},{4,7},{5,6},{6,9},{7,8},{8,11},{9,10},{10,... | collective-permute-start | bytes 24584 | tf_op jit(solution)/shard_map/ppermute | solution.py:34
  9.4 4.2 %collective-permute-start = (bf16[32,2048]{1,0:T(8,128)(2,1)S(1)}, bf16[32,2048]{1,0:T(8,128)(2,1)S(1)}, u32[]{:S(2)}, u32[]{:S(2)}) collective-permute-start(bf16[32,2048]{1,0:T(8,128)(2,1)S(1)} %bitcast.10), channel_id=1, source_target_pairs={{0,1},{1,0},{2,3},{3,2},{4,5},{5,4},{6,7},{7,6},{8,9},{9,8},{10,11... | collective-permute-start | bytes 393224 | tf_op jit(solution)/shard_map/ppermute | solution.py:28
  13.6 2.2 %copy-start = (bf16[2048,1024]{1,0:T(8,128)(2,1)S(1)}, bf16[2048,1024]{1,0:T(8,128)(2,1)}, u32[]{:S(2)}) copy-start(bf16[2048,1024]{1,0:T(8,128)(2,1)} %strain.11) | copy-start | bytes 12582916
  18.7 12.4 %collective-permute-start.3 = (f32[8,1024]{1,0:T(8,128)S(1)}, f32[8,1024]{1,0:T(8,128)S(1)}, u32[]{:S(2)}, u32[]{:S(2)}) collective-permute-start(f32[8,1024]{1,0:T(8,128)S(1)} %get-tuple-element.11.powers), channel_id=1, source_target_pairs={{0,2},{2,0},{4,6},{6,4},{8,10},{10,8},{12,14},{14,12},{1,3},{3,1},... | collective-permute-start | bytes 98312 | tf_op jit(solution)/shard_map/ppermute | solution.py:28
  20.2 10.8 %collective-permute-start.11 = (bf16[128,1024]{1,0:T(8,128)(2,1)S(1)}, bf16[128,1024]{1,0:T(8,128)(2,1)S(1)}, u32[]{:S(2)}, u32[]{:S(2)}) collective-permute-start(bf16[128,1024]{1,0:T(8,128)(2,1)S(1)} %get-tuple-element.19), channel_id=1, source_target_pairs={{0,2},{2,0},{4,6},{6,4},{8,10},{10,8},{12,14},{14,12},{1,3},{3,1},... | collective-permute-start | bytes 786440 | tf_op jit(solution)/shard_map/ppermute | solution.py:28
  28.9 21.6 %collective-permute-start.10 = (bf16[128,1024]{1,0:T(8,128)(2,1)S(1)}, bf16[128,1024]{1,0:T(8,128)(2,1)S(1)}, u32[]{:S(2)}, u32[]{:S(2)}) collective-permute-start(bf16[128,1024]{1,0:T(8,128)(2,1)S(1)} %get-tuple-element.17), channel_id=1, source_target_pairs={{0,2},{2,0},{4,6},{6,4},{8,10},{10,8},{12,14},{14,12},{1,3},{3,1},... | collective-permute-start | bytes 786440 | tf_op jit(solution)/shard_map/ppermute | solution.py:28
  30.5 17.9 %collective-permute-start.8 = (bf16[128,1024]{1,0:T(8,128)(2,1)}, bf16[128,1024]{1,0:T(8,128)(2,1)S(1)}, u32[]{:S(2)}, u32[]{:S(2)}) collective-permute-start(bf16[128,1024]{1,0:T(8,128)(2,1)} %get-tuple-element.15), channel_id=1, source_target_pairs={{0,2},{2,0},{4,6},{6,4},{8,10},{10,8},{12,14},{14,12},{1,3},{3,1},... | collective-permute-start | bytes 786440 | tf_op jit(solution)/shard_map/ppermute | solution.py:28
  31.6 19.0 %collective-permute-start.12 = (bf16[128,1024]{1,0:T(8,128)(2,1)S(1)}, bf16[128,1024]{1,0:T(8,128)(2,1)S(1)}, u32[]{:S(2)}, u32[]{:S(2)}) collective-permute-start(bf16[128,1024]{1,0:T(8,128)(2,1)S(1)} %merged.4), channel_id=1, source_target_pairs={{0,4},{2,6},{4,0},{6,2},{8,12},{10,14},{12,8},{14,10},{1,5},{3,7},... | collective-permute-start | bytes 786440 | tf_op jit(solution)/shard_map/ppermute | solution.py:28
  34.0 9.0 %collective-permute-start.6 = (bf16[16,1024]{1,0:T(8,128)(2,1)S(1)}, bf16[16,1024]{1,0:T(8,128)(2,1)S(1)}, u32[]{:S(2)}, u32[]{:S(2)}) collective-permute-start(bf16[16,1024]{1,0:T(8,128)(2,1)S(1)} %slice.11), channel_id=1, source_target_pairs={{2,0},{4,2},{6,4},{8,6},{10,8},{12,10},{14,12},{3,1},{5,3},{7,5},{... | collective-permute-start | bytes 98312 | tf_op jit(solution)/shard_map/ppermute | solution.py:23
  35.5 12.9 %collective-permute-start.4 = (f32[8,1024]{1,0:T(8,128)S(1)}, f32[8,1024]{1,0:T(8,128)S(1)}, u32[]{:S(2)}, u32[]{:S(2)}) collective-permute-start(f32[8,1024]{1,0:T(8,128)S(1)} %add.9.powers), channel_id=1, source_target_pairs={{0,4},{2,6},{4,0},{6,2},{8,12},{10,14},{12,8},{14,10},{1,5},{3,7},... | collective-permute-start | bytes 98312 | tf_op jit(solution)/shard_map/ppermute | solution.py:28
  43.0 2.2 %copy-start.1 = (bf16[2048,1024]{1,0:T(8,128)(2,1)S(1)}, bf16[2048,1024]{1,0:T(8,128)(2,1)}, u32[]{:S(2)}) copy-start(bf16[2048,1024]{1,0:T(8,128)(2,1)} %strain.11) | copy-start | bytes 12582916
  45.2 7.6 %copy-start.2 = (bf16[2048,1024]{1,0:T(8,128)(2,1)S(1)}, bf16[2048,1024]{1,0:T(8,128)(2,1)}, u32[]{:S(2)}) copy-start(bf16[2048,1024]{1,0:T(8,128)(2,1)} %strain.11) | copy-start | bytes 12582916
  48.3 18.8 %collective-permute-start.7 = (bf16[128,1024]{1,0:T(8,128)(2,1)S(1)}, bf16[128,1024]{1,0:T(8,128)(2,1)S(1)}, u32[]{:S(2)}, u32[]{:S(2)}) collective-permute-start(bf16[128,1024]{1,0:T(8,128)(2,1)S(1)} %get-tuple-element.13), channel_id=1, source_target_pairs={{0,2},{2,0},{4,6},{6,4},{8,10},{10,8},{12,14},{14,12},{1,3},{3,1},... | collective-permute-start | bytes 786440 | tf_op jit(solution)/shard_map/ppermute | solution.py:28
  48.9 18.2 %collective-permute-start.9 = (bf16[128,1024]{1,0:T(8,128)(2,1)S(1)}, bf16[128,1024]{1,0:T(8,128)(2,1)S(1)}, u32[]{:S(2)}, u32[]{:S(2)}) collective-permute-start(bf16[128,1024]{1,0:T(8,128)(2,1)S(1)} %merged.3), channel_id=1, source_target_pairs={{0,4},{2,6},{4,0},{6,2},{8,12},{10,14},{12,8},{14,10},{1,5},{3,7},... | collective-permute-start | bytes 786440 | tf_op jit(solution)/shard_map/ppermute | solution.py:28
  51.3 15.8 %collective-permute-start.13 = (bf16[128,1024]{1,0:T(8,128)(2,1)S(1)}, bf16[128,1024]{1,0:T(8,128)(2,1)S(1)}, u32[]{:S(2)}, u32[]{:S(2)}) collective-permute-start(bf16[128,1024]{1,0:T(8,128)(2,1)S(1)} %merged.5), channel_id=1, source_target_pairs={{0,8},{2,10},{4,12},{6,14},{8,0},{10,2},{12,4},{14,6},{1,9},{3,11}... | collective-permute-start | bytes 786440 | tf_op jit(solution)/shard_map/ppermute | solution.py:28
  62.2 4.9 %collective-permute-start.5 = (f32[8,1024]{1,0:T(8,128)S(1)}, f32[8,1024]{1,0:T(8,128)S(1)}, u32[]{:S(2)}, u32[]{:S(2)}) collective-permute-start(f32[8,1024]{1,0:T(8,128)S(1)} %add.10.powers), channel_id=1, source_target_pairs={{0,8},{2,10},{4,12},{6,14},{8,0},{10,2},{12,4},{14,6},{1,9},{3,11}... | collective-permute-start | bytes 98312 | tf_op jit(solution)/shard_map/ppermute | solution.py:28

commit v3 on v2

v3 whole, which is shorter than its diff:
```python
import jax
import jax.numpy as jnp
from jax import lax
from jax.experimental import pallas as pl
from jax.experimental.pallas import tpu as pltpu
from jax.sharding import PartitionSpec as P

LAGS = 16
REF = 64
HALF = REF // 2
LANES = 128
EXTRA = 8
FETCHES = 8
GROUP = 4
POWER = 16
CODE_SCALE = 2.0 ** (126 / POWER)
TINY = 1e-35
VMEM_BYTES = 48 * 1024 * 1024


def passed_along(value, axis, steps):
    count = lax.axis_size(axis)
    initial, last = (max(0, -steps), min(count, count - steps))
    return lax.ppermute(value, axis, [(source, source + steps) for source in range(initial, last)])


def exchanged(value, axis, bit):
    count = lax.axis_size(axis)
    return lax.ppermute(value, axis, [(source, source ^ bit) for source in range(count)])


def as_column(row):
    size = row.shape[1]
    eye = lax.broadcasted_iota(jnp.int32, (size, size), 0) == lax.broadcasted_iota(jnp.int32, (size, size), 1)
    return jnp.sum(jnp.where(eye, row, 0.0), axis=1, keepdims=True)


def as_row(column):
    size = column.shape[0]
    eye = lax.broadcasted_iota(jnp.int32, (size, size), 0) == lax.broadcasted_iota(jnp.int32, (size, size), 1)
    return jnp.sum(jnp.where(eye, column, 0.0), axis=0, keepdims=True)


def for_chunk(ref_column, rows):
    return jnp.concatenate([ref_column] * (rows // REF), axis=0)


def bf16_pieces(value):
    high = value.astype(jnp.bfloat16).astype(jnp.float32)
    middle = (value - high).astype(jnp.bfloat16).astype(jnp.float32)
    return high, middle, value - high - middle


def packed(powers, ref_powers, channel_bound):
    rows = list(bf16_pieces(powers))
    refs = jnp.concatenate(bf16_pieces(ref_powers), axis=1)
    pad = jnp.zeros((1, powers.shape[1] - refs.shape[1]), jnp.float32)
    rows += [jnp.concatenate([refs, pad], axis=1), channel_bound]
    rows += [jnp.zeros_like(powers)] * (EXTRA - len(rows))
    return jnp.concatenate(rows, axis=0).astype(jnp.bfloat16)


def unpacked(block):
    wide = block.astype(jnp.float32)
    powers = wide[0:1] + wide[1:2] + wide[2:3]
    refs = wide[3:4, :LANES] + wide[3:4, LANES : 2 * LANES] + wide[3:4, 2 * LANES : 3 * LANES]
    return powers, refs, wide[4:5]


def rounded_up(value):
    return (value * (1.0 + 2.0**-7)).astype(jnp.bfloat16).astype(jnp.float32)


def coded(values, channel_bound, ref_bound):
    channel = lax.rsqrt(jnp.maximum(channel_bound, TINY))
    refs = lax.rsqrt(jnp.maximum(ref_bound, TINY)) * CODE_SCALE
    power = values * channel * for_chunk(refs, values.shape[0])
    for _ in range(4):
        power = power * jnp.abs(power)
    return power.astype(jnp.bfloat16)


def expanded(code, channel_bound, ref_bound):
    channel = jnp.sqrt(jnp.maximum(channel_bound, TINY))
    refs = jnp.sqrt(jnp.maximum(ref_bound, TINY)) * (1.0 / CODE_SCALE)
    wide = code.astype(jnp.float32)
    root = jnp.exp2(jnp.log2(jnp.abs(wide)) * (1.0 / POWER))
    return jnp.where(wide < 0.0, -root, root) * channel * for_chunk(refs, code.shape[0])


def ref_column(ref_powers):
    return as_column(ref_powers)[:REF]


def prepare_kernel(left, top, own, head):
    own[...] = left[...].astype(jnp.float32).T[:HALF].astype(jnp.bfloat16)
    head[...] = top[...]


def prepared(strain):
    rows, width = strain.shape
    return pl.pallas_call(
        prepare_kernel,
        grid=(1,),
        in_specs=[
            pl.BlockSpec((rows, LANES), lambda index: (0, 0)),
            pl.BlockSpec((LAGS, width), lambda index: (0, 0)),
        ],
        out_specs=[
            pl.BlockSpec((HALF, rows), lambda index: (0, 0)),
            pl.BlockSpec((LAGS, width), lambda index: (0, 0)),
        ],
        out_shape=[
            jax.ShapeDtypeStruct((HALF, rows), strain.dtype),
            jax.ShapeDtypeStruct((LAGS, width), strain.dtype),
        ],
        name="prepared",
    )(strain, strain)


def lag_rows(own, other, chan, first_lag, shifted):
    rows = own.shape[1]
    zeros = jnp.zeros((HALF, LANES), jnp.float32)
    for refs, half in ((own, chan), (other, 1 - chan)):
        long = jnp.concatenate([refs[...].astype(jnp.float32), zeros], axis=1)
        for index in range(GROUP):
            moved = pltpu.roll(long, first_lag + index, 1)
            start = pl.multiple_of(index * REF + half * HALF, HALF)
            shifted[pl.ds(start, HALF), :] = moved.astype(jnp.bfloat16)


def fetches(strain, held, sems):
    step = held.shape[0] // FETCHES
    return [
        pltpu.make_async_copy(
            strain.at[pl.ds(index * step, step)], held.at[pl.ds(index * step, step)], sems.at[index]
        )
        for index in range(FETCHES)
    ]


def product_of(shifted, held, tail, copies):
    rows = held.shape[0]
    total = jnp.dot(
        shifted[:, rows:], tail[...], preferred_element_type=jnp.float32
    )
    step = rows // FETCHES
    for index in range(FETCHES):
        if copies:
            copies[index].wait()
        here = slice(index * step, (index + 1) * step)
        total += jnp.dot(shifted[:, here], held[here, :], preferred_element_type=jnp.float32)
    return total


def padded(tail):
    wide = tail[...]
    return jnp.concatenate([wide, jnp.zeros((LANES - LAGS, wide.shape[1]), wide.dtype)], axis=0)


def first_products_kernel(place, strain, own, other, tail, keep, send, powers, held, shifted, edge, sems):
    chan, group, near = place[0], place[1], place[2]
    copies = fetches(strain, held, sems)
    for copy in copies:
        copy.start()
    edge[...] = padded(tail)
    lag_rows(own, other, chan, group * GROUP, shifted)
    ours, theirs = [
        jnp.sum(jnp.square(refs[...].astype(jnp.float32)), axis=1, keepdims=True) for refs in (own, other)
    ]
    refs = jnp.where(
        chan == 0, jnp.concatenate([ours, theirs], axis=0), jnp.concatenate([theirs, ours], axis=0)
    )
    product = product_of(shifted, held, edge, copies)
    channel = jnp.sum(jnp.square(held[...].astype(jnp.float32)), axis=0, keepdims=True)
    beyond = jnp.sum(jnp.square(tail[...].astype(jnp.float32)), axis=0, keepdims=True)
    bound = rounded_up(channel + beyond)
    pad = jnp.zeros((1, LANES - REF), jnp.float32)
    extra = packed(channel, jnp.concatenate([as_row(refs), pad], axis=1), bound)
    powers[...] = extra
    chunk = keep.shape[0]
    keep[...] = jnp.where(near == 0, product[:chunk], product[chunk:])
    other_half = jnp.where(near == 0, product[chunk:], product[:chunk])
    send[:chunk] = coded(other_half, bound, refs)
    send[chunk:] = extra


def product_scratch(rows, width, *slots):
    return [
        pltpu.VMEM((rows, width), jnp.bfloat16),
        pltpu.VMEM((*slots, GROUP * REF, rows + LANES), jnp.bfloat16),
        pltpu.VMEM((LANES, width), jnp.bfloat16),
        pltpu.SemaphoreType.DMA((FETCHES,)),
    ]


def product_specs(count):
    return [
        pl.BlockSpec(memory_space=pltpu.SMEM),
        pl.BlockSpec(memory_space=pl.ANY),
    ] + [pl.BlockSpec(memory_space=pltpu.VMEM)] * count


def first_products(place, strain, own, other, tail, chunk):
    rows, width = strain.shape
    return pl.pallas_call(
        first_products_kernel,
        in_specs=product_specs(3),
        out_specs=[pl.BlockSpec(memory_space=pltpu.VMEM)] * 3,
        out_shape=[
            jax.ShapeDtypeStruct((chunk, width), jnp.float32),
            jax.ShapeDtypeStruct((chunk + EXTRA, width), jnp.bfloat16),
            jax.ShapeDtypeStruct((EXTRA, width), jnp.bfloat16),
        ],
        scratch_shapes=product_scratch(rows, width),
        compiler_params=pltpu.CompilerParams(vmem_limit_bytes=VMEM_BYTES),
        cost_estimate=pl.CostEstimate(
            flops=2 * 4 * chunk * rows * width, bytes_accessed=rows * width * 2, transcendentals=0
        ),
        name="first_products",
    )(place, strain, own, other, tail)


def later_products_kernel(place, strain, own, other, tail, powers, *rest):
    chan, near = place[0], place[2]
    held, shifted, edge, sems = rest[-4:]
    copies = fetches(strain, held, sems)
    for copy in copies:
        copy.start()
    edge[...] = padded(tail)
    _, ref_powers, bound = unpacked(powers[...])
    refs = ref_column(ref_powers)
    for slot in range((len(rest) - 4) // 2):
        keep, send = rest[2 * slot], rest[2 * slot + 1]
        chunk = keep.shape[0]
        lag_rows(own, other, chan, place[3 + slot] * GROUP, shifted.at[slot])
        product = product_of(shifted.at[slot], held, edge, copies if slot == 0 else None)
        keep[...] = jnp.where(near == 0, product[:chunk], product[chunk:])
        other_half = jnp.where(near == 0, product[chunk:], product[:chunk])
        send[...] = coded(other_half, bound, refs)


def later_products(place, strain, own, other, tail, powers, chunk, slots):
    rows, width = strain.shape
    return pl.pallas_call(
        later_products_kernel,
        in_specs=product_specs(4),
        out_specs=[pl.BlockSpec(memory_space=pltpu.VMEM)] * (2 * slots),
        out_shape=[
            jax.ShapeDtypeStruct((chunk, width), jnp.float32),
            jax.ShapeDtypeStruct((chunk, width), jnp.bfloat16),
        ]
        * slots,
        scratch_shapes=product_scratch(rows, width, slots),
        compiler_params=pltpu.CompilerParams(vmem_limit_bytes=VMEM_BYTES),
        cost_estimate=pl.CostEstimate(
            flops=2 * 4 * chunk * slots * rows * width, bytes_accessed=rows * width * 2, transcendentals=0
        ),
        name="later_products",
    )(place, strain, own, other, tail, powers)


def call_on_blocks(kernel, outs, *arrays, name):
    vmem = pl.BlockSpec(memory_space=pltpu.VMEM)
    smem = pl.BlockSpec(memory_space=pltpu.SMEM)
    return pl.pallas_call(
        kernel,
        in_specs=[smem if array.dtype == jnp.int32 else vmem for array in arrays],
        out_specs=[vmem] * len(outs),
        out_shape=[jax.ShapeDtypeStruct(shape, dtype) for shape, dtype in outs],
        compiler_params=pltpu.CompilerParams(vmem_limit_bytes=VMEM_BYTES),
        cost_estimate=pl.CostEstimate(flops=0, bytes_accessed=2**21, transcendentals=0),
        name=name,
    )(*arrays)


def received(code, powers):
    chunk = code.shape[0] // REF * REF
    _, refs, bound = unpacked(powers[...])
    return expanded(code[:chunk], bound, ref_column(refs))


def joined(powers, arrived):
    ours, ours_refs, ours_bound = unpacked(powers)
    theirs, theirs_refs, theirs_bound = unpacked(arrived)
    bound = rounded_up(ours_bound + theirs_bound)
    return ours + theirs, ours_refs + theirs_refs, bound


def merge_kernel(*refs):
    keep, powers, arrived, out, extra = refs[0], refs[1], refs[2], refs[-2], refs[-1]
    chunk = keep.shape[0]
    total = keep[...] + received(arrived, arrived[chunk:])
    for code, sender in zip(refs[3:-2:2], refs[4:-2:2]):
        total = total + received(code, sender)
    sums, sum_refs, bound = joined(powers[...], arrived[chunk:])
    extra[...] = packed(sums, sum_refs, bound)
    out[:chunk] = coded(total, bound, ref_column(sum_refs))
    out[chunk:] = extra[...]


def merged(keep, powers, arrived, *others):
    chunk, width = keep.shape
    outs = [((chunk + EXTRA, width), jnp.bfloat16), ((EXTRA, width), jnp.bfloat16)]
    return call_on_blocks(merge_kernel, outs, keep, powers, arrived, *others, name="merged")


def resend_kernel(keep, code, sender, powers, out):
    _, refs, bound = unpacked(powers[...])
    out[...] = coded(keep[...] + received(code, sender), bound, ref_column(refs))


def resent(keep, code, sender, powers):
    outs = [(keep.shape, jnp.bfloat16)]
    return call_on_blocks(resend_kernel, outs, keep, code, sender, powers, name="resent")[0]


def add_kernel(keep, code, sender, other, other_sender, out):
    out[...] = keep[...] + received(code, sender) + received(other, other_sender)


def added(*arrays):
    outs = [(arrays[0].shape, jnp.float32)]
    return call_on_blocks(add_kernel, outs, *arrays, name="added")[0]


def finished(segment, slab_rows, place, powers, auto, partial, arrived):
    def kernel(place, powers, auto, partial, arrived, covariance, segment_auto):
        chunk = partial.shape[0]
        total = partial[...] + received(arrived, arrived[chunk:])
        sums, sum_refs, _ = joined(powers[...], arrived[chunk:])
        scale = 1.0 / jnp.sqrt(sums / slab_rows + 1e-06)
        ref_scale = 1.0 / jnp.sqrt(ref_column(sum_refs) / slab_rows + 1e-06)
        lag = lax.broadcasted_iota(jnp.int32, (chunk, 1), 0) // REF + place[0] * (chunk // REF)
        denom = (slab_rows - lag).astype(jnp.float32)
        covariance[...] = total * scale * (for_chunk(ref_scale, chunk) / denom)
        segment_auto[...] = auto[...] * (scale * scale) / segment

    outs = [(partial.shape, jnp.float32), (auto.shape, jnp.float32)]
    return call_on_blocks(kernel, outs, place, powers, auto, partial, arrived, name="finished")


def segment_kernel(strain, tail, out, wide):
    rows, lanes = strain.shape
    pitch = rows // 8
    for lane in range(0, lanes, LANES):
        wide[:rows, :] = strain[:, lane : lane + LANES].astype(jnp.float32)
        wide[rows:, :] = tail[:, lane : lane + LANES].astype(jnp.float32)
        taken = lambda first: wide[pl.ds(first, 8, stride=pitch), :]

        def step(index, carry):
            window, sums = carry
            window = window + (taken(index + LAGS - 1),)
            sums = tuple(total + window[0] * window[lag] for lag, total in enumerate(sums))
            return window[1:], sums

        window = tuple(taken(first) for first in range(LAGS - 1))
        zero = jnp.zeros((8, LANES), jnp.float32)
        _, sums = lax.fori_loop(0, pitch, step, (window, (zero,) * LAGS), unroll=16)
        out[:, lane : lane + LANES] = jnp.concatenate(
            [jnp.sum(total, axis=0, keepdims=True) for total in sums], axis=0
        )


def segment_rows(strain, tail, first, size):
    rows = strain.shape[0]
    return pl.pallas_call(
        segment_kernel,
        grid=(1,),
        in_specs=[
            pl.BlockSpec((rows, size), lambda index: (0, first)),
            pl.BlockSpec((LAGS, size), lambda index: (0, first)),
        ],
        out_specs=pl.BlockSpec((LAGS, size), lambda index: (0, 0)),
        out_shape=jax.ShapeDtypeStruct((LAGS, size), jnp.float32),
        scratch_shapes=[pltpu.VMEM((rows + LAGS, LANES), jnp.float32)],
        compiler_params=pltpu.CompilerParams(vmem_limit_bytes=VMEM_BYTES),
        cost_estimate=pl.CostEstimate(
            flops=64 * LAGS * rows * size, bytes_accessed=rows * size * 2, transcendentals=0
        ),
        name="segment_rows",
    )(strain, tail)


def all_products_kernel(place, strain, own, other, tail, out, held, shifted, edge, sems):
    group = pl.program_id(0)
    copies = fetches(strain, held, sems)
    for copy in copies:
        copy.start()
    edge[...] = padded(tail)
    lag_rows(own, other, place[0], group * GROUP, shifted)
    out[...] = product_of(shifted, held, edge, copies)


def all_products(place, strain, own, other, tail):
    rows, width = strain.shape
    return pl.pallas_call(
        all_products_kernel,
        grid=(LAGS // GROUP,),
        in_specs=product_specs(3),
        out_specs=pl.BlockSpec((GROUP * REF, width), lambda group: (group, 0)),
        out_shape=jax.ShapeDtypeStruct((LAGS * REF, width), jnp.float32),
        scratch_shapes=product_scratch(rows, width),
        compiler_params=pltpu.CompilerParams(vmem_limit_bytes=VMEM_BYTES),
        name="all_products",
    )(place, strain, own, other, tail)


def local(strain):
    rows, width = strain.shape
    count = lax.axis_size("tm")
    chan = lax.axis_index("chan").astype(jnp.int32)
    time = lax.axis_index("tm").astype(jnp.int32)
    slab_rows = rows * count
    chunk = LAGS * REF // count
    pair = lax.shift_right_logical(time, 1)

    own, head = prepared(strain)
    other = exchanged(own, "chan", 1)
    tail = passed_along(head, "tm", -1)

    size = 256
    pieces = [segment_rows(strain, tail, first, size) for first in range(width // size)]
    auto = jnp.concatenate(pieces, axis=1)

    if chunk * 2 == GROUP * REF:
        place = jnp.stack([chan, pair ^ 3, time & 1, pair ^ 2, pair ^ 1, pair])
        keep6, send7, powers0 = first_products(place, strain, own, other, tail, chunk)
        got7 = exchanged(send7, "tm", 1)
        keep4, send5, keep2, send3, keep0, send1 = later_products(
            place, strain, own, other, tail, powers0, chunk, 3
        )
        near0 = got7[chunk:]
        got5 = exchanged(send5, "tm", 1)
        got3 = exchanged(send3, "tm", 1)
        got1 = exchanged(send1, "tm", 1)
        send6, powers1 = merged(keep6, powers0, got7)
        got6 = exchanged(send6, "tm", 2)
        near1 = got6[chunk:]
        send4, powers2 = merged(keep4, powers1, got6, got5, near0)
        got4 = exchanged(send4, "tm", 4)
        got2 = exchanged(resent(keep2, got3, near0, powers1), "tm", 2)
        partial = added(keep0, got1, near0, got2, near1)
        return tuple(finished(rows, slab_rows, time[None], powers2, auto, partial, got4))

    place = jnp.stack([chan, time])
    powers = [jnp.sum(jnp.square(array.astype(jnp.float32)), axis=axis) for array, axis in ((strain, 0), (other, 1))]
    power = lax.psum(jnp.concatenate(powers), "tm")
    inv = 1.0 / jnp.sqrt(power / slab_rows + 1e-06)
    scale = inv[:width]
    ref_scale = jnp.where(
        chan == 0,
        jnp.concatenate([inv[:HALF], inv[width:]]),
        jnp.concatenate([inv[width:], inv[:HALF]]),
    )
    products = all_products(place, strain, own, other, tail)
    summed = lax.psum_scatter(products, "tm", scatter_dimension=0, tiled=True)
    row = time * chunk + jnp.arange(chunk, dtype=jnp.int32)
    row_scale = ref_scale[row % REF] / (slab_rows - row // REF).astype(jnp.float32)
    covariance = summed * scale[None, :] * row_scale[:, None]
    segment_auto = auto * (scale * scale)[None, :] / rows
    return (covariance, segment_auto)


def solution(mesh):
    in_specs = (P(("groups", "tm"), "chan"),)
    out_specs = (P(("groups", "tm"), "chan"), P(("groups", "tm"), "chan"))
    return jax.shard_map(local, mesh=mesh, in_specs=in_specs, out_specs=out_specs, check_vma=False)
```

time: 69.8 us -> 66 us (0.946)
  waiting for transfers between devices: 7.24 us -> 18.7 us
  starting transfers between devices: 24.1 us -> 13.2 us
  local copies, waits for them, and re-layouts: 6.58 us -> 3.19 us
  other arithmetic: 3.13 us -> 0.01 us
  Pallas kernels: 27.4 us -> 29.9 us
    ppermute x11 -> x8, waiting for transfers between devices: 3.34 us -> 13.4 us  [exchanged(): lax.ppermute(value, axis, [(source, source ^ bit) for source in range(cou...]
    ppermute x2 -> x1, starting transfers between devices: 6.3 us -> 1.28 us  [passed_along(): lax.ppermute(value, axis, [(source, source + steps) for source in range(i...]
    ppermute x11 -> x8, starting transfers between devices: 15.2 us -> 11.9 us  [exchanged(): lax.ppermute(value, axis, [(source, source ^ bit) for source in range(cou...]
    reduce_sum x1 -> x0, other arithmetic: 3.11 us -> none  [local(): power = jnp.sum(wide * wide, axis=0, keepdims=True)]
    ppermute x1 -> x0, starting transfers between devices: 2.62 us -> none  [passed_across(): return lax.ppermute(value, ('tm', 'chan'), route)]
    pallas_call x6 -> x8, Pallas kernels: 14.9 us -> 17.4 us  [the longest x1 8.19 us: later_products(): pl.pallas_call(later_products_kernel, in_specs=product_specs(4), out_spec...]
    slice x3 -> x2, local copies, waits for them, and re-layouts: 1.84 us -> 0.01 us  [the longest x1 0.01 us: local(): near1 = got6[chunk:]]
    unnamed x7 -> x8, local copies, waits for them, and re-layouts: 4.56 us -> 3.1 us
  transfers between devices with their start and end apart: 14 -> 9, of which waited for: 2 -> 3; matrix products, arithmetic and copies ran while one was open for 6% -> 0% of each run, Pallas kernels for 32% -> 34%
where the time goes in v3:
time: 66 us; the launch traced here: 65.8 us
  Pallas kernels  29.9 us (45%)
  waiting for transfers between devices  18.7 us (28%)
  starting transfers between devices  13.2 us (20%)
  local copies, waits for them, and re-layouts  3.19 us (5%)
  between operations  0.78 us (1%)
    ppermute x8, waiting for transfers between devices, exchanged(): lax.ppermute(value, axis, [(source, source ^ bit) for source in range(cou...  13.4 us
    pallas_call x4, Pallas kernels, segment_rows(): pl.pallas_call(segment_kernel, grid=(1,), in_specs=[pl.BlockSpec((rows, s...  12.5 us
    ppermute x8, starting transfers between devices, exchanged(): lax.ppermute(value, axis, [(source, source ^ bit) for source in range(cou...  11.9 us
    pallas_call x1, Pallas kernels, later_products(): pl.pallas_call(later_products_kernel, in_specs=product_specs(4), out_spec...  8.19 us
    ppermute x1, waiting for transfers between devices, passed_along(): lax.ppermute(value, axis, [(source, source + steps) for source in range(i...  5.27 us
    pallas_call x1, Pallas kernels, first_products(): pl.pallas_call(first_products_kernel, in_specs=product_specs(3), out_spec...  3.72 us
    pallas_call x5, Pallas kernels, call_on_blocks(): pl.pallas_call(kernel, in_specs=[smem if array.dtype == jnp.int32 else vm...  3.61 us
    unnamed x8, local copies, waits for them, and re-layouts  3.1 us
  transfers between devices with their start and end apart: 9, of which 3 were waited for; matrix products, arithmetic and copies ran while one was open for 0% of the time, Pallas kernels for 34%

profile of v3, /device:TPU:0, one launch (start us, length us, event | category | flops | bytes accessed | tf_op | source)
XLA Modules:
  0.0 65.8 jit_solution(2761778889467031660)
XLA Ops:
  0.6 1.9 %prepared.1 = (bf16[32,2048]{1,0:T(8,128)(2,1)}, bf16[16,1024]{1,0:T(8,128)(2,1)}) custom-call(bf16[2048,1024]{1,0:T(8,128)(2,1)} %strain.11, bf16[2048,1024]{1,0:T(8,128)(2,1)} %strain.11), custom_call_target="tpu_custom_call" | custom-call | tf_op jit(solution)/shard_map/prepared/pallas_call | solution.py:102
  2.5 0.5 collective-permute-start
  3.0 1.3 %collective-permute-start.1 = (bf16[16,1024]{1,0:T(8,128)(2,1)}, bf16[16,1024]{1,0:T(8,128)(2,1)S(1)}, u32[]{:S(2)}, u32[]{:S(2)}) collective-permute-start(bf16[16,1024]{1,0:T(8,128)(2,1)} %get-tuple-element.18), channel_id=1, source_target_pairs={{2,0},{4,2},{6,4},{8,6},{10,8},{12,10},{14,12},{3,1},{5,3},{7,5},{... | collective-permute-start | bytes 98312 | tf_op jit(solution)/shard_map/ppermute | solution.py:24
  4.3 0.1 stack.27.place
  4.4 5.3 %collective-permute-done.1.tail = bf16[16,1024]{1,0:T(8,128)(2,1)S(1)} collective-permute-done((bf16[16,1024]{1,0:T(8,128)(2,1)}, bf16[16,1024]{1,0:T(8,128)(2,1)S(1)}, u32[]{:S(2)}, u32[]{:S(2)}) %collective-permute-start.1) | collective-permute-done | bytes 32800 | tf_op jit(solution)/shard_map/ppermute | solution.py:24
  9.6 0.0 collective-permute-done.other
  9.6 0.0 copy-start
  9.6 2.2 %copy-done = bf16[2048,1024]{1,0:T(8,128)(2,1)S(1)} copy-done((bf16[2048,1024]{1,0:T(8,128)(2,1)S(1)}, bf16[2048,1024]{1,0:T(8,128)(2,1)}, u32[]{:S(2)}) %copy-start) | copy-done | bytes 4194328
  11.8 0.0 copy-start.2
  11.8 0.9 %copy-done.2 = bf16[32,2048]{1,0:T(8,128)(2,1)S(1)} copy-done((bf16[32,2048]{1,0:T(8,128)(2,1)S(1)}, bf16[32,2048]{1,0:T(8,128)(2,1)}, u32[]{:S(2)}) %copy-start.2) | copy-done | bytes 131096
  12.7 0.0 copy-start.3
  12.7 3.7 %first_products.1 = (f32[128,1024]{1,0:T(8,128)S(1)}, bf16[136,1024]{1,0:T(8,128)(2,1)S(1)}, bf16[8,1024]{1,0:T(8,128)(2,1)S(1)}) custom-call(s32[6]{0:T(128)S(1)} %stack.27.place, bf16[2048,1024]{1,0:T(8,128)(2,1)S(1)} %copy-done, bf16[32,2048]{1,0:T(8,128)(2,1)S(1)} %copy-done.2, bf16[32,2048]{1,0:T(8,128)(2,1)S(1)} %collective-permute-done.other, ...), custom_call_target="tpu_custom_call" | custom-call | flops 2147483648 | bytes 4194304 | tf_op jit(solution)/shard_map/first_products/pallas_call | solution.py:206
  16.4 2.8 %collective-permute-start.2 = (bf16[136,1024]{1,0:T(8,128)(2,1)S(1)}, bf16[136,1024]{1,0:T(8,128)(2,1)S(1)}, u32[]{:S(2)}, u32[]{:S(2)}) collective-permute-start(bf16[136,1024]{1,0:T(8,128)(2,1)S(1)} %get-tuple-element.22), channel_id=1, source_target_pairs={{0,2},{2,0},{4,6},{6,4},{8,10},{10,8},{12,14},{14,12},{1,3},{3,1},... | collective-permute-start | bytes 835592 | tf_op jit(solution)/shard_map/ppermute | solution.py:29
  19.3 6.2 %collective-permute-done.2.refs_2_ = bf16[136,1024]{1,0:T(8,128)(2,1)S(1)} collective-permute-done((bf16[136,1024]{1,0:T(8,128)(2,1)S(1)}, bf16[136,1024]{1,0:T(8,128)(2,1)S(1)}, u32[]{:S(2)}, u32[]{:S(2)}) %collective-permute-start.2) | collective-permute-done | bytes 278560 | tf_op jit(solution)/shard_map/ppermute | solution.py:29
  25.4 0.6 merged.2
  26.0 0.0 copy-start.1
  26.0 1.6 %collective-permute-start.3 = (bf16[136,1024]{1,0:T(8,128)(2,1)S(1)}, bf16[136,1024]{1,0:T(8,128)(2,1)S(1)}, u32[]{:S(2)}, u32[]{:S(2)}) collective-permute-start(bf16[136,1024]{1,0:T(8,128)(2,1)S(1)} %get-tuple-element.24), channel_id=1, source_target_pairs={{0,4},{2,6},{4,0},{6,2},{8,12},{10,14},{12,8},{14,10},{1,5},{3,7},... | collective-permute-start | bytes 835592 | tf_op jit(solution)/shard_map/ppermute | solution.py:29
  27.7 0.0 copy-done.3
  27.7 8.2 %later_products.1 = (f32[128,1024]{1,0:T(8,128)S(1)}, bf16[128,1024]{1,0:T(8,128)(2,1)S(1)}, f32[128,1024]{1,0:T(8,128)S(1)}, bf16[128,1024]{1,0:T(8,128)(2,1)S(...) custom-call(s32[6]{0:T(128)S(1)} %stack.27.place, bf16[2048,1024]{1,0:T(8,128)(2,1)} %strain.11, ...), custom_call_target="tpu_custom_call" | custom-call | flops 6442450944 | bytes 4194304 | tf_op jit(solution)/shard_map/later_products/pallas_call | solution.py:245
  35.9 1.8 %collective-permute-start.4 = (bf16[128,1024]{1,0:T(8,128)(2,1)S(1)}, bf16[128,1024]{1,0:T(8,128)(2,1)S(1)}, u32[]{:S(2)}, u32[]{:S(2)}) collective-permute-start(bf16[128,1024]{1,0:T(8,128)(2,1)S(1)} %get-tuple-element.25), channel_id=1, source_target_pairs={{0,2},{2,0},{4,6},{6,4},{8,10},{10,8},{12,14},{14,12},{1,3},{3,1},... | collective-permute-start | bytes 786440 | tf_op jit(solution)/shard_map/ppermute | solution.py:29
  37.7 0.3 collective-permute-start.6
  37.9 7.2 %collective-permute-done.4.refs_3_ = bf16[128,1024]{1,0:T(8,128)(2,1)S(1)} collective-permute-done((bf16[128,1024]{1,0:T(8,128)(2,1)S(1)}, bf16[128,1024]{1,0:T(8,128)(2,1)S(1)}, u32[]{:S(2)}, u32[]{:S(2)}) %collective-permute-start.4) | collective-permute-done | bytes 262176 | tf_op jit(solution)/shard_map/ppermute | solution.py:29
  45.2 0.0 collective-permute-done.3.refs_2_
  45.2 0.8 %merged.3 = (bf16[136,1024]{1,0:T(8,128)(2,1)S(1)}, bf16[8,1024]{1,0:T(8,128)(2,1)S(1)}) custom-call(f32[128,1024]{1,0:T(8,128)S(1)} %get-tuple-element.20.refs_0_, bf16[8,1024]{1,0:T(8,128)(2,1)S(1)} %get-tuple-element.23.refs_1_.powers, bf16[136,1024]{1,0:T(8,128)(2,1)S(1)} %collective-permute-done.3.refs_2_, ...), custom_call_target="tpu_custom_call" | custom-call | bytes 2097152 | tf_op jit(solution)/shard_map/merged/pallas_call | solution.py:266
  46.0 1.9 %collective-permute-start.8 = (bf16[136,1024]{1,0:T(8,128)(2,1)S(1)}, bf16[136,1024]{1,0:T(8,128)(2,1)S(1)}, u32[]{:S(2)}, u32[]{:S(2)}) collective-permute-start(bf16[136,1024]{1,0:T(8,128)(2,1)S(1)} %get-tuple-element.31), channel_id=1, source_target_pairs={{0,8},{2,10},{4,12},{6,14},{8,0},{10,2},{12,4},{14,6},{1,9},{3,11}... | collective-permute-start | bytes 835592 | tf_op jit(solution)/shard_map/ppermute | solution.py:29
  47.9 0.0 copy-done.1
  47.9 3.1 %segment_rows.7 = f32[16,256]{1,0:T(8,128)S(1)} custom-call(bf16[2048,1024]{1,0:T(8,128)(2,1)S(1)} %copy-done.1, bf16[16,1024]{1,0:T(8,128)(2,1)S(1)} %collective-permute-done.1.tail), custom_call_target="tpu_custom_call" | custom-call | flops 536870912 | bytes 1048576 | tf_op jit(solution)/shard_map/segment_rows/pallas_call | solution.py:367
  51.0 1.1 %collective-permute-start.5 = (bf16[128,1024]{1,0:T(8,128)(2,1)S(1)}, bf16[128,1024]{1,0:T(8,128)(2,1)S(1)}, u32[]{:S(2)}, u32[]{:S(2)}) collective-permute-start(bf16[128,1024]{1,0:T(8,128)(2,1)S(1)} %get-tuple-element.28), channel_id=1, source_target_pairs={{0,2},{2,0},{4,6},{6,4},{8,10},{10,8},{12,14},{14,12},{1,3},{3,1},... | collective-permute-start | bytes 786440 | tf_op jit(solution)/shard_map/ppermute | solution.py:29
  52.2 0.0 collective-permute-done.6.code
  52.2 0.5 resent.1
  52.7 1.8 %collective-permute-start.7 = (bf16[128,1024]{1,0:T(8,128)(2,1)S(1)}, bf16[128,1024]{1,0:T(8,128)(2,1)S(1)}, u32[]{:S(2)}, u32[]{:S(2)}) collective-permute-start(bf16[128,1024]{1,0:T(8,128)(2,1)S(1)} %resent.1), channel_id=1, source_target_pairs={{0,4},{2,6},{4,0},{6,2},{8,12},{10,14},{12,8},{14,10},{1,5},{3,7},... | collective-permute-start | bytes 786440 | tf_op jit(solution)/shard_map/ppermute | solution.py:29
  54.5 3.1 %segment_rows.6 = f32[16,256]{1,0:T(8,128)S(1)} custom-call(bf16[2048,1024]{1,0:T(8,128)(2,1)S(1)} %copy-done.1, bf16[16,1024]{1,0:T(8,128)(2,1)S(1)} %collective-permute-done.1.tail), custom_call_target="tpu_custom_call" | custom-call | flops 536870912 | bytes 1048576 | tf_op jit(solution)/shard_map/segment_rows/pallas_call | solution.py:367
  57.7 3.1 %segment_rows.5 = f32[16,256]{1,0:T(8,128)S(1)} custom-call(bf16[2048,1024]{1,0:T(8,128)(2,1)S(1)} %copy-done.1, bf16[16,1024]{1,0:T(8,128)(2,1)S(1)} %collective-permute-done.1.tail), custom_call_target="tpu_custom_call" | custom-call | flops 536870912 | bytes 1048576 | tf_op jit(solution)/shard_map/segment_rows/pallas_call | solution.py:367
  60.8 3.1 %segment_rows.4 = f32[16,256]{1,0:T(8,128)S(1)} custom-call(bf16[2048,1024]{1,0:T(8,128)(2,1)S(1)} %copy-done.1, bf16[16,1024]{1,0:T(8,128)(2,1)S(1)} %collective-permute-done.1.tail), custom_call_target="tpu_custom_call" | custom-call | flops 536870912 | bytes 1048576 | tf_op jit(solution)/shard_map/segment_rows/pallas_call | solution.py:367
  64.0 0.0 collective-permute-done.5.code
  64.0 0.0 collective-permute-done.7.other
  64.0 0.6 added.1.partial
  64.6 0.0 collective-permute-done.8.arrived
  64.6 1.2 %finished.1 = (f32[128,1024]{1,0:T(8,128)}, f32[16,1024]{1,0:T(8,128)}) custom-call(s32[1]{0:T(128)} %bitcast.place, bf16[8,1024]{1,0:T(8,128)(2,1)S(1)} %get-tuple-element.26.powers, f32[16,1024]{1,0:T(8,128)S(1)} %pad_maximum_fusion.auto, f32[128,1024]{1,0:T(8,128)S(1)} %added.1.partial, bf16[136,1024]{1,0:T(8,128)(2,1)S(1)} %collective-permute-done.8.arrived), custom_call_target="tpu_custom_call" | custom-call | bytes 2097152 | tf_op jit(solution)/shard_map/finished/pallas_call | solution.py:266
  (3 shorter events, 0.0 us)
Async XLA Ops:
  2.5 7.1 %collective-permute-start = (bf16[32,2048]{1,0:T(8,128)(2,1)}, bf16[32,2048]{1,0:T(8,128)(2,1)S(1)}, u32[]{:S(2)}, u32[]{:S(2)}) collective-permute-start(bf16[32,2048]{1,0:T(8,128)(2,1)} %get-tuple-element.17.own), channel_id=1, source_target_pairs={{0,1},{1,0},{2,3},{3,2},{4,5},{5,4},{6,7},{7,6},{8,9},{9,8},{10,11... | collective-permute-start | bytes 393224 | tf_op jit(solution)/shard_map/ppermute | solution.py:29
  3.0 6.6 %collective-permute-start.1 = (bf16[16,1024]{1,0:T(8,128)(2,1)}, bf16[16,1024]{1,0:T(8,128)(2,1)S(1)}, u32[]{:S(2)}, u32[]{:S(2)}) collective-permute-start(bf16[16,1024]{1,0:T(8,128)(2,1)} %get-tuple-element.18), channel_id=1, source_target_pairs={{2,0},{4,2},{6,4},{8,6},{10,8},{12,10},{14,12},{3,1},{5,3},{7,5},{... | collective-permute-start | bytes 98312 | tf_op jit(solution)/shard_map/ppermute | solution.py:24
  9.6 2.2 %copy-start = (bf16[2048,1024]{1,0:T(8,128)(2,1)S(1)}, bf16[2048,1024]{1,0:T(8,128)(2,1)}, u32[]{:S(2)}) copy-start(bf16[2048,1024]{1,0:T(8,128)(2,1)} %strain.11) | copy-start | bytes 12582916
  11.8 0.9 %copy-start.2 = (bf16[32,2048]{1,0:T(8,128)(2,1)S(1)}, bf16[32,2048]{1,0:T(8,128)(2,1)}, u32[]{:S(2)}) copy-start(bf16[32,2048]{1,0:T(8,128)(2,1)} %get-tuple-element.17.own) | copy-start | bytes 393220
  12.7 14.9 %copy-start.3 = (bf16[32,2048]{1,0:T(8,128)(2,1)S(1)}, bf16[32,2048]{1,0:T(8,128)(2,1)}, u32[]{:S(2)}) copy-start(bf16[32,2048]{1,0:T(8,128)(2,1)} %get-tuple-element.17.own) | copy-start | bytes 393220
  16.4 9.0 %collective-permute-start.2 = (bf16[136,1024]{1,0:T(8,128)(2,1)S(1)}, bf16[136,1024]{1,0:T(8,128)(2,1)S(1)}, u32[]{:S(2)}, u32[]{:S(2)}) collective-permute-start(bf16[136,1024]{1,0:T(8,128)(2,1)S(1)} %get-tuple-element.22), channel_id=1, source_target_pairs={{0,2},{2,0},{4,6},{6,4},{8,10},{10,8},{12,14},{14,12},{1,3},{3,1},... | collective-permute-start | bytes 835592 | tf_op jit(solution)/shard_map/ppermute | solution.py:29
  26.0 21.9 %copy-start.1 = (bf16[2048,1024]{1,0:T(8,128)(2,1)S(1)}, bf16[2048,1024]{1,0:T(8,128)(2,1)}, u32[]{:S(2)}) copy-start(bf16[2048,1024]{1,0:T(8,128)(2,1)} %strain.11) | copy-start | bytes 12582916
  26.0 19.2 %collective-permute-start.3 = (bf16[136,1024]{1,0:T(8,128)(2,1)S(1)}, bf16[136,1024]{1,0:T(8,128)(2,1)S(1)}, u32[]{:S(2)}, u32[]{:S(2)}) collective-permute-start(bf16[136,1024]{1,0:T(8,128)(2,1)S(1)} %get-tuple-element.24), channel_id=1, source_target_pairs={{0,4},{2,6},{4,0},{6,2},{8,12},{10,14},{12,8},{14,10},{1,5},{3,7},... | collective-permute-start | bytes 835592 | tf_op jit(solution)/shard_map/ppermute | solution.py:29
  35.9 9.3 %collective-permute-start.4 = (bf16[128,1024]{1,0:T(8,128)(2,1)S(1)}, bf16[128,1024]{1,0:T(8,128)(2,1)S(1)}, u32[]{:S(2)}, u32[]{:S(2)}) collective-permute-start(bf16[128,1024]{1,0:T(8,128)(2,1)S(1)} %get-tuple-element.25), channel_id=1, source_target_pairs={{0,2},{2,0},{4,6},{6,4},{8,10},{10,8},{12,14},{14,12},{1,3},{3,1},... | collective-permute-start | bytes 786440 | tf_op jit(solution)/shard_map/ppermute | solution.py:29
  37.7 14.5 %collective-permute-start.6 = (bf16[128,1024]{1,0:T(8,128)(2,1)S(1)}, bf16[128,1024]{1,0:T(8,128)(2,1)S(1)}, u32[]{:S(2)}, u32[]{:S(2)}) collective-permute-start(bf16[128,1024]{1,0:T(8,128)(2,1)S(1)} %get-tuple-element.30), channel_id=1, source_target_pairs={{0,2},{2,0},{4,6},{6,4},{8,10},{10,8},{12,14},{14,12},{1,3},{3,1},... | collective-permute-start | bytes 786440 | tf_op jit(solution)/shard_map/ppermute | solution.py:29
  46.0 18.6 %collective-permute-start.8 = (bf16[136,1024]{1,0:T(8,128)(2,1)S(1)}, bf16[136,1024]{1,0:T(8,128)(2,1)S(1)}, u32[]{:S(2)}, u32[]{:S(2)}) collective-permute-start(bf16[136,1024]{1,0:T(8,128)(2,1)S(1)} %get-tuple-element.31), channel_id=1, source_target_pairs={{0,8},{2,10},{4,12},{6,14},{8,0},{10,2},{12,4},{14,6},{1,9},{3,11}... | collective-permute-start | bytes 835592 | tf_op jit(solution)/shard_map/ppermute | solution.py:29
  51.0 12.9 %collective-permute-start.5 = (bf16[128,1024]{1,0:T(8,128)(2,1)S(1)}, bf16[128,1024]{1,0:T(8,128)(2,1)S(1)}, u32[]{:S(2)}, u32[]{:S(2)}) collective-permute-start(bf16[128,1024]{1,0:T(8,128)(2,1)S(1)} %get-tuple-element.28), channel_id=1, source_target_pairs={{0,2},{2,0},{4,6},{6,4},{8,10},{10,8},{12,14},{14,12},{1,3},{3,1},... | collective-permute-start | bytes 786440 | tf_op jit(solution)/shard_map/ppermute | solution.py:29
  52.7 11.3 %collective-permute-start.7 = (bf16[128,1024]{1,0:T(8,128)(2,1)S(1)}, bf16[128,1024]{1,0:T(8,128)(2,1)S(1)}, u32[]{:S(2)}, u32[]{:S(2)}) collective-permute-start(bf16[128,1024]{1,0:T(8,128)(2,1)S(1)} %resent.1), channel_id=1, source_target_pairs={{0,4},{2,6},{4,0},{6,2},{8,12},{10,14},{12,8},{14,10},{1,5},{3,7},... | collective-permute-start | bytes 786440 | tf_op jit(solution)/shard_map/ppermute | solution.py:29

commit v4 on v3

v4 whole, which is shorter than its diff:
```python
import jax
import jax.numpy as jnp
from jax import lax
from jax.experimental import pallas as pl
from jax.experimental.pallas import tpu as pltpu
from jax.sharding import PartitionSpec as P

LAGS = 16
REF = 64
HALF = REF // 2
LANES = 128
EXTRA = 8
FETCHES = 8
GROUP = 4
POWER = 16
CODE_SCALE = 2.0 ** (126 / POWER)
TINY = 1e-35
PIECES = 4
VMEM_BYTES = 32 * 1024 * 1024
SMALL = pl.CostEstimate(flops=0, bytes_accessed=1024, transcendentals=0)


def passed_along(value, axis, steps):
    count = lax.axis_size(axis)
    initial, last = (max(0, -steps), min(count, count - steps))
    return lax.ppermute(value, axis, [(source, source + steps) for source in range(initial, last)])


def exchanged(value, axis, bit):
    count = lax.axis_size(axis)
    return lax.ppermute(value, axis, [(source, source ^ bit) for source in range(count)])


def as_column(row):
    size = row.shape[1]
    eye = lax.broadcasted_iota(jnp.int32, (size, size), 0) == lax.broadcasted_iota(jnp.int32, (size, size), 1)
    return jnp.sum(jnp.where(eye, row, 0.0), axis=1, keepdims=True)


def as_row(column):
    size = column.shape[0]
    eye = lax.broadcasted_iota(jnp.int32, (size, size), 0) == lax.broadcasted_iota(jnp.int32, (size, size), 1)
    return jnp.sum(jnp.where(eye, column, 0.0), axis=0, keepdims=True)


def for_chunk(ref_column, rows):
    return jnp.concatenate([ref_column] * (rows // REF), axis=0)


def bf16_pieces(value):
    high = value.astype(jnp.bfloat16).astype(jnp.float32)
    middle = (value - high).astype(jnp.bfloat16).astype(jnp.float32)
    return high, middle, value - high - middle


def packed(powers, ref_powers, channel_bound):
    rows = list(bf16_pieces(powers))
    refs = jnp.concatenate(bf16_pieces(ref_powers), axis=1)
    pad = jnp.zeros((1, powers.shape[1] - refs.shape[1]), jnp.float32)
    rows += [jnp.concatenate([refs, pad], axis=1), channel_bound]
    rows += [jnp.zeros_like(powers)] * (EXTRA - len(rows))
    return jnp.concatenate(rows, axis=0).astype(jnp.bfloat16)


def unpacked(block):
    wide = block.astype(jnp.float32)
    powers = wide[0:1] + wide[1:2] + wide[2:3]
    refs = wide[3:4, :LANES] + wide[3:4, LANES : 2 * LANES] + wide[3:4, 2 * LANES : 3 * LANES]
    return powers, refs, wide[4:5]


def rounded_up(value):
    return (value * (1.0 + 2.0**-7)).astype(jnp.bfloat16).astype(jnp.float32)


def coded(values, channel_bound, ref_bound):
    channel = lax.rsqrt(jnp.maximum(channel_bound, TINY))
    refs = lax.rsqrt(jnp.maximum(ref_bound, TINY)) * CODE_SCALE
    power = values * channel * for_chunk(refs, values.shape[0])
    for _ in range(4):
        power = power * jnp.abs(power)
    return power.astype(jnp.bfloat16)


def expanded(code, channel_bound, ref_bound):
    channel = jnp.sqrt(jnp.maximum(channel_bound, TINY))
    refs = jnp.sqrt(jnp.maximum(ref_bound, TINY)) * (1.0 / CODE_SCALE)
    wide = code.astype(jnp.float32)
    root = jnp.exp2(jnp.log2(jnp.abs(wide)) * (1.0 / POWER))
    return jnp.where(wide < 0.0, -root, root) * channel * for_chunk(refs, code.shape[0])


def ref_column(ref_powers):
    return as_column(ref_powers)[:REF]


def prepare_kernel(strain, own, head, left, sems):
    rows = left.shape[0]
    step = rows // PIECES
    copies = [
        pltpu.make_async_copy(
            strain.at[pl.ds(index * step, step), pl.ds(0, LANES)], left.at[pl.ds(index * step, step)], sems.at[index]
        )
        for index in range(PIECES)
    ]
    copies.append(pltpu.make_async_copy(strain.at[pl.ds(0, LAGS)], head, sems.at[PIECES]))
    for copy in copies:
        copy.start()
    for index in range(PIECES):
        copies[index].wait()
        here = slice(index * step, (index + 1) * step)
        own[:, here] = left[here, :].astype(jnp.float32).T[:HALF].astype(jnp.bfloat16)
    copies[PIECES].wait()


def prepared(strain):
    rows, width = strain.shape
    vmem = pl.BlockSpec(memory_space=pltpu.VMEM)
    return pl.pallas_call(
        prepare_kernel,
        in_specs=[pl.BlockSpec(memory_space=pl.ANY)],
        out_specs=[vmem, vmem],
        out_shape=[pltpu.VMEM((HALF, rows), strain.dtype), pltpu.VMEM((LAGS, width), strain.dtype)],
        scratch_shapes=[pltpu.VMEM((rows, LANES), strain.dtype), pltpu.SemaphoreType.DMA((PIECES + 1,))],
        compiler_params=pltpu.CompilerParams(vmem_limit_bytes=VMEM_BYTES),
        cost_estimate=SMALL,
        name="prepared",
    )(pltpu.with_memory_space_constraint(strain, pltpu.HBM))


def lag_rows(own, other, chan, first_lag, shifted):
    rows = own.shape[1]
    zeros = jnp.zeros((HALF, LANES), jnp.float32)
    for refs, half in ((own, chan), (other, 1 - chan)):
        long = jnp.concatenate([refs[...].astype(jnp.float32), zeros], axis=1)
        for index in range(GROUP):
            moved = pltpu.roll(long, first_lag + index, 1)
            start = pl.multiple_of(index * REF + half * HALF, HALF)
            shifted[pl.ds(start, HALF), :] = moved.astype(jnp.bfloat16)


def loaded_kernel(strain, held, power, sems):
    step = held.shape[0] // FETCHES
    pieces = [slice(index * step, (index + 1) * step) for index in range(FETCHES)]
    copies = [
        pltpu.make_async_copy(strain.at[pl.ds(here.start, step)], held.at[pl.ds(here.start, step)], sems.at[index])
        for index, here in enumerate(pieces)
    ]
    for copy in copies:
        copy.start()
    total = jnp.zeros((8, held.shape[1]), jnp.float32)
    for copy, here in zip(copies, pieces):
        copy.wait()
        squares = jnp.square(held[here, :].astype(jnp.float32))
        total += jnp.sum(squares.reshape(step // 8, 8, held.shape[1]), axis=0)
    power[...] = jnp.sum(total, axis=0, keepdims=True)


def loaded(strain, after):
    rows, width = strain.shape
    vmem = pl.BlockSpec(memory_space=pltpu.VMEM)

    def kernel(strain, after, held, power, sems):
        loaded_kernel(strain, held, power, sems)

    return pl.pallas_call(
        kernel,
        in_specs=[pl.BlockSpec(memory_space=pl.ANY)] * 2,
        out_specs=[vmem, vmem],
        out_shape=[pltpu.VMEM((rows, width), strain.dtype), pltpu.VMEM((1, width), jnp.float32)],
        scratch_shapes=[pltpu.SemaphoreType.DMA((FETCHES,))],
        compiler_params=pltpu.CompilerParams(vmem_limit_bytes=VMEM_BYTES),
        cost_estimate=SMALL,
        name="loaded",
    )(pltpu.with_memory_space_constraint(strain, pltpu.HBM), after)


def product_of(shifted, held, tail):
    rows = held.shape[0]
    total = jnp.dot(shifted[:, :rows], held[...], preferred_element_type=jnp.float32)
    edge = jnp.concatenate([tail[...], jnp.zeros((LANES - LAGS, tail.shape[1]), tail.dtype)], axis=0)
    return total + jnp.dot(shifted[:, rows:], edge, preferred_element_type=jnp.float32)


def first_products_kernel(place, held, power, own, other, tail, keep, send, powers, shifted):
    chan, group, near = place[0], place[1], place[2]
    lag_rows(own, other, chan, group * GROUP, shifted)
    ours, theirs = [
        jnp.sum(jnp.square(refs[...].astype(jnp.float32)), axis=1, keepdims=True) for refs in (own, other)
    ]
    refs = jnp.where(
        chan == 0, jnp.concatenate([ours, theirs], axis=0), jnp.concatenate([theirs, ours], axis=0)
    )
    product = product_of(shifted, held, tail)
    beyond = jnp.sum(jnp.square(tail[...].astype(jnp.float32)), axis=0, keepdims=True)
    bound = rounded_up(power[...] + beyond)
    pad = jnp.zeros((1, LANES - REF), jnp.float32)
    extra = packed(power[...], jnp.concatenate([as_row(refs), pad], axis=1), bound)
    powers[...] = extra
    chunk = keep.shape[0]
    keep[...] = jnp.where(near == 0, product[:chunk], product[chunk:])
    other_half = jnp.where(near == 0, product[chunk:], product[:chunk])
    send[:chunk] = coded(other_half, bound, refs)
    send[chunk:] = extra


def shifted_scratch(rows, *slots):
    return [pltpu.VMEM((*slots, GROUP * REF, rows + LANES), jnp.bfloat16)]


def first_products(place, held, power, own, other, tail, chunk):
    rows, width = held.shape
    outs = [
        ((chunk, width), jnp.float32),
        ((chunk + EXTRA, width), jnp.bfloat16),
        ((EXTRA, width), jnp.bfloat16),
    ]
    return call_on_blocks(
        first_products_kernel,
        outs,
        place,
        held,
        power,
        own,
        other,
        tail,
        name="first_products",
        scratch=shifted_scratch(rows),
    )


def later_products_kernel(place, held, own, other, tail, powers, *rest):
    chan, near = place[0], place[2]
    shifted = rest[-1]
    _, ref_powers, bound = unpacked(powers[...])
    refs = ref_column(ref_powers)
    slots = (len(rest) - 1) // 2
    for slot in range(slots):
        keep, send = rest[2 * slot], rest[2 * slot + 1]
        chunk = keep.shape[0]
        lag_rows(own, other, chan, place[3 + slot] * GROUP, shifted.at[slot])
        product = product_of(shifted.at[slot], held, tail)
        keep[...] = jnp.where(near == 0, product[:chunk], product[chunk:])
        other_half = jnp.where(near == 0, product[chunk:], product[:chunk])
        send[...] = coded(other_half, bound, refs)


def later_products(place, held, own, other, tail, powers, chunk, slots):
    rows, width = held.shape
    return call_on_blocks(
        later_products_kernel,
        [((chunk, width), jnp.float32), ((chunk, width), jnp.bfloat16)] * slots,
        place,
        held,
        own,
        other,
        tail,
        powers,
        name="later_products",
        scratch=shifted_scratch(rows, slots),
    )


def call_on_blocks(kernel, outs, *arrays, name, after=(), scratch=(), space=pltpu.VMEM):
    vmem = pl.BlockSpec(memory_space=pltpu.VMEM)
    smem = pl.BlockSpec(memory_space=pltpu.SMEM)
    count = len(arrays)

    def body(*refs):
        kernel(*refs[:count], *refs[count + len(after) :])

    return pl.pallas_call(
        body,
        in_specs=[smem if array.dtype == jnp.int32 else vmem for array in arrays]
        + [pl.BlockSpec(memory_space=pl.ANY)] * len(after),
        out_specs=[vmem] * len(outs),
        out_shape=[space(shape, dtype) for shape, dtype in outs],
        scratch_shapes=list(scratch),
        compiler_params=pltpu.CompilerParams(vmem_limit_bytes=VMEM_BYTES),
        cost_estimate=SMALL,
        name=name,
    )(*arrays, *after)


def received(code, powers):
    chunk = code.shape[0] // REF * REF
    _, refs, bound = unpacked(powers[...])
    return expanded(code[:chunk], bound, ref_column(refs))


def joined(powers, arrived):
    ours, ours_refs, ours_bound = unpacked(powers)
    theirs, theirs_refs, theirs_bound = unpacked(arrived)
    bound = rounded_up(ours_bound + theirs_bound)
    return ours + theirs, ours_refs + theirs_refs, bound


def merge_kernel(*refs):
    keep, powers, arrived, out, extra = refs[0], refs[1], refs[2], refs[-2], refs[-1]
    chunk = keep.shape[0]
    total = keep[...] + received(arrived, arrived[chunk:])
    for code, sender in zip(refs[3:-2:2], refs[4:-2:2]):
        total = total + received(code, sender)
    sums, sum_refs, bound = joined(powers[...], arrived[chunk:])
    extra[...] = packed(sums, sum_refs, bound)
    out[:chunk] = coded(total, bound, ref_column(sum_refs))
    out[chunk:] = extra[...]


def merged(keep, powers, arrived, *others, after):
    chunk, width = keep.shape
    outs = [((chunk + EXTRA, width), jnp.bfloat16), ((EXTRA, width), jnp.bfloat16)]
    return call_on_blocks(merge_kernel, outs, keep, powers, arrived, *others, name="merged", after=after)


def resend_kernel(keep, code, sender, powers, out):
    _, refs, bound = unpacked(powers[...])
    out[...] = coded(keep[...] + received(code, sender), bound, ref_column(refs))


def resent(keep, code, sender, powers, after):
    outs = [(keep.shape, jnp.bfloat16)]
    return call_on_blocks(resend_kernel, outs, keep, code, sender, powers, name="resent", after=after)[0]


def add_kernel(keep, code, sender, other, other_sender, out):
    out[...] = keep[...] + received(code, sender) + received(other, other_sender)


def added(*arrays, after):
    outs = [(arrays[0].shape, jnp.float32)]
    return call_on_blocks(add_kernel, outs, *arrays, name="added", after=after)[0]


def finished(segment, slab_rows, place, powers, auto, partial, arrived):
    def kernel(place, powers, auto, partial, arrived, covariance, segment_auto):
        chunk = partial.shape[0]
        total = partial[...] + received(arrived, arrived[chunk:])
        sums, sum_refs, _ = joined(powers[...], arrived[chunk:])
        scale = 1.0 / jnp.sqrt(sums / slab_rows + 1e-06)
        ref_scale = 1.0 / jnp.sqrt(ref_column(sum_refs) / slab_rows + 1e-06)
        lag = lax.broadcasted_iota(jnp.int32, (chunk, 1), 0) // REF + place[0] * (chunk // REF)
        denom = (slab_rows - lag).astype(jnp.float32)
        covariance[...] = total * scale * (for_chunk(ref_scale, chunk) / denom)
        segment_auto[...] = auto[...] * (scale * scale) / segment

    outs = [(partial.shape, jnp.float32), (auto.shape, jnp.float32)]
    return call_on_blocks(kernel, outs, place, powers, auto, partial, arrived, name="finished", space=jax.ShapeDtypeStruct)


def segment_kernel(first, strain, tail, out, wide):
    rows = strain.shape[0]
    pitch = rows // 8
    for index in range(out.shape[1] // LANES):
        here = slice(first + index * LANES, first + (index + 1) * LANES)
        wide[:rows, :] = strain[:, here].astype(jnp.float32)
        wide[rows:, :] = tail[:, here].astype(jnp.float32)
        taken = lambda first: wide[pl.ds(first, 8, stride=pitch), :]

        def step(index, carry):
            window, sums = carry
            window = window + (taken(index + LAGS - 1),)
            sums = tuple(total + window[0] * window[lag] for lag, total in enumerate(sums))
            return window[1:], sums

        window = tuple(taken(first) for first in range(LAGS - 1))
        zero = jnp.zeros((8, LANES), jnp.float32)
        _, sums = lax.fori_loop(0, pitch, step, (window, (zero,) * LAGS), unroll=16)
        out[:, index * LANES : (index + 1) * LANES] = jnp.concatenate(
            [jnp.sum(total, axis=0, keepdims=True) for total in sums], axis=0
        )


def segment_rows(held, tail, first, size, after=()):
    rows = held.shape[0]

    def kernel(*refs):
        segment_kernel(first, *refs)

    return call_on_blocks(
        kernel,
        [((LAGS, size), jnp.float32)],
        held,
        tail,
        name="segment_rows",
        after=after,
        scratch=[pltpu.VMEM((rows + LAGS, LANES), jnp.float32)],
    )[0]


def all_products_kernel(place, held, own, other, tail, out, shifted):
    group = pl.program_id(0)
    lag_rows(own, other, place[0], group * GROUP, shifted)
    out[...] = product_of(shifted, held, tail)


def all_products(place, held, own, other, tail):
    rows, width = held.shape
    vmem = pl.BlockSpec(memory_space=pltpu.VMEM)
    return pl.pallas_call(
        all_products_kernel,
        grid=(LAGS // GROUP,),
        in_specs=[pl.BlockSpec(memory_space=pltpu.SMEM)] + [vmem] * 4,
        out_specs=pl.BlockSpec((GROUP * REF, width), lambda group: (group, 0)),
        out_shape=jax.ShapeDtypeStruct((LAGS * REF, width), jnp.float32),
        scratch_shapes=shifted_scratch(rows),
        compiler_params=pltpu.CompilerParams(vmem_limit_bytes=VMEM_BYTES),
        name="all_products",
    )(place, held, own, other, tail)


def local(strain):
    rows, width = strain.shape
    count = lax.axis_size("tm")
    chan = lax.axis_index("chan").astype(jnp.int32)
    time = lax.axis_index("tm").astype(jnp.int32)
    slab_rows = rows * count
    chunk = LAGS * REF // count
    pair = lax.shift_right_logical(time, 1)

    own, head = prepared(strain)
    other = exchanged(own, "chan", 1)
    tail = passed_along(head, "tm", -1)
    held, power = loaded(strain, own)
    size = width // 4

    if chunk * 2 == GROUP * REF:
        place = jnp.stack([chan, pair ^ 3, time & 1, pair ^ 2, pair ^ 1, pair])
        keep6, send7, powers0 = first_products(place, held, power, own, other, tail, chunk)
        got7 = exchanged(send7, "tm", 1)
        keep4, send5, keep2, send3, keep0, send1 = later_products(
            place, held, own, other, tail, powers0, chunk, 3
        )
        near0 = got7[chunk:]
        got5 = exchanged(send5, "tm", 1)
        got3 = exchanged(send3, "tm", 1)
        got1 = exchanged(send1, "tm", 1)
        send6, powers1 = merged(keep6, powers0, got7, after=(send5,))
        got6 = exchanged(send6, "tm", 2)
        near1 = got6[chunk:]
        autos = [segment_rows(held, tail, 0, size, after=(powers1,))]
        send4, powers2 = merged(keep4, powers1, got6, got5, near0, after=(autos[0],))
        got4 = exchanged(send4, "tm", 4)
        send2 = resent(keep2, got3, near0, powers1, after=(powers2,))
        got2 = exchanged(send2, "tm", 2)
        autos += [segment_rows(held, tail, size * index, size, after=(send2,)) for index in (1, 2, 3)]
        partial = added(keep0, got1, near0, got2, near1, after=(autos[1], autos[2]))
        auto = jnp.concatenate(autos, axis=1)
        return tuple(finished(rows, slab_rows, time[None], powers2, auto, partial, got4))

    place = jnp.stack([chan, time])
    auto = jnp.concatenate([segment_rows(held, tail, size * index, size) for index in range(4)], axis=1)
    power_other = jnp.sum(jnp.square(other.astype(jnp.float32)), axis=1)
    power = lax.psum(jnp.concatenate([power[0], power_other]), "tm")
    inv = 1.0 / jnp.sqrt(power / slab_rows + 1e-06)
    scale = inv[:width]
    ref_scale = jnp.where(
        chan == 0,
        jnp.concatenate([inv[:HALF], inv[width:]]),
        jnp.concatenate([inv[width:], inv[:HALF]]),
    )
    products = all_products(place, held, own, other, tail)
    summed = lax.psum_scatter(products, "tm", scatter_dimension=0, tiled=True)
    row = time * chunk + jnp.arange(chunk, dtype=jnp.int32)
    row_scale = ref_scale[row % REF] / (slab_rows - row // REF).astype(jnp.float32)
    covariance = summed * scale[None, :] * row_scale[:, None]
    segment_auto = auto * (scale * scale)[None, :] / rows
    return (covariance, segment_auto)


def solution(mesh):
    in_specs = (P(("groups", "tm"), "chan"),)
    out_specs = (P(("groups", "tm"), "chan"), P(("groups", "tm"), "chan"))
    return jax.shard_map(local, mesh=mesh, in_specs=in_specs, out_specs=out_specs, check_vma=False)
```

time: 66 us -> 53.9 us (0.82)
  waiting for transfers between devices: 18.7 us -> 5.9 us
  local copies, waits for them, and re-layouts: 3.19 us -> 4.24 us
    ppermute x8, waiting for transfers between devices: 13.4 us -> 5.07 us  [exchanged(): lax.ppermute(value, axis, [(source, source ^ bit) for source in range(cou...]
    ppermute x1, waiting for transfers between devices: 5.27 us -> 0.83 us  [passed_along(): lax.ppermute(value, axis, [(source, source + steps) for source in range(i...]
    unnamed x8 -> x6, local copies, waits for them, and re-layouts: 3.1 us -> 4.15 us
    pallas_call x12 -> x13, Pallas kernels: 29.9 us -> 30 us  [the longest x11 26.5 us: call_on_blocks(): pl.pallas_call(body, in_specs=[smem if array.dtype == jnp.int32 else vmem...]
  transfers between devices with their start and end apart: 9 -> 9, of which waited for: 3 -> 3; matrix products, arithmetic and copies ran while one was open for 0% -> 0% of each run, Pallas kernels for 34% -> 45%
where the time goes in v4:
time: 53.9 us; the launch traced here: 53.7 us
  Pallas kernels  30 us (56%)
  starting transfers between devices  12.8 us (24%)
  waiting for transfers between devices  5.9 us (11%)
  local copies, waits for them, and re-layouts  4.24 us (8%)
  between operations  0.79 us (1%)
    pallas_call x11, Pallas kernels, call_on_blocks(): pl.pallas_call(body, in_specs=[smem if array.dtype == jnp.int32 else vmem...  26.5 us
    ppermute x8, starting transfers between devices, exchanged(): lax.ppermute(value, axis, [(source, source ^ bit) for source in range(cou...  11.5 us
    ppermute x8, waiting for transfers between devices, exchanged(): lax.ppermute(value, axis, [(source, source ^ bit) for source in range(cou...  5.07 us
    unnamed x6, local copies, waits for them, and re-layouts  4.15 us
    pallas_call x1, Pallas kernels, loaded(): pl.pallas_call(kernel, in_specs=[pl.BlockSpec(memory_space=pl.ANY)] * 2,...  2.26 us
    ppermute x1, starting transfers between devices, passed_along(): lax.ppermute(value, axis, [(source, source + steps) for source in range(i...  1.28 us
    pallas_call x1, Pallas kernels, prepared(): pl.pallas_call(prepare_kernel, in_specs=[pl.BlockSpec(memory_space=pl.ANY...  1.28 us
  transfers between devices with their start and end apart: 9, of which 3 were waited for; matrix products, arithmetic and copies ran while one was open for 0% of the time, Pallas kernels for 45%

profile of v4, /device:TPU:0, one launch (start us, length us, event | category | flops | bytes accessed | tf_op | source)
XLA Modules:
  0.0 53.7 jit_solution(12687684255189061226)
XLA Ops:
  0.6 1.3 %prepared.1 = (bf16[32,2048]{1,0:T(8,128)(2,1)S(1)}, bf16[16,1024]{1,0:T(8,128)(2,1)S(1)}) custom-call(bf16[2048,1024]{1,0:T(8,128)(2,1)} %strain.3), custom_call_target="tpu_custom_call" | custom-call | bytes 1024 | tf_op jit(solution)/shard_map/prepared/pallas_call | solution.py:119
  1.9 0.5 collective-permute-start
  2.4 1.3 %collective-permute-start.1 = (bf16[16,1024]{1,0:T(8,128)(2,1)S(1)}, bf16[16,1024]{1,0:T(8,128)(2,1)S(1)}, u32[]{:S(2)}, u32[]{:S(2)}) collective-permute-start(bf16[16,1024]{1,0:T(8,128)(2,1)S(1)} %get-tuple-element.21), channel_id=1, source_target_pairs={{2,0},{4,2},{6,4},{8,6},{10,8},{12,10},{14,12},{3,1},{5,3},{7,5},{... | collective-permute-start | bytes 98312 | tf_op jit(solution)/shard_map/ppermute | solution.py:26
  3.7 2.3 %loaded.1 = (bf16[2048,1024]{1,0:T(8,128)(2,1)S(1)}, f32[1,1024]{1,0:T(1,128)S(1)}) custom-call(bf16[2048,1024]{1,0:T(8,128)(2,1)} %strain.3, bf16[32,2048]{1,0:T(8,128)(2,1)S(1)} %get-tuple-element.19.after.refs_3_.refs_2_), custom_call_target="tpu_custom_call" | custom-call | bytes 1024 | tf_op jit(solution)/shard_map/loaded/pallas_call | solution.py:166
  6.0 0.0 copy-start
  6.0 2.0 %copy-done = bf16[2048,1024]{1,0:T(8,128)(2,1)} copy-done((bf16[2048,1024]{1,0:T(8,128)(2,1)}, bf16[2048,1024]{1,0:T(8,128)(2,1)S(1)}, u32[]{:S(2)}) %copy-start) | copy-done | bytes 4194328
  8.0 0.1 stack.27.refs_0_
  8.0 0.8 %collective-permute-done.1.refs_5_.refs_4_.refs_1_ = bf16[16,1024]{1,0:T(8,128)(2,1)S(1)} collective-permute-done((bf16[16,1024]{1,0:T(8,128)(2,1)S(1)}, bf16[16,1024]{1,0:T(8,128)(2,1)S(1)}, u32[]{:S(2)}, u32[]{:S(2)}) %collective-permute-start.1) | collective-permute-done | bytes 32800 | tf_op jit(solution)/shard_map/ppermute | solution.py:26
  8.9 0.0 collective-permute-done.refs_4_.refs_3_
  8.9 0.0 copy-start.1
  8.9 2.2 %copy-done.1 = bf16[2048,1024]{1,0:T(8,128)(2,1)S(1)} copy-done((bf16[2048,1024]{1,0:T(8,128)(2,1)S(1)}, bf16[2048,1024]{1,0:T(8,128)(2,1)}, u32[]{:S(2)}) %copy-start.1) | copy-done | bytes 4194328
  11.1 0.0 copy-start.2
  11.1 3.0 %first_products.1 = (f32[128,1024]{1,0:T(8,128)S(1)}, bf16[136,1024]{1,0:T(8,128)(2,1)S(1)}, bf16[8,1024]{1,0:T(8,128)(2,1)S(1)}) custom-call(s32[6]{0:T(128)S(1)} %stack.27.refs_0_, bf16[2048,1024]{1,0:T(8,128)(2,1)S(1)} %copy-done.1, f32[1,1024]{1,0:T(1,128)S(1)} %get-tuple-element.22.refs_2_, ...), custom_call_target="tpu_custom_call" | custom-call | bytes 1024 | tf_op jit(solution)/shard_map/first_products/pallas_call | solution.py:272
  14.1 2.8 %collective-permute-start.2 = (bf16[136,1024]{1,0:T(8,128)(2,1)S(1)}, bf16[136,1024]{1,0:T(8,128)(2,1)S(1)}, u32[]{:S(2)}, u32[]{:S(2)}) collective-permute-start(bf16[136,1024]{1,0:T(8,128)(2,1)S(1)} %get-tuple-element.26), channel_id=1, source_target_pairs={{0,2},{2,0},{4,6},{6,4},{8,10},{10,8},{12,14},{14,12},{1,3},{3,1},... | collective-permute-start | bytes 835592 | tf_op jit(solution)/shard_map/ppermute | solution.py:31
  17.0 7.1 %later_products.1 = (f32[128,1024]{1,0:T(8,128)S(1)}, bf16[128,1024]{1,0:T(8,128)(2,1)S(1)}, f32[128,1024]{1,0:T(8,128)S(1)}, bf16[128,1024]{1,0:T(8,128)(2,1)S(...) custom-call(s32[6]{0:T(128)S(1)} %stack.27.refs_0_, bf16[2048,1024]{1,0:T(8,128)(2,1)S(1)} %copy-done.1, ...), custom_call_target="tpu_custom_call" | custom-call | bytes 1024 | tf_op jit(solution)/shard_map/later_products/pallas_call | solution.py:272
  24.1 0.0 collective-permute-done.2.refs_2_
  24.1 0.6 %merged.2 = (bf16[136,1024]{1,0:T(8,128)(2,1)S(1)}, bf16[8,1024]{1,0:T(8,128)(2,1)S(1)}) custom-call(f32[128,1024]{1,0:T(8,128)S(1)} %get-tuple-element.25.refs_0_, bf16[8,1024]{1,0:T(8,128)(2,1)S(1)} %get-tuple-element.23.refs_5_.refs_1_, bf16[136,1024]{1,0:T(8,128)(2,1)S(1)} %collective-permute-done.2.refs_2_, bf16[128,1024]{1,0:T(8,128)(2,1)S(1)} %get-tuple-element.27.refs_3_), custom_call_target="tpu_custom_call" | custom-call | bytes 1024 | tf_op jit(solution)/shard_map/merged/pallas_call | solution.py:272
  24.6 2.7 %collective-permute-start.3 = (bf16[136,1024]{1,0:T(8,128)(2,1)S(1)}, bf16[136,1024]{1,0:T(8,128)(2,1)S(1)}, u32[]{:S(2)}, u32[]{:S(2)}) collective-permute-start(bf16[136,1024]{1,0:T(8,128)(2,1)S(1)} %get-tuple-element.29), channel_id=1, source_target_pairs={{0,4},{2,6},{4,0},{6,2},{8,12},{10,14},{12,8},{14,10},{1,5},{3,7},... | collective-permute-start | bytes 835592 | tf_op jit(solution)/shard_map/ppermute | solution.py:31
  27.3 0.7 %collective-permute-start.4 = (bf16[128,1024]{1,0:T(8,128)(2,1)S(1)}, bf16[128,1024]{1,0:T(8,128)(2,1)S(1)}, u32[]{:S(2)}, u32[]{:S(2)}) collective-permute-start(bf16[128,1024]{1,0:T(8,128)(2,1)S(1)} %get-tuple-element.27.refs_3_), channel_id=1, source_target_pairs={{0,2},{2,0},{4,6},{6,4},{8,10},{10,8},{12,14},{14,12},{1,3},{3,1},... | collective-permute-start | bytes 786440 | tf_op jit(solution)/shard_map/ppermute | solution.py:31
  28.0 1.4 %collective-permute-start.5 = (bf16[128,1024]{1,0:T(8,128)(2,1)S(1)}, bf16[128,1024]{1,0:T(8,128)(2,1)S(1)}, u32[]{:S(2)}, u32[]{:S(2)}) collective-permute-start(bf16[128,1024]{1,0:T(8,128)(2,1)S(1)} %get-tuple-element.32), channel_id=1, source_target_pairs={{0,2},{2,0},{4,6},{6,4},{8,10},{10,8},{12,14},{14,12},{1,3},{3,1},... | collective-permute-start | bytes 786440 | tf_op jit(solution)/shard_map/ppermute | solution.py:31
  29.4 0.0 copy-done.2
  29.4 3.3 %segment_rows.4.refs_5_ = f32[16,256]{1,0:T(8,128)S(1)} custom-call(bf16[2048,1024]{1,0:T(8,128)(2,1)S(1)} %copy-done.2, bf16[16,1024]{1,0:T(8,128)(2,1)S(1)} %collective-permute-done.1.refs_5_.refs_4_.refs_1_, bf16[8,1024]{1,0:T(8,128)(2,1)S(1)} %get-tuple-element.28.refs_2_.refs_1_.refs_3_), custom_call_target="tpu_custom_call" | custom-call | bytes 1024 | tf_op jit(solution)/shard_map/segment_rows/pallas_call | solution.py:272
  32.7 3.9 %collective-permute-done.4.refs_3_ = bf16[128,1024]{1,0:T(8,128)(2,1)S(1)} collective-permute-done((bf16[128,1024]{1,0:T(8,128)(2,1)S(1)}, bf16[128,1024]{1,0:T(8,128)(2,1)S(1)}, u32[]{:S(2)}, u32[]{:S(2)}) %collective-permute-start.4) | collective-permute-done | bytes 262176 | tf_op jit(solution)/shard_map/ppermute | solution.py:31
  36.6 0.0 collective-permute-done.3.refs_2_
  36.6 0.8 %merged.3 = (bf16[136,1024]{1,0:T(8,128)(2,1)S(1)}, bf16[8,1024]{1,0:T(8,128)(2,1)S(1)}) custom-call(f32[128,1024]{1,0:T(8,128)S(1)} %get-tuple-element.24.refs_0_, bf16[8,1024]{1,0:T(8,128)(2,1)S(1)} %get-tuple-element.28.refs_2_.refs_1_.refs_3_, bf16[136,1024]{1,0:T(8,128)(2,1)S(1)} %collective-permute-done.3.refs_2_, ...), custom_call_target="tpu_custom_call" | custom-call | bytes 1024 | tf_op jit(solution)/shard_map/merged/pallas_call | solution.py:272
  37.4 2.7 %collective-permute-start.8 = (bf16[136,1024]{1,0:T(8,128)(2,1)S(1)}, bf16[136,1024]{1,0:T(8,128)(2,1)S(1)}, u32[]{:S(2)}, u32[]{:S(2)}) collective-permute-start(bf16[136,1024]{1,0:T(8,128)(2,1)S(1)} %get-tuple-element.35), channel_id=1, source_target_pairs={{0,8},{2,10},{4,12},{6,14},{8,0},{10,2},{12,4},{14,6},{1,9},{3,11}... | collective-permute-start | bytes 835592 | tf_op jit(solution)/shard_map/ppermute | solution.py:31
  40.1 0.6 %collective-permute-start.6 = (bf16[128,1024]{1,0:T(8,128)(2,1)S(1)}, bf16[128,1024]{1,0:T(8,128)(2,1)S(1)}, u32[]{:S(2)}, u32[]{:S(2)}) collective-permute-start(bf16[128,1024]{1,0:T(8,128)(2,1)S(1)} %get-tuple-element.34), channel_id=1, source_target_pairs={{0,2},{2,0},{4,6},{6,4},{8,10},{10,8},{12,14},{14,12},{1,3},{3,1},... | collective-permute-start | bytes 786440 | tf_op jit(solution)/shard_map/ppermute | solution.py:31
  40.7 1.1 %collective-permute-done.5.refs_1_ = bf16[128,1024]{1,0:T(8,128)(2,1)S(1)} collective-permute-done((bf16[128,1024]{1,0:T(8,128)(2,1)S(1)}, bf16[128,1024]{1,0:T(8,128)(2,1)S(1)}, u32[]{:S(2)}, u32[]{:S(2)}) %collective-permute-start.5) | collective-permute-done | bytes 262176 | tf_op jit(solution)/shard_map/ppermute | solution.py:31
  41.8 0.5 resent.1.refs_2_
  42.3 0.1 collective-permute-start.7
  42.4 3.1 %segment_rows.5.refs_5_ = f32[16,256]{1,0:T(8,128)S(1)} custom-call(bf16[2048,1024]{1,0:T(8,128)(2,1)S(1)} %copy-done.2, bf16[16,1024]{1,0:T(8,128)(2,1)S(1)} %collective-permute-done.1.refs_5_.refs_4_.refs_1_, bf16[128,1024]{1,0:T(8,128)(2,1)S(1)} %resent.1.refs_2_), custom_call_target="tpu_custom_call" | custom-call | bytes 1024 | tf_op jit(solution)/shard_map/segment_rows/pallas_call | solution.py:272
  45.6 3.1 %segment_rows.6.refs_6_ = f32[16,256]{1,0:T(8,128)S(1)} custom-call(bf16[2048,1024]{1,0:T(8,128)(2,1)S(1)} %copy-done.2, bf16[16,1024]{1,0:T(8,128)(2,1)S(1)} %collective-permute-done.1.refs_5_.refs_4_.refs_1_, bf16[128,1024]{1,0:T(8,128)(2,1)S(1)} %resent.1.refs_2_), custom_call_target="tpu_custom_call" | custom-call | bytes 1024 | tf_op jit(solution)/shard_map/segment_rows/pallas_call | solution.py:272
  48.7 3.1 %segment_rows.7 = f32[16,256]{1,0:T(8,128)S(1)} custom-call(bf16[2048,1024]{1,0:T(8,128)(2,1)S(1)} %copy-done.2, bf16[16,1024]{1,0:T(8,128)(2,1)S(1)} %collective-permute-done.1.refs_5_.refs_4_.refs_1_, bf16[128,1024]{1,0:T(8,128)(2,1)S(1)} %resent.1.refs_2_), custom_call_target="tpu_custom_call" | custom-call | bytes 1024 | tf_op jit(solution)/shard_map/segment_rows/pallas_call | solution.py:272
  51.9 0.0 collective-permute-done.6.refs_1_
  51.9 0.0 collective-permute-done.7.refs_3_
  51.9 0.5 %added.1.refs_3_ = f32[128,1024]{1,0:T(8,128)S(1)} custom-call(f32[128,1024]{1,0:T(8,128)S(1)} %get-tuple-element.33.refs_0_, bf16[128,1024]{1,0:T(8,128)(2,1)S(1)} %collective-permute-done.6.refs_1_, bf16[8,1024]{1,0:T(8,128)(2,1)S(1)} %slice.8.refs_4_.refs_2_, bf16[128,1024]{1,0:T(8,128)(2,1)S(1)} %collective-permute-done.7.refs_3_, ...), custom_call_target="tpu_custom_call" | custom-call | bytes 1024 | tf_op jit(solution)/shard_map/added/pallas_call | solution.py:272
  52.5 0.0 collective-permute-done.8.refs_4_
  52.5 1.2 %finished.1 = (f32[128,1024]{1,0:T(8,128)}, f32[16,1024]{1,0:T(8,128)}) custom-call(s32[1]{0:T(128)} %bitcast.refs_0_, bf16[8,1024]{1,0:T(8,128)(2,1)S(1)} %get-tuple-element.30.refs_4_.refs_1_, f32[16,1024]{1,0:T(8,128)S(1)} %pad_maximum_fusion.refs_2_, f32[128,1024]{1,0:T(8,128)S(1)} %added.1.refs_3_, bf16[136,1024]{1,0:T(8,128)(2,1)S(1)} %collective-permute-done.8.refs_4_), custom_call_target="tpu_custom_call" | custom-call | bytes 1024 | tf_op jit(solution)/shard_map/finished/pallas_call | solution.py:272
  (3 shorter events, 0.0 us)
Async XLA Ops:
  1.9 7.0 %collective-permute-start = (bf16[32,2048]{1,0:T(8,128)(2,1)S(1)}, bf16[32,2048]{1,0:T(8,128)(2,1)S(1)}, u32[]{:S(2)}, u32[]{:S(2)}) collective-permute-start(bf16[32,2048]{1,0:T(8,128)(2,1)S(1)} %get-tuple-element.19.after.refs_3_.refs_2_), channel_id=1, source_target_pairs={{0,1},{1,0},{2,3},{3,2},{4,5},{5,4},{6,7},{7,6},{8,9},{9,8},{10,11... | collective-permute-start | bytes 393224 | tf_op jit(solution)/shard_map/ppermute | solution.py:31
  2.4 6.4 %collective-permute-start.1 = (bf16[16,1024]{1,0:T(8,128)(2,1)S(1)}, bf16[16,1024]{1,0:T(8,128)(2,1)S(1)}, u32[]{:S(2)}, u32[]{:S(2)}) collective-permute-start(bf16[16,1024]{1,0:T(8,128)(2,1)S(1)} %get-tuple-element.21), channel_id=1, source_target_pairs={{2,0},{4,2},{6,4},{8,6},{10,8},{12,10},{14,12},{3,1},{5,3},{7,5},{... | collective-permute-start | bytes 98312 | tf_op jit(solution)/shard_map/ppermute | solution.py:26
  6.0 2.0 %copy-start = (bf16[2048,1024]{1,0:T(8,128)(2,1)}, bf16[2048,1024]{1,0:T(8,128)(2,1)S(1)}, u32[]{:S(2)}) copy-start(bf16[2048,1024]{1,0:T(8,128)(2,1)S(1)} %get-tuple-element.20.refs_1_.refs_0_) | copy-start | bytes 12582916
  8.9 2.2 %copy-start.1 = (bf16[2048,1024]{1,0:T(8,128)(2,1)S(1)}, bf16[2048,1024]{1,0:T(8,128)(2,1)}, u32[]{:S(2)}) copy-start(bf16[2048,1024]{1,0:T(8,128)(2,1)} %copy-done) | copy-start | bytes 12582916
  11.1 18.3 %copy-start.2 = (bf16[2048,1024]{1,0:T(8,128)(2,1)S(1)}, bf16[2048,1024]{1,0:T(8,128)(2,1)}, u32[]{:S(2)}) copy-start(bf16[2048,1024]{1,0:T(8,128)(2,1)} %copy-done) | copy-start | bytes 12582916
  14.1 9.9 %collective-permute-start.2 = (bf16[136,1024]{1,0:T(8,128)(2,1)S(1)}, bf16[136,1024]{1,0:T(8,128)(2,1)S(1)}, u32[]{:S(2)}, u32[]{:S(2)}) collective-permute-start(bf16[136,1024]{1,0:T(8,128)(2,1)S(1)} %get-tuple-element.26), channel_id=1, source_target_pairs={{0,2},{2,0},{4,6},{6,4},{8,10},{10,8},{12,14},{14,12},{1,3},{3,1},... | collective-permute-start | bytes 835592 | tf_op jit(solution)/shard_map/ppermute | solution.py:31
  24.6 12.0 %collective-permute-start.3 = (bf16[136,1024]{1,0:T(8,128)(2,1)S(1)}, bf16[136,1024]{1,0:T(8,128)(2,1)S(1)}, u32[]{:S(2)}, u32[]{:S(2)}) collective-permute-start(bf16[136,1024]{1,0:T(8,128)(2,1)S(1)} %get-tuple-element.29), channel_id=1, source_target_pairs={{0,4},{2,6},{4,0},{6,2},{8,12},{10,14},{12,8},{14,10},{1,5},{3,7},... | collective-permute-start | bytes 835592 | tf_op jit(solution)/shard_map/ppermute | solution.py:31
  27.3 9.2 %collective-permute-start.4 = (bf16[128,1024]{1,0:T(8,128)(2,1)S(1)}, bf16[128,1024]{1,0:T(8,128)(2,1)S(1)}, u32[]{:S(2)}, u32[]{:S(2)}) collective-permute-start(bf16[128,1024]{1,0:T(8,128)(2,1)S(1)} %get-tuple-element.27.refs_3_), channel_id=1, source_target_pairs={{0,2},{2,0},{4,6},{6,4},{8,10},{10,8},{12,14},{14,12},{1,3},{3,1},... | collective-permute-start | bytes 786440 | tf_op jit(solution)/shard_map/ppermute | solution.py:31
  28.0 13.8 %collective-permute-start.5 = (bf16[128,1024]{1,0:T(8,128)(2,1)S(1)}, bf16[128,1024]{1,0:T(8,128)(2,1)S(1)}, u32[]{:S(2)}, u32[]{:S(2)}) collective-permute-start(bf16[128,1024]{1,0:T(8,128)(2,1)S(1)} %get-tuple-element.32), channel_id=1, source_target_pairs={{0,2},{2,0},{4,6},{6,4},{8,10},{10,8},{12,14},{14,12},{1,3},{3,1},... | collective-permute-start | bytes 786440 | tf_op jit(solution)/shard_map/ppermute | solution.py:31
  37.4 15.1 %collective-permute-start.8 = (bf16[136,1024]{1,0:T(8,128)(2,1)S(1)}, bf16[136,1024]{1,0:T(8,128)(2,1)S(1)}, u32[]{:S(2)}, u32[]{:S(2)}) collective-permute-start(bf16[136,1024]{1,0:T(8,128)(2,1)S(1)} %get-tuple-element.35), channel_id=1, source_target_pairs={{0,8},{2,10},{4,12},{6,14},{8,0},{10,2},{12,4},{14,6},{1,9},{3,11}... | collective-permute-start | bytes 835592 | tf_op jit(solution)/shard_map/ppermute | solution.py:31
  40.1 11.8 %collective-permute-start.6 = (bf16[128,1024]{1,0:T(8,128)(2,1)S(1)}, bf16[128,1024]{1,0:T(8,128)(2,1)S(1)}, u32[]{:S(2)}, u32[]{:S(2)}) collective-permute-start(bf16[128,1024]{1,0:T(8,128)(2,1)S(1)} %get-tuple-element.34), channel_id=1, source_target_pairs={{0,2},{2,0},{4,6},{6,4},{8,10},{10,8},{12,14},{14,12},{1,3},{3,1},... | collective-permute-start | bytes 786440 | tf_op jit(solution)/shard_map/ppermute | solution.py:31
  42.3 9.6 %collective-permute-start.7 = (bf16[128,1024]{1,0:T(8,128)(2,1)S(1)}, bf16[128,1024]{1,0:T(8,128)(2,1)S(1)}, u32[]{:S(2)}, u32[]{:S(2)}) collective-permute-start(bf16[128,1024]{1,0:T(8,128)(2,1)S(1)} %resent.1.refs_2_), channel_id=1, source_target_pairs={{0,4},{2,6},{4,0},{6,2},{8,12},{10,14},{12,8},{14,10},{1,5},{3,7},... | collective-permute-start | bytes 786440 | tf_op jit(solution)/shard_map/ppermute | solution.py:31

commit v5 on v4

v5 whole, which is shorter than its diff:
```python
import jax
import jax.numpy as jnp
from jax import lax
from jax.experimental import pallas as pl
from jax.experimental.pallas import tpu as pltpu
from jax.sharding import PartitionSpec as P

LAGS = 16
REF = 64
HALF = REF // 2
LANES = 128
EXTRA = 8
FETCHES = 8
GROUP = 4
POWER = 16
CODE_SCALE = 2.0 ** (126 / POWER)
TINY = 1e-35
PIECES = 4
VMEM_BYTES = 32 * 1024 * 1024
SMALL = pl.CostEstimate(flops=0, bytes_accessed=1024, transcendentals=0)


def passed_along(value, axis, steps):
    count = lax.axis_size(axis)
    initial, last = (max(0, -steps), min(count, count - steps))
    return lax.ppermute(value, axis, [(source, source + steps) for source in range(initial, last)])


def exchanged(value, axis, bit):
    count = lax.axis_size(axis)
    return lax.ppermute(value, axis, [(source, source ^ bit) for source in range(count)])


def as_column(row):
    size = row.shape[1]
    eye = lax.broadcasted_iota(jnp.int32, (size, size), 0) == lax.broadcasted_iota(jnp.int32, (size, size), 1)
    return jnp.sum(jnp.where(eye, row, 0.0), axis=1, keepdims=True)


def as_row(column):
    size = column.shape[0]
    eye = lax.broadcasted_iota(jnp.int32, (size, size), 0) == lax.broadcasted_iota(jnp.int32, (size, size), 1)
    return jnp.sum(jnp.where(eye, column, 0.0), axis=0, keepdims=True)


def for_chunk(ref_column, rows):
    return jnp.concatenate([ref_column] * (rows // REF), axis=0)


def bf16_pieces(value):
    high = value.astype(jnp.bfloat16).astype(jnp.float32)
    middle = (value - high).astype(jnp.bfloat16).astype(jnp.float32)
    return high, middle, value - high - middle


def packed(powers, ref_powers, channel_bound):
    rows = list(bf16_pieces(powers))
    refs = jnp.concatenate(bf16_pieces(ref_powers), axis=1)
    pad = jnp.zeros((1, powers.shape[1] - refs.shape[1]), jnp.float32)
    rows += [jnp.concatenate([refs, pad], axis=1), channel_bound]
    rows += [jnp.zeros_like(powers)] * (EXTRA - len(rows))
    return jnp.concatenate(rows, axis=0).astype(jnp.bfloat16)


def unpacked(block):
    wide = block.astype(jnp.float32)
    powers = wide[0:1] + wide[1:2] + wide[2:3]
    refs = wide[3:4, :LANES] + wide[3:4, LANES : 2 * LANES] + wide[3:4, 2 * LANES : 3 * LANES]
    return powers, refs, wide[4:5]


def rounded_up(value):
    return (value * (1.0 + 2.0**-7)).astype(jnp.bfloat16).astype(jnp.float32)


def coded(values, channel_bound, ref_bound):
    channel = lax.rsqrt(jnp.maximum(channel_bound, TINY))
    refs = lax.rsqrt(jnp.maximum(ref_bound, TINY)) * CODE_SCALE
    power = values * channel * for_chunk(refs, values.shape[0])
    for _ in range(4):
        power = power * jnp.abs(power)
    return power.astype(jnp.bfloat16)


def expanded(code, channel_bound, ref_bound):
    channel = jnp.sqrt(jnp.maximum(channel_bound, TINY))
    refs = jnp.sqrt(jnp.maximum(ref_bound, TINY)) * (1.0 / CODE_SCALE)
    wide = code.astype(jnp.float32)
    root = jnp.exp2(jnp.log2(jnp.abs(wide)) * (1.0 / POWER))
    return jnp.where(wide < 0.0, -root, root) * channel * for_chunk(refs, code.shape[0])


def ref_column(ref_powers):
    return as_column(ref_powers)[:REF]


def prepare_kernel(strain, own, head, left, sems):
    rows = left.shape[0]
    step = rows // PIECES
    copies = [
        pltpu.make_async_copy(
            strain.at[pl.ds(index * step, step), pl.ds(0, LANES)], left.at[pl.ds(index * step, step)], sems.at[index]
        )
        for index in range(PIECES)
    ]
    copies.append(pltpu.make_async_copy(strain.at[pl.ds(0, LAGS)], head, sems.at[PIECES]))
    for copy in copies:
        copy.start()
    for index in range(PIECES):
        copies[index].wait()
        here = slice(index * step, (index + 1) * step)
        own[:, here] = left[here, :].astype(jnp.float32).T[:HALF].astype(jnp.bfloat16)
    copies[PIECES].wait()


def prepared(strain):
    rows, width = strain.shape
    vmem = pl.BlockSpec(memory_space=pltpu.VMEM)
    return pl.pallas_call(
        prepare_kernel,
        in_specs=[pl.BlockSpec(memory_space=pl.ANY)],
        out_specs=[vmem, vmem],
        out_shape=[pltpu.VMEM((HALF, rows), strain.dtype), pltpu.VMEM((LAGS, width), strain.dtype)],
        scratch_shapes=[pltpu.VMEM((rows, LANES), strain.dtype), pltpu.SemaphoreType.DMA((PIECES + 1,))],
        compiler_params=pltpu.CompilerParams(vmem_limit_bytes=VMEM_BYTES),
        cost_estimate=SMALL,
        name="prepared",
    )(pltpu.with_memory_space_constraint(strain, pltpu.HBM))


def lag_rows(own, other, group, shifted):
    chan, near = lax.axis_index("chan"), lax.axis_index("tm") & 1
    zeros = jnp.zeros((HALF, LANES), jnp.float32)
    for refs, half in ((own, chan), (other, 1 - chan)):
        long = jnp.concatenate([refs[...].astype(jnp.float32), zeros], axis=1)
        for index in range(GROUP):
            ahead = near if index < GROUP // 2 else 1 - near
            lag = group * GROUP + ahead * (GROUP // 2) + index % (GROUP // 2)
            start = pl.multiple_of(index * REF + half * HALF, HALF)
            shifted[pl.ds(start, HALF), :] = pltpu.roll(long, lag, 1).astype(jnp.bfloat16)


def own_group(bits):
    return lax.shift_right_logical(lax.axis_index("tm").astype(jnp.int32), 1) ^ bits


def loaded_kernel(strain, held, power, sems):
    step = held.shape[0] // FETCHES
    pieces = [slice(index * step, (index + 1) * step) for index in range(FETCHES)]
    copies = [
        pltpu.make_async_copy(strain.at[pl.ds(here.start, step)], held.at[pl.ds(here.start, step)], sems.at[index])
        for index, here in enumerate(pieces)
    ]
    for copy in copies:
        copy.start()
    total = jnp.zeros((8, held.shape[1]), jnp.float32)
    for copy, here in zip(copies, pieces):
        copy.wait()
        squares = jnp.square(held[here, :].astype(jnp.float32))
        total += jnp.sum(squares.reshape(step // 8, 8, held.shape[1]), axis=0)
    power[...] = jnp.sum(total, axis=0, keepdims=True)


def loaded(strain, after):
    rows, width = strain.shape
    vmem = pl.BlockSpec(memory_space=pltpu.VMEM)

    def kernel(strain, after, held, power, sems):
        loaded_kernel(strain, held, power, sems)

    return pl.pallas_call(
        kernel,
        in_specs=[pl.BlockSpec(memory_space=pl.ANY)] * 2,
        out_specs=[vmem, vmem],
        out_shape=[pltpu.VMEM((rows, width), strain.dtype), pltpu.VMEM((1, width), jnp.float32)],
        scratch_shapes=[pltpu.SemaphoreType.DMA((FETCHES,))],
        compiler_params=pltpu.CompilerParams(vmem_limit_bytes=VMEM_BYTES),
        cost_estimate=SMALL,
        name="loaded",
    )(pltpu.with_memory_space_constraint(strain, pltpu.HBM), after)


def edge_of(tail):
    return jnp.concatenate([tail[...], jnp.zeros((LANES - LAGS, tail.shape[1]), tail.dtype)], axis=0)


def product_of(shifted, held, edge, here):
    rows = held.shape[0]
    total = jnp.dot(shifted[:, rows:], edge[:, here], preferred_element_type=jnp.float32)
    return total + jnp.dot(shifted[:, :rows], held[:, here], preferred_element_type=jnp.float32)


def columns(width, step=256):
    return [slice(first, first + step) for first in range(0, width, step)]


def first_products_kernel(held, power, own, other, tail, keep, send, shifted):
    lag_rows(own, other, own_group(3), shifted)
    ours, theirs = [
        jnp.sum(jnp.square(refs[...].astype(jnp.float32)), axis=1, keepdims=True) for refs in (own, other)
    ]
    refs = jnp.where(
        lax.axis_index("chan") == 0,
        jnp.concatenate([ours, theirs], axis=0),
        jnp.concatenate([theirs, ours], axis=0),
    )
    beyond = jnp.sum(jnp.square(tail[...].astype(jnp.float32)), axis=0, keepdims=True)
    bound = rounded_up(power[...] + beyond)
    pad = jnp.zeros((1, LANES - REF), jnp.float32)
    chunk = keep.shape[0]
    send[chunk:] = packed(power[...], jnp.concatenate([as_row(refs), pad], axis=1), bound)
    edge = edge_of(tail)
    for here in columns(held.shape[1]):
        product = product_of(shifted, held, edge, here)
        keep[:, here] = product[:chunk]
        send[:chunk, here] = coded(product[chunk:], bound[:, here], refs)


def shifted_scratch(rows):
    return [pltpu.VMEM((GROUP * REF, rows + LANES), jnp.bfloat16)]


def first_products(held, power, own, other, tail, chunk, after):
    rows, width = held.shape
    outs = [
        ((chunk, width), jnp.float32),
        ((chunk + EXTRA, width), jnp.bfloat16),
    ]
    return call_on_blocks(
        first_products_kernel,
        outs,
        held,
        power,
        own,
        other,
        tail,
        name="first_products",
        after=after,
        scratch=shifted_scratch(rows),
    )


def later_products(bits, held, own, other, tail, powers, chunk, after=()):
    rows, width = held.shape

    def kernel(held, own, other, tail, powers, keep, send, shifted):
        _, ref_powers, bound = sent_powers(powers)
        refs = ref_column(ref_powers)
        lag_rows(own, other, own_group(bits), shifted)
        edge = edge_of(tail)
        for here in columns(width):
            product = product_of(shifted, held, edge, here)
            keep[:, here] = product[:chunk]
            send[:, here] = coded(product[chunk:], bound[:, here], refs)

    return call_on_blocks(
        kernel,
        [((chunk, width), jnp.float32), ((chunk, width), jnp.bfloat16)],
        held,
        own,
        other,
        tail,
        powers,
        name="later_products",
        after=after,
        scratch=shifted_scratch(rows),
    )


def call_on_blocks(kernel, outs, *arrays, name, after=(), scratch=(), space=pltpu.VMEM):
    vmem = pl.BlockSpec(memory_space=pltpu.VMEM)
    count = len(arrays)

    def body(*refs):
        kernel(*refs[:count], *refs[count + len(after) :])

    return pl.pallas_call(
        body,
        in_specs=[vmem] * count + [pl.BlockSpec(memory_space=pl.ANY)] * len(after),
        out_specs=[vmem] * len(outs),
        out_shape=[space(shape, dtype) for shape, dtype in outs],
        scratch_shapes=list(scratch),
        compiler_params=pltpu.CompilerParams(vmem_limit_bytes=VMEM_BYTES),
        cost_estimate=SMALL,
        name=name,
    )(*arrays, *after)


def half_of(width, part):
    return slice(part * width // 2, (part + 1) * width // 2)


def sent_powers(code, here=slice(None)):
    powers, refs, bound = unpacked(code[-EXTRA:])
    return powers[:, here], refs, bound[:, here]


def merge_near(keep, ours, theirs):
    chunk, width = keep.shape

    def kernel(keep, ours, theirs, *outs):
        for part, out in enumerate(outs):
            here = half_of(width, part)
            powers, refs, bound = sent_powers(ours, here)
            their_powers, their_refs, their_bound = sent_powers(theirs, here)
            total = keep[:, here] + expanded(theirs[:chunk, here], their_bound, ref_column(their_refs))
            sums, sum_refs, sum_bound = powers + their_powers, refs + their_refs, rounded_up(bound + their_bound)
            out[chunk:] = packed(sums, sum_refs, sum_bound)
            out[:chunk] = coded(total, sum_bound, ref_column(sum_refs))

    outs = [((chunk + EXTRA, width // 2), jnp.bfloat16)] * 2
    return lambda after: call_on_blocks(kernel, outs, keep, ours, theirs, name="merge_near", after=after)


def merge_far(part, keep, ours, theirs, direct, direct_powers, after):
    chunk, width = keep.shape
    here = half_of(width, part)

    def kernel(keep, ours, theirs, direct, direct_powers, out):
        powers, refs, bound = sent_powers(ours)
        their_powers, their_refs, their_bound = sent_powers(theirs)
        total = keep[:, here] + expanded(theirs[:chunk], their_bound, ref_column(their_refs))
        _, direct_refs, direct_bound = sent_powers(direct_powers, here)
        total += expanded(direct[:, here], direct_bound, ref_column(direct_refs))
        sums, sum_refs, sum_bound = powers + their_powers, refs + their_refs, rounded_up(bound + their_bound)
        out[chunk:] = packed(sums, sum_refs, sum_bound)
        out[:chunk] = coded(total, sum_bound, ref_column(sum_refs))

    outs = [((chunk + EXTRA, width // 2), jnp.bfloat16)]
    return call_on_blocks(
        kernel, outs, keep, ours, theirs, direct, direct_powers, name="merge_far", after=after
    )[0]


def resent(keep, direct, direct_powers, ours, after):
    width = keep.shape[1]

    def kernel(keep, direct, direct_powers, first, second, out):
        for part, powers in enumerate((first, second)):
            here = half_of(width, part)
            _, direct_refs, direct_bound = sent_powers(direct_powers, here)
            _, refs, bound = sent_powers(powers)
            total = keep[:, here] + expanded(direct[:, here], direct_bound, ref_column(direct_refs))
            out[:, here] = coded(total, bound, ref_column(refs))

    outs = [(keep.shape, jnp.bfloat16)]
    return call_on_blocks(kernel, outs, keep, direct, direct_powers, *ours, name="resent", after=after)[0]


def added(keep, direct, direct_powers, near, near_powers, held, tail, size, after):
    rows, width = held.shape

    def kernel(keep, direct, direct_powers, near, first, second, held, tail, out, edge):
        for part, powers in enumerate((first, second)):
            here = half_of(width, part)
            _, direct_refs, direct_bound = sent_powers(direct_powers, here)
            _, refs, bound = sent_powers(powers)
            total = keep[:, here] + expanded(direct[:, here], direct_bound, ref_column(direct_refs))
            out[:, here] = total + expanded(near[:, here], bound, ref_column(refs))
        last = held[rows - LAGS :, :size].astype(jnp.float32)
        beyond = tail[:, :size].astype(jnp.float32)
        place = lax.broadcasted_iota(jnp.int32, last.shape, 0)
        sums = [jnp.zeros((1, size), jnp.float32)]
        for lag in range(1, LAGS):
            pairs = jnp.where(place >= LAGS - lag, last * pltpu.roll(beyond, LAGS - lag, 0), 0.0)
            sums.append(jnp.sum(pairs, axis=0, keepdims=True))
        edge[...] = jnp.concatenate(sums, axis=0)

    outs = [(keep.shape, jnp.float32), ((LAGS, size), jnp.float32)]
    return call_on_blocks(
        kernel, outs, keep, direct, direct_powers, near, *near_powers, held, tail, name="added", after=after
    )


def finished(slab_rows, segment, partial, edge, ours, theirs, autos):
    chunk, width = partial.shape

    def kernel(partial, edge, *refs):
        ours, theirs, autos, (covariance, segment_auto) = refs[:2], refs[2:4], refs[4:-2], refs[-2:]
        first_lag = lax.axis_index("tm").astype(jnp.int32) * (chunk // REF)
        lag = lax.broadcasted_iota(jnp.int32, (chunk, 1), 0) // REF + first_lag
        denom = (slab_rows - lag).astype(jnp.float32)
        size = width // len(autos)
        for part in range(2):
            here = half_of(width, part)
            powers, own_refs, _ = sent_powers(ours[part])
            their_powers, their_refs, their_bound = sent_powers(theirs[part])
            total = partial[:, here] + expanded(theirs[part][:chunk], their_bound, ref_column(their_refs))
            scale = 1.0 / jnp.sqrt((powers + their_powers) / slab_rows + 1e-06)
            ref_scale = 1.0 / jnp.sqrt(ref_column(own_refs + their_refs) / slab_rows + 1e-06)
            covariance[:, here] = total * scale * (for_chunk(ref_scale, chunk) / denom)
            for index in range(len(autos)):
                first = index * size - here.start
                if 0 <= first < width // 2:
                    auto = autos[index][...] + edge[...] if index == 0 else autos[index][...]
                    own_scale = scale[:, first : first + size]
                    segment_auto[:, index * size : (index + 1) * size] = auto * (own_scale * own_scale) / segment

    outs = [(partial.shape, jnp.float32), ((LAGS, width), jnp.float32)]
    return call_on_blocks(
        kernel, outs, partial, edge, *ours, *theirs, *autos, name="finished", space=jax.ShapeDtypeStruct
    )


def segment_kernel(first, held, power, tail, out, wide):
    rows = held.shape[0]
    step = rows // 8
    pitch = step + LAGS
    for index in range(out.shape[1] // LANES):
        here = slice(first + index * LANES, first + (index + 1) * LANES)
        there = slice(index * LANES, (index + 1) * LANES)
        for part in range(8):
            end = (part + 1) * step
            wide[part * pitch : part * pitch + step, :] = held[end - step : end, here].astype(jnp.float32)
            if part < 7:
                following = held[end : end + LAGS, here].astype(jnp.float32)
            elif tail is None:
                following = jnp.zeros((LAGS, LANES), jnp.float32)
            else:
                following = tail[:, here].astype(jnp.float32)
            wide[part * pitch + step : (part + 1) * pitch, :] = following
        taken = lambda first: wide[pl.ds(first, 8, stride=pitch), :]

        def advance(index, carry):
            window, sums = carry
            window = window + (taken(index + LAGS - 1),)
            sums = tuple(total + window[0] * window[lag + 1] for lag, total in enumerate(sums))
            return window[1:], sums

        window = tuple(taken(first) for first in range(LAGS - 1))
        zero = jnp.zeros((8, LANES), jnp.float32)
        _, sums = lax.fori_loop(0, step, advance, (window, (zero,) * (LAGS - 1)), unroll=16)
        out[:, there] = jnp.concatenate(
            [power[:, here]] + [jnp.sum(total, axis=0, keepdims=True) for total in sums], axis=0
        )


def segment_rows(held, power, tail, first, size, after=()):
    rows = held.shape[0]
    arrays = (held, power) if tail is None else (held, power, tail)

    def kernel(*refs):
        held, power, *rest = refs
        if tail is None:
            rest = [None] + rest
        segment_kernel(first, held, power, *rest)

    return call_on_blocks(
        kernel,
        [((LAGS, size), jnp.float32)],
        *arrays,
        name="segment_rows",
        after=after,
        scratch=[pltpu.VMEM((rows + 8 * LAGS, LANES), jnp.float32)],
    )[0]


def all_products_kernel(held, own, other, tail, out, shifted):
    chan = lax.axis_index("chan")
    zeros = jnp.zeros((HALF, LANES), jnp.float32)
    for refs, half in ((own, chan), (other, 1 - chan)):
        long = jnp.concatenate([refs[...].astype(jnp.float32), zeros], axis=1)
        for index in range(GROUP):
            start = pl.multiple_of(index * REF + half * HALF, HALF)
            lag = pl.program_id(0) * GROUP + index
            shifted[pl.ds(start, HALF), :] = pltpu.roll(long, lag, 1).astype(jnp.bfloat16)
    edge = edge_of(tail)
    for here in columns(held.shape[1]):
        out[:, here] = product_of(shifted, held, edge, here)


def all_products(held, own, other, tail):
    rows, width = held.shape
    vmem = pl.BlockSpec(memory_space=pltpu.VMEM)
    return pl.pallas_call(
        all_products_kernel,
        grid=(LAGS // GROUP,),
        in_specs=[vmem] * 4,
        out_specs=pl.BlockSpec((GROUP * REF, width), lambda group: (group, 0)),
        out_shape=jax.ShapeDtypeStruct((LAGS * REF, width), jnp.float32),
        scratch_shapes=shifted_scratch(rows),
        compiler_params=pltpu.CompilerParams(vmem_limit_bytes=VMEM_BYTES),
        name="all_products",
    )(held, own, other, tail)


def local(strain):
    rows, width = strain.shape
    count = lax.axis_size("tm")
    slab_rows = rows * count
    chunk = LAGS * REF // count

    own, head = prepared(strain)
    other = exchanged(own, "chan", 1)
    tail = passed_along(head, "tm", -1)
    held, power = loaded(strain, own)
    size = width // 4

    if chunk * 2 == GROUP * REF:
        refs = (own, other, tail)
        autos = [segment_rows(held, power, None, 0, size)]
        keep6, send7 = first_products(held, power, *refs, chunk, after=(autos[0],))
        got7 = exchanged(send7, "tm", 1)
        keep4, send5 = later_products(2, held, *refs, send7, chunk)
        got5 = exchanged(send5, "tm", 1)
        autos.append(segment_rows(held, power, tail, size, size, after=(send5,)))
        sends6 = merge_near(keep6, send7, got7)(after=(autos[1],))
        gots6 = [exchanged(code, "tm", 2) for code in sends6]
        keep2, send3 = later_products(1, held, *refs, send7, chunk, after=tuple(sends6))
        got3 = exchanged(send3, "tm", 1)
        sends4, gots4 = [], []
        for part in range(2):
            after = (sends4[0] if part else send3,)
            sends4.append(merge_far(part, keep4, sends6[part], gots6[part], got5, got7, after))
            gots4.append(exchanged(sends4[part], "tm", 4))
        keep0, send1 = later_products(0, held, *refs, send7, chunk, after=(sends4[1],))
        got1 = exchanged(send1, "tm", 1)
        send2 = resent(keep2, got3, got7, sends6, after=(send1,))
        got2 = exchanged(send2, "tm", 2)
        for index in (2, 3):
            autos.append(segment_rows(held, power, tail, size * index, size, after=(send2,)))
        partial, edge = added(keep0, got1, got7, got2, gots6, held, tail, size, after=tuple(autos[2:]))
        return tuple(finished(slab_rows, rows, partial, edge, sends4, gots4, autos))

    chan = lax.axis_index("chan").astype(jnp.int32)
    time = lax.axis_index("tm").astype(jnp.int32)
    auto = jnp.concatenate(
        [segment_rows(held, power, tail, size * index, size) for index in range(4)], axis=1
    )
    power_other = jnp.sum(jnp.square(other.astype(jnp.float32)), axis=1)
    power = lax.psum(jnp.concatenate([power[0], power_other]), "tm")
    inv = 1.0 / jnp.sqrt(power / slab_rows + 1e-06)
    scale = inv[:width]
    ref_scale = jnp.where(
        chan == 0,
        jnp.concatenate([inv[:HALF], inv[width:]]),
        jnp.concatenate([inv[width:], inv[:HALF]]),
    )
    products = all_products(held, own, other, tail)
    summed = lax.psum_scatter(products, "tm", scatter_dimension=0, tiled=True)
    row = time * chunk + jnp.arange(chunk, dtype=jnp.int32)
    row_scale = ref_scale[row % REF] / (slab_rows - row // REF).astype(jnp.float32)
    covariance = summed * scale[None, :] * row_scale[:, None]
    segment_auto = auto * (scale * scale)[None, :] / rows
    return (covariance, segment_auto)


def solution(mesh):
    in_specs = (P(("groups", "tm"), "chan"),)
    out_specs = (P(("groups", "tm"), "chan"), P(("groups", "tm"), "chan"))
    return jax.shard_map(local, mesh=mesh, in_specs=in_specs, out_specs=out_specs, check_vma=False)
```

time: 53.9 us -> 54.5 us (1.011)
  waiting for transfers between devices: 5.9 us -> 12 us
  local copies, waits for them, and re-layouts: 4.24 us -> 0 us
  Pallas kernels: 30 us -> 26.5 us
  starting transfers between devices: 12.8 us -> 15.1 us
    ppermute x8 -> x10, waiting for transfers between devices: 5.07 us -> 11.7 us  [exchanged(): lax.ppermute(value, axis, [(source, source ^ bit) for source in range(cou...]
    unnamed x6 -> x0, local copies, waits for them, and re-layouts: 4.15 us -> none
    pallas_call x11 -> x14, Pallas kernels: 26.5 us -> 23 us  [call_on_blocks(): pl.pallas_call(body, in_specs=[vmem] * count + [pl.BlockSpec(memory_space...]
    ppermute x8 -> x10, starting transfers between devices: 11.5 us -> 13.8 us  [exchanged(): lax.ppermute(value, axis, [(source, source ^ bit) for source in range(cou...]
    ppermute x1, waiting for transfers between devices: 0.83 us -> 0.22 us  [passed_along(): lax.ppermute(value, axis, [(source, source + steps) for source in range(i...]
  transfers between devices with their start and end apart: 9 -> 11, of which waited for: 3 -> 5; matrix products, arithmetic and copies ran while one was open for 0% -> 0% of each run, Pallas kernels for 45% -> 40%
where the time goes in v5:
time: 54.5 us; the launch traced here: 54.3 us
  Pallas kernels  26.5 us (49%)
  starting transfers between devices  15.1 us (28%)
  waiting for transfers between devices  12 us (22%)
  between operations  0.77 us (1%)
    pallas_call x14, Pallas kernels, call_on_blocks(): pl.pallas_call(body, in_specs=[vmem] * count + [pl.BlockSpec(memory_space...  23 us
    ppermute x10, starting transfers between devices, exchanged(): lax.ppermute(value, axis, [(source, source ^ bit) for source in range(cou...  13.8 us
    ppermute x10, waiting for transfers between devices, exchanged(): lax.ppermute(value, axis, [(source, source ^ bit) for source in range(cou...  11.7 us
    pallas_call x1, Pallas kernels, loaded(): pl.pallas_call(kernel, in_specs=[pl.BlockSpec(memory_space=pl.ANY)] * 2,...  2.26 us
    ppermute x1, starting transfers between devices, passed_along(): lax.ppermute(value, axis, [(source, source + steps) for source in range(i...  1.28 us
    pallas_call x1, Pallas kernels, prepared(): pl.pallas_call(prepare_kernel, in_specs=[pl.BlockSpec(memory_space=pl.ANY...  1.28 us
  transfers between devices with their start and end apart: 11, of which 5 were waited for; matrix products, arithmetic and copies ran while one was open for 0% of the time, Pallas kernels for 40%

profile of v5, /device:TPU:0, one launch (start us, length us, event | category | flops | bytes accessed | tf_op | source)
XLA Modules:
  0.0 54.3 jit_solution(5432971552535870551)
XLA Ops:
  0.6 1.3 %prepared.1 = (bf16[32,2048]{1,0:T(8,128)(2,1)S(1)}, bf16[16,1024]{1,0:T(8,128)(2,1)S(1)}) custom-call(bf16[2048,1024]{1,0:T(8,128)(2,1)} %strain.3), custom_call_target="tpu_custom_call" | custom-call | bytes 1024 | tf_op jit(solution)/shard_map/prepared/pallas_call | solution.py:119
  1.9 0.5 collective-permute-start
  2.4 1.3 %collective-permute-start.1 = (bf16[16,1024]{1,0:T(8,128)(2,1)S(1)}, bf16[16,1024]{1,0:T(8,128)(2,1)S(1)}, u32[]{:S(2)}, u32[]{:S(2)}) collective-permute-start(bf16[16,1024]{1,0:T(8,128)(2,1)S(1)} %get-tuple-element.20), channel_id=1, source_target_pairs={{2,0},{4,2},{6,4},{8,6},{10,8},{12,10},{14,12},{3,1},{5,3},{7,5},{... | collective-permute-start | bytes 98312 | tf_op jit(solution)/shard_map/ppermute | solution.py:26
  3.7 2.3 %loaded.1 = (bf16[2048,1024]{1,0:T(8,128)(2,1)S(1)}, f32[1,1024]{1,0:T(1,128)S(1)}) custom-call(bf16[2048,1024]{1,0:T(8,128)(2,1)} %strain.3, bf16[32,2048]{1,0:T(8,128)(2,1)S(1)} %get-tuple-element.18.after.refs_2_.refs_1_), custom_call_target="tpu_custom_call" | custom-call | bytes 1024 | tf_op jit(solution)/shard_map/loaded/pallas_call | solution.py:171
  6.0 2.7 %segment_rows.4.refs_5_.refs_6_ = f32[16,256]{1,0:T(8,128)S(1)} custom-call(bf16[2048,1024]{1,0:T(8,128)(2,1)S(1)} %get-tuple-element.19.refs_0_.refs_6_, f32[1,1024]{1,0:T(1,128)S(1)} %get-tuple-element.21.refs_1_), custom_call_target="tpu_custom_call" | custom-call | bytes 1024 | tf_op jit(solution)/shard_map/segment_rows/pallas_call | solution.py:277
  8.7 0.2 collective-permute-done.1.refs_4_.refs_3_.refs_2_.refs_7_
  8.9 0.0 collective-permute-done.refs_3_.refs_2_
  8.9 2.2 %first_products.1 = (f32[128,1024]{1,0:T(8,128)S(1)}, bf16[136,1024]{1,0:T(8,128)(2,1)S(1)}) custom-call(bf16[2048,1024]{1,0:T(8,128)(2,1)S(1)} %get-tuple-element.19.refs_0_.refs_6_, f32[1,1024]{1,0:T(1,128)S(1)} %get-tuple-element.21.refs_1_, bf16[32,2048]{1,0:T(8,128)(2,1)S(1)} %get-tuple-element.18.after.refs_2_.refs_1_, ...), custom_call_target="tpu_custom_call" | custom-call | bytes 1024 | tf_op jit(solution)/shard_map/first_products/pallas_call | solution.py:277
  11.0 3.0 %collective-permute-start.2 = (bf16[136,1024]{1,0:T(8,128)(2,1)S(1)}, bf16[136,1024]{1,0:T(8,128)(2,1)S(1)}, u32[]{:S(2)}, u32[]{:S(2)}) collective-permute-start(bf16[136,1024]{1,0:T(8,128)(2,1)S(1)} %get-tuple-element.22.refs_4_.refs_1_), channel_id=1, source_target_pairs={{0,2},{2,0},{4,6},{6,4},{8,10},{10,8},{12,14},{14,12},{1,3},{3,1},... | collective-permute-start | bytes 835592 | tf_op jit(solution)/shard_map/ppermute | solution.py:31
  14.1 2.1 %later_products.3 = (f32[128,1024]{1,0:T(8,128)S(1)}, bf16[128,1024]{1,0:T(8,128)(2,1)S(1)}) custom-call(bf16[2048,1024]{1,0:T(8,128)(2,1)S(1)} %get-tuple-element.19.refs_0_.refs_6_, bf16[32,2048]{1,0:T(8,128)(2,1)S(1)} %get-tuple-element.18.after.refs_2_.refs_1_, bf16[32,2048]{1,0:T(8,128)(2,1)S(1)} %collective-permute-done.refs_3_.refs_2_, ...), custom_call_target="tpu_custom_call" | custom-call | bytes 1024 | tf_op jit(solution)/shard_map/later_products/pallas_call | solution.py:277
  16.2 0.1 collective-permute-start.4
  16.3 2.7 %segment_rows.5.refs_3_.refs_7_ = f32[16,256]{1,0:T(8,128)S(1)} custom-call(bf16[2048,1024]{1,0:T(8,128)(2,1)S(1)} %get-tuple-element.19.refs_0_.refs_6_, f32[1,1024]{1,0:T(1,128)S(1)} %get-tuple-element.21.refs_1_, bf16[16,1024]{1,0:T(8,128)(2,1)S(1)} %collective-permute-done.1.refs_4_.refs_3_.refs_2_.refs_7_, bf16[128,1024]{1,0:T(8,128)(2,1)S(1)} %get-tuple-element.25.refs_3_), custom_call_target="tpu_custom_call" | custom-call | bytes 1024 | tf_op jit(solution)/shard_map/segment_rows/pallas_call | solution.py:277
  19.0 2.6 %collective-permute-done.2.refs_2_.refs_4_ = bf16[136,1024]{1,0:T(8,128)(2,1)S(1)} collective-permute-done((bf16[136,1024]{1,0:T(8,128)(2,1)S(1)}, bf16[136,1024]{1,0:T(8,128)(2,1)S(1)}, u32[]{:S(2)}, u32[]{:S(2)}) %collective-permute-start.2) | collective-permute-done | bytes 278560 | tf_op jit(solution)/shard_map/ppermute | solution.py:31
  21.6 0.5 merge_near.1
  22.1 2.1 %later_products.4 = (f32[128,1024]{1,0:T(8,128)S(1)}, bf16[128,1024]{1,0:T(8,128)(2,1)S(1)}) custom-call(bf16[2048,1024]{1,0:T(8,128)(2,1)S(1)} %get-tuple-element.19.refs_0_.refs_6_, bf16[32,2048]{1,0:T(8,128)(2,1)S(1)} %get-tuple-element.18.after.refs_2_.refs_1_, bf16[32,2048]{1,0:T(8,128)(2,1)S(1)} %collective-permute-done.refs_3_.refs_2_, ...), custom_call_target="tpu_custom_call" | custom-call | bytes 1024 | tf_op jit(solution)/shard_map/later_products/pallas_call | solution.py:277
  24.3 2.0 %collective-permute-start.7 = (bf16[128,1024]{1,0:T(8,128)(2,1)S(1)}, bf16[128,1024]{1,0:T(8,128)(2,1)S(1)}, u32[]{:S(2)}, u32[]{:S(2)}) collective-permute-start(bf16[128,1024]{1,0:T(8,128)(2,1)S(1)} %get-tuple-element.28.refs_5_), channel_id=1, source_target_pairs={{0,2},{2,0},{4,6},{6,4},{8,10},{10,8},{12,14},{14,12},{1,3},{3,1},... | collective-permute-start | bytes 786440 | tf_op jit(solution)/shard_map/ppermute | solution.py:31
  26.3 2.1 %collective-permute-start.5 = (bf16[136,512]{1,0:T(8,128)(2,1)S(1)}, bf16[136,512]{1,0:T(8,128)(2,1)S(1)}, u32[]{:S(2)}, u32[]{:S(2)}) collective-permute-start(bf16[136,512]{1,0:T(8,128)(2,1)S(1)} %get-tuple-element.27.refs_5_.refs_1_.refs_3_), channel_id=1, source_target_pairs={{0,4},{2,6},{4,0},{6,2},{8,12},{10,14},{12,8},{14,10},{1,5},{3,7},... | collective-permute-start | bytes 417800 | tf_op jit(solution)/shard_map/ppermute | solution.py:31
  28.4 0.0 collective-permute-start.3
  28.4 0.0 collective-permute-done.4.refs_3_
  28.5 3.9 %collective-permute-done.5.refs_2_.refs_4_ = bf16[136,512]{1,0:T(8,128)(2,1)S(1)} collective-permute-done((bf16[136,512]{1,0:T(8,128)(2,1)S(1)}, bf16[136,512]{1,0:T(8,128)(2,1)S(1)}, u32[]{:S(2)}, u32[]{:S(2)}) %collective-permute-start.5) | collective-permute-done | bytes 139296 | tf_op jit(solution)/shard_map/ppermute | solution.py:31
  32.3 0.4 merge_far.2.refs_5_.refs_2_
  32.8 1.0 %collective-permute-done.3.refs_2_.refs_5_ = bf16[136,512]{1,0:T(8,128)(2,1)S(1)} collective-permute-done((bf16[136,512]{1,0:T(8,128)(2,1)S(1)}, bf16[136,512]{1,0:T(8,128)(2,1)S(1)}, u32[]{:S(2)}, u32[]{:S(2)}) %collective-permute-start.3) | collective-permute-done | bytes 139296 | tf_op jit(solution)/shard_map/ppermute | solution.py:31
  33.8 0.4 merge_far.3.refs_5_.refs_3_
  34.3 2.1 %later_products.5 = (f32[128,1024]{1,0:T(8,128)S(1)}, bf16[128,1024]{1,0:T(8,128)(2,1)S(1)}) custom-call(bf16[2048,1024]{1,0:T(8,128)(2,1)S(1)} %get-tuple-element.19.refs_0_.refs_6_, bf16[32,2048]{1,0:T(8,128)(2,1)S(1)} %get-tuple-element.18.after.refs_2_.refs_1_, bf16[32,2048]{1,0:T(8,128)(2,1)S(1)} %collective-permute-done.refs_3_.refs_2_, ...), custom_call_target="tpu_custom_call" | custom-call | bytes 1024 | tf_op jit(solution)/shard_map/later_products/pallas_call | solution.py:277
  36.4 1.2 %collective-permute-start.6 = (bf16[128,1024]{1,0:T(8,128)(2,1)S(1)}, bf16[128,1024]{1,0:T(8,128)(2,1)S(1)}, u32[]{:S(2)}, u32[]{:S(2)}) collective-permute-start(bf16[128,1024]{1,0:T(8,128)(2,1)S(1)} %get-tuple-element.30.refs_5_), channel_id=1, source_target_pairs={{0,2},{2,0},{4,6},{6,4},{8,10},{10,8},{12,14},{14,12},{1,3},{3,1},... | collective-permute-start | bytes 786440 | tf_op jit(solution)/shard_map/ppermute | solution.py:31
  37.6 0.0 collective-permute-done.7.refs_1_
  37.6 0.5 resent.1.refs_3_
  38.2 1.8 %collective-permute-start.8 = (bf16[128,1024]{1,0:T(8,128)(2,1)S(1)}, bf16[128,1024]{1,0:T(8,128)(2,1)S(1)}, u32[]{:S(2)}, u32[]{:S(2)}) collective-permute-start(bf16[128,1024]{1,0:T(8,128)(2,1)S(1)} %resent.1.refs_3_), channel_id=1, source_target_pairs={{0,4},{2,6},{4,0},{6,2},{8,12},{10,14},{12,8},{14,10},{1,5},{3,7},... | collective-permute-start | bytes 786440 | tf_op jit(solution)/shard_map/ppermute | solution.py:31
  40.0 2.6 %collective-permute-start.10 = (bf16[136,512]{1,0:T(8,128)(2,1)S(1)}, bf16[136,512]{1,0:T(8,128)(2,1)S(1)}, u32[]{:S(2)}, u32[]{:S(2)}) collective-permute-start(bf16[136,512]{1,0:T(8,128)(2,1)S(1)} %merge_far.3.refs_5_.refs_3_), channel_id=1, source_target_pairs={{0,8},{2,10},{4,12},{6,14},{8,0},{10,2},{12,4},{14,6},{1,9},{3,11}... | collective-permute-start | bytes 417800 | tf_op jit(solution)/shard_map/ppermute | solution.py:31
  42.6 0.4 collective-permute-start.9
  42.9 2.7 %segment_rows.7.refs_9_ = f32[16,256]{1,0:T(8,128)S(1)} custom-call(bf16[2048,1024]{1,0:T(8,128)(2,1)S(1)} %get-tuple-element.19.refs_0_.refs_6_, f32[1,1024]{1,0:T(1,128)S(1)} %get-tuple-element.21.refs_1_, bf16[16,1024]{1,0:T(8,128)(2,1)S(1)} %collective-permute-done.1.refs_4_.refs_3_.refs_2_.refs_7_, bf16[128,1024]{1,0:T(8,128)(2,1)S(1)} %resent.1.refs_3_), custom_call_target="tpu_custom_call" | custom-call | bytes 1024 | tf_op jit(solution)/shard_map/segment_rows/pallas_call | solution.py:277
  45.6 2.7 %segment_rows.6.refs_8_ = f32[16,256]{1,0:T(8,128)S(1)} custom-call(bf16[2048,1024]{1,0:T(8,128)(2,1)S(1)} %get-tuple-element.19.refs_0_.refs_6_, f32[1,1024]{1,0:T(1,128)S(1)} %get-tuple-element.21.refs_1_, bf16[16,1024]{1,0:T(8,128)(2,1)S(1)} %collective-permute-done.1.refs_4_.refs_3_.refs_2_.refs_7_, bf16[128,1024]{1,0:T(8,128)(2,1)S(1)} %resent.1.refs_3_), custom_call_target="tpu_custom_call" | custom-call | bytes 1024 | tf_op jit(solution)/shard_map/segment_rows/pallas_call | solution.py:277
  48.3 0.0 collective-permute-done.6.refs_1_
  48.3 0.0 collective-permute-done.8.refs_3_
  48.3 0.6 %added.1 = (f32[128,1024]{1,0:T(8,128)S(1)}, f32[16,256]{1,0:T(8,128)S(1)}) custom-call(f32[128,1024]{1,0:T(8,128)S(1)} %get-tuple-element.29.refs_0_, bf16[128,1024]{1,0:T(8,128)(2,1)S(1)} %collective-permute-done.6.refs_1_, bf16[136,1024]{1,0:T(8,128)(2,1)S(1)} %collective-permute-done.2.refs_2_.refs_4_, ...), custom_call_target="tpu_custom_call" | custom-call | bytes 1024 | tf_op jit(solution)/shard_map/added/pallas_call | solution.py:277
  48.9 0.0 collective-permute-done.10.refs_5_
  48.9 4.2 %collective-permute-done.9.refs_4_ = bf16[136,512]{1,0:T(8,128)(2,1)S(1)} collective-permute-done((bf16[136,512]{1,0:T(8,128)(2,1)S(1)}, bf16[136,512]{1,0:T(8,128)(2,1)S(1)}, u32[]{:S(2)}, u32[]{:S(2)}) %collective-permute-start.9) | collective-permute-done | bytes 139296 | tf_op jit(solution)/shard_map/ppermute | solution.py:31
  53.1 1.2 %finished.1 = (f32[128,1024]{1,0:T(8,128)}, f32[16,1024]{1,0:T(8,128)}) custom-call(f32[128,1024]{1,0:T(8,128)S(1)} %get-tuple-element.32.refs_0_, f32[16,256]{1,0:T(8,128)S(1)} %get-tuple-element.33.refs_1_, bf16[136,512]{1,0:T(8,128)(2,1)S(1)} %merge_far.2.refs_5_.refs_2_, bf16[136,512]{1,0:T(8,128)(2,1)S(1)} %merge_far.3.refs_5_.refs_3_, ...), custom_call_target="tpu_custom_call" | custom-call | bytes 1024 | tf_op jit(solution)/shard_map/finished/pallas_call | solution.py:277
Async XLA Ops:
  1.9 7.0 %collective-permute-start = (bf16[32,2048]{1,0:T(8,128)(2,1)S(1)}, bf16[32,2048]{1,0:T(8,128)(2,1)S(1)}, u32[]{:S(2)}, u32[]{:S(2)}) collective-permute-start(bf16[32,2048]{1,0:T(8,128)(2,1)S(1)} %get-tuple-element.18.after.refs_2_.refs_1_), channel_id=1, source_target_pairs={{0,1},{1,0},{2,3},{3,2},{4,5},{5,4},{6,7},{7,6},{8,9},{9,8},{10,11... | collective-permute-start | bytes 393224 | tf_op jit(solution)/shard_map/ppermute | solution.py:31
  2.4 6.4 %collective-permute-start.1 = (bf16[16,1024]{1,0:T(8,128)(2,1)S(1)}, bf16[16,1024]{1,0:T(8,128)(2,1)S(1)}, u32[]{:S(2)}, u32[]{:S(2)}) collective-permute-start(bf16[16,1024]{1,0:T(8,128)(2,1)S(1)} %get-tuple-element.20), channel_id=1, source_target_pairs={{2,0},{4,2},{6,4},{8,6},{10,8},{12,10},{14,12},{3,1},{5,3},{7,5},{... | collective-permute-start | bytes 98312 | tf_op jit(solution)/shard_map/ppermute | solution.py:26
  11.0 10.5 %collective-permute-start.2 = (bf16[136,1024]{1,0:T(8,128)(2,1)S(1)}, bf16[136,1024]{1,0:T(8,128)(2,1)S(1)}, u32[]{:S(2)}, u32[]{:S(2)}) collective-permute-start(bf16[136,1024]{1,0:T(8,128)(2,1)S(1)} %get-tuple-element.22.refs_4_.refs_1_), channel_id=1, source_target_pairs={{0,2},{2,0},{4,6},{6,4},{8,10},{10,8},{12,14},{14,12},{1,3},{3,1},... | collective-permute-start | bytes 835592 | tf_op jit(solution)/shard_map/ppermute | solution.py:31
  16.2 12.2 %collective-permute-start.4 = (bf16[128,1024]{1,0:T(8,128)(2,1)S(1)}, bf16[128,1024]{1,0:T(8,128)(2,1)S(1)}, u32[]{:S(2)}, u32[]{:S(2)}) collective-permute-start(bf16[128,1024]{1,0:T(8,128)(2,1)S(1)} %get-tuple-element.25.refs_3_), channel_id=1, source_target_pairs={{0,2},{2,0},{4,6},{6,4},{8,10},{10,8},{12,14},{14,12},{1,3},{3,1},... | collective-permute-start | bytes 786440 | tf_op jit(solution)/shard_map/ppermute | solution.py:31
  24.3 13.4 %collective-permute-start.7 = (bf16[128,1024]{1,0:T(8,128)(2,1)S(1)}, bf16[128,1024]{1,0:T(8,128)(2,1)S(1)}, u32[]{:S(2)}, u32[]{:S(2)}) collective-permute-start(bf16[128,1024]{1,0:T(8,128)(2,1)S(1)} %get-tuple-element.28.refs_5_), channel_id=1, source_target_pairs={{0,2},{2,0},{4,6},{6,4},{8,10},{10,8},{12,14},{14,12},{1,3},{3,1},... | collective-permute-start | bytes 786440 | tf_op jit(solution)/shard_map/ppermute | solution.py:31
  26.3 6.0 %collective-permute-start.5 = (bf16[136,512]{1,0:T(8,128)(2,1)S(1)}, bf16[136,512]{1,0:T(8,128)(2,1)S(1)}, u32[]{:S(2)}, u32[]{:S(2)}) collective-permute-start(bf16[136,512]{1,0:T(8,128)(2,1)S(1)} %get-tuple-element.27.refs_5_.refs_1_.refs_3_), channel_id=1, source_target_pairs={{0,4},{2,6},{4,0},{6,2},{8,12},{10,14},{12,8},{14,10},{1,5},{3,7},... | collective-permute-start | bytes 417800 | tf_op jit(solution)/shard_map/ppermute | solution.py:31
  28.4 5.4 %collective-permute-start.3 = (bf16[136,512]{1,0:T(8,128)(2,1)S(1)}, bf16[136,512]{1,0:T(8,128)(2,1)S(1)}, u32[]{:S(2)}, u32[]{:S(2)}) collective-permute-start(bf16[136,512]{1,0:T(8,128)(2,1)S(1)} %get-tuple-element.26.refs_6_.refs_1_.refs_4_), channel_id=1, source_target_pairs={{0,4},{2,6},{4,0},{6,2},{8,12},{10,14},{12,8},{14,10},{1,5},{3,7},... | collective-permute-start | bytes 417800 | tf_op jit(solution)/shard_map/ppermute | solution.py:31
  36.4 11.8 %collective-permute-start.6 = (bf16[128,1024]{1,0:T(8,128)(2,1)S(1)}, bf16[128,1024]{1,0:T(8,128)(2,1)S(1)}, u32[]{:S(2)}, u32[]{:S(2)}) collective-permute-start(bf16[128,1024]{1,0:T(8,128)(2,1)S(1)} %get-tuple-element.30.refs_5_), channel_id=1, source_target_pairs={{0,2},{2,0},{4,6},{6,4},{8,10},{10,8},{12,14},{14,12},{1,3},{3,1},... | collective-permute-start | bytes 786440 | tf_op jit(solution)/shard_map/ppermute | solution.py:31
  38.2 10.1 %collective-permute-start.8 = (bf16[128,1024]{1,0:T(8,128)(2,1)S(1)}, bf16[128,1024]{1,0:T(8,128)(2,1)S(1)}, u32[]{:S(2)}, u32[]{:S(2)}) collective-permute-start(bf16[128,1024]{1,0:T(8,128)(2,1)S(1)} %resent.1.refs_3_), channel_id=1, source_target_pairs={{0,4},{2,6},{4,0},{6,2},{8,12},{10,14},{12,8},{14,10},{1,5},{3,7},... | collective-permute-start | bytes 786440 | tf_op jit(solution)/shard_map/ppermute | solution.py:31
  40.0 8.9 %collective-permute-start.10 = (bf16[136,512]{1,0:T(8,128)(2,1)S(1)}, bf16[136,512]{1,0:T(8,128)(2,1)S(1)}, u32[]{:S(2)}, u32[]{:S(2)}) collective-permute-start(bf16[136,512]{1,0:T(8,128)(2,1)S(1)} %merge_far.3.refs_5_.refs_3_), channel_id=1, source_target_pairs={{0,8},{2,10},{4,12},{6,14},{8,0},{10,2},{12,4},{14,6},{1,9},{3,11}... | collective-permute-start | bytes 417800 | tf_op jit(solution)/shard_map/ppermute | solution.py:31
  42.6 10.5 %collective-permute-start.9 = (bf16[136,512]{1,0:T(8,128)(2,1)S(1)}, bf16[136,512]{1,0:T(8,128)(2,1)S(1)}, u32[]{:S(2)}, u32[]{:S(2)}) collective-permute-start(bf16[136,512]{1,0:T(8,128)(2,1)S(1)} %merge_far.2.refs_5_.refs_2_), channel_id=1, source_target_pairs={{0,8},{2,10},{4,12},{6,14},{8,0},{10,2},{12,4},{14,6},{1,9},{3,11}... | collective-permute-start | bytes 417800 | tf_op jit(solution)/shard_map/ppermute | solution.py:31

commit v6 on v5

--- a/solution.py
+++ b/solution.py
@@ -11,13 +11,21 @@
 LANES = 128
 EXTRA = 8
 FETCHES = 8
+STEP = 256
 GROUP = 4
 POWER = 16
 CODE_SCALE = 2.0 ** (126 / POWER)
 TINY = 1e-35
 PIECES = 4
 VMEM_BYTES = 32 * 1024 * 1024
-SMALL = pl.CostEstimate(flops=0, bytes_accessed=1024, transcendentals=0)
+HBM_RATE = 3.69e6
+PRODUCT_MICROS = 1.0
+SEGMENT_MICROS = 1.2
+MERGE_MICROS = 0.3
+
+
+def lasting(micros):
+    return pl.CostEstimate(flops=0, bytes_accessed=int(micros * HBM_RATE), transcendentals=0)
 
 
 def passed_along(value, axis, steps):
@@ -85,7 +93,7 @@
 def expanded(code, channel_bound, ref_bound):
     channel = jnp.sqrt(jnp.maximum(channel_bound, TINY))
     refs = jnp.sqrt(jnp.maximum(ref_bound, TINY)) * (1.0 / CODE_SCALE)
-    wide = code.astype(jnp.float32)
+    wide = code[...].astype(jnp.float32)
     root = jnp.exp2(jnp.log2(jnp.abs(wide)) * (1.0 / POWER))
     return jnp.where(wide < 0.0, -root, root) * channel * for_chunk(refs, code.shape[0])
 
@@ -123,7 +131,7 @@
         out_shape=[pltpu.VMEM((HALF, rows), strain.dtype), pltpu.VMEM((LAGS, width), strain.dtype)],
         scratch_shapes=[pltpu.VMEM((rows, LANES), strain.dtype), pltpu.SemaphoreType.DMA((PIECES + 1,))],
         compiler_params=pltpu.CompilerParams(vmem_limit_bytes=VMEM_BYTES),
-        cost_estimate=SMALL,
+        cost_estimate=lasting(PRODUCT_MICROS),
         name="prepared",
     )(pltpu.with_memory_space_constraint(strain, pltpu.HBM))
 
@@ -175,7 +183,7 @@
         out_shape=[pltpu.VMEM((rows, width), strain.dtype), pltpu.VMEM((1, width), jnp.float32)],
         scratch_shapes=[pltpu.SemaphoreType.DMA((FETCHES,))],
         compiler_params=pltpu.CompilerParams(vmem_limit_bytes=VMEM_BYTES),
-        cost_estimate=SMALL,
+        cost_estimate=lasting(PRODUCT_MICROS),
         name="loaded",
     )(pltpu.with_memory_space_constraint(strain, pltpu.HBM), after)
 
@@ -190,8 +198,8 @@
     return total + jnp.dot(shifted[:, :rows], held[:, here], preferred_element_type=jnp.float32)
 
 
-def columns(width, step=256):
-    return [slice(first, first + step) for first in range(0, width, step)]
+def columns(width):
+    return [slice(first, first + STEP) for first in range(0, width, STEP)]
 
 
 def first_products_kernel(held, power, own, other, tail, keep, send, shifted):
@@ -235,6 +243,7 @@
         other,
         tail,
         name="first_products",
+        micros=PRODUCT_MICROS,
         after=after,
         scratch=shifted_scratch(rows),
     )
@@ -243,7 +252,7 @@
 def later_products(bits, held, own, other, tail, powers, chunk, after=()):
     rows, width = held.shape
 
-    def kernel(held, own, other, tail, powers, keep, send, shifted):
+    def kernel(held, own, other, tail, powers, keep, first, second, shifted):
         _, ref_powers, bound = sent_powers(powers)
         refs = ref_column(ref_powers)
         lag_rows(own, other, own_group(bits), shifted)
@@ -251,23 +260,28 @@
         for here in columns(width):
             product = product_of(shifted, held, edge, here)
             keep[:, here] = product[:chunk]
-            send[:, here] = coded(product[chunk:], bound[:, here], refs)
-
-    return call_on_blocks(
+            part, start = divmod(here.start, width // 2)
+            send = (first, second)[part]
+            send[:, start : start + STEP] = coded(product[chunk:], bound[:, here], refs)
+
+    half = ((chunk, width // 2), jnp.bfloat16)
+    keep, *sends = call_on_blocks(
         kernel,
-        [((chunk, width), jnp.float32), ((chunk, width), jnp.bfloat16)],
+        [((chunk, width), jnp.float32), half, half],
         held,
         own,
         other,
         tail,
         powers,
         name="later_products",
+        micros=PRODUCT_MICROS,
         after=after,
         scratch=shifted_scratch(rows),
     )
-
-
-def call_on_blocks(kernel, outs, *arrays, name, after=(), scratch=(), space=pltpu.VMEM):
+    return keep, sends
+
+
+def call_on_blocks(kernel, outs, *arrays, name, micros, after=(), scratch=(), space=pltpu.VMEM):
     vmem = pl.BlockSpec(memory_space=pltpu.VMEM)
     count = len(arrays)
 
@@ -281,7 +295,7 @@
         out_shape=[space(shape, dtype) for shape, dtype in outs],
         scratch_shapes=list(scratch),
         compiler_params=pltpu.CompilerParams(vmem_limit_bytes=VMEM_BYTES),
-        cost_estimate=SMALL,
+        cost_estimate=lasting(micros),
         name=name,
     )(*arrays, *after)
 
@@ -295,7 +309,7 @@
     return powers[:, here], refs, bound[:, here]
 
 
-def merge_near(keep, ours, theirs):
+def merge_near(keep, ours, theirs, after):
     chunk, width = keep.shape
 
     def kernel(keep, ours, theirs, *outs):
@@ -309,7 +323,9 @@
             out[:chunk] = coded(total, sum_bound, ref_column(sum_refs))
 
     outs = [((chunk + EXTRA, width // 2), jnp.bfloat16)] * 2
-    return lambda after: call_on_blocks(kernel, outs, keep, ours, theirs, name="merge_near", after=after)
+    return call_on_blocks(
+        kernel, outs, keep, ours, theirs, name="merge_near", micros=MERGE_MICROS, after=after
+    )
 
 
 def merge_far(part, keep, ours, theirs, direct, direct_powers, after):
@@ -321,42 +337,46 @@
         their_powers, their_refs, their_bound = sent_powers(theirs)
         total = keep[:, here] + expanded(theirs[:chunk], their_bound, ref_column(their_refs))
         _, direct_refs, direct_bound = sent_powers(direct_powers, here)
-        total += expanded(direct[:, here], direct_bound, ref_column(direct_refs))
+        total += expanded(direct, direct_bound, ref_column(direct_refs))
         sums, sum_refs, sum_bound = powers + their_powers, refs + their_refs, rounded_up(bound + their_bound)
         out[chunk:] = packed(sums, sum_refs, sum_bound)
         out[:chunk] = coded(total, sum_bound, ref_column(sum_refs))
 
     outs = [((chunk + EXTRA, width // 2), jnp.bfloat16)]
     return call_on_blocks(
-        kernel, outs, keep, ours, theirs, direct, direct_powers, name="merge_far", after=after
+        kernel, outs, keep, ours, theirs, direct, direct_powers, name="merge_far", micros=MERGE_MICROS, after=after
     )[0]
 
 
 def resent(keep, direct, direct_powers, ours, after):
-    width = keep.shape[1]
-
-    def kernel(keep, direct, direct_powers, first, second, out):
-        for part, powers in enumerate((first, second)):
+    chunk, width = keep.shape
+
+    def kernel(keep, direct_powers, *refs):
+        direct, ours, outs = refs[:2], refs[2:4], refs[4:]
+        for part in range(2):
             here = half_of(width, part)
             _, direct_refs, direct_bound = sent_powers(direct_powers, here)
-            _, refs, bound = sent_powers(powers)
-            total = keep[:, here] + expanded(direct[:, here], direct_bound, ref_column(direct_refs))
-            out[:, here] = coded(total, bound, ref_column(refs))
-
-    outs = [(keep.shape, jnp.bfloat16)]
-    return call_on_blocks(kernel, outs, keep, direct, direct_powers, *ours, name="resent", after=after)[0]
+            _, refs, bound = sent_powers(ours[part])
+            total = keep[:, here] + expanded(direct[part], direct_bound, ref_column(direct_refs))
+            outs[part][...] = coded(total, bound, ref_column(refs))
+
+    outs = [((chunk, width // 2), jnp.bfloat16)] * 2
+    return call_on_blocks(
+        kernel, outs, keep, direct_powers, *direct, *ours, name="resent", micros=MERGE_MICROS, after=after
+    )
 
 
 def added(keep, direct, direct_powers, near, near_powers, held, tail, size, after):
     rows, width = held.shape
 
-    def kernel(keep, direct, direct_powers, near, first, second, held, tail, out, edge):
-        for part, powers in enumerate((first, second)):
+    def kernel(keep, direct_powers, held, tail, *refs):
+        direct, near, near_powers, (out, edge) = refs[:2], refs[2:4], refs[4:6], refs[6:]
+        for part in range(2):
             here = half_of(width, part)
             _, direct_refs, direct_bound = sent_powers(direct_powers, here)
-            _, refs, bound = sent_powers(powers)
-            total = keep[:, here] + expanded(direct[:, here], direct_bound, ref_column(direct_refs))
-            out[:, here] = total + expanded(near[:, here], bound, ref_column(refs))
+            _, near_refs, near_bound = sent_powers(near_powers[part])
+            total = keep[:, here] + expanded(direct[part], direct_bound, ref_column(direct_refs))
+            out[:, here] = total + expanded(near[part], near_bound, ref_column(near_refs))
         last = held[rows - LAGS :, :size].astype(jnp.float32)
         beyond = tail[:, :size].astype(jnp.float32)
         place = lax.broadcasted_iota(jnp.int32, last.shape, 0)
@@ -367,9 +387,8 @@
         edge[...] = jnp.concatenate(sums, axis=0)
 
     outs = [(keep.shape, jnp.float32), ((LAGS, size), jnp.float32)]
-    return call_on_blocks(
-        kernel, outs, keep, direct, direct_powers, near, *near_powers, held, tail, name="added", after=after
-    )
+    arrays = (keep, direct_powers, held, tail, *direct, *near, *near_powers)
+    return call_on_blocks(kernel, outs, *arrays, name="added", micros=MERGE_MICROS, after=after)
 
 
 def finished(slab_rows, segment, partial, edge, ours, theirs, autos):
@@ -398,7 +417,7 @@
 
     outs = [(partial.shape, jnp.float32), ((LAGS, width), jnp.float32)]
     return call_on_blocks(
-        kernel, outs, partial, edge, *ours, *theirs, *autos, name="finished", space=jax.ShapeDtypeStruct
+        kernel, outs, partial, edge, *ours, *theirs, *autos, name="finished", micros=MERGE_MICROS, space=jax.ShapeDtypeStruct
     )
 
 
@@ -450,6 +469,7 @@
         [((LAGS, size), jnp.float32)],
         *arrays,
         name="segment_rows",
+        micros=SEGMENT_MICROS,
         after=after,
         scratch=[pltpu.VMEM((rows + 8 * LAGS, LANES), jnp.float32)],
     )[0]
@@ -501,25 +521,25 @@
         autos = [segment_rows(held, power, None, 0, size)]
         keep6, send7 = first_products(held, power, *refs, chunk, after=(autos[0],))
         got7 = exchanged(send7, "tm", 1)
-        keep4, send5 = later_products(2, held, *refs, send7, chunk)
-        got5 = exchanged(send5, "tm", 1)
-        autos.append(segment_rows(held, power, tail, size, size, after=(send5,)))
-        sends6 = merge_near(keep6, send7, got7)(after=(autos[1],))
+        keep4, sends5 = later_products(2, held, *refs, send7, chunk)
+        gots5 = [exchanged(code, "tm", 1) for code in sends5]
+        autos.append(segment_rows(held, power, tail, size, size, after=tuple(sends5)))
+        sends6 = merge_near(keep6, send7, got7, after=(autos[1],))
         gots6 = [exchanged(code, "tm", 2) for code in sends6]
-        keep2, send3 = later_products(1, held, *refs, send7, chunk, after=tuple(sends6))
-        got3 = exchanged(send3, "tm", 1)
+        keep2, sends3 = later_products(1, held, *refs, send7, chunk, after=tuple(sends6))
+        gots3 = [exchanged(code, "tm", 1) for code in sends3]
+        keep0, sends1 = later_products(0, held, *refs, send7, chunk, after=tuple(sends3))
+        gots1 = [exchanged(code, "tm", 1) for code in sends1]
         sends4, gots4 = [], []
         for part in range(2):
-            after = (sends4[0] if part else send3,)
-            sends4.append(merge_far(part, keep4, sends6[part], gots6[part], got5, got7, after))
+            after = (sends4[0] if part else sends1[0],)
+            sends4.append(merge_far(part, keep4, sends6[part], gots6[part], gots5[part], got7, after))
             gots4.append(exchanged(sends4[part], "tm", 4))
-        keep0, send1 = later_products(0, held, *refs, send7, chunk, after=(sends4[1],))
-        got1 = exchanged(send1, "tm", 1)
-        send2 = resent(keep2, got3, got7, sends6, after=(send1,))
-        got2 = exchanged(send2, "tm", 2)
+        sends2 = resent(keep2, gots3, got7, sends6, after=(sends4[1],))
+        gots2 = [exchanged(code, "tm", 2) for code in sends2]
         for index in (2, 3):
-            autos.append(segment_rows(held, power, tail, size * index, size, after=(send2,)))
-        partial, edge = added(keep0, got1, got7, got2, gots6, held, tail, size, after=tuple(autos[2:]))
+            autos.append(segment_rows(held, power, tail, size * index, size, after=tuple(sends2)))
+        partial, edge = added(keep0, gots1, got7, gots2, gots6, held, tail, size, after=tuple(autos[2:]))
         return tuple(finished(slab_rows, rows, partial, edge, sends4, gots4, autos))
 
     chan = lax.axis_index("chan").astype(jnp.int32)

time: 54.5 us -> 51.9 us (0.952)
  waiting for transfers between devices: 12 us -> 5.98 us
  starting transfers between devices: 15.1 us -> 18.4 us
    ppermute x10 -> x14, waiting for transfers between devices: 11.7 us -> 5.76 us  [exchanged(): lax.ppermute(value, axis, [(source, source ^ bit) for source in range(cou...]
    ppermute x10 -> x14, starting transfers between devices: 13.8 us -> 17.1 us  [exchanged(): lax.ppermute(value, axis, [(source, source ^ bit) for source in range(cou...]
  transfers between devices with their start and end apart: 11 -> 15, of which waited for: 5 -> 5; matrix products, arithmetic and copies ran while one was open for 0% -> 0% of each run, Pallas kernels for 40% -> 41%
where the time goes in v6:
time: 51.9 us; the launch traced here: 51.7 us
  Pallas kernels  26.5 us (51%)
  starting transfers between devices  18.4 us (35%)
  waiting for transfers between devices  5.98 us (12%)
  between operations  0.8 us (2%)
    pallas_call x14, Pallas kernels, call_on_blocks(): pl.pallas_call(body, in_specs=[vmem] * count + [pl.BlockSpec(memory_space...  23 us
    ppermute x14, starting transfers between devices, exchanged(): lax.ppermute(value, axis, [(source, source ^ bit) for source in range(cou...  17.1 us
    ppermute x14, waiting for transfers between devices, exchanged(): lax.ppermute(value, axis, [(source, source ^ bit) for source in range(cou...  5.76 us
    pallas_call x1, Pallas kernels, loaded(): pl.pallas_call(kernel, in_specs=[pl.BlockSpec(memory_space=pl.ANY)] * 2,...  2.26 us
    ppermute x1, starting transfers between devices, passed_along(): lax.ppermute(value, axis, [(source, source + steps) for source in range(i...  1.28 us
    pallas_call x1, Pallas kernels, prepared(): pl.pallas_call(prepare_kernel, in_specs=[pl.BlockSpec(memory_space=pl.ANY...  1.28 us
  transfers between devices with their start and end apart: 15, of which 5 were waited for; matrix products, arithmetic and copies ran while one was open for 0% of the time, Pallas kernels for 41%

profile of v6, /device:TPU:0, one launch (start us, length us, event | category | flops | bytes accessed | tf_op | source)
XLA Modules:
  0.0 51.7 jit_solution(1479916082685435937)
XLA Ops:
  0.6 1.3 %prepared.1 = (bf16[32,2048]{1,0:T(8,128)(2,1)S(1)}, bf16[16,1024]{1,0:T(8,128)(2,1)S(1)}) custom-call(bf16[2048,1024]{1,0:T(8,128)(2,1)} %strain.3), custom_call_target="tpu_custom_call" | custom-call | bytes 3690000 | tf_op jit(solution)/shard_map/prepared/pallas_call | solution.py:127
  1.9 0.5 %collective-permute-start = (bf16[32,2048]{1,0:T(8,128)(2,1)S(1)}, bf16[32,2048]{1,0:T(8,128)(2,1)S(1)}, u32[]{:S(2)}, u32[]{:S(2)}) collective-permute-start(bf16[32,2048]{1,0:T(8,128)(2,1)S(1)} %get-tuple-element.23.after.refs_2_.refs_1_), channel_id=1, source_target_pairs={{0,1},{1,0},{2,3},{3,2},{4,5},{5,4},{6,7},{7,6},{8,9},{9,8},{10,11... | collective-permute-start | bytes 393224 | tf_op jit(solution)/shard_map/ppermute | solution.py:39
  2.4 1.3 %collective-permute-start.1 = (bf16[16,1024]{1,0:T(8,128)(2,1)S(1)}, bf16[16,1024]{1,0:T(8,128)(2,1)S(1)}, u32[]{:S(2)}, u32[]{:S(2)}) collective-permute-start(bf16[16,1024]{1,0:T(8,128)(2,1)S(1)} %get-tuple-element.25), channel_id=1, source_target_pairs={{2,0},{4,2},{6,4},{8,6},{10,8},{12,10},{14,12},{3,1},{5,3},{7,5},{... | collective-permute-start | bytes 98312 | tf_op jit(solution)/shard_map/ppermute | solution.py:34
  3.7 2.3 %loaded.1 = (bf16[2048,1024]{1,0:T(8,128)(2,1)S(1)}, f32[1,1024]{1,0:T(1,128)S(1)}) custom-call(bf16[2048,1024]{1,0:T(8,128)(2,1)} %strain.3, bf16[32,2048]{1,0:T(8,128)(2,1)S(1)} %get-tuple-element.23.after.refs_2_.refs_1_), custom_call_target="tpu_custom_call" | custom-call | bytes 3690000 | tf_op jit(solution)/shard_map/loaded/pallas_call | solution.py:179
  6.0 2.7 %segment_rows.4.refs_5_.refs_6_ = f32[16,256]{1,0:T(8,128)S(1)} custom-call(bf16[2048,1024]{1,0:T(8,128)(2,1)S(1)} %get-tuple-element.24.refs_0_.refs_2_, f32[1,1024]{1,0:T(1,128)S(1)} %get-tuple-element.26.refs_1_), custom_call_target="tpu_custom_call" | custom-call | bytes 4428000 | tf_op jit(solution)/shard_map/segment_rows/pallas_call | solution.py:291
  8.7 0.2 collective-permute-done.1.refs_4_.refs_3_.refs_2_
  8.9 0.0 collective-permute-done.refs_3_.refs_2_
  8.9 2.2 %first_products.1 = (f32[128,1024]{1,0:T(8,128)S(1)}, bf16[136,1024]{1,0:T(8,128)(2,1)S(1)}) custom-call(bf16[2048,1024]{1,0:T(8,128)(2,1)S(1)} %get-tuple-element.24.refs_0_.refs_2_, f32[1,1024]{1,0:T(1,128)S(1)} %get-tuple-element.26.refs_1_, bf16[32,2048]{1,0:T(8,128)(2,1)S(1)} %get-tuple-element.23.after.refs_2_.refs_1_, ...), custom_call_target="tpu_custom_call" | custom-call | bytes 3690000 | tf_op jit(solution)/shard_map/first_products/pallas_call | solution.py:291
  11.0 3.0 %collective-permute-start.2 = (bf16[136,1024]{1,0:T(8,128)(2,1)S(1)}, bf16[136,1024]{1,0:T(8,128)(2,1)S(1)}, u32[]{:S(2)}, u32[]{:S(2)}) collective-permute-start(bf16[136,1024]{1,0:T(8,128)(2,1)S(1)} %get-tuple-element.27.refs_4_.refs_1_), channel_id=1, source_target_pairs={{0,2},{2,0},{4,6},{6,4},{8,10},{10,8},{12,14},{14,12},{1,3},{3,1},... | collective-permute-start | bytes 835592 | tf_op jit(solution)/shard_map/ppermute | solution.py:39
  14.0 2.1 %later_products.3 = (f32[128,1024]{1,0:T(8,128)S(1)}, bf16[128,512]{1,0:T(8,128)(2,1)S(1)}, bf16[128,512]{1,0:T(8,128)(2,1)S(1)}) custom-call(bf16[2048,1024]{1,0:T(8,128)(2,1)S(1)} %get-tuple-element.24.refs_0_.refs_2_, bf16[32,2048]{1,0:T(8,128)(2,1)S(1)} %get-tuple-element.23.after.refs_2_.refs_1_, ...), custom_call_target="tpu_custom_call" | custom-call | bytes 3690000 | tf_op jit(solution)/shard_map/later_products/pallas_call | solution.py:291
  16.2 2.7 %segment_rows.5.refs_3_.refs_7_ = f32[16,256]{1,0:T(8,128)S(1)} custom-call(bf16[2048,1024]{1,0:T(8,128)(2,1)S(1)} %get-tuple-element.24.refs_0_.refs_2_, f32[1,1024]{1,0:T(1,128)S(1)} %get-tuple-element.26.refs_1_, bf16[16,1024]{1,0:T(8,128)(2,1)S(1)} %collective-permute-done.1.refs_4_.refs_3_.refs_2_, bf16[128,512]{1,0:T(8,128)(2,1)S(1)} %get-tuple-element.29.refs_3_, ...), custom_call_target="tpu_custom_call" | custom-call | bytes 4428000 | tf_op jit(solution)/shard_map/segment_rows/pallas_call | solution.py:291
  18.9 2.5 %collective-permute-done.2.refs_2_.refs_4_.refs_1_ = bf16[136,1024]{1,0:T(8,128)(2,1)S(1)} collective-permute-done((bf16[136,1024]{1,0:T(8,128)(2,1)S(1)}, bf16[136,1024]{1,0:T(8,128)(2,1)S(1)}, u32[]{:S(2)}, u32[]{:S(2)}) %collective-permute-start.2) | collective-permute-done | bytes 278560 | tf_op jit(solution)/shard_map/ppermute | solution.py:39
  21.4 0.5 %merge_near.1 = (bf16[136,512]{1,0:T(8,128)(2,1)S(1)}, bf16[136,512]{1,0:T(8,128)(2,1)S(1)}) custom-call(f32[128,1024]{1,0:T(8,128)S(1)} %get-tuple-element.28.refs_0_, bf16[136,1024]{1,0:T(8,128)(2,1)S(1)} %get-tuple-element.27.refs_4_.refs_1_, bf16[136,1024]{1,0:T(8,128)(2,1)S(1)} %collective-permute-done.2.refs_2_.refs_4_.refs_1_, ...), custom_call_target="tpu_custom_call" | custom-call | bytes 1107000 | tf_op jit(solution)/shard_map/merge_near/pallas_call | solution.py:291
  21.9 3.0 %collective-permute-start.9 = (bf16[136,512]{1,0:T(8,128)(2,1)S(1)}, bf16[136,512]{1,0:T(8,128)(2,1)S(1)}, u32[]{:S(2)}, u32[]{:S(2)}) collective-permute-start(bf16[136,512]{1,0:T(8,128)(2,1)S(1)} %get-tuple-element.31.refs_5_.refs_1_.refs_4_), channel_id=1, source_target_pairs={{0,4},{2,6},{4,0},{6,2},{8,12},{10,14},{12,8},{14,10},{1,5},{3,7},... | collective-permute-start | bytes 417800 | tf_op jit(solution)/shard_map/ppermute | solution.py:39
  24.9 0.6 %collective-permute-start.10 = (bf16[128,512]{1,0:T(8,128)(2,1)S(1)}, bf16[128,512]{1,0:T(8,128)(2,1)S(1)}, u32[]{:S(2)}, u32[]{:S(2)}) collective-permute-start(bf16[128,512]{1,0:T(8,128)(2,1)S(1)} %get-tuple-element.29.refs_3_), channel_id=1, source_target_pairs={{0,2},{2,0},{4,6},{6,4},{8,10},{10,8},{12,14},{14,12},{1,3},{3,1},... | collective-permute-start | bytes 393224 | tf_op jit(solution)/shard_map/ppermute | solution.py:39
  25.5 0.2 collective-permute-start.7
  25.7 1.3 %collective-permute-start.8 = (bf16[128,512]{1,0:T(8,128)(2,1)S(1)}, bf16[128,512]{1,0:T(8,128)(2,1)S(1)}, u32[]{:S(2)}, u32[]{:S(2)}) collective-permute-start(bf16[128,512]{1,0:T(8,128)(2,1)S(1)} %get-tuple-element.30.refs_4_), channel_id=1, source_target_pairs={{0,2},{2,0},{4,6},{6,4},{8,10},{10,8},{12,14},{14,12},{1,3},{3,1},... | collective-permute-start | bytes 393224 | tf_op jit(solution)/shard_map/ppermute | solution.py:39
  27.0 2.1 %later_products.4 = (f32[128,1024]{1,0:T(8,128)S(1)}, bf16[128,512]{1,0:T(8,128)(2,1)S(1)}, bf16[128,512]{1,0:T(8,128)(2,1)S(1)}) custom-call(bf16[2048,1024]{1,0:T(8,128)(2,1)S(1)} %get-tuple-element.24.refs_0_.refs_2_, bf16[32,2048]{1,0:T(8,128)(2,1)S(1)} %get-tuple-element.23.after.refs_2_.refs_1_, ...), custom_call_target="tpu_custom_call" | custom-call | bytes 3690000 | tf_op jit(solution)/shard_map/later_products/pallas_call | solution.py:291
  29.1 0.8 %collective-permute-start.5 = (bf16[128,512]{1,0:T(8,128)(2,1)S(1)}, bf16[128,512]{1,0:T(8,128)(2,1)S(1)}, u32[]{:S(2)}, u32[]{:S(2)}) collective-permute-start(bf16[128,512]{1,0:T(8,128)(2,1)S(1)} %get-tuple-element.33.refs_5_), channel_id=1, source_target_pairs={{0,2},{2,0},{4,6},{6,4},{8,10},{10,8},{12,14},{14,12},{1,3},{3,1},... | collective-permute-start | bytes 393224 | tf_op jit(solution)/shard_map/ppermute | solution.py:39
  30.0 1.2 %collective-permute-done.10.refs_3_ = bf16[128,512]{1,0:T(8,128)(2,1)S(1)} collective-permute-done((bf16[128,512]{1,0:T(8,128)(2,1)S(1)}, bf16[128,512]{1,0:T(8,128)(2,1)S(1)}, u32[]{:S(2)}, u32[]{:S(2)}) %collective-permute-start.10) | collective-permute-done | bytes 131104 | tf_op jit(solution)/shard_map/ppermute | solution.py:39
  31.2 0.5 %collective-permute-start.6 = (bf16[128,512]{1,0:T(8,128)(2,1)S(1)}, bf16[128,512]{1,0:T(8,128)(2,1)S(1)}, u32[]{:S(2)}, u32[]{:S(2)}) collective-permute-start(bf16[128,512]{1,0:T(8,128)(2,1)S(1)} %get-tuple-element.34.refs_6_), channel_id=1, source_target_pairs={{0,2},{2,0},{4,6},{6,4},{8,10},{10,8},{12,14},{14,12},{1,3},{3,1},... | collective-permute-start | bytes 393224 | tf_op jit(solution)/shard_map/ppermute | solution.py:39
  31.7 2.1 %later_products.5 = (f32[128,1024]{1,0:T(8,128)S(1)}, bf16[128,512]{1,0:T(8,128)(2,1)S(1)}, bf16[128,512]{1,0:T(8,128)(2,1)S(1)}) custom-call(bf16[2048,1024]{1,0:T(8,128)(2,1)S(1)} %get-tuple-element.24.refs_0_.refs_2_, bf16[32,2048]{1,0:T(8,128)(2,1)S(1)} %get-tuple-element.23.after.refs_2_.refs_1_, ...), custom_call_target="tpu_custom_call" | custom-call | bytes 3690000 | tf_op jit(solution)/shard_map/later_products/pallas_call | solution.py:291
  33.8 0.0 collective-permute-done.9.refs_2_.refs_8_
  33.9 1.6 %collective-permute-start.3 = (bf16[128,512]{1,0:T(8,128)(2,1)S(1)}, bf16[128,512]{1,0:T(8,128)(2,1)S(1)}, u32[]{:S(2)}, u32[]{:S(2)}) collective-permute-start(bf16[128,512]{1,0:T(8,128)(2,1)S(1)} %get-tuple-element.36.refs_5_), channel_id=1, source_target_pairs={{0,2},{2,0},{4,6},{6,4},{8,10},{10,8},{12,14},{14,12},{1,3},{3,1},... | collective-permute-start | bytes 393224 | tf_op jit(solution)/shard_map/ppermute | solution.py:39
  35.4 0.4 merge_far.2.refs_5_.refs_2_
  35.9 0.0 collective-permute-done.8.refs_3_
  35.9 0.0 collective-permute-done.7.refs_2_.refs_9_
  35.9 0.4 merge_far.3.refs_6_.refs_3_
  36.4 2.5 %collective-permute-start.14 = (bf16[136,512]{1,0:T(8,128)(2,1)S(1)}, bf16[136,512]{1,0:T(8,128)(2,1)S(1)}, u32[]{:S(2)}, u32[]{:S(2)}) collective-permute-start(bf16[136,512]{1,0:T(8,128)(2,1)S(1)} %merge_far.3.refs_6_.refs_3_), channel_id=1, source_target_pairs={{0,8},{2,10},{4,12},{6,14},{8,0},{10,2},{12,4},{14,6},{1,9},{3,11}... | collective-permute-start | bytes 417800 | tf_op jit(solution)/shard_map/ppermute | solution.py:39
  38.9 0.5 collective-permute-start.13
  39.4 0.0 collective-permute-done.5.refs_2_
  39.4 0.5 collective-permute-start.4
  39.9 0.0 collective-permute-done.6.refs_3_
  39.9 0.5 resent.1
  40.4 1.6 %collective-permute-start.11 = (bf16[128,512]{1,0:T(8,128)(2,1)S(1)}, bf16[128,512]{1,0:T(8,128)(2,1)S(1)}, u32[]{:S(2)}, u32[]{:S(2)}) collective-permute-start(bf16[128,512]{1,0:T(8,128)(2,1)S(1)} %get-tuple-element.40.refs_3_), channel_id=1, source_target_pairs={{0,4},{2,6},{4,0},{6,2},{8,12},{10,14},{12,8},{14,10},{1,5},{3,7},... | collective-permute-start | bytes 393224 | tf_op jit(solution)/shard_map/ppermute | solution.py:39
  41.9 0.1 collective-permute-done.3.refs_4_
  42.0 0.5 %collective-permute-start.12 = (bf16[128,512]{1,0:T(8,128)(2,1)S(1)}, bf16[128,512]{1,0:T(8,128)(2,1)S(1)}, u32[]{:S(2)}, u32[]{:S(2)}) collective-permute-start(bf16[128,512]{1,0:T(8,128)(2,1)S(1)} %get-tuple-element.41.refs_4_), channel_id=1, source_target_pairs={{0,4},{2,6},{4,0},{6,2},{8,12},{10,14},{12,8},{14,10},{1,5},{3,7},... | collective-permute-start | bytes 393224 | tf_op jit(solution)/shard_map/ppermute | solution.py:39
  42.6 2.7 %segment_rows.7.refs_11_.refs_9_ = f32[16,256]{1,0:T(8,128)S(1)} custom-call(bf16[2048,1024]{1,0:T(8,128)(2,1)S(1)} %get-tuple-element.24.refs_0_.refs_2_, f32[1,1024]{1,0:T(1,128)S(1)} %get-tuple-element.26.refs_1_, bf16[16,1024]{1,0:T(8,128)(2,1)S(1)} %collective-permute-done.1.refs_4_.refs_3_.refs_2_, bf16[128,512]{1,0:T(8,128)(2,1)S(1)} %get-tuple-element.40.refs_3_, ...), custom_call_target="tpu_custom_call" | custom-call | bytes 4428000 | tf_op jit(solution)/shard_map/segment_rows/pallas_call | solution.py:291
  45.2 2.7 %segment_rows.6.refs_10_.refs_8_ = f32[16,256]{1,0:T(8,128)S(1)} custom-call(bf16[2048,1024]{1,0:T(8,128)(2,1)S(1)} %get-tuple-element.24.refs_0_.refs_2_, f32[1,1024]{1,0:T(1,128)S(1)} %get-tuple-element.26.refs_1_, bf16[16,1024]{1,0:T(8,128)(2,1)S(1)} %collective-permute-done.1.refs_4_.refs_3_.refs_2_, bf16[128,512]{1,0:T(8,128)(2,1)S(1)} %get-tuple-element.40.refs_3_, ...), custom_call_target="tpu_custom_call" | custom-call | bytes 4428000 | tf_op jit(solution)/shard_map/segment_rows/pallas_call | solution.py:291
  47.9 0.0 collective-permute-done.4.refs_5_
  47.9 0.0 collective-permute-done.11.refs_6_
  47.9 1.9 %collective-permute-done.12.refs_7_ = bf16[128,512]{1,0:T(8,128)(2,1)S(1)} collective-permute-done((bf16[128,512]{1,0:T(8,128)(2,1)S(1)}, bf16[128,512]{1,0:T(8,128)(2,1)S(1)}, u32[]{:S(2)}, u32[]{:S(2)}) %collective-permute-start.12) | collective-permute-done | bytes 131104 | tf_op jit(solution)/shard_map/ppermute | solution.py:39
  49.9 0.6 %added.1 = (f32[128,1024]{1,0:T(8,128)S(1)}, f32[16,256]{1,0:T(8,128)S(1)}) custom-call(f32[128,1024]{1,0:T(8,128)S(1)} %get-tuple-element.35.refs_0_, bf16[136,1024]{1,0:T(8,128)(2,1)S(1)} %collective-permute-done.2.refs_2_.refs_4_.refs_1_, bf16[2048,1024]{1,0:T(8,128)(2,1)S(1)} %get-tuple-element.24.refs_0_.refs_2_, ...), custom_call_target="tpu_custom_call" | custom-call | bytes 1107000 | tf_op jit(solution)/shard_map/added/pallas_call | solution.py:291
  50.5 0.0 collective-permute-done.14.refs_5_
  50.5 0.0 collective-permute-done.13.refs_4_
  50.5 1.2 %finished.1 = (f32[128,1024]{1,0:T(8,128)}, f32[16,1024]{1,0:T(8,128)}) custom-call(f32[128,1024]{1,0:T(8,128)S(1)} %get-tuple-element.42.refs_0_, f32[16,256]{1,0:T(8,128)S(1)} %get-tuple-element.43.refs_1_, bf16[136,512]{1,0:T(8,128)(2,1)S(1)} %merge_far.2.refs_5_.refs_2_, bf16[136,512]{1,0:T(8,128)(2,1)S(1)} %merge_far.3.refs_6_.refs_3_, ...), custom_call_target="tpu_custom_call" | custom-call | bytes 1107000 | tf_op jit(solution)/shard_map/finished/pallas_call | solution.py:291
Async XLA Ops:
  1.9 7.0 %collective-permute-start = (bf16[32,2048]{1,0:T(8,128)(2,1)S(1)}, bf16[32,2048]{1,0:T(8,128)(2,1)S(1)}, u32[]{:S(2)}, u32[]{:S(2)}) collective-permute-start(bf16[32,2048]{1,0:T(8,128)(2,1)S(1)} %get-tuple-element.23.after.refs_2_.refs_1_), channel_id=1, source_target_pairs={{0,1},{1,0},{2,3},{3,2},{4,5},{5,4},{6,7},{7,6},{8,9},{9,8},{10,11... | collective-permute-start | bytes 393224 | tf_op jit(solution)/shard_map/ppermute | solution.py:39
  2.4 6.4 %collective-permute-start.1 = (bf16[16,1024]{1,0:T(8,128)(2,1)S(1)}, bf16[16,1024]{1,0:T(8,128)(2,1)S(1)}, u32[]{:S(2)}, u32[]{:S(2)}) collective-permute-start(bf16[16,1024]{1,0:T(8,128)(2,1)S(1)} %get-tuple-element.25), channel_id=1, source_target_pairs={{2,0},{4,2},{6,4},{8,6},{10,8},{12,10},{14,12},{3,1},{5,3},{7,5},{... | collective-permute-start | bytes 98312 | tf_op jit(solution)/shard_map/ppermute | solution.py:34
  11.0 10.3 %collective-permute-start.2 = (bf16[136,1024]{1,0:T(8,128)(2,1)S(1)}, bf16[136,1024]{1,0:T(8,128)(2,1)S(1)}, u32[]{:S(2)}, u32[]{:S(2)}) collective-permute-start(bf16[136,1024]{1,0:T(8,128)(2,1)S(1)} %get-tuple-element.27.refs_4_.refs_1_), channel_id=1, source_target_pairs={{0,2},{2,0},{4,6},{6,4},{8,10},{10,8},{12,14},{14,12},{1,3},{3,1},... | collective-permute-start | bytes 835592 | tf_op jit(solution)/shard_map/ppermute | solution.py:39
  21.9 11.9 %collective-permute-start.9 = (bf16[136,512]{1,0:T(8,128)(2,1)S(1)}, bf16[136,512]{1,0:T(8,128)(2,1)S(1)}, u32[]{:S(2)}, u32[]{:S(2)}) collective-permute-start(bf16[136,512]{1,0:T(8,128)(2,1)S(1)} %get-tuple-element.31.refs_5_.refs_1_.refs_4_), channel_id=1, source_target_pairs={{0,4},{2,6},{4,0},{6,2},{8,12},{10,14},{12,8},{14,10},{1,5},{3,7},... | collective-permute-start | bytes 417800 | tf_op jit(solution)/shard_map/ppermute | solution.py:39
  24.9 6.3 %collective-permute-start.10 = (bf16[128,512]{1,0:T(8,128)(2,1)S(1)}, bf16[128,512]{1,0:T(8,128)(2,1)S(1)}, u32[]{:S(2)}, u32[]{:S(2)}) collective-permute-start(bf16[128,512]{1,0:T(8,128)(2,1)S(1)} %get-tuple-element.29.refs_3_), channel_id=1, source_target_pairs={{0,2},{2,0},{4,6},{6,4},{8,10},{10,8},{12,14},{14,12},{1,3},{3,1},... | collective-permute-start | bytes 393224 | tf_op jit(solution)/shard_map/ppermute | solution.py:39
  25.5 10.4 %collective-permute-start.7 = (bf16[136,512]{1,0:T(8,128)(2,1)S(1)}, bf16[136,512]{1,0:T(8,128)(2,1)S(1)}, u32[]{:S(2)}, u32[]{:S(2)}) collective-permute-start(bf16[136,512]{1,0:T(8,128)(2,1)S(1)} %get-tuple-element.32.refs_6_.refs_1_.refs_5_), channel_id=1, source_target_pairs={{0,4},{2,6},{4,0},{6,2},{8,12},{10,14},{12,8},{14,10},{1,5},{3,7},... | collective-permute-start | bytes 417800 | tf_op jit(solution)/shard_map/ppermute | solution.py:39
  25.7 10.2 %collective-permute-start.8 = (bf16[128,512]{1,0:T(8,128)(2,1)S(1)}, bf16[128,512]{1,0:T(8,128)(2,1)S(1)}, u32[]{:S(2)}, u32[]{:S(2)}) collective-permute-start(bf16[128,512]{1,0:T(8,128)(2,1)S(1)} %get-tuple-element.30.refs_4_), channel_id=1, source_target_pairs={{0,2},{2,0},{4,6},{6,4},{8,10},{10,8},{12,14},{14,12},{1,3},{3,1},... | collective-permute-start | bytes 393224 | tf_op jit(solution)/shard_map/ppermute | solution.py:39
  29.1 10.2 %collective-permute-start.5 = (bf16[128,512]{1,0:T(8,128)(2,1)S(1)}, bf16[128,512]{1,0:T(8,128)(2,1)S(1)}, u32[]{:S(2)}, u32[]{:S(2)}) collective-permute-start(bf16[128,512]{1,0:T(8,128)(2,1)S(1)} %get-tuple-element.33.refs_5_), channel_id=1, source_target_pairs={{0,2},{2,0},{4,6},{6,4},{8,10},{10,8},{12,14},{14,12},{1,3},{3,1},... | collective-permute-start | bytes 393224 | tf_op jit(solution)/shard_map/ppermute | solution.py:39
  31.2 8.7 %collective-permute-start.6 = (bf16[128,512]{1,0:T(8,128)(2,1)S(1)}, bf16[128,512]{1,0:T(8,128)(2,1)S(1)}, u32[]{:S(2)}, u32[]{:S(2)}) collective-permute-start(bf16[128,512]{1,0:T(8,128)(2,1)S(1)} %get-tuple-element.34.refs_6_), channel_id=1, source_target_pairs={{0,2},{2,0},{4,6},{6,4},{8,10},{10,8},{12,14},{14,12},{1,3},{3,1},... | collective-permute-start | bytes 393224 | tf_op jit(solution)/shard_map/ppermute | solution.py:39
  33.9 8.2 %collective-permute-start.3 = (bf16[128,512]{1,0:T(8,128)(2,1)S(1)}, bf16[128,512]{1,0:T(8,128)(2,1)S(1)}, u32[]{:S(2)}, u32[]{:S(2)}) collective-permute-start(bf16[128,512]{1,0:T(8,128)(2,1)S(1)} %get-tuple-element.36.refs_5_), channel_id=1, source_target_pairs={{0,2},{2,0},{4,6},{6,4},{8,10},{10,8},{12,14},{14,12},{1,3},{3,1},... | collective-permute-start | bytes 393224 | tf_op jit(solution)/shard_map/ppermute | solution.py:39
  36.4 14.1 %collective-permute-start.14 = (bf16[136,512]{1,0:T(8,128)(2,1)S(1)}, bf16[136,512]{1,0:T(8,128)(2,1)S(1)}, u32[]{:S(2)}, u32[]{:S(2)}) collective-permute-start(bf16[136,512]{1,0:T(8,128)(2,1)S(1)} %merge_far.3.refs_6_.refs_3_), channel_id=1, source_target_pairs={{0,8},{2,10},{4,12},{6,14},{8,0},{10,2},{12,4},{14,6},{1,9},{3,11}... | collective-permute-start | bytes 417800 | tf_op jit(solution)/shard_map/ppermute | solution.py:39
  38.9 11.6 %collective-permute-start.13 = (bf16[136,512]{1,0:T(8,128)(2,1)S(1)}, bf16[136,512]{1,0:T(8,128)(2,1)S(1)}, u32[]{:S(2)}, u32[]{:S(2)}) collective-permute-start(bf16[136,512]{1,0:T(8,128)(2,1)S(1)} %merge_far.2.refs_5_.refs_2_), channel_id=1, source_target_pairs={{0,8},{2,10},{4,12},{6,14},{8,0},{10,2},{12,4},{14,6},{1,9},{3,11}... | collective-permute-start | bytes 417800 | tf_op jit(solution)/shard_map/ppermute | solution.py:39
  39.4 8.6 %collective-permute-start.4 = (bf16[128,512]{1,0:T(8,128)(2,1)S(1)}, bf16[128,512]{1,0:T(8,128)(2,1)S(1)}, u32[]{:S(2)}, u32[]{:S(2)}) collective-permute-start(bf16[128,512]{1,0:T(8,128)(2,1)S(1)} %get-tuple-element.37), channel_id=1, source_target_pairs={{0,2},{2,0},{4,6},{6,4},{8,10},{10,8},{12,14},{14,12},{1,3},{3,1},... | collective-permute-start | bytes 393224 | tf_op jit(solution)/shard_map/ppermute | solution.py:39
  40.4 7.5 %collective-permute-start.11 = (bf16[128,512]{1,0:T(8,128)(2,1)S(1)}, bf16[128,512]{1,0:T(8,128)(2,1)S(1)}, u32[]{:S(2)}, u32[]{:S(2)}) collective-permute-start(bf16[128,512]{1,0:T(8,128)(2,1)S(1)} %get-tuple-element.40.refs_3_), channel_id=1, source_target_pairs={{0,4},{2,6},{4,0},{6,2},{8,12},{10,14},{12,8},{14,10},{1,5},{3,7},... | collective-permute-start | bytes 393224 | tf_op jit(solution)/shard_map/ppermute | solution.py:39
  42.0 7.8 %collective-permute-start.12 = (bf16[128,512]{1,0:T(8,128)(2,1)S(1)}, bf16[128,512]{1,0:T(8,128)(2,1)S(1)}, u32[]{:S(2)}, u32[]{:S(2)}) collective-permute-start(bf16[128,512]{1,0:T(8,128)(2,1)S(1)} %get-tuple-element.41.refs_4_), channel_id=1, source_target_pairs={{0,4},{2,6},{4,0},{6,2},{8,12},{10,14},{12,8},{14,10},{1,5},{3,7},... | collective-permute-start | bytes 393224 | tf_op jit(solution)/shard_map/ppermute | solution.py:39

commit v7 on v6

--- a/solution.py
+++ b/solution.py
@@ -224,8 +224,8 @@
         send[:chunk, here] = coded(product[chunk:], bound[:, here], refs)
 
 
-def shifted_scratch(rows):
-    return [pltpu.VMEM((GROUP * REF, rows + LANES), jnp.bfloat16)]
+def shifted_scratch(rows, groups=1):
+    return [pltpu.VMEM((groups * GROUP * REF, rows + LANES), jnp.bfloat16)]
 
 
 def first_products(held, power, own, other, tail, chunk, after):
@@ -249,25 +249,27 @@
     )
 
 
-def later_products(bits, held, own, other, tail, powers, chunk, after=()):
+def later_products(groups, held, own, other, tail, powers, chunk, after=()):
     rows, width = held.shape
 
-    def kernel(held, own, other, tail, powers, keep, first, second, shifted):
+    def kernel(held, own, other, tail, powers, *rest):
+        outs, shifted = rest[:-1], rest[-1]
         _, ref_powers, bound = sent_powers(powers)
         refs = ref_column(ref_powers)
-        lag_rows(own, other, own_group(bits), shifted)
+        for index, bits in enumerate(groups):
+            lag_rows(own, other, own_group(bits), shifted.at[pl.ds(index * 2 * chunk, 2 * chunk)])
         edge = edge_of(tail)
         for here in columns(width):
             product = product_of(shifted, held, edge, here)
-            keep[:, here] = product[:chunk]
-            part, start = divmod(here.start, width // 2)
-            send = (first, second)[part]
-            send[:, start : start + STEP] = coded(product[chunk:], bound[:, here], refs)
-
-    half = ((chunk, width // 2), jnp.bfloat16)
-    keep, *sends = call_on_blocks(
+            for index in range(len(groups)):
+                keep, send = outs[2 * index : 2 * index + 2]
+                first = 2 * index * chunk
+                keep[:, here] = product[first : first + chunk]
+                send[:, here] = coded(product[first + chunk : first + 2 * chunk], bound[:, here], refs)
+
+    return call_on_blocks(
         kernel,
-        [((chunk, width), jnp.float32), half, half],
+        [((chunk, width), jnp.float32), ((chunk, width), jnp.bfloat16)] * len(groups),
         held,
         own,
         other,
@@ -276,9 +278,8 @@
         name="later_products",
         micros=PRODUCT_MICROS,
         after=after,
-        scratch=shifted_scratch(rows),
-    )
-    return keep, sends
+        scratch=shifted_scratch(rows, len(groups)),
+    )
 
 
 def call_on_blocks(kernel, outs, *arrays, name, micros, after=(), scratch=(), space=pltpu.VMEM):
@@ -309,11 +310,12 @@
     return powers[:, here], refs, bound[:, here]
 
 
-def merge_near(keep, ours, theirs, after):
+def merge_near(keep, ours, theirs, held_back, after):
     chunk, width = keep.shape
 
-    def kernel(keep, ours, theirs, *outs):
-        for part, out in enumerate(outs):
+    def kernel(keep, ours, theirs, held_back, *outs):
+        outs[2][...] = held_back[...]
+        for part, out in enumerate(outs[:2]):
             here = half_of(width, part)
             powers, refs, bound = sent_powers(ours, here)
             their_powers, their_refs, their_bound = sent_powers(theirs, here)
@@ -322,60 +324,60 @@
             out[chunk:] = packed(sums, sum_refs, sum_bound)
             out[:chunk] = coded(total, sum_bound, ref_column(sum_refs))
 
-    outs = [((chunk + EXTRA, width // 2), jnp.bfloat16)] * 2
+    outs = [((chunk + EXTRA, width // 2), jnp.bfloat16)] * 2 + [(held_back.shape, jnp.bfloat16)]
     return call_on_blocks(
-        kernel, outs, keep, ours, theirs, name="merge_near", micros=MERGE_MICROS, after=after
-    )
-
-
-def merge_far(part, keep, ours, theirs, direct, direct_powers, after):
+        kernel, outs, keep, ours, theirs, held_back, name="merge_near", micros=MERGE_MICROS, after=after
+    )
+
+
+def merge_far(part, keep, ours, theirs, direct, direct_powers, *held_back, after):
     chunk, width = keep.shape
     here = half_of(width, part)
 
-    def kernel(keep, ours, theirs, direct, direct_powers, out):
+    def kernel(keep, ours, theirs, direct, direct_powers, *rest):
+        out = rest[len(held_back)]
+        if held_back:
+            rest[2][...] = rest[0][...]
         powers, refs, bound = sent_powers(ours)
         their_powers, their_refs, their_bound = sent_powers(theirs)
         total = keep[:, here] + expanded(theirs[:chunk], their_bound, ref_column(their_refs))
         _, direct_refs, direct_bound = sent_powers(direct_powers, here)
-        total += expanded(direct, direct_bound, ref_column(direct_refs))
+        total += expanded(direct[:, here], direct_bound, ref_column(direct_refs))
         sums, sum_refs, sum_bound = powers + their_powers, refs + their_refs, rounded_up(bound + their_bound)
         out[chunk:] = packed(sums, sum_refs, sum_bound)
         out[:chunk] = coded(total, sum_bound, ref_column(sum_refs))
 
-    outs = [((chunk + EXTRA, width // 2), jnp.bfloat16)]
-    return call_on_blocks(
-        kernel, outs, keep, ours, theirs, direct, direct_powers, name="merge_far", micros=MERGE_MICROS, after=after
-    )[0]
+    outs = [((chunk + EXTRA, width // 2), jnp.bfloat16)] + [(array.shape, jnp.bfloat16) for array in held_back]
+    arrays = (keep, ours, theirs, direct, direct_powers, *held_back)
+    return call_on_blocks(kernel, outs, *arrays, name="merge_far", micros=MERGE_MICROS, after=after)
 
 
 def resent(keep, direct, direct_powers, ours, after):
     chunk, width = keep.shape
 
-    def kernel(keep, direct_powers, *refs):
-        direct, ours, outs = refs[:2], refs[2:4], refs[4:]
-        for part in range(2):
+    def kernel(keep, direct, direct_powers, first, second, *outs):
+        for part, powers in enumerate((first, second)):
             here = half_of(width, part)
             _, direct_refs, direct_bound = sent_powers(direct_powers, here)
-            _, refs, bound = sent_powers(ours[part])
-            total = keep[:, here] + expanded(direct[part], direct_bound, ref_column(direct_refs))
+            _, refs, bound = sent_powers(powers)
+            total = keep[:, here] + expanded(direct[:, here], direct_bound, ref_column(direct_refs))
             outs[part][...] = coded(total, bound, ref_column(refs))
 
     outs = [((chunk, width // 2), jnp.bfloat16)] * 2
-    return call_on_blocks(
-        kernel, outs, keep, direct_powers, *direct, *ours, name="resent", micros=MERGE_MICROS, after=after
-    )
+    arrays = (keep, direct, direct_powers, *ours)
+    return call_on_blocks(kernel, outs, *arrays, name="resent", micros=MERGE_MICROS, after=after)
 
 
 def added(keep, direct, direct_powers, near, near_powers, held, tail, size, after):
     rows, width = held.shape
 
-    def kernel(keep, direct_powers, held, tail, *refs):
-        direct, near, near_powers, (out, edge) = refs[:2], refs[2:4], refs[4:6], refs[6:]
+    def kernel(keep, direct, direct_powers, held, tail, *refs):
+        near, near_powers, (out, edge) = refs[:2], refs[2:4], refs[4:]
         for part in range(2):
             here = half_of(width, part)
             _, direct_refs, direct_bound = sent_powers(direct_powers, here)
             _, near_refs, near_bound = sent_powers(near_powers[part])
-            total = keep[:, here] + expanded(direct[part], direct_bound, ref_column(direct_refs))
+            total = keep[:, here] + expanded(direct[:, here], direct_bound, ref_column(direct_refs))
             out[:, here] = total + expanded(near[part], near_bound, ref_column(near_refs))
         last = held[rows - LAGS :, :size].astype(jnp.float32)
         beyond = tail[:, :size].astype(jnp.float32)
@@ -387,7 +389,7 @@
         edge[...] = jnp.concatenate(sums, axis=0)
 
     outs = [(keep.shape, jnp.float32), ((LAGS, size), jnp.float32)]
-    arrays = (keep, direct_powers, held, tail, *direct, *near, *near_powers)
+    arrays = (keep, direct, direct_powers, held, tail, *near, *near_powers)
     return call_on_blocks(kernel, outs, *arrays, name="added", micros=MERGE_MICROS, after=after)
 
 
@@ -399,7 +401,6 @@
         first_lag = lax.axis_index("tm").astype(jnp.int32) * (chunk // REF)
         lag = lax.broadcasted_iota(jnp.int32, (chunk, 1), 0) // REF + first_lag
         denom = (slab_rows - lag).astype(jnp.float32)
-        size = width // len(autos)
         for part in range(2):
             here = half_of(width, part)
             powers, own_refs, _ = sent_powers(ours[part])
@@ -408,12 +409,14 @@
             scale = 1.0 / jnp.sqrt((powers + their_powers) / slab_rows + 1e-06)
             ref_scale = 1.0 / jnp.sqrt(ref_column(own_refs + their_refs) / slab_rows + 1e-06)
             covariance[:, here] = total * scale * (for_chunk(ref_scale, chunk) / denom)
-            for index in range(len(autos)):
-                first = index * size - here.start
-                if 0 <= first < width // 2:
-                    auto = autos[index][...] + edge[...] if index == 0 else autos[index][...]
-                    own_scale = scale[:, first : first + size]
-                    segment_auto[:, index * size : (index + 1) * size] = auto * (own_scale * own_scale) / segment
+            first = 0
+            for auto in autos:
+                size = auto.shape[1]
+                if here.start <= first < here.stop:
+                    own_scale = scale[:, first - here.start : first - here.start + size]
+                    sums = auto[...] + edge[...] if first == 0 else auto[...]
+                    segment_auto[:, first : first + size] = sums * (own_scale * own_scale) / segment
+                first += size
 
     outs = [(partial.shape, jnp.float32), ((LAGS, width), jnp.float32)]
     return call_on_blocks(
@@ -521,25 +524,22 @@
         autos = [segment_rows(held, power, None, 0, size)]
         keep6, send7 = first_products(held, power, *refs, chunk, after=(autos[0],))
         got7 = exchanged(send7, "tm", 1)
-        keep4, sends5 = later_products(2, held, *refs, send7, chunk)
-        gots5 = [exchanged(code, "tm", 1) for code in sends5]
-        autos.append(segment_rows(held, power, tail, size, size, after=tuple(sends5)))
-        sends6 = merge_near(keep6, send7, got7, after=(autos[1],))
+        keep4, send5, keep2, send3 = later_products((2, 1), held, *refs, send7, chunk)
+        got5 = exchanged(send5, "tm", 1)
+        keep0, send1 = later_products((0,), held, *refs, send7, chunk, after=(send5,))
+        *sends6, send3 = merge_near(keep6, send7, got7, send3, after=(send1,))
         gots6 = [exchanged(code, "tm", 2) for code in sends6]
-        keep2, sends3 = later_products(1, held, *refs, send7, chunk, after=tuple(sends6))
-        gots3 = [exchanged(code, "tm", 1) for code in sends3]
-        keep0, sends1 = later_products(0, held, *refs, send7, chunk, after=tuple(sends3))
-        gots1 = [exchanged(code, "tm", 1) for code in sends1]
-        sends4, gots4 = [], []
-        for part in range(2):
-            after = (sends4[0] if part else sends1[0],)
-            sends4.append(merge_far(part, keep4, sends6[part], gots6[part], gots5[part], got7, after))
-            gots4.append(exchanged(sends4[part], "tm", 4))
-        sends2 = resent(keep2, gots3, got7, sends6, after=(sends4[1],))
+        got3 = exchanged(send3, "tm", 1)
+        autos.append(segment_rows(held, power, tail, size, size, after=(send3,)))
+        far = [merge_far(0, keep4, sends6[0], gots6[0], got5, got7, after=(autos[1],))]
+        far += [merge_far(1, keep4, sends6[1], gots6[1], got5, got7, send1, after=(far[0][0],))]
+        sends4 = [far[0][0], far[1][0]]
+        gots4 = [exchanged(code, "tm", 4) for code in sends4]
+        got1 = exchanged(far[1][1], "tm", 1)
+        sends2 = resent(keep2, got3, got7, sends6, after=(sends4[1],))
         gots2 = [exchanged(code, "tm", 2) for code in sends2]
-        for index in (2, 3):
-            autos.append(segment_rows(held, power, tail, size * index, size, after=tuple(sends2)))
-        partial, edge = added(keep0, gots1, got7, gots2, gots6, held, tail, size, after=tuple(autos[2:]))
+        autos.append(segment_rows(held, power, tail, 2 * size, 2 * size, after=tuple(sends2)))
+        partial, edge = added(keep0, got1, got7, gots2, gots6, held, tail, size, after=(autos[2],))
         return tuple(finished(slab_rows, rows, partial, edge, sends4, gots4, autos))
 
     chan = lax.axis_index("chan").astype(jnp.int32)

time: 51.9 us -> 49 us (0.944)
  starting transfers between devices: 18.4 us -> 15.1 us
  waiting for transfers between devices: 5.98 us -> 6.74 us
    ppermute x14 -> x11, starting transfers between devices: 17.1 us -> 13.8 us  [exchanged(): lax.ppermute(value, axis, [(source, source ^ bit) for source in range(cou...]
    ppermute x14 -> x11, waiting for transfers between devices: 5.76 us -> 6.52 us  [exchanged(): lax.ppermute(value, axis, [(source, source ^ bit) for source in range(cou...]
    pallas_call x14 -> x12, Pallas kernels: 23 us -> 22.7 us  [call_on_blocks(): pl.pallas_call(body, in_specs=[vmem] * count + [pl.BlockSpec(memory_space...]
  transfers between devices with their start and end apart: 15 -> 12, of which waited for: 5 -> 5; matrix products, arithmetic and copies ran while one was open for 0% -> 0% of each run, Pallas kernels for 41% -> 44%
where the time goes in v7:
time: 49 us; the launch traced here: 48.8 us
  Pallas kernels  26.2 us (53%)
  starting transfers between devices  15.1 us (31%)
  waiting for transfers between devices  6.74 us (14%)
  between operations  0.77 us (2%)
    pallas_call x12, Pallas kernels, call_on_blocks(): pl.pallas_call(body, in_specs=[vmem] * count + [pl.BlockSpec(memory_space...  22.7 us
    ppermute x11, starting transfers between devices, exchanged(): lax.ppermute(value, axis, [(source, source ^ bit) for source in range(cou...  13.8 us
    ppermute x11, waiting for transfers between devices, exchanged(): lax.ppermute(value, axis, [(source, source ^ bit) for source in range(cou...  6.52 us
    pallas_call x1, Pallas kernels, loaded(): pl.pallas_call(kernel, in_specs=[pl.BlockSpec(memory_space=pl.ANY)] * 2,...  2.26 us
    ppermute x1, starting transfers between devices, passed_along(): lax.ppermute(value, axis, [(source, source + steps) for source in range(i...  1.28 us
    pallas_call x1, Pallas kernels, prepared(): pl.pallas_call(prepare_kernel, in_specs=[pl.BlockSpec(memory_space=pl.ANY...  1.28 us
  transfers between devices with their start and end apart: 12, of which 5 were waited for; matrix products, arithmetic and copies ran while one was open for 0% of the time, Pallas kernels for 44%

profile of v7, /device:TPU:0, one launch (start us, length us, event | category | flops | bytes accessed | tf_op | source)
XLA Modules:
  0.0 48.8 jit_solution(12663181201276807927)
XLA Ops:
  0.6 1.3 %prepared.1 = (bf16[32,2048]{1,0:T(8,128)(2,1)S(1)}, bf16[16,1024]{1,0:T(8,128)(2,1)S(1)}) custom-call(bf16[2048,1024]{1,0:T(8,128)(2,1)} %strain.3), custom_call_target="tpu_custom_call" | custom-call | bytes 3690000 | tf_op jit(solution)/shard_map/prepared/pallas_call | solution.py:127
  1.9 0.5 %collective-permute-start = (bf16[32,2048]{1,0:T(8,128)(2,1)S(1)}, bf16[32,2048]{1,0:T(8,128)(2,1)S(1)}, u32[]{:S(2)}, u32[]{:S(2)}) collective-permute-start(bf16[32,2048]{1,0:T(8,128)(2,1)S(1)} %get-tuple-element.23.after.refs_2_.refs_1_), channel_id=1, source_target_pairs={{0,1},{1,0},{2,3},{3,2},{4,5},{5,4},{6,7},{7,6},{8,9},{9,8},{10,11... | collective-permute-start | bytes 393224 | tf_op jit(solution)/shard_map/ppermute | solution.py:39
  2.4 1.3 %collective-permute-start.1 = (bf16[16,1024]{1,0:T(8,128)(2,1)S(1)}, bf16[16,1024]{1,0:T(8,128)(2,1)S(1)}, u32[]{:S(2)}, u32[]{:S(2)}) collective-permute-start(bf16[16,1024]{1,0:T(8,128)(2,1)S(1)} %get-tuple-element.25), channel_id=1, source_target_pairs={{2,0},{4,2},{6,4},{8,6},{10,8},{12,10},{14,12},{3,1},{5,3},{7,5},{... | collective-permute-start | bytes 98312 | tf_op jit(solution)/shard_map/ppermute | solution.py:34
  3.7 2.3 %loaded.1 = (bf16[2048,1024]{1,0:T(8,128)(2,1)S(1)}, f32[1,1024]{1,0:T(1,128)S(1)}) custom-call(bf16[2048,1024]{1,0:T(8,128)(2,1)} %strain.3, bf16[32,2048]{1,0:T(8,128)(2,1)S(1)} %get-tuple-element.23.after.refs_2_.refs_1_), custom_call_target="tpu_custom_call" | custom-call | bytes 3690000 | tf_op jit(solution)/shard_map/loaded/pallas_call | solution.py:179
  6.0 2.7 %segment_rows.3.refs_5_.refs_6_ = f32[16,256]{1,0:T(8,128)S(1)} custom-call(bf16[2048,1024]{1,0:T(8,128)(2,1)S(1)} %get-tuple-element.24.refs_0_.refs_3_, f32[1,1024]{1,0:T(1,128)S(1)} %get-tuple-element.26.refs_1_), custom_call_target="tpu_custom_call" | custom-call | bytes 4428000 | tf_op jit(solution)/shard_map/segment_rows/pallas_call | solution.py:292
  8.7 0.2 collective-permute-done.1.refs_4_.refs_3_.refs_2_
  8.9 0.0 collective-permute-done.refs_3_.refs_2_
  8.9 2.2 %first_products.1 = (f32[128,1024]{1,0:T(8,128)S(1)}, bf16[136,1024]{1,0:T(8,128)(2,1)S(1)}) custom-call(bf16[2048,1024]{1,0:T(8,128)(2,1)S(1)} %get-tuple-element.24.refs_0_.refs_3_, f32[1,1024]{1,0:T(1,128)S(1)} %get-tuple-element.26.refs_1_, bf16[32,2048]{1,0:T(8,128)(2,1)S(1)} %get-tuple-element.23.after.refs_2_.refs_1_, ...), custom_call_target="tpu_custom_call" | custom-call | bytes 3690000 | tf_op jit(solution)/shard_map/first_products/pallas_call | solution.py:292
  11.0 3.0 %collective-permute-start.2 = (bf16[136,1024]{1,0:T(8,128)(2,1)S(1)}, bf16[136,1024]{1,0:T(8,128)(2,1)S(1)}, u32[]{:S(2)}, u32[]{:S(2)}) collective-permute-start(bf16[136,1024]{1,0:T(8,128)(2,1)S(1)} %get-tuple-element.27.refs_4_.refs_1_), channel_id=1, source_target_pairs={{0,2},{2,0},{4,6},{6,4},{8,10},{10,8},{12,14},{14,12},{1,3},{3,1},... | collective-permute-start | bytes 835592 | tf_op jit(solution)/shard_map/ppermute | solution.py:39
  14.1 4.0 %later_products.2 = (f32[128,1024]{1,0:T(8,128)S(1)}, bf16[128,1024]{1,0:T(8,128)(2,1)S(1)}, f32[128,1024]{1,0:T(8,128)S(1)}, bf16[128,1024]{1,0:T(8,128)(2,1)S(1)}) custom-call(bf16[2048,1024]{1,0:T(8,128)(2,1)S(1)} %get-tuple-element.24.refs_0_.refs_3_, bf16[32,2048]{1,0:T(8,128)(2,1)S(1)} %get-tuple-element.23.after.refs_2_.refs_1_, ...), custom_call_target="tpu_custom_call" | custom-call | bytes 3690000 | tf_op jit(solution)/shard_map/later_products/pallas_call | solution.py:292
  18.0 0.1 collective-permute-start.4
  18.1 2.1 %later_products.3 = (f32[128,1024]{1,0:T(8,128)S(1)}, bf16[128,1024]{1,0:T(8,128)(2,1)S(1)}) custom-call(bf16[2048,1024]{1,0:T(8,128)(2,1)S(1)} %get-tuple-element.24.refs_0_.refs_3_, bf16[32,2048]{1,0:T(8,128)(2,1)S(1)} %get-tuple-element.23.after.refs_2_.refs_1_, bf16[32,2048]{1,0:T(8,128)(2,1)S(1)} %collective-permute-done.refs_3_.refs_2_, ...), custom_call_target="tpu_custom_call" | custom-call | bytes 3690000 | tf_op jit(solution)/shard_map/later_products/pallas_call | solution.py:292
  20.3 1.3 %collective-permute-done.2.refs_2_.refs_4_ = bf16[136,1024]{1,0:T(8,128)(2,1)S(1)} collective-permute-done((bf16[136,1024]{1,0:T(8,128)(2,1)S(1)}, bf16[136,1024]{1,0:T(8,128)(2,1)S(1)}, u32[]{:S(2)}, u32[]{:S(2)}) %collective-permute-start.2) | collective-permute-done | bytes 278560 | tf_op jit(solution)/shard_map/ppermute | solution.py:39
  21.6 0.5 %merge_near.1 = (bf16[136,512]{1,0:T(8,128)(2,1)S(1)}, bf16[136,512]{1,0:T(8,128)(2,1)S(1)}, bf16[128,1024]{1,0:T(8,128)(2,1)S(1)}) custom-call(f32[128,1024]{1,0:T(8,128)S(1)} %get-tuple-element.31.refs_0_, bf16[136,1024]{1,0:T(8,128)(2,1)S(1)} %get-tuple-element.27.refs_4_.refs_1_, bf16[136,1024]{1,0:T(8,128)(2,1)S(1)} %collective-permute-done.2.refs_2_.refs_4_, ...), custom_call_target="tpu_custom_call" | custom-call | bytes 1107000 | tf_op jit(solution)/shard_map/merge_near/pallas_call | solution.py:292
  22.1 3.5 %collective-permute-start.5 = (bf16[136,512]{1,0:T(8,128)(2,1)S(1)}, bf16[136,512]{1,0:T(8,128)(2,1)S(1)}, u32[]{:S(2)}, u32[]{:S(2)}) collective-permute-start(bf16[136,512]{1,0:T(8,128)(2,1)S(1)} %get-tuple-element.35.refs_1_.refs_3_), channel_id=1, source_target_pairs={{0,4},{2,6},{4,0},{6,2},{8,12},{10,14},{12,8},{14,10},{1,5},{3,7},... | collective-permute-start | bytes 417800 | tf_op jit(solution)/shard_map/ppermute | solution.py:39
  25.6 0.1 collective-permute-start.3
  25.7 0.7 %collective-permute-start.7 = (bf16[128,1024]{1,0:T(8,128)(2,1)S(1)}, bf16[128,1024]{1,0:T(8,128)(2,1)S(1)}, u32[]{:S(2)}, u32[]{:S(2)}) collective-permute-start(bf16[128,1024]{1,0:T(8,128)(2,1)S(1)} %get-tuple-element.36.refs_3_), channel_id=1, source_target_pairs={{0,2},{2,0},{4,6},{6,4},{8,10},{10,8},{12,14},{14,12},{1,3},{3,1},... | collective-permute-start | bytes 786440 | tf_op jit(solution)/shard_map/ppermute | solution.py:39
  26.3 2.7 %segment_rows.4.refs_5_.refs_7_ = f32[16,256]{1,0:T(8,128)S(1)} custom-call(bf16[2048,1024]{1,0:T(8,128)(2,1)S(1)} %get-tuple-element.24.refs_0_.refs_3_, f32[1,1024]{1,0:T(1,128)S(1)} %get-tuple-element.26.refs_1_, bf16[16,1024]{1,0:T(8,128)(2,1)S(1)} %collective-permute-done.1.refs_4_.refs_3_.refs_2_, bf16[128,1024]{1,0:T(8,128)(2,1)S(1)} %get-tuple-element.36.refs_3_), custom_call_target="tpu_custom_call" | custom-call | bytes 4428000 | tf_op jit(solution)/shard_map/segment_rows/pallas_call | solution.py:292
  29.0 0.0 collective-permute-done.4.refs_3_
  29.0 0.6 %collective-permute-done.5.refs_2_.refs_7_ = bf16[136,512]{1,0:T(8,128)(2,1)S(1)} collective-permute-done((bf16[136,512]{1,0:T(8,128)(2,1)S(1)}, bf16[136,512]{1,0:T(8,128)(2,1)S(1)}, u32[]{:S(2)}, u32[]{:S(2)}) %collective-permute-start.5) | collective-permute-done | bytes 139296 | tf_op jit(solution)/shard_map/ppermute | solution.py:39
  29.6 0.4 merge_far.2.refs_6_.refs_2_
  30.0 1.0 %collective-permute-done.3.refs_2_.refs_8_ = bf16[136,512]{1,0:T(8,128)(2,1)S(1)} collective-permute-done((bf16[136,512]{1,0:T(8,128)(2,1)S(1)}, bf16[136,512]{1,0:T(8,128)(2,1)S(1)}, u32[]{:S(2)}, u32[]{:S(2)}) %collective-permute-start.3) | collective-permute-done | bytes 139296 | tf_op jit(solution)/shard_map/ppermute | solution.py:39
  31.1 0.4 merge_far.3
  31.5 0.9 %collective-permute-start.6 = (bf16[128,1024]{1,0:T(8,128)(2,1)S(1)}, bf16[128,1024]{1,0:T(8,128)(2,1)S(1)}, u32[]{:S(2)}, u32[]{:S(2)}) collective-permute-start(bf16[128,1024]{1,0:T(8,128)(2,1)S(1)} %get-tuple-element.37), channel_id=1, source_target_pairs={{0,2},{2,0},{4,6},{6,4},{8,10},{10,8},{12,14},{14,12},{1,3},{3,1},... | collective-permute-start | bytes 786440 | tf_op jit(solution)/shard_map/ppermute | solution.py:39
  32.5 2.5 %collective-permute-start.11 = (bf16[136,512]{1,0:T(8,128)(2,1)S(1)}, bf16[136,512]{1,0:T(8,128)(2,1)S(1)}, u32[]{:S(2)}, u32[]{:S(2)}) collective-permute-start(bf16[136,512]{1,0:T(8,128)(2,1)S(1)} %get-tuple-element.39.refs_5_.refs_3_), channel_id=1, source_target_pairs={{0,8},{2,10},{4,12},{6,14},{8,0},{10,2},{12,4},{14,6},{1,9},{3,11}... | collective-permute-start | bytes 417800 | tf_op jit(solution)/shard_map/ppermute | solution.py:39
  35.0 0.4 collective-permute-start.10
  35.4 0.0 collective-permute-done.7.refs_1_
  35.4 0.5 %resent.1 = (bf16[128,512]{1,0:T(8,128)(2,1)S(1)}, bf16[128,512]{1,0:T(8,128)(2,1)S(1)}) custom-call(f32[128,1024]{1,0:T(8,128)S(1)} %get-tuple-element.38.refs_0_, bf16[128,1024]{1,0:T(8,128)(2,1)S(1)} %collective-permute-done.7.refs_1_, bf16[136,1024]{1,0:T(8,128)(2,1)S(1)} %collective-permute-done.2.refs_2_.refs_4_, ...), custom_call_target="tpu_custom_call" | custom-call | bytes 1107000 | tf_op jit(solution)/shard_map/resent/pallas_call | solution.py:292
  35.9 1.6 %collective-permute-start.8 = (bf16[128,512]{1,0:T(8,128)(2,1)S(1)}, bf16[128,512]{1,0:T(8,128)(2,1)S(1)}, u32[]{:S(2)}, u32[]{:S(2)}) collective-permute-start(bf16[128,512]{1,0:T(8,128)(2,1)S(1)} %get-tuple-element.40.refs_3_), channel_id=1, source_target_pairs={{0,4},{2,6},{4,0},{6,2},{8,12},{10,14},{12,8},{14,10},{1,5},{3,7},... | collective-permute-start | bytes 393224 | tf_op jit(solution)/shard_map/ppermute | solution.py:39
  37.5 0.5 %collective-permute-start.9 = (bf16[128,512]{1,0:T(8,128)(2,1)S(1)}, bf16[128,512]{1,0:T(8,128)(2,1)S(1)}, u32[]{:S(2)}, u32[]{:S(2)}) collective-permute-start(bf16[128,512]{1,0:T(8,128)(2,1)S(1)} %get-tuple-element.41.refs_4_), channel_id=1, source_target_pairs={{0,4},{2,6},{4,0},{6,2},{8,12},{10,14},{12,8},{14,10},{1,5},{3,7},... | collective-permute-start | bytes 393224 | tf_op jit(solution)/shard_map/ppermute | solution.py:39
  38.0 5.3 %segment_rows.5.refs_9_.refs_8_ = f32[16,512]{1,0:T(8,128)S(1)} custom-call(bf16[2048,1024]{1,0:T(8,128)(2,1)S(1)} %get-tuple-element.24.refs_0_.refs_3_, f32[1,1024]{1,0:T(1,128)S(1)} %get-tuple-element.26.refs_1_, bf16[16,1024]{1,0:T(8,128)(2,1)S(1)} %collective-permute-done.1.refs_4_.refs_3_.refs_2_, bf16[128,512]{1,0:T(8,128)(2,1)S(1)} %get-tuple-element.40.refs_3_, ...), custom_call_target="tpu_custom_call" | custom-call | bytes 4428000 | tf_op jit(solution)/shard_map/segment_rows/pallas_call | solution.py:292
  43.3 0.0 collective-permute-done.8.refs_5_
  43.3 3.6 %collective-permute-done.9.refs_6_ = bf16[128,512]{1,0:T(8,128)(2,1)S(1)} collective-permute-done((bf16[128,512]{1,0:T(8,128)(2,1)S(1)}, bf16[128,512]{1,0:T(8,128)(2,1)S(1)}, u32[]{:S(2)}, u32[]{:S(2)}) %collective-permute-start.9) | collective-permute-done | bytes 131104 | tf_op jit(solution)/shard_map/ppermute | solution.py:39
  46.9 0.0 collective-permute-done.6.refs_1_
  46.9 0.6 %added.1 = (f32[128,1024]{1,0:T(8,128)S(1)}, f32[16,256]{1,0:T(8,128)S(1)}) custom-call(f32[128,1024]{1,0:T(8,128)S(1)} %get-tuple-element.29.refs_0_, bf16[128,1024]{1,0:T(8,128)(2,1)S(1)} %collective-permute-done.6.refs_1_, bf16[136,1024]{1,0:T(8,128)(2,1)S(1)} %collective-permute-done.2.refs_2_.refs_4_, ...), custom_call_target="tpu_custom_call" | custom-call | bytes 1107000 | tf_op jit(solution)/shard_map/added/pallas_call | solution.py:292
  47.6 0.0 collective-permute-done.11.refs_5_
  47.6 0.0 collective-permute-done.10.refs_4_
  47.6 1.2 %finished.1 = (f32[128,1024]{1,0:T(8,128)}, f32[16,1024]{1,0:T(8,128)}) custom-call(f32[128,1024]{1,0:T(8,128)S(1)} %get-tuple-element.42.refs_0_, f32[16,256]{1,0:T(8,128)S(1)} %get-tuple-element.43.refs_1_, bf16[136,512]{1,0:T(8,128)(2,1)S(1)} %merge_far.2.refs_6_.refs_2_, bf16[136,512]{1,0:T(8,128)(2,1)S(1)} %get-tuple-element.39.refs_5_.refs_3_, ...), custom_call_target="tpu_custom_call" | custom-call | bytes 1107000 | tf_op jit(solution)/shard_map/finished/pallas_call | solution.py:292
Async XLA Ops:
  1.9 7.0 %collective-permute-start = (bf16[32,2048]{1,0:T(8,128)(2,1)S(1)}, bf16[32,2048]{1,0:T(8,128)(2,1)S(1)}, u32[]{:S(2)}, u32[]{:S(2)}) collective-permute-start(bf16[32,2048]{1,0:T(8,128)(2,1)S(1)} %get-tuple-element.23.after.refs_2_.refs_1_), channel_id=1, source_target_pairs={{0,1},{1,0},{2,3},{3,2},{4,5},{5,4},{6,7},{7,6},{8,9},{9,8},{10,11... | collective-permute-start | bytes 393224 | tf_op jit(solution)/shard_map/ppermute | solution.py:39
  2.4 6.4 %collective-permute-start.1 = (bf16[16,1024]{1,0:T(8,128)(2,1)S(1)}, bf16[16,1024]{1,0:T(8,128)(2,1)S(1)}, u32[]{:S(2)}, u32[]{:S(2)}) collective-permute-start(bf16[16,1024]{1,0:T(8,128)(2,1)S(1)} %get-tuple-element.25), channel_id=1, source_target_pairs={{2,0},{4,2},{6,4},{8,6},{10,8},{12,10},{14,12},{3,1},{5,3},{7,5},{... | collective-permute-start | bytes 98312 | tf_op jit(solution)/shard_map/ppermute | solution.py:34
  11.0 10.5 %collective-permute-start.2 = (bf16[136,1024]{1,0:T(8,128)(2,1)S(1)}, bf16[136,1024]{1,0:T(8,128)(2,1)S(1)}, u32[]{:S(2)}, u32[]{:S(2)}) collective-permute-start(bf16[136,1024]{1,0:T(8,128)(2,1)S(1)} %get-tuple-element.27.refs_4_.refs_1_), channel_id=1, source_target_pairs={{0,2},{2,0},{4,6},{6,4},{8,10},{10,8},{12,14},{14,12},{1,3},{3,1},... | collective-permute-start | bytes 835592 | tf_op jit(solution)/shard_map/ppermute | solution.py:39
  18.0 11.0 %collective-permute-start.4 = (bf16[128,1024]{1,0:T(8,128)(2,1)S(1)}, bf16[128,1024]{1,0:T(8,128)(2,1)S(1)}, u32[]{:S(2)}, u32[]{:S(2)}) collective-permute-start(bf16[128,1024]{1,0:T(8,128)(2,1)S(1)} %get-tuple-element.28.refs_5_), channel_id=1, source_target_pairs={{0,2},{2,0},{4,6},{6,4},{8,10},{10,8},{12,14},{14,12},{1,3},{3,1},... | collective-permute-start | bytes 786440 | tf_op jit(solution)/shard_map/ppermute | solution.py:39
  22.1 7.5 %collective-permute-start.5 = (bf16[136,512]{1,0:T(8,128)(2,1)S(1)}, bf16[136,512]{1,0:T(8,128)(2,1)S(1)}, u32[]{:S(2)}, u32[]{:S(2)}) collective-permute-start(bf16[136,512]{1,0:T(8,128)(2,1)S(1)} %get-tuple-element.35.refs_1_.refs_3_), channel_id=1, source_target_pairs={{0,4},{2,6},{4,0},{6,2},{8,12},{10,14},{12,8},{14,10},{1,5},{3,7},... | collective-permute-start | bytes 417800 | tf_op jit(solution)/shard_map/ppermute | solution.py:39
  25.6 5.5 %collective-permute-start.3 = (bf16[136,512]{1,0:T(8,128)(2,1)S(1)}, bf16[136,512]{1,0:T(8,128)(2,1)S(1)}, u32[]{:S(2)}, u32[]{:S(2)}) collective-permute-start(bf16[136,512]{1,0:T(8,128)(2,1)S(1)} %get-tuple-element.34.refs_1_.refs_4_), channel_id=1, source_target_pairs={{0,4},{2,6},{4,0},{6,2},{8,12},{10,14},{12,8},{14,10},{1,5},{3,7},... | collective-permute-start | bytes 417800 | tf_op jit(solution)/shard_map/ppermute | solution.py:39
  25.7 9.7 %collective-permute-start.7 = (bf16[128,1024]{1,0:T(8,128)(2,1)S(1)}, bf16[128,1024]{1,0:T(8,128)(2,1)S(1)}, u32[]{:S(2)}, u32[]{:S(2)}) collective-permute-start(bf16[128,1024]{1,0:T(8,128)(2,1)S(1)} %get-tuple-element.36.refs_3_), channel_id=1, source_target_pairs={{0,2},{2,0},{4,6},{6,4},{8,10},{10,8},{12,14},{14,12},{1,3},{3,1},... | collective-permute-start | bytes 786440 | tf_op jit(solution)/shard_map/ppermute | solution.py:39
  31.5 15.4 %collective-permute-start.6 = (bf16[128,1024]{1,0:T(8,128)(2,1)S(1)}, bf16[128,1024]{1,0:T(8,128)(2,1)S(1)}, u32[]{:S(2)}, u32[]{:S(2)}) collective-permute-start(bf16[128,1024]{1,0:T(8,128)(2,1)S(1)} %get-tuple-element.37), channel_id=1, source_target_pairs={{0,2},{2,0},{4,6},{6,4},{8,10},{10,8},{12,14},{14,12},{1,3},{3,1},... | collective-permute-start | bytes 786440 | tf_op jit(solution)/shard_map/ppermute | solution.py:39
  32.5 15.1 %collective-permute-start.11 = (bf16[136,512]{1,0:T(8,128)(2,1)S(1)}, bf16[136,512]{1,0:T(8,128)(2,1)S(1)}, u32[]{:S(2)}, u32[]{:S(2)}) collective-permute-start(bf16[136,512]{1,0:T(8,128)(2,1)S(1)} %get-tuple-element.39.refs_5_.refs_3_), channel_id=1, source_target_pairs={{0,8},{2,10},{4,12},{6,14},{8,0},{10,2},{12,4},{14,6},{1,9},{3,11}... | collective-permute-start | bytes 417800 | tf_op jit(solution)/shard_map/ppermute | solution.py:39
  35.0 12.6 %collective-permute-start.10 = (bf16[136,512]{1,0:T(8,128)(2,1)S(1)}, bf16[136,512]{1,0:T(8,128)(2,1)S(1)}, u32[]{:S(2)}, u32[]{:S(2)}) collective-permute-start(bf16[136,512]{1,0:T(8,128)(2,1)S(1)} %merge_far.2.refs_6_.refs_2_), channel_id=1, source_target_pairs={{0,8},{2,10},{4,12},{6,14},{8,0},{10,2},{12,4},{14,6},{1,9},{3,11}... | collective-permute-start | bytes 417800 | tf_op jit(solution)/shard_map/ppermute | solution.py:39
  35.9 7.4 %collective-permute-start.8 = (bf16[128,512]{1,0:T(8,128)(2,1)S(1)}, bf16[128,512]{1,0:T(8,128)(2,1)S(1)}, u32[]{:S(2)}, u32[]{:S(2)}) collective-permute-start(bf16[128,512]{1,0:T(8,128)(2,1)S(1)} %get-tuple-element.40.refs_3_), channel_id=1, source_target_pairs={{0,4},{2,6},{4,0},{6,2},{8,12},{10,14},{12,8},{14,10},{1,5},{3,7},... | collective-permute-start | bytes 393224 | tf_op jit(solution)/shard_map/ppermute | solution.py:39
  37.5 9.4 %collective-permute-start.9 = (bf16[128,512]{1,0:T(8,128)(2,1)S(1)}, bf16[128,512]{1,0:T(8,128)(2,1)S(1)}, u32[]{:S(2)}, u32[]{:S(2)}) collective-permute-start(bf16[128,512]{1,0:T(8,128)(2,1)S(1)} %get-tuple-element.41.refs_4_), channel_id=1, source_target_pairs={{0,4},{2,6},{4,0},{6,2},{8,12},{10,14},{12,8},{14,10},{1,5},{3,7},... | collective-permute-start | bytes 393224 | tf_op jit(solution)/shard_map/ppermute | solution.py:39

commit v8 on v7

--- a/solution.py
+++ b/solution.py
@@ -136,6 +136,10 @@
     )(pltpu.with_memory_space_constraint(strain, pltpu.HBM))
 
 
+def half_of(width, part):
+    return slice(part * width // 2, (part + 1) * width // 2)
+
+
 def lag_rows(own, other, group, shifted):
     chan, near = lax.axis_index("chan"), lax.axis_index("tm") & 1
     zeros = jnp.zeros((HALF, LANES), jnp.float32)
@@ -198,11 +202,16 @@
     return total + jnp.dot(shifted[:, :rows], held[:, here], preferred_element_type=jnp.float32)
 
 
-def columns(width):
-    return [slice(first, first + STEP) for first in range(0, width, STEP)]
-
-
-def first_products_kernel(held, power, own, other, tail, keep, send, shifted):
+def half_columns(width):
+    half = width // 2
+    return [
+        (part, slice(part * half + first, part * half + first + STEP), slice(first, first + STEP))
+        for part in range(2)
+        for first in range(0, half, STEP)
+    ]
+
+
+def first_products_kernel(held, power, own, other, tail, keep, first, second, shifted):
     lag_rows(own, other, own_group(3), shifted)
     ours, theirs = [
         jnp.sum(jnp.square(refs[...].astype(jnp.float32)), axis=1, keepdims=True) for refs in (own, other)
@@ -215,13 +224,17 @@
     beyond = jnp.sum(jnp.square(tail[...].astype(jnp.float32)), axis=0, keepdims=True)
     bound = rounded_up(power[...] + beyond)
     pad = jnp.zeros((1, LANES - REF), jnp.float32)
-    chunk = keep.shape[0]
-    send[chunk:] = packed(power[...], jnp.concatenate([as_row(refs), pad], axis=1), bound)
+    refs_row = jnp.concatenate([as_row(refs), pad], axis=1)
+    chunk, width = keep.shape
+    sends = (first, second)
+    for part, send in enumerate(sends):
+        here = half_of(width, part)
+        send[chunk:] = packed(power[:, here], refs_row, bound[:, here])
     edge = edge_of(tail)
-    for here in columns(held.shape[1]):
+    for part, here, there in half_columns(width):
         product = product_of(shifted, held, edge, here)
         keep[:, here] = product[:chunk]
-        send[:chunk, here] = coded(product[chunk:], bound[:, here], refs)
+        sends[part][:chunk, there] = coded(product[chunk:], bound[:, here], refs)
 
 
 def shifted_scratch(rows, groups=1):
@@ -230,13 +243,10 @@
 
 def first_products(held, power, own, other, tail, chunk, after):
     rows, width = held.shape
-    outs = [
-        ((chunk, width), jnp.float32),
-        ((chunk + EXTRA, width), jnp.bfloat16),
-    ]
-    return call_on_blocks(
+    half = ((chunk + EXTRA, width // 2), jnp.bfloat16)
+    keep, *sends = call_on_blocks(
         first_products_kernel,
-        outs,
+        [((chunk, width), jnp.float32), half, half],
         held,
         power,
         own,
@@ -247,39 +257,43 @@
         after=after,
         scratch=shifted_scratch(rows),
     )
+    return keep, sends
 
 
 def later_products(groups, held, own, other, tail, powers, chunk, after=()):
     rows, width = held.shape
 
-    def kernel(held, own, other, tail, powers, *rest):
+    def kernel(held, own, other, tail, first, second, *rest):
         outs, shifted = rest[:-1], rest[-1]
-        _, ref_powers, bound = sent_powers(powers)
-        refs = ref_column(ref_powers)
+        sent = [sent_powers(powers) for powers in (first, second)]
+        refs = ref_column(sent[0][1])
         for index, bits in enumerate(groups):
             lag_rows(own, other, own_group(bits), shifted.at[pl.ds(index * 2 * chunk, 2 * chunk)])
         edge = edge_of(tail)
-        for here in columns(width):
+        for part, here, there in half_columns(width):
             product = product_of(shifted, held, edge, here)
             for index in range(len(groups)):
-                keep, send = outs[2 * index : 2 * index + 2]
-                first = 2 * index * chunk
-                keep[:, here] = product[first : first + chunk]
-                send[:, here] = coded(product[first + chunk : first + 2 * chunk], bound[:, here], refs)
-
-    return call_on_blocks(
+                keep, *sends = outs[3 * index : 3 * index + 3]
+                start = 2 * index * chunk
+                keep[:, here] = product[start : start + chunk]
+                others = product[start + chunk : start + 2 * chunk]
+                sends[part][:, there] = coded(others, sent[part][2][:, there], refs)
+
+    half = ((chunk, width // 2), jnp.bfloat16)
+    outs = call_on_blocks(
         kernel,
-        [((chunk, width), jnp.float32), ((chunk, width), jnp.bfloat16)] * len(groups),
+        [((chunk, width), jnp.float32), half, half] * len(groups),
         held,
         own,
         other,
         tail,
-        powers,
+        *powers,
         name="later_products",
         micros=PRODUCT_MICROS,
         after=after,
         scratch=shifted_scratch(rows, len(groups)),
     )
+    return [(outs[first], outs[first + 1 : first + 3]) for first in range(0, len(outs), 3)]
 
 
 def call_on_blocks(kernel, outs, *arrays, name, micros, after=(), scratch=(), space=pltpu.VMEM):
@@ -301,84 +315,66 @@
     )(*arrays, *after)
 
 
-def half_of(width, part):
-    return slice(part * width // 2, (part + 1) * width // 2)
-
-
-def sent_powers(code, here=slice(None)):
-    powers, refs, bound = unpacked(code[-EXTRA:])
-    return powers[:, here], refs, bound[:, here]
-
-
-def merge_near(keep, ours, theirs, held_back, after):
-    chunk, width = keep.shape
-
-    def kernel(keep, ours, theirs, held_back, *outs):
-        outs[2][...] = held_back[...]
-        for part, out in enumerate(outs[:2]):
-            here = half_of(width, part)
-            powers, refs, bound = sent_powers(ours, here)
-            their_powers, their_refs, their_bound = sent_powers(theirs, here)
-            total = keep[:, here] + expanded(theirs[:chunk, here], their_bound, ref_column(their_refs))
-            sums, sum_refs, sum_bound = powers + their_powers, refs + their_refs, rounded_up(bound + their_bound)
-            out[chunk:] = packed(sums, sum_refs, sum_bound)
-            out[:chunk] = coded(total, sum_bound, ref_column(sum_refs))
-
-    outs = [((chunk + EXTRA, width // 2), jnp.bfloat16)] * 2 + [(held_back.shape, jnp.bfloat16)]
-    return call_on_blocks(
-        kernel, outs, keep, ours, theirs, held_back, name="merge_near", micros=MERGE_MICROS, after=after
-    )
-
-
-def merge_far(part, keep, ours, theirs, direct, direct_powers, *held_back, after):
+def sent_powers(code):
+    return unpacked(code[-EXTRA:])
+
+
+def merged(part, keep, ours, theirs, *direct, after):
     chunk, width = keep.shape
     here = half_of(width, part)
 
-    def kernel(keep, ours, theirs, direct, direct_powers, *rest):
-        out = rest[len(held_back)]
-        if held_back:
-            rest[2][...] = rest[0][...]
+    def kernel(keep, ours, theirs, *rest):
+        out = rest[-1]
         powers, refs, bound = sent_powers(ours)
         their_powers, their_refs, their_bound = sent_powers(theirs)
         total = keep[:, here] + expanded(theirs[:chunk], their_bound, ref_column(their_refs))
-        _, direct_refs, direct_bound = sent_powers(direct_powers, here)
-        total += expanded(direct[:, here], direct_bound, ref_column(direct_refs))
+        if direct:
+            total += direct_sums(*rest[:2])
         sums, sum_refs, sum_bound = powers + their_powers, refs + their_refs, rounded_up(bound + their_bound)
         out[chunk:] = packed(sums, sum_refs, sum_bound)
         out[:chunk] = coded(total, sum_bound, ref_column(sum_refs))
 
-    outs = [((chunk + EXTRA, width // 2), jnp.bfloat16)] + [(array.shape, jnp.bfloat16) for array in held_back]
-    arrays = (keep, ours, theirs, direct, direct_powers, *held_back)
-    return call_on_blocks(kernel, outs, *arrays, name="merge_far", micros=MERGE_MICROS, after=after)
+    outs = [((chunk + EXTRA, width // 2), jnp.bfloat16)]
+    return call_on_blocks(
+        kernel, outs, keep, ours, theirs, *direct, name="merged", micros=MERGE_MICROS, after=after
+    )[0]
+
+
+def direct_sums(direct, powers):
+    _, refs, bound = sent_powers(powers)
+    return expanded(direct, bound, ref_column(refs))
 
 
 def resent(keep, direct, direct_powers, ours, after):
     chunk, width = keep.shape
 
-    def kernel(keep, direct, direct_powers, first, second, *outs):
-        for part, powers in enumerate((first, second)):
-            here = half_of(width, part)
-            _, direct_refs, direct_bound = sent_powers(direct_powers, here)
-            _, refs, bound = sent_powers(powers)
-            total = keep[:, here] + expanded(direct[:, here], direct_bound, ref_column(direct_refs))
+    def kernel(keep, *refs):
+        direct, direct_powers, ours, outs = refs[:2], refs[2:4], refs[4:6], refs[6:]
+        for part in range(2):
+            _, refs, bound = sent_powers(ours[part])
+            total = keep[:, half_of(width, part)] + direct_sums(direct[part], direct_powers[part])
             outs[part][...] = coded(total, bound, ref_column(refs))
 
     outs = [((chunk, width // 2), jnp.bfloat16)] * 2
-    arrays = (keep, direct, direct_powers, *ours)
+    arrays = (keep, *direct, *direct_powers, *ours)
     return call_on_blocks(kernel, outs, *arrays, name="resent", micros=MERGE_MICROS, after=after)
 
 
 def added(keep, direct, direct_powers, near, near_powers, held, tail, size, after):
     rows, width = held.shape
 
-    def kernel(keep, direct, direct_powers, held, tail, *refs):
-        near, near_powers, (out, edge) = refs[:2], refs[2:4], refs[4:]
+    def kernel(keep, held, tail, *refs):
+        direct, direct_powers, near, near_powers, (out, edge) = (
+            refs[:2],
+            refs[2:4],
+            refs[4:6],
+            refs[6:8],
+            refs[8:],
+        )
         for part in range(2):
             here = half_of(width, part)
-            _, direct_refs, direct_bound = sent_powers(direct_powers, here)
-            _, near_refs, near_bound = sent_powers(near_powers[part])
-            total = keep[:, here] + expanded(direct[:, here], direct_bound, ref_column(direct_refs))
-            out[:, here] = total + expanded(near[part], near_bound, ref_column(near_refs))
+            total = keep[:, here] + direct_sums(direct[part], direct_powers[part])
+            out[:, here] = total + direct_sums(near[part], near_powers[part])
         last = held[rows - LAGS :, :size].astype(jnp.float32)
         beyond = tail[:, :size].astype(jnp.float32)
         place = lax.broadcasted_iota(jnp.int32, last.shape, 0)
@@ -389,7 +385,7 @@
         edge[...] = jnp.concatenate(sums, axis=0)
 
     outs = [(keep.shape, jnp.float32), ((LAGS, size), jnp.float32)]
-    arrays = (keep, direct, direct_powers, held, tail, *near, *near_powers)
+    arrays = (keep, held, tail, *direct, *direct_powers, *near, *near_powers)
     return call_on_blocks(kernel, outs, *arrays, name="added", micros=MERGE_MICROS, after=after)
 
 
@@ -488,7 +484,7 @@
             lag = pl.program_id(0) * GROUP + index
             shifted[pl.ds(start, HALF), :] = pltpu.roll(long, lag, 1).astype(jnp.bfloat16)
     edge = edge_of(tail)
-    for here in columns(held.shape[1]):
+    for _, here, _ in half_columns(held.shape[1]):
         out[:, here] = product_of(shifted, held, edge, here)
 
 
@@ -521,25 +517,32 @@
 
     if chunk * 2 == GROUP * REF:
         refs = (own, other, tail)
-        autos = [segment_rows(held, power, None, 0, size)]
-        keep6, send7 = first_products(held, power, *refs, chunk, after=(autos[0],))
-        got7 = exchanged(send7, "tm", 1)
-        keep4, send5, keep2, send3 = later_products((2, 1), held, *refs, send7, chunk)
-        got5 = exchanged(send5, "tm", 1)
-        keep0, send1 = later_products((0,), held, *refs, send7, chunk, after=(send5,))
-        *sends6, send3 = merge_near(keep6, send7, got7, send3, after=(send1,))
-        gots6 = [exchanged(code, "tm", 2) for code in sends6]
-        got3 = exchanged(send3, "tm", 1)
-        autos.append(segment_rows(held, power, tail, size, size, after=(send3,)))
-        far = [merge_far(0, keep4, sends6[0], gots6[0], got5, got7, after=(autos[1],))]
-        far += [merge_far(1, keep4, sends6[1], gots6[1], got5, got7, send1, after=(far[0][0],))]
-        sends4 = [far[0][0], far[1][0]]
-        gots4 = [exchanged(code, "tm", 4) for code in sends4]
-        got1 = exchanged(far[1][1], "tm", 1)
-        sends2 = resent(keep2, got3, got7, sends6, after=(sends4[1],))
-        gots2 = [exchanged(code, "tm", 2) for code in sends2]
-        autos.append(segment_rows(held, power, tail, 2 * size, 2 * size, after=tuple(sends2)))
-        partial, edge = added(keep0, got1, got7, gots2, gots6, held, tail, size, after=(autos[2],))
+
+        def both(codes, bit):
+            return [exchanged(code, "tm", bit) for code in codes]
+
+        def piece(index, after):
+            return segment_rows(held, power, tail if index else None, size * index, size, after=tuple(after))
+
+        autos = [piece(0, ())]
+        keep6, sends7 = first_products(held, power, *refs, chunk, after=(autos[0],))
+        gots7 = both(sends7, 1)
+        ((keep4, sends5),) = later_products((2,), held, *refs, sends7, chunk)
+        gots5 = both(sends5, 1)
+        autos.append(piece(1, sends5))
+        sends6 = [merged(0, keep6, sends7[0], gots7[0], after=(autos[1],))]
+        sends6.append(merged(1, keep6, sends7[1], gots7[1], after=(sends6[0],)))
+        gots6 = both(sends6, 2)
+        (keep2, sends3), (keep0, sends1) = later_products((1, 0), held, *refs, sends7, chunk, after=tuple(sends6))
+        gots3, gots1 = both(sends3, 1), both(sends1, 1)
+        sends4 = [merged(0, keep4, sends6[0], gots6[0], gots5[0], gots7[0], after=(sends3[0],))]
+        sends4.append(merged(1, keep4, sends6[1], gots6[1], gots5[1], gots7[1], after=(sends4[0],)))
+        gots4 = both(sends4, 4)
+        autos.append(piece(2, sends4))
+        sends2 = resent(keep2, gots3, gots7, sends6, after=(autos[2],))
+        gots2 = both(sends2, 2)
+        autos.append(piece(3, sends2))
+        partial, edge = added(keep0, gots1, gots7, gots2, gots6, held, tail, size, after=(autos[3],))
         return tuple(finished(slab_rows, rows, partial, edge, sends4, gots4, autos))
 
     chan = lax.axis_index("chan").astype(jnp.int32)

time: 49 us -> 52.9 us (1.080)
  starting transfers between devices: 15.1 us -> 19.9 us
  waiting for transfers between devices: 6.74 us -> 5.61 us
    ppermute x11 -> x15, starting transfers between devices: 13.8 us -> 18.6 us  [exchanged(): lax.ppermute(value, axis, [(source, source ^ bit) for source in range(cou...]
    ppermute x11 -> x15, waiting for transfers between devices: 6.52 us -> 5.4 us  [exchanged(): lax.ppermute(value, axis, [(source, source ^ bit) for source in range(cou...]
    pallas_call x12 -> x14, Pallas kernels: 22.7 us -> 22.9 us  [call_on_blocks(): pl.pallas_call(body, in_specs=[vmem] * count + [pl.BlockSpec(memory_space...]
  transfers between devices with their start and end apart: 12 -> 16, of which waited for: 5 -> 3; matrix products, arithmetic and copies ran while one was open for 0% -> 0% of each run, Pallas kernels for 44% -> 41%
where the time goes in v8:
time: 52.9 us; the launch traced here: 52.7 us
  Pallas kernels  26.4 us (50%)
  starting transfers between devices  19.9 us (38%)
  waiting for transfers between devices  5.61 us (11%)
  between operations  0.81 us (2%)
    pallas_call x14, Pallas kernels, call_on_blocks(): pl.pallas_call(body, in_specs=[vmem] * count + [pl.BlockSpec(memory_space...  22.9 us
    ppermute x15, starting transfers between devices, exchanged(): lax.ppermute(value, axis, [(source, source ^ bit) for source in range(cou...  18.6 us
    ppermute x15, waiting for transfers between devices, exchanged(): lax.ppermute(value, axis, [(source, source ^ bit) for source in range(cou...  5.4 us
    pallas_call x1, Pallas kernels, loaded(): pl.pallas_call(kernel, in_specs=[pl.BlockSpec(memory_space=pl.ANY)] * 2,...  2.26 us
    ppermute x1, starting transfers between devices, passed_along(): lax.ppermute(value, axis, [(source, source + steps) for source in range(i...  1.28 us
    pallas_call x1, Pallas kernels, prepared(): pl.pallas_call(prepare_kernel, in_specs=[pl.BlockSpec(memory_space=pl.ANY...  1.28 us
  transfers between devices with their start and end apart: 16, of which 3 were waited for; matrix products, arithmetic and copies ran while one was open for 0% of the time, Pallas kernels for 41%

profile of v8, /device:TPU:0, one launch (start us, length us, event | category | flops | bytes accessed | tf_op | source)
XLA Modules:
  0.0 52.7 jit_solution(10154521576906326603)
XLA Ops:
  0.6 1.3 %prepared.1 = (bf16[32,2048]{1,0:T(8,128)(2,1)S(1)}, bf16[16,1024]{1,0:T(8,128)(2,1)S(1)}) custom-call(bf16[2048,1024]{1,0:T(8,128)(2,1)} %strain.3), custom_call_target="tpu_custom_call" | custom-call | bytes 3690000 | tf_op jit(solution)/shard_map/prepared/pallas_call | solution.py:127
  1.9 0.5 collective-permute-start
  2.4 1.3 %collective-permute-start.1 = (bf16[16,1024]{1,0:T(8,128)(2,1)S(1)}, bf16[16,1024]{1,0:T(8,128)(2,1)S(1)}, u32[]{:S(2)}, u32[]{:S(2)}) collective-permute-start(bf16[16,1024]{1,0:T(8,128)(2,1)S(1)} %get-tuple-element.24), channel_id=1, source_target_pairs={{2,0},{4,2},{6,4},{8,6},{10,8},{12,10},{14,12},{3,1},{5,3},{7,5},{... | collective-permute-start | bytes 98312 | tf_op jit(solution)/shard_map/ppermute | solution.py:34
  3.7 2.3 %loaded.1 = (bf16[2048,1024]{1,0:T(8,128)(2,1)S(1)}, f32[1,1024]{1,0:T(1,128)S(1)}) custom-call(bf16[2048,1024]{1,0:T(8,128)(2,1)} %strain.3, bf16[32,2048]{1,0:T(8,128)(2,1)S(1)} %get-tuple-element.22.after.refs_2_.refs_1_), custom_call_target="tpu_custom_call" | custom-call | bytes 3690000 | tf_op jit(solution)/shard_map/loaded/pallas_call | solution.py:183
  6.0 2.7 %segment_rows.4.refs_5_.refs_6_ = f32[16,256]{1,0:T(8,128)S(1)} custom-call(bf16[2048,1024]{1,0:T(8,128)(2,1)S(1)} %get-tuple-element.23.refs_0_.refs_1_, f32[1,1024]{1,0:T(1,128)S(1)} %get-tuple-element.25.refs_1_), custom_call_target="tpu_custom_call" | custom-call | bytes 4428000 | tf_op jit(solution)/shard_map/segment_rows/pallas_call | solution.py:306
  8.7 0.2 collective-permute-done.1.refs_4_.refs_3_.refs_2_
  8.9 0.0 collective-permute-done.refs_3_.refs_2_
  8.9 2.2 %first_products.1 = (f32[128,1024]{1,0:T(8,128)S(1)}, bf16[136,512]{1,0:T(8,128)(2,1)S(1)}, bf16[136,512]{1,0:T(8,128)(2,1)S(1)}) custom-call(bf16[2048,1024]{1,0:T(8,128)(2,1)S(1)} %get-tuple-element.23.refs_0_.refs_1_, f32[1,1024]{1,0:T(1,128)S(1)} %get-tuple-element.25.refs_1_, bf16[32,2048]{1,0:T(8,128)(2,1)S(1)} %get-tuple-element.22.after.refs_2_.refs_1_, ...), custom_call_target="tpu_custom_call" | custom-call | bytes 3690000 | tf_op jit(solution)/shard_map/first_products/pallas_call | solution.py:306
  11.1 3.0 %collective-permute-start.2 = (bf16[136,512]{1,0:T(8,128)(2,1)S(1)}, bf16[136,512]{1,0:T(8,128)(2,1)S(1)}, u32[]{:S(2)}, u32[]{:S(2)}) collective-permute-start(bf16[136,512]{1,0:T(8,128)(2,1)S(1)} %get-tuple-element.26.refs_4_.refs_1_), channel_id=1, source_target_pairs={{0,2},{2,0},{4,6},{6,4},{8,10},{10,8},{12,14},{14,12},{1,3},{3,1},... | collective-permute-start | bytes 417800 | tf_op jit(solution)/shard_map/ppermute | solution.py:39
  14.1 0.1 collective-permute-start.3
  14.2 2.2 %later_products.2 = (f32[128,1024]{1,0:T(8,128)S(1)}, bf16[128,512]{1,0:T(8,128)(2,1)S(1)}, bf16[128,512]{1,0:T(8,128)(2,1)S(1)}) custom-call(bf16[2048,1024]{1,0:T(8,128)(2,1)S(1)} %get-tuple-element.23.refs_0_.refs_1_, bf16[32,2048]{1,0:T(8,128)(2,1)S(1)} %get-tuple-element.22.after.refs_2_.refs_1_, ...), custom_call_target="tpu_custom_call" | custom-call | bytes 3690000 | tf_op jit(solution)/shard_map/later_products/pallas_call | solution.py:306
  16.3 2.7 %segment_rows.5.refs_3_.refs_7_ = f32[16,256]{1,0:T(8,128)S(1)} custom-call(bf16[2048,1024]{1,0:T(8,128)(2,1)S(1)} %get-tuple-element.23.refs_0_.refs_1_, f32[1,1024]{1,0:T(1,128)S(1)} %get-tuple-element.25.refs_1_, bf16[16,1024]{1,0:T(8,128)(2,1)S(1)} %collective-permute-done.1.refs_4_.refs_3_.refs_2_, bf16[128,512]{1,0:T(8,128)(2,1)S(1)} %get-tuple-element.29.refs_3_, ...), custom_call_target="tpu_custom_call" | custom-call | bytes 4428000 | tf_op jit(solution)/shard_map/segment_rows/pallas_call | solution.py:306
  19.0 0.0 collective-permute-done.2.refs_2_.refs_4_.refs_3_.refs_5_
  19.0 0.3 merged.4.refs_3_.refs_6_.refs_1_.refs_5_
  19.3 3.4 %collective-permute-start.8 = (bf16[136,512]{1,0:T(8,128)(2,1)S(1)}, bf16[136,512]{1,0:T(8,128)(2,1)S(1)}, u32[]{:S(2)}, u32[]{:S(2)}) collective-permute-start(bf16[136,512]{1,0:T(8,128)(2,1)S(1)} %merged.4.refs_3_.refs_6_.refs_1_.refs_5_), channel_id=1, source_target_pairs={{0,4},{2,6},{4,0},{6,2},{8,12},{10,14},{12,8},{14,10},{1,5},{3,7},... | collective-permute-start | bytes 417800 | tf_op jit(solution)/shard_map/ppermute | solution.py:39
  22.8 0.7 %collective-permute-start.9 = (bf16[128,512]{1,0:T(8,128)(2,1)S(1)}, bf16[128,512]{1,0:T(8,128)(2,1)S(1)}, u32[]{:S(2)}, u32[]{:S(2)}) collective-permute-start(bf16[128,512]{1,0:T(8,128)(2,1)S(1)} %get-tuple-element.29.refs_3_), channel_id=1, source_target_pairs={{0,2},{2,0},{4,6},{6,4},{8,10},{10,8},{12,14},{14,12},{1,3},{3,1},... | collective-permute-start | bytes 393224 | tf_op jit(solution)/shard_map/ppermute | solution.py:39
  23.4 0.0 collective-permute-done.3.refs_2_.refs_4_.refs_6_
  23.4 0.3 merged.5.refs_7_.refs_1_.refs_6_
  23.8 0.9 %collective-permute-start.10 = (bf16[136,512]{1,0:T(8,128)(2,1)S(1)}, bf16[136,512]{1,0:T(8,128)(2,1)S(1)}, u32[]{:S(2)}, u32[]{:S(2)}) collective-permute-start(bf16[136,512]{1,0:T(8,128)(2,1)S(1)} %merged.5.refs_7_.refs_1_.refs_6_), channel_id=1, source_target_pairs={{0,4},{2,6},{4,0},{6,2},{8,12},{10,14},{12,8},{14,10},{1,5},{3,7},... | collective-permute-start | bytes 417800 | tf_op jit(solution)/shard_map/ppermute | solution.py:39
  24.7 0.6 %collective-permute-start.11 = (bf16[128,512]{1,0:T(8,128)(2,1)S(1)}, bf16[128,512]{1,0:T(8,128)(2,1)S(1)}, u32[]{:S(2)}, u32[]{:S(2)}) collective-permute-start(bf16[128,512]{1,0:T(8,128)(2,1)S(1)} %get-tuple-element.30.refs_4_), channel_id=1, source_target_pairs={{0,2},{2,0},{4,6},{6,4},{8,10},{10,8},{12,14},{14,12},{1,3},{3,1},... | collective-permute-start | bytes 393224 | tf_op jit(solution)/shard_map/ppermute | solution.py:39
  25.3 4.0 %later_products.3 = (f32[128,1024]{1,0:T(8,128)S(1)}, bf16[128,512]{1,0:T(8,128)(2,1)S(1)}, bf16[128,512]{1,0:T(8,128)(2,1)S(1)}, f32[128,1024]{1,0:T(8,128)S(1)...) custom-call(bf16[2048,1024]{1,0:T(8,128)(2,1)S(1)} %get-tuple-element.23.refs_0_.refs_1_, ...), custom_call_target="tpu_custom_call" | custom-call | bytes 3690000 | tf_op jit(solution)/shard_map/later_products/pallas_call | solution.py:306
  29.3 1.4 %collective-permute-start.6 = (bf16[128,512]{1,0:T(8,128)(2,1)S(1)}, bf16[128,512]{1,0:T(8,128)(2,1)S(1)}, u32[]{:S(2)}, u32[]{:S(2)}) collective-permute-start(bf16[128,512]{1,0:T(8,128)(2,1)S(1)} %get-tuple-element.35.refs_5_), channel_id=1, source_target_pairs={{0,2},{2,0},{4,6},{6,4},{8,10},{10,8},{12,14},{14,12},{1,3},{3,1},... | collective-permute-start | bytes 393224 | tf_op jit(solution)/shard_map/ppermute | solution.py:39
  30.8 0.0 collective-permute-done.9.refs_3_
  30.8 0.6 %collective-permute-start.7 = (bf16[128,512]{1,0:T(8,128)(2,1)S(1)}, bf16[128,512]{1,0:T(8,128)(2,1)S(1)}, u32[]{:S(2)}, u32[]{:S(2)}) collective-permute-start(bf16[128,512]{1,0:T(8,128)(2,1)S(1)} %get-tuple-element.36), channel_id=1, source_target_pairs={{0,2},{2,0},{4,6},{6,4},{8,10},{10,8},{12,14},{14,12},{1,3},{3,1},... | collective-permute-start | bytes 393224 | tf_op jit(solution)/shard_map/ppermute | solution.py:39
  31.4 0.0 collective-permute-done.8.refs_2_.refs_9_
  31.4 1.4 %collective-permute-start.4 = (bf16[128,512]{1,0:T(8,128)(2,1)S(1)}, bf16[128,512]{1,0:T(8,128)(2,1)S(1)}, u32[]{:S(2)}, u32[]{:S(2)}) collective-permute-start(bf16[128,512]{1,0:T(8,128)(2,1)S(1)} %get-tuple-element.32), channel_id=1, source_target_pairs={{0,2},{2,0},{4,6},{6,4},{8,10},{10,8},{12,14},{14,12},{1,3},{3,1},... | collective-permute-start | bytes 393224 | tf_op jit(solution)/shard_map/ppermute | solution.py:39
  32.8 0.5 merged.6.refs_5_.refs_3_.refs_2_
  33.3 0.0 collective-permute-done.11.refs_3_
  33.3 0.0 collective-permute-done.10.refs_2_.refs_10_
  33.3 0.5 merged.7.refs_4_.refs_3_
  33.7 2.7 %collective-permute-start.15 = (bf16[136,512]{1,0:T(8,128)(2,1)S(1)}, bf16[136,512]{1,0:T(8,128)(2,1)S(1)}, u32[]{:S(2)}, u32[]{:S(2)}) collective-permute-start(bf16[136,512]{1,0:T(8,128)(2,1)S(1)} %merged.7.refs_4_.refs_3_), channel_id=1, source_target_pairs={{0,8},{2,10},{4,12},{6,14},{8,0},{10,2},{12,4},{14,6},{1,9},{3,11}... | collective-permute-start | bytes 417800 | tf_op jit(solution)/shard_map/ppermute | solution.py:39
  36.4 0.3 collective-permute-start.14
  36.7 2.7 %segment_rows.6.refs_7_.refs_8_ = f32[16,256]{1,0:T(8,128)S(1)} custom-call(bf16[2048,1024]{1,0:T(8,128)(2,1)S(1)} %get-tuple-element.23.refs_0_.refs_1_, f32[1,1024]{1,0:T(1,128)S(1)} %get-tuple-element.25.refs_1_, bf16[16,1024]{1,0:T(8,128)(2,1)S(1)} %collective-permute-done.1.refs_4_.refs_3_.refs_2_, bf16[136,512]{1,0:T(8,128)(2,1)S(1)} %merged.6.refs_5_.refs_3_.refs_2_, ...), custom_call_target="tpu_custom_call" | custom-call | bytes 4428000 | tf_op jit(solution)/shard_map/segment_rows/pallas_call | solution.py:306
  39.4 0.0 collective-permute-done.6.refs_1_
  39.4 0.8 %collective-permute-start.5 = (bf16[128,512]{1,0:T(8,128)(2,1)S(1)}, bf16[128,512]{1,0:T(8,128)(2,1)S(1)}, u32[]{:S(2)}, u32[]{:S(2)}) collective-permute-start(bf16[128,512]{1,0:T(8,128)(2,1)S(1)} %get-tuple-element.33), channel_id=1, source_target_pairs={{0,2},{2,0},{4,6},{6,4},{8,10},{10,8},{12,14},{14,12},{1,3},{3,1},... | collective-permute-start | bytes 393224 | tf_op jit(solution)/shard_map/ppermute | solution.py:39
  40.2 0.0 collective-permute-done.7.refs_2_
  40.2 0.5 resent.1
  40.7 1.9 %collective-permute-start.12 = (bf16[128,512]{1,0:T(8,128)(2,1)S(1)}, bf16[128,512]{1,0:T(8,128)(2,1)S(1)}, u32[]{:S(2)}, u32[]{:S(2)}) collective-permute-start(bf16[128,512]{1,0:T(8,128)(2,1)S(1)} %get-tuple-element.38.refs_3_), channel_id=1, source_target_pairs={{0,4},{2,6},{4,0},{6,2},{8,12},{10,14},{12,8},{14,10},{1,5},{3,7},... | collective-permute-start | bytes 393224 | tf_op jit(solution)/shard_map/ppermute | solution.py:39
  42.6 0.0 collective-permute-done.4.refs_3_
  42.6 0.2 collective-permute-start.13
  42.8 2.7 %segment_rows.7.refs_11_.refs_9_ = f32[16,256]{1,0:T(8,128)S(1)} custom-call(bf16[2048,1024]{1,0:T(8,128)(2,1)S(1)} %get-tuple-element.23.refs_0_.refs_1_, f32[1,1024]{1,0:T(1,128)S(1)} %get-tuple-element.25.refs_1_, bf16[16,1024]{1,0:T(8,128)(2,1)S(1)} %collective-permute-done.1.refs_4_.refs_3_.refs_2_, bf16[128,512]{1,0:T(8,128)(2,1)S(1)} %get-tuple-element.38.refs_3_, ...), custom_call_target="tpu_custom_call" | custom-call | bytes 4428000 | tf_op jit(solution)/shard_map/segment_rows/pallas_call | solution.py:306
  45.5 0.0 collective-permute-done.5.refs_4_
  45.5 4.0 %collective-permute-done.12.refs_7_ = bf16[128,512]{1,0:T(8,128)(2,1)S(1)} collective-permute-done((bf16[128,512]{1,0:T(8,128)(2,1)S(1)}, bf16[128,512]{1,0:T(8,128)(2,1)S(1)}, u32[]{:S(2)}, u32[]{:S(2)}) %collective-permute-start.12) | collective-permute-done | bytes 131104 | tf_op jit(solution)/shard_map/ppermute | solution.py:39
  49.5 1.4 %collective-permute-done.13.refs_8_ = bf16[128,512]{1,0:T(8,128)(2,1)S(1)} collective-permute-done((bf16[128,512]{1,0:T(8,128)(2,1)S(1)}, bf16[128,512]{1,0:T(8,128)(2,1)S(1)}, u32[]{:S(2)}, u32[]{:S(2)}) %collective-permute-start.13) | collective-permute-done | bytes 131104 | tf_op jit(solution)/shard_map/ppermute | solution.py:39
  50.9 0.6 %added.1 = (f32[128,1024]{1,0:T(8,128)S(1)}, f32[16,256]{1,0:T(8,128)S(1)}) custom-call(f32[128,1024]{1,0:T(8,128)S(1)} %get-tuple-element.31.refs_0_, bf16[2048,1024]{1,0:T(8,128)(2,1)S(1)} %get-tuple-element.23.refs_0_.refs_1_, bf16[16,1024]{1,0:T(8,128)(2,1)S(1)} %collective-permute-done.1.refs_4_.refs_3_.refs_2_, ...), custom_call_target="tpu_custom_call" | custom-call | bytes 1107000 | tf_op jit(solution)/shard_map/added/pallas_call | solution.py:306
  51.5 0.0 collective-permute-done.15.refs_5_
  51.5 0.0 collective-permute-done.14.refs_4_
  51.5 1.2 %finished.1 = (f32[128,1024]{1,0:T(8,128)}, f32[16,1024]{1,0:T(8,128)}) custom-call(f32[128,1024]{1,0:T(8,128)S(1)} %get-tuple-element.40.refs_0_, f32[16,256]{1,0:T(8,128)S(1)} %get-tuple-element.41.refs_1_, bf16[136,512]{1,0:T(8,128)(2,1)S(1)} %merged.6.refs_5_.refs_3_.refs_2_, bf16[136,512]{1,0:T(8,128)(2,1)S(1)} %merged.7.refs_4_.refs_3_, ...), custom_call_target="tpu_custom_call" | custom-call | bytes 1107000 | tf_op jit(solution)/shard_map/finished/pallas_call | solution.py:306
Async XLA Ops:
  1.9 7.0 %collective-permute-start = (bf16[32,2048]{1,0:T(8,128)(2,1)S(1)}, bf16[32,2048]{1,0:T(8,128)(2,1)S(1)}, u32[]{:S(2)}, u32[]{:S(2)}) collective-permute-start(bf16[32,2048]{1,0:T(8,128)(2,1)S(1)} %get-tuple-element.22.after.refs_2_.refs_1_), channel_id=1, source_target_pairs={{0,1},{1,0},{2,3},{3,2},{4,5},{5,4},{6,7},{7,6},{8,9},{9,8},{10,11... | collective-permute-start | bytes 393224 | tf_op jit(solution)/shard_map/ppermute | solution.py:39
  2.4 6.4 %collective-permute-start.1 = (bf16[16,1024]{1,0:T(8,128)(2,1)S(1)}, bf16[16,1024]{1,0:T(8,128)(2,1)S(1)}, u32[]{:S(2)}, u32[]{:S(2)}) collective-permute-start(bf16[16,1024]{1,0:T(8,128)(2,1)S(1)} %get-tuple-element.24), channel_id=1, source_target_pairs={{2,0},{4,2},{6,4},{8,6},{10,8},{12,10},{14,12},{3,1},{5,3},{7,5},{... | collective-permute-start | bytes 98312 | tf_op jit(solution)/shard_map/ppermute | solution.py:34
  11.1 7.9 %collective-permute-start.2 = (bf16[136,512]{1,0:T(8,128)(2,1)S(1)}, bf16[136,512]{1,0:T(8,128)(2,1)S(1)}, u32[]{:S(2)}, u32[]{:S(2)}) collective-permute-start(bf16[136,512]{1,0:T(8,128)(2,1)S(1)} %get-tuple-element.26.refs_4_.refs_1_), channel_id=1, source_target_pairs={{0,2},{2,0},{4,6},{6,4},{8,10},{10,8},{12,14},{14,12},{1,3},{3,1},... | collective-permute-start | bytes 417800 | tf_op jit(solution)/shard_map/ppermute | solution.py:39
  14.1 9.3 %collective-permute-start.3 = (bf16[136,512]{1,0:T(8,128)(2,1)S(1)}, bf16[136,512]{1,0:T(8,128)(2,1)S(1)}, u32[]{:S(2)}, u32[]{:S(2)}) collective-permute-start(bf16[136,512]{1,0:T(8,128)(2,1)S(1)} %get-tuple-element.27.refs_5_.refs_1_), channel_id=1, source_target_pairs={{0,2},{2,0},{4,6},{6,4},{8,10},{10,8},{12,14},{14,12},{1,3},{3,1},... | collective-permute-start | bytes 417800 | tf_op jit(solution)/shard_map/ppermute | solution.py:39
  19.3 12.1 %collective-permute-start.8 = (bf16[136,512]{1,0:T(8,128)(2,1)S(1)}, bf16[136,512]{1,0:T(8,128)(2,1)S(1)}, u32[]{:S(2)}, u32[]{:S(2)}) collective-permute-start(bf16[136,512]{1,0:T(8,128)(2,1)S(1)} %merged.4.refs_3_.refs_6_.refs_1_.refs_5_), channel_id=1, source_target_pairs={{0,4},{2,6},{4,0},{6,2},{8,12},{10,14},{12,8},{14,10},{1,5},{3,7},... | collective-permute-start | bytes 417800 | tf_op jit(solution)/shard_map/ppermute | solution.py:39
  22.8 8.0 %collective-permute-start.9 = (bf16[128,512]{1,0:T(8,128)(2,1)S(1)}, bf16[128,512]{1,0:T(8,128)(2,1)S(1)}, u32[]{:S(2)}, u32[]{:S(2)}) collective-permute-start(bf16[128,512]{1,0:T(8,128)(2,1)S(1)} %get-tuple-element.29.refs_3_), channel_id=1, source_target_pairs={{0,2},{2,0},{4,6},{6,4},{8,10},{10,8},{12,14},{14,12},{1,3},{3,1},... | collective-permute-start | bytes 393224 | tf_op jit(solution)/shard_map/ppermute | solution.py:39
  23.8 9.5 %collective-permute-start.10 = (bf16[136,512]{1,0:T(8,128)(2,1)S(1)}, bf16[136,512]{1,0:T(8,128)(2,1)S(1)}, u32[]{:S(2)}, u32[]{:S(2)}) collective-permute-start(bf16[136,512]{1,0:T(8,128)(2,1)S(1)} %merged.5.refs_7_.refs_1_.refs_6_), channel_id=1, source_target_pairs={{0,4},{2,6},{4,0},{6,2},{8,12},{10,14},{12,8},{14,10},{1,5},{3,7},... | collective-permute-start | bytes 417800 | tf_op jit(solution)/shard_map/ppermute | solution.py:39
  24.7 8.6 %collective-permute-start.11 = (bf16[128,512]{1,0:T(8,128)(2,1)S(1)}, bf16[128,512]{1,0:T(8,128)(2,1)S(1)}, u32[]{:S(2)}, u32[]{:S(2)}) collective-permute-start(bf16[128,512]{1,0:T(8,128)(2,1)S(1)} %get-tuple-element.30.refs_4_), channel_id=1, source_target_pairs={{0,2},{2,0},{4,6},{6,4},{8,10},{10,8},{12,14},{14,12},{1,3},{3,1},... | collective-permute-start | bytes 393224 | tf_op jit(solution)/shard_map/ppermute | solution.py:39
  29.3 10.1 %collective-permute-start.6 = (bf16[128,512]{1,0:T(8,128)(2,1)S(1)}, bf16[128,512]{1,0:T(8,128)(2,1)S(1)}, u32[]{:S(2)}, u32[]{:S(2)}) collective-permute-start(bf16[128,512]{1,0:T(8,128)(2,1)S(1)} %get-tuple-element.35.refs_5_), channel_id=1, source_target_pairs={{0,2},{2,0},{4,6},{6,4},{8,10},{10,8},{12,14},{14,12},{1,3},{3,1},... | collective-permute-start | bytes 393224 | tf_op jit(solution)/shard_map/ppermute | solution.py:39
  30.8 9.4 %collective-permute-start.7 = (bf16[128,512]{1,0:T(8,128)(2,1)S(1)}, bf16[128,512]{1,0:T(8,128)(2,1)S(1)}, u32[]{:S(2)}, u32[]{:S(2)}) collective-permute-start(bf16[128,512]{1,0:T(8,128)(2,1)S(1)} %get-tuple-element.36), channel_id=1, source_target_pairs={{0,2},{2,0},{4,6},{6,4},{8,10},{10,8},{12,14},{14,12},{1,3},{3,1},... | collective-permute-start | bytes 393224 | tf_op jit(solution)/shard_map/ppermute | solution.py:39
  31.4 11.2 %collective-permute-start.4 = (bf16[128,512]{1,0:T(8,128)(2,1)S(1)}, bf16[128,512]{1,0:T(8,128)(2,1)S(1)}, u32[]{:S(2)}, u32[]{:S(2)}) collective-permute-start(bf16[128,512]{1,0:T(8,128)(2,1)S(1)} %get-tuple-element.32), channel_id=1, source_target_pairs={{0,2},{2,0},{4,6},{6,4},{8,10},{10,8},{12,14},{14,12},{1,3},{3,1},... | collective-permute-start | bytes 393224 | tf_op jit(solution)/shard_map/ppermute | solution.py:39
  33.7 17.7 %collective-permute-start.15 = (bf16[136,512]{1,0:T(8,128)(2,1)S(1)}, bf16[136,512]{1,0:T(8,128)(2,1)S(1)}, u32[]{:S(2)}, u32[]{:S(2)}) collective-permute-start(bf16[136,512]{1,0:T(8,128)(2,1)S(1)} %merged.7.refs_4_.refs_3_), channel_id=1, source_target_pairs={{0,8},{2,10},{4,12},{6,14},{8,0},{10,2},{12,4},{14,6},{1,9},{3,11}... | collective-permute-start | bytes 417800 | tf_op jit(solution)/shard_map/ppermute | solution.py:39
  36.4 15.1 %collective-permute-start.14 = (bf16[136,512]{1,0:T(8,128)(2,1)S(1)}, bf16[136,512]{1,0:T(8,128)(2,1)S(1)}, u32[]{:S(2)}, u32[]{:S(2)}) collective-permute-start(bf16[136,512]{1,0:T(8,128)(2,1)S(1)} %merged.6.refs_5_.refs_3_.refs_2_), channel_id=1, source_target_pairs={{0,8},{2,10},{4,12},{6,14},{8,0},{10,2},{12,4},{14,6},{1,9},{3,11}... | collective-permute-start | bytes 417800 | tf_op jit(solution)/shard_map/ppermute | solution.py:39
  39.4 6.1 %collective-permute-start.5 = (bf16[128,512]{1,0:T(8,128)(2,1)S(1)}, bf16[128,512]{1,0:T(8,128)(2,1)S(1)}, u32[]{:S(2)}, u32[]{:S(2)}) collective-permute-start(bf16[128,512]{1,0:T(8,128)(2,1)S(1)} %get-tuple-element.33), channel_id=1, source_target_pairs={{0,2},{2,0},{4,6},{6,4},{8,10},{10,8},{12,14},{14,12},{1,3},{3,1},... | collective-permute-start | bytes 393224 | tf_op jit(solution)/shard_map/ppermute | solution.py:39
  40.7 8.7 %collective-permute-start.12 = (bf16[128,512]{1,0:T(8,128)(2,1)S(1)}, bf16[128,512]{1,0:T(8,128)(2,1)S(1)}, u32[]{:S(2)}, u32[]{:S(2)}) collective-permute-start(bf16[128,512]{1,0:T(8,128)(2,1)S(1)} %get-tuple-element.38.refs_3_), channel_id=1, source_target_pairs={{0,4},{2,6},{4,0},{6,2},{8,12},{10,14},{12,8},{14,10},{1,5},{3,7},... | collective-permute-start | bytes 393224 | tf_op jit(solution)/shard_map/ppermute | solution.py:39
  42.6 8.3 %collective-permute-start.13 = (bf16[128,512]{1,0:T(8,128)(2,1)S(1)}, bf16[128,512]{1,0:T(8,128)(2,1)S(1)}, u32[]{:S(2)}, u32[]{:S(2)}) collective-permute-start(bf16[128,512]{1,0:T(8,128)(2,1)S(1)} %get-tuple-element.39.refs_4_), channel_id=1, source_target_pairs={{0,4},{2,6},{4,0},{6,2},{8,12},{10,14},{12,8},{14,10},{1,5},{3,7},... | collective-permute-start | bytes 393224 | tf_op jit(solution)/shard_map/ppermute | solution.py:39

commit v9 on v7

--- a/solution.py
+++ b/solution.py
@@ -77,6 +77,10 @@
     return powers, refs, wide[4:5]
 
 
+def sent_powers(code):
+    return unpacked(code[-EXTRA:])
+
+
 def rounded_up(value):
     return (value * (1.0 + 2.0**-7)).astype(jnp.bfloat16).astype(jnp.float32)
 
@@ -138,14 +142,16 @@
 
 def lag_rows(own, other, group, shifted):
     chan, near = lax.axis_index("chan"), lax.axis_index("tm") & 1
+    rows = own.shape[1]
     zeros = jnp.zeros((HALF, LANES), jnp.float32)
     for refs, half in ((own, chan), (other, 1 - chan)):
-        long = jnp.concatenate([refs[...].astype(jnp.float32), zeros], axis=1)
+        long = jnp.concatenate([zeros, refs[...].astype(jnp.float32)], axis=1)
         for index in range(GROUP):
             ahead = near if index < GROUP // 2 else 1 - near
             lag = group * GROUP + ahead * (GROUP // 2) + index % (GROUP // 2)
             start = pl.multiple_of(index * REF + half * HALF, HALF)
-            shifted[pl.ds(start, HALF), :] = pltpu.roll(long, lag, 1).astype(jnp.bfloat16)
+            moved = pltpu.roll(long, lag, 1)[:, LANES : LANES + rows]
+            shifted[pl.ds(start, HALF), :] = moved.astype(jnp.bfloat16)
 
 
 def own_group(bits):
@@ -188,21 +194,44 @@
     )(pltpu.with_memory_space_constraint(strain, pltpu.HBM), after)
 
 
-def edge_of(tail):
-    return jnp.concatenate([tail[...], jnp.zeros((LANES - LAGS, tail.shape[1]), tail.dtype)], axis=0)
-
-
-def product_of(shifted, held, edge, here):
-    rows = held.shape[0]
-    total = jnp.dot(shifted[:, rows:], edge[:, here], preferred_element_type=jnp.float32)
-    return total + jnp.dot(shifted[:, :rows], held[:, here], preferred_element_type=jnp.float32)
-
-
 def columns(width):
     return [slice(first, first + STEP) for first in range(0, width, STEP)]
 
 
-def first_products_kernel(held, power, own, other, tail, keep, send, shifted):
+def product_of(shifted, held, here):
+    return jnp.dot(shifted[...], held[:, here], preferred_element_type=jnp.float32)
+
+
+def boundary_rows(group, ends, their_ends, edges):
+    chan, near = lax.axis_index("chan"), lax.axis_index("tm") & 1
+    zeros = jnp.zeros((HALF, LANES), jnp.float32)
+    ours = [(refs[:, refs.shape[1] - LANES :].astype(jnp.float32), half) for refs, half in zip(ends, (chan, 1 - chan))]
+    theirs = [(their_ends[half * HALF : (half + 1) * HALF], half) for half in range(2)]
+    for side, parts in enumerate((ours, theirs)):
+        for end, half in parts:
+            long = jnp.concatenate([end, zeros], axis=1)
+            for index in range(GROUP // 2):
+                lag = group * GROUP + near * (GROUP // 2) + index
+                start = pl.multiple_of(index * REF + half * HALF, HALF)
+                moved = pltpu.roll(long, lag, 1)[:, LANES:]
+                edges[pl.ds(start, HALF), side * LANES : (side + 1) * LANES] = moved.astype(jnp.bfloat16)
+
+
+def ends_of(code):
+    rows = code[LAGS : 2 * LAGS, :LANES].astype(jnp.float32)
+    return jnp.concatenate([jnp.zeros((LANES - LAGS, LANES), jnp.float32), rows], axis=0).T[:REF]
+
+
+def tails_of(sent, arrived, here):
+    zeros = jnp.zeros((LANES - LAGS, here.stop - here.start), jnp.bfloat16)
+    return jnp.concatenate([arrived[:LAGS, here], zeros, sent[:LAGS, here], zeros], axis=0)
+
+
+def boundary_of(edges, sent, arrived, here):
+    return jnp.dot(edges[...], tails_of(sent, arrived, here), preferred_element_type=jnp.float32)
+
+
+def first_products_kernel(held, power, own, other, keep, send, shifted):
     lag_rows(own, other, own_group(3), shifted)
     ours, theirs = [
         jnp.sum(jnp.square(refs[...].astype(jnp.float32)), axis=1, keepdims=True) for refs in (own, other)
@@ -212,59 +241,56 @@
         jnp.concatenate([ours, theirs], axis=0),
         jnp.concatenate([theirs, ours], axis=0),
     )
-    beyond = jnp.sum(jnp.square(tail[...].astype(jnp.float32)), axis=0, keepdims=True)
-    bound = rounded_up(power[...] + beyond)
+    bound = rounded_up(power[...])
     pad = jnp.zeros((1, LANES - REF), jnp.float32)
     chunk = keep.shape[0]
     send[chunk:] = packed(power[...], jnp.concatenate([as_row(refs), pad], axis=1), bound)
-    edge = edge_of(tail)
     for here in columns(held.shape[1]):
-        product = product_of(shifted, held, edge, here)
+        product = product_of(shifted, held, here)
         keep[:, here] = product[:chunk]
         send[:chunk, here] = coded(product[chunk:], bound[:, here], refs)
 
 
 def shifted_scratch(rows, groups=1):
-    return [pltpu.VMEM((groups * GROUP * REF, rows + LANES), jnp.bfloat16)]
-
-
-def first_products(held, power, own, other, tail, chunk, after):
+    return [pltpu.VMEM((groups * GROUP * REF, rows), jnp.bfloat16)]
+
+
+def first_products(held, power, own, other, chunk):
     rows, width = held.shape
-    outs = [
-        ((chunk, width), jnp.float32),
-        ((chunk + EXTRA, width), jnp.bfloat16),
-    ]
     return call_on_blocks(
         first_products_kernel,
-        outs,
+        [((chunk, width), jnp.float32), ((chunk + EXTRA, width), jnp.bfloat16)],
         held,
         power,
         own,
         other,
-        tail,
         name="first_products",
         micros=PRODUCT_MICROS,
-        after=after,
         scratch=shifted_scratch(rows),
     )
 
 
-def later_products(groups, held, own, other, tail, powers, chunk, after=()):
+def later_products(groups, held, own, other, powers, chunk, tails=(), after=()):
     rows, width = held.shape
 
-    def kernel(held, own, other, tail, powers, *rest):
-        outs, shifted = rest[:-1], rest[-1]
+    def kernel(held, own, other, powers, *rest):
+        sides, rest = rest[: len(tails)], rest[len(tails) :]
+        outs, shifted, edges = rest[:-2], rest[-2], rest[-1]
         _, ref_powers, bound = sent_powers(powers)
         refs = ref_column(ref_powers)
         for index, bits in enumerate(groups):
             lag_rows(own, other, own_group(bits), shifted.at[pl.ds(index * 2 * chunk, 2 * chunk)])
-        edge = edge_of(tail)
+            if sides:
+                boundary_rows(own_group(bits), (own, other), ends_of(sides[1]), edges.at[index])
         for here in columns(width):
-            product = product_of(shifted, held, edge, here)
+            product = product_of(shifted, held, here)
             for index in range(len(groups)):
                 keep, send = outs[2 * index : 2 * index + 2]
                 first = 2 * index * chunk
-                keep[:, here] = product[first : first + chunk]
+                kept = product[first : first + chunk]
+                if sides:
+                    kept += boundary_of(edges.at[index], *sides, here)
+                keep[:, here] = kept
                 send[:, here] = coded(product[first + chunk : first + 2 * chunk], bound[:, here], refs)
 
     return call_on_blocks(
@@ -273,12 +299,67 @@
         held,
         own,
         other,
-        tail,
         powers,
+        *tails,
         name="later_products",
         micros=PRODUCT_MICROS,
         after=after,
-        scratch=shifted_scratch(rows, len(groups)),
+        scratch=shifted_scratch(rows, len(groups)) + edges_scratch(len(groups), chunk),
+    )
+
+
+def edges_scratch(count, chunk):
+    return [pltpu.VMEM((count, chunk, 2 * LANES), jnp.bfloat16)]
+
+
+def sides_to_swap(head, after_next, own, other, held_back):
+    def kernel(head, after_next, own, other, held_back, sides, passed):
+        chan, near = lax.axis_index("chan"), lax.axis_index("tm") & 1
+        passed[...] = widened(held_back[...], LAGS)
+        sides[:LAGS] = jnp.where(near == 0, after_next[...], head[...])
+        ours, theirs = [
+            refs[:, refs.shape[1] - LANES :].astype(jnp.float32) for refs in (own, other)
+        ]
+        first, second = jnp.where(chan == 0, ours, theirs), jnp.where(chan == 0, theirs, ours)
+        square = jnp.concatenate([first, second, jnp.zeros((LANES - REF, LANES), jnp.float32)], axis=0)
+        sides[LAGS:, :LANES] = square.T[LANES - LAGS :].astype(jnp.bfloat16)
+        sides[LAGS:, LANES:] = jnp.zeros((LAGS, head.shape[1] - LANES), jnp.bfloat16)
+
+    rows, width = held_back.shape
+    outs = [((2 * LAGS, width), jnp.bfloat16), ((rows + LAGS, width), jnp.bfloat16)]
+    return call_on_blocks(
+        kernel, outs, head, after_next, own, other, held_back, name="sides", micros=MERGE_MICROS
+    )
+
+
+def with_boundaries(keeps, groups, own, other, sent, arrived, after):
+    chunk, width = keeps[0].shape
+
+    def kernel(own, other, sent, arrived, *rest):
+        keeps, rest = rest[: len(groups)], rest[len(groups) :]
+        outs, beyond, edges = rest[: len(groups)], rest[-2], rest[-1]
+        for index, bits in enumerate(groups):
+            boundary_rows(own_group(bits), (own, other), ends_of(arrived), edges.at[index])
+        for here in columns(width):
+            tails = tails_of(sent, arrived, here)
+            for index in range(len(groups)):
+                added = jnp.dot(edges[index], tails, preferred_element_type=jnp.float32)
+                outs[index][:, here] = keeps[index][:, here] + added
+            beyond[:, here] = jnp.sum(jnp.square(tails.astype(jnp.float32)), axis=0, keepdims=True)
+
+    outs = [((chunk, width), jnp.float32)] * len(groups) + [((1, width), jnp.float32)]
+    return call_on_blocks(
+        kernel,
+        outs,
+        own,
+        other,
+        sent,
+        arrived,
+        *keeps,
+        name="with_boundaries",
+        micros=MERGE_MICROS,
+        after=after,
+        scratch=edges_scratch(len(groups), chunk),
     )
 
 
@@ -301,86 +382,57 @@
     )(*arrays, *after)
 
 
-def half_of(width, part):
-    return slice(part * width // 2, (part + 1) * width // 2)
-
-
-def sent_powers(code, here=slice(None)):
-    powers, refs, bound = unpacked(code[-EXTRA:])
-    return powers[:, here], refs, bound[:, here]
-
-
-def merge_near(keep, ours, theirs, held_back, after):
+def direct_sums(direct, powers):
+    _, refs, bound = sent_powers(powers)
+    chunk = direct.shape[0] // REF * REF
+    return expanded(direct[:chunk], bound, ref_column(refs))
+
+
+def widened(code, rows):
+    return jnp.concatenate([code, jnp.zeros((rows, code.shape[1]), code.dtype)], axis=0)
+
+
+def merged(keep, ours, theirs, direct=(), beyond=(), held_back=(), after=()):
     chunk, width = keep.shape
 
-    def kernel(keep, ours, theirs, held_back, *outs):
-        outs[2][...] = held_back[...]
-        for part, out in enumerate(outs[:2]):
-            here = half_of(width, part)
-            powers, refs, bound = sent_powers(ours, here)
-            their_powers, their_refs, their_bound = sent_powers(theirs, here)
-            total = keep[:, here] + expanded(theirs[:chunk, here], their_bound, ref_column(their_refs))
-            sums, sum_refs, sum_bound = powers + their_powers, refs + their_refs, rounded_up(bound + their_bound)
-            out[chunk:] = packed(sums, sum_refs, sum_bound)
-            out[:chunk] = coded(total, sum_bound, ref_column(sum_refs))
-
-    outs = [((chunk + EXTRA, width // 2), jnp.bfloat16)] * 2 + [(held_back.shape, jnp.bfloat16)]
-    return call_on_blocks(
-        kernel, outs, keep, ours, theirs, held_back, name="merge_near", micros=MERGE_MICROS, after=after
-    )
-
-
-def merge_far(part, keep, ours, theirs, direct, direct_powers, *held_back, after):
-    chunk, width = keep.shape
-    here = half_of(width, part)
-
-    def kernel(keep, ours, theirs, direct, direct_powers, *rest):
-        out = rest[len(held_back)]
-        if held_back:
-            rest[2][...] = rest[0][...]
+    def kernel(keep, ours, theirs, *refs):
+        inputs, out, passed = refs[: -1 - len(held_back)], refs[len(arrays) - 3], refs[len(arrays) - 2 :]
         powers, refs, bound = sent_powers(ours)
         their_powers, their_refs, their_bound = sent_powers(theirs)
-        total = keep[:, here] + expanded(theirs[:chunk], their_bound, ref_column(their_refs))
-        _, direct_refs, direct_bound = sent_powers(direct_powers, here)
-        total += expanded(direct[:, here], direct_bound, ref_column(direct_refs))
-        sums, sum_refs, sum_bound = powers + their_powers, refs + their_refs, rounded_up(bound + their_bound)
+        sums, sum_refs, sum_bound = powers + their_powers, refs + their_refs, bound + their_bound
+        total = keep[...] + expanded(theirs[:chunk], their_bound, ref_column(their_refs))
+        if direct:
+            total += direct_sums(inputs[0], inputs[1])
+        if beyond:
+            sum_bound += inputs[len(direct)][...]
+        if held_back:
+            passed[0][...] = widened(inputs[-1][...], EXTRA)
+        sum_bound = rounded_up(sum_bound)
         out[chunk:] = packed(sums, sum_refs, sum_bound)
         out[:chunk] = coded(total, sum_bound, ref_column(sum_refs))
 
-    outs = [((chunk + EXTRA, width // 2), jnp.bfloat16)] + [(array.shape, jnp.bfloat16) for array in held_back]
-    arrays = (keep, ours, theirs, direct, direct_powers, *held_back)
-    return call_on_blocks(kernel, outs, *arrays, name="merge_far", micros=MERGE_MICROS, after=after)
+    outs = [((chunk + EXTRA, width), jnp.bfloat16)] * (1 + len(held_back))
+    arrays = (keep, ours, theirs, *direct, *beyond, *held_back)
+    return call_on_blocks(kernel, outs, *arrays, name="merged", micros=MERGE_MICROS, after=after)
 
 
 def resent(keep, direct, direct_powers, ours, after):
-    chunk, width = keep.shape
-
-    def kernel(keep, direct, direct_powers, first, second, *outs):
-        for part, powers in enumerate((first, second)):
-            here = half_of(width, part)
-            _, direct_refs, direct_bound = sent_powers(direct_powers, here)
-            _, refs, bound = sent_powers(powers)
-            total = keep[:, here] + expanded(direct[:, here], direct_bound, ref_column(direct_refs))
-            outs[part][...] = coded(total, bound, ref_column(refs))
-
-    outs = [((chunk, width // 2), jnp.bfloat16)] * 2
-    arrays = (keep, direct, direct_powers, *ours)
-    return call_on_blocks(kernel, outs, *arrays, name="resent", micros=MERGE_MICROS, after=after)
-
-
-def added(keep, direct, direct_powers, near, near_powers, held, tail, size, after):
+    def kernel(keep, direct, direct_powers, ours, out):
+        _, refs, bound = sent_powers(ours)
+        out[...] = coded(keep[...] + direct_sums(direct, direct_powers), bound, ref_column(refs))
+
+    outs = [(keep.shape, jnp.bfloat16)]
+    arrays = (keep, direct, direct_powers, ours)
+    return call_on_blocks(kernel, outs, *arrays, name="resent", micros=MERGE_MICROS, after=after)[0]
+
+
+def added(keep, direct, direct_powers, near, near_powers, held, sides, size, after):
     rows, width = held.shape
 
-    def kernel(keep, direct, direct_powers, held, tail, *refs):
-        near, near_powers, (out, edge) = refs[:2], refs[2:4], refs[4:]
-        for part in range(2):
-            here = half_of(width, part)
-            _, direct_refs, direct_bound = sent_powers(direct_powers, here)
-            _, near_refs, near_bound = sent_powers(near_powers[part])
-            total = keep[:, here] + expanded(direct[:, here], direct_bound, ref_column(direct_refs))
-            out[:, here] = total + expanded(near[part], near_bound, ref_column(near_refs))
+    def kernel(keep, direct, direct_powers, near, near_powers, held, sides, out, edge):
+        out[...] = keep[...] + direct_sums(direct, direct_powers) + direct_sums(near, near_powers)
         last = held[rows - LAGS :, :size].astype(jnp.float32)
-        beyond = tail[:, :size].astype(jnp.float32)
+        beyond = sides[:LAGS, :size].astype(jnp.float32)
         place = lax.broadcasted_iota(jnp.int32, last.shape, 0)
         sums = [jnp.zeros((1, size), jnp.float32)]
         for lag in range(1, LAGS):
@@ -389,38 +441,43 @@
         edge[...] = jnp.concatenate(sums, axis=0)
 
     outs = [(keep.shape, jnp.float32), ((LAGS, size), jnp.float32)]
-    arrays = (keep, direct, direct_powers, held, tail, *near, *near_powers)
+    arrays = (keep, direct, direct_powers, near, near_powers, held, sides)
     return call_on_blocks(kernel, outs, *arrays, name="added", micros=MERGE_MICROS, after=after)
 
 
 def finished(slab_rows, segment, partial, edge, ours, theirs, autos):
     chunk, width = partial.shape
 
-    def kernel(partial, edge, *refs):
-        ours, theirs, autos, (covariance, segment_auto) = refs[:2], refs[2:4], refs[4:-2], refs[-2:]
+    def kernel(partial, edge, ours, theirs, *refs):
+        autos, (covariance, segment_auto) = refs[:-2], refs[-2:]
         first_lag = lax.axis_index("tm").astype(jnp.int32) * (chunk // REF)
         lag = lax.broadcasted_iota(jnp.int32, (chunk, 1), 0) // REF + first_lag
         denom = (slab_rows - lag).astype(jnp.float32)
-        for part in range(2):
-            here = half_of(width, part)
-            powers, own_refs, _ = sent_powers(ours[part])
-            their_powers, their_refs, their_bound = sent_powers(theirs[part])
-            total = partial[:, here] + expanded(theirs[part][:chunk], their_bound, ref_column(their_refs))
-            scale = 1.0 / jnp.sqrt((powers + their_powers) / slab_rows + 1e-06)
-            ref_scale = 1.0 / jnp.sqrt(ref_column(own_refs + their_refs) / slab_rows + 1e-06)
-            covariance[:, here] = total * scale * (for_chunk(ref_scale, chunk) / denom)
-            first = 0
-            for auto in autos:
-                size = auto.shape[1]
-                if here.start <= first < here.stop:
-                    own_scale = scale[:, first - here.start : first - here.start + size]
-                    sums = auto[...] + edge[...] if first == 0 else auto[...]
-                    segment_auto[:, first : first + size] = sums * (own_scale * own_scale) / segment
-                first += size
+        powers, own_refs, _ = sent_powers(ours)
+        their_powers, their_refs, their_bound = sent_powers(theirs)
+        total = partial[...] + expanded(theirs[:chunk], their_bound, ref_column(their_refs))
+        scale = 1.0 / jnp.sqrt((powers + their_powers) / slab_rows + 1e-06)
+        ref_scale = 1.0 / jnp.sqrt(ref_column(own_refs + their_refs) / slab_rows + 1e-06)
+        covariance[...] = total * scale * (for_chunk(ref_scale, chunk) / denom)
+        first = 0
+        for auto in autos:
+            here = slice(first, first + auto.shape[1])
+            sums = auto[...] + edge[...] if first == 0 else auto[...]
+            segment_auto[:, here] = sums * (scale[:, here] * scale[:, here]) / segment
+            first = here.stop
 
     outs = [(partial.shape, jnp.float32), ((LAGS, width), jnp.float32)]
     return call_on_blocks(
-        kernel, outs, partial, edge, *ours, *theirs, *autos, name="finished", micros=MERGE_MICROS, space=jax.ShapeDtypeStruct
+        kernel,
+        outs,
+        partial,
+        edge,
+        ours,
+        theirs,
+        *autos,
+        name="finished",
+        micros=MERGE_MICROS,
+        space=jax.ShapeDtypeStruct,
     )
 
 
@@ -439,7 +496,7 @@
             elif tail is None:
                 following = jnp.zeros((LAGS, LANES), jnp.float32)
             else:
-                following = tail[:, here].astype(jnp.float32)
+                following = tail[:LAGS, here].astype(jnp.float32)
             wide[part * pitch + step : (part + 1) * pitch, :] = following
         taken = lambda first: wide[pl.ds(first, 8, stride=pitch), :]
 
@@ -487,9 +544,11 @@
             start = pl.multiple_of(index * REF + half * HALF, HALF)
             lag = pl.program_id(0) * GROUP + index
             shifted[pl.ds(start, HALF), :] = pltpu.roll(long, lag, 1).astype(jnp.bfloat16)
-    edge = edge_of(tail)
-    for here in columns(held.shape[1]):
-        out[:, here] = product_of(shifted, held, edge, here)
+    rows, width = held.shape
+    edge = jnp.concatenate([tail[...], jnp.zeros((LANES - LAGS, width), tail.dtype)], axis=0)
+    for here in columns(width):
+        total = jnp.dot(shifted[:, rows:], edge[:, here], preferred_element_type=jnp.float32)
+        out[:, here] = total + jnp.dot(shifted[:, :rows], held[:, here], preferred_element_type=jnp.float32)
 
 
 def all_products(held, own, other, tail):
@@ -501,10 +560,15 @@
         in_specs=[vmem] * 4,
         out_specs=pl.BlockSpec((GROUP * REF, width), lambda group: (group, 0)),
         out_shape=jax.ShapeDtypeStruct((LAGS * REF, width), jnp.float32),
-        scratch_shapes=shifted_scratch(rows),
+        scratch_shapes=[pltpu.VMEM((GROUP * REF, rows + LANES), jnp.bfloat16)],
         compiler_params=pltpu.CompilerParams(vmem_limit_bytes=VMEM_BYTES),
         name="all_products",
     )(held, own, other, tail)
+
+
+def from_pair_ahead(value):
+    count = lax.axis_size("tm")
+    return lax.ppermute(value, "tm", [(time + 2, time) for time in range(0, count - 2, 2)])
 
 
 def local(strain):
@@ -515,33 +579,36 @@
 
     own, head = prepared(strain)
     other = exchanged(own, "chan", 1)
-    tail = passed_along(head, "tm", -1)
     held, power = loaded(strain, own)
     size = width // 4
 
     if chunk * 2 == GROUP * REF:
-        refs = (own, other, tail)
-        autos = [segment_rows(held, power, None, 0, size)]
-        keep6, send7 = first_products(held, power, *refs, chunk, after=(autos[0],))
+        keep6, send7 = first_products(held, power, own, other, chunk)
         got7 = exchanged(send7, "tm", 1)
-        keep4, send5, keep2, send3 = later_products((2, 1), held, *refs, send7, chunk)
+        after_next = from_pair_ahead(head)
+        keep4, send5 = later_products((2,), held, own, other, send7, chunk)
+        sides, send5 = sides_to_swap(head, after_next, own, other, send5)
         got5 = exchanged(send5, "tm", 1)
-        keep0, send1 = later_products((0,), held, *refs, send7, chunk, after=(send5,))
-        *sends6, send3 = merge_near(keep6, send7, got7, send3, after=(send1,))
-        gots6 = [exchanged(code, "tm", 2) for code in sends6]
+        tails = (sides, exchanged(sides, "tm", 1))
+        autos = [segment_rows(held, power, None, 0, size, after=(sides,))]
+        keep6, keep4, beyond = with_boundaries((keep6, keep4), (3, 2), own, other, *tails, after=(autos[0],))
+        (send6,) = merged(keep6, send7, got7, beyond=(beyond,))
+        got6 = exchanged(send6, "tm", 2)
+        keep2, send3, keep0, send1 = later_products(
+            (1, 0), held, own, other, send7, chunk, tails=tails, after=(send6,)
+        )
         got3 = exchanged(send3, "tm", 1)
-        autos.append(segment_rows(held, power, tail, size, size, after=(send3,)))
-        far = [merge_far(0, keep4, sends6[0], gots6[0], got5, got7, after=(autos[1],))]
-        far += [merge_far(1, keep4, sends6[1], gots6[1], got5, got7, send1, after=(far[0][0],))]
-        sends4 = [far[0][0], far[1][0]]
-        gots4 = [exchanged(code, "tm", 4) for code in sends4]
-        got1 = exchanged(far[1][1], "tm", 1)
-        sends2 = resent(keep2, got3, got7, sends6, after=(sends4[1],))
-        gots2 = [exchanged(code, "tm", 2) for code in sends2]
-        autos.append(segment_rows(held, power, tail, 2 * size, 2 * size, after=tuple(sends2)))
-        partial, edge = added(keep0, got1, got7, gots2, gots6, held, tail, size, after=(autos[2],))
-        return tuple(finished(slab_rows, rows, partial, edge, sends4, gots4, autos))
-
+        send4, send1 = merged(keep4, send6, got6, direct=(got5, got7), held_back=(send1,), after=(send3,))
+        got4 = exchanged(send4, "tm", 4)
+        got1 = exchanged(send1, "tm", 1)
+        autos.append(segment_rows(held, power, tails[1], size, size, after=(send4,)))
+        send2 = resent(keep2, got3, got7, send6, after=(autos[1],))
+        got2 = exchanged(send2, "tm", 2)
+        autos.append(segment_rows(held, power, tails[1], 2 * size, 2 * size, after=(send2,)))
+        partial, edge = added(keep0, got1, got7, got2, got6, held, tails[1], size, after=(autos[2],))
+        return tuple(finished(slab_rows, rows, partial, edge, send4, got4, autos))
+
+    tail = passed_along(head, "tm", -1)
     chan = lax.axis_index("chan").astype(jnp.int32)
     time = lax.axis_index("tm").astype(jnp.int32)
     auto = jnp.concatenate(

time: 49 us -> 48.1 us (0.982)
  starting transfers between devices: 15.1 us -> 12.4 us
  waiting for transfers between devices: 6.74 us -> 8.66 us
    ppermute x11 -> x9, starting transfers between devices: 13.8 us -> 10.9 us  [exchanged(): lax.ppermute(value, axis, [(source, source ^ bit) for source in range(cou...]
    ppermute x1, waiting for transfers between devices: 0.22 us -> 2.33 us  [from_pair_ahead(): lax.ppermute(value, 'tm', [(time + 2, time) for time in range(0, count -...]
    ppermute x11 -> x9, waiting for transfers between devices: 6.52 us -> 6.33 us  [exchanged(): lax.ppermute(value, axis, [(source, source ^ bit) for source in range(cou...]
    pallas_call x12 -> x13, Pallas kernels: 22.7 us -> 22.6 us  [call_on_blocks(): pl.pallas_call(body, in_specs=[vmem] * count + [pl.BlockSpec(memory_space...]
  transfers between devices with their start and end apart: 12 -> 10, of which waited for: 5 -> 5; matrix products, arithmetic and copies ran while one was open for 0% -> 0% of each run, Pallas kernels for 44% -> 45%
where the time goes in v9:
time: 48.1 us; the launch traced here: 48 us
  Pallas kernels  26.2 us (54%)
  starting transfers between devices  12.4 us (26%)
  waiting for transfers between devices  8.66 us (18%)
  between operations  0.78 us (2%)
    pallas_call x13, Pallas kernels, call_on_blocks(): pl.pallas_call(body, in_specs=[vmem] * count + [pl.BlockSpec(memory_space...  22.6 us
    ppermute x9, starting transfers between devices, exchanged(): lax.ppermute(value, axis, [(source, source ^ bit) for source in range(cou...  10.9 us
    ppermute x9, waiting for transfers between devices, exchanged(): lax.ppermute(value, axis, [(source, source ^ bit) for source in range(cou...  6.33 us
    ppermute x1, waiting for transfers between devices, from_pair_ahead(): lax.ppermute(value, 'tm', [(time + 2, time) for time in range(0, count -...  2.33 us
    pallas_call x1, Pallas kernels, loaded(): pl.pallas_call(kernel, in_specs=[pl.BlockSpec(memory_space=pl.ANY)] * 2,...  2.25 us
    ppermute x1, starting transfers between devices, from_pair_ahead(): lax.ppermute(value, 'tm', [(time + 2, time) for time in range(0, count -...  1.46 us
    pallas_call x1, Pallas kernels, prepared(): pl.pallas_call(prepare_kernel, in_specs=[pl.BlockSpec(memory_space=pl.ANY...  1.28 us
  transfers between devices with their start and end apart: 10, of which 5 were waited for; matrix products, arithmetic and copies ran while one was open for 0% of the time, Pallas kernels for 45%

profile of v9, /device:TPU:0, one launch (start us, length us, event | category | flops | bytes accessed | tf_op | source)
XLA Modules:
  0.0 48.0 jit_solution(16267988956914738478)
XLA Ops:
  0.6 1.3 %prepared.1 = (bf16[32,2048]{1,0:T(8,128)(2,1)S(1)}, bf16[16,1024]{1,0:T(8,128)(2,1)S(1)}) custom-call(bf16[2048,1024]{1,0:T(8,128)(2,1)} %strain.3), custom_call_target="tpu_custom_call" | custom-call | bytes 3690000 | tf_op jit(solution)/shard_map/prepared/pallas_call | solution.py:131
  1.9 0.5 %collective-permute-start = (bf16[32,2048]{1,0:T(8,128)(2,1)S(1)}, bf16[32,2048]{1,0:T(8,128)(2,1)S(1)}, u32[]{:S(2)}, u32[]{:S(2)}) collective-permute-start(bf16[32,2048]{1,0:T(8,128)(2,1)S(1)} %get-tuple-element.23.after.refs_2_.refs_1_.refs_0_), channel_id=1, source_target_pairs={{0,1},{1,0},{2,3},{3,2},{4,5},{5,4},{6,7},{7,6},{8,9},{9,8},{10,11... | collective-permute-start | bytes 393224 | tf_op jit(solution)/shard_map/ppermute | solution.py:39
  2.4 2.3 %loaded.1 = (bf16[2048,1024]{1,0:T(8,128)(2,1)S(1)}, f32[1,1024]{1,0:T(1,128)S(1)}) custom-call(bf16[2048,1024]{1,0:T(8,128)(2,1)} %strain.3, bf16[32,2048]{1,0:T(8,128)(2,1)S(1)} %get-tuple-element.23.after.refs_2_.refs_1_.refs_0_), custom_call_target="tpu_custom_call" | custom-call | bytes 3690000 | tf_op jit(solution)/shard_map/loaded/pallas_call | solution.py:185
  4.7 0.0 collective-permute-done.refs_3_.refs_2_.refs_1_
  4.7 2.0 %first_products.1 = (f32[128,1024]{1,0:T(8,128)S(1)}, bf16[136,1024]{1,0:T(8,128)(2,1)S(1)}) custom-call(bf16[2048,1024]{1,0:T(8,128)(2,1)S(1)} %get-tuple-element.24.refs_0_.refs_5_, f32[1,1024]{1,0:T(1,128)S(1)} %get-tuple-element.25.refs_1_, bf16[32,2048]{1,0:T(8,128)(2,1)S(1)} %get-tuple-element.23.after.refs_2_.refs_1_.refs_0_, ...), custom_call_target="tpu_custom_call" | custom-call | bytes 3690000 | tf_op jit(solution)/shard_map/first_products/pallas_call | solution.py:373
  6.8 2.6 %collective-permute-start.3 = (bf16[136,1024]{1,0:T(8,128)(2,1)S(1)}, bf16[136,1024]{1,0:T(8,128)(2,1)S(1)}, u32[]{:S(2)}, u32[]{:S(2)}) collective-permute-start(bf16[136,1024]{1,0:T(8,128)(2,1)S(1)} %get-tuple-element.26.refs_3_.refs_1_), channel_id=1, source_target_pairs={{0,2},{2,0},{4,6},{6,4},{8,10},{10,8},{12,14},{14,12},{1,3},{3,1},... | collective-permute-start | bytes 835592 | tf_op jit(solution)/shard_map/ppermute | solution.py:39
  9.3 1.5 %collective-permute-start.1 = (bf16[16,1024]{1,0:T(8,128)(2,1)S(1)}, bf16[16,1024]{1,0:T(8,128)(2,1)S(1)}, u32[]{:S(2)}, u32[]{:S(2)}) collective-permute-start(bf16[16,1024]{1,0:T(8,128)(2,1)S(1)} %get-tuple-element.27.refs_0_), channel_id=1, source_target_pairs={{4,0},{8,4},{12,8},{5,1},{9,5},{13,9},{20,16},{24,20},{28,24},{21,... | collective-permute-start | bytes 98312 | tf_op jit(solution)/shard_map/ppermute | solution.py:571
  10.8 2.0 %later_products.2 = (f32[128,1024]{1,0:T(8,128)S(1)}, bf16[128,1024]{1,0:T(8,128)(2,1)S(1)}) custom-call(bf16[2048,1024]{1,0:T(8,128)(2,1)S(1)} %get-tuple-element.24.refs_0_.refs_5_, bf16[32,2048]{1,0:T(8,128)(2,1)S(1)} %get-tuple-element.23.after.refs_2_.refs_1_.refs_0_, bf16[32,2048]{1,0:T(8,128)(2,1)S(1)} %collective-permute-done.refs_3_.refs_2_.refs_1_, ...), custom_call_target="tpu_custom_call" | custom-call | bytes 3690000 | tf_op jit(solution)/shard_map/later_products/pallas_call | solution.py:373
  12.8 2.3 %collective-permute-done.1.refs_1_ = bf16[16,1024]{1,0:T(8,128)(2,1)S(1)} collective-permute-done((bf16[16,1024]{1,0:T(8,128)(2,1)S(1)}, bf16[16,1024]{1,0:T(8,128)(2,1)S(1)}, u32[]{:S(2)}, u32[]{:S(2)}) %collective-permute-start.1) | collective-permute-done | bytes 32800 | tf_op jit(solution)/shard_map/ppermute | solution.py:571
  15.1 0.1 sides.1
  15.2 0.1 collective-permute-start.2
  15.3 2.0 %collective-permute-start.5 = (bf16[144,1024]{1,0:T(8,128)(2,1)S(1)}, bf16[144,1024]{1,0:T(8,128)(2,1)S(1)}, u32[]{:S(2)}, u32[]{:S(2)}) collective-permute-start(bf16[144,1024]{1,0:T(8,128)(2,1)S(1)} %get-tuple-element.36), channel_id=1, source_target_pairs={{0,2},{2,0},{4,6},{6,4},{8,10},{10,8},{12,14},{14,12},{1,3},{3,1},... | collective-permute-start | bytes 884744 | tf_op jit(solution)/shard_map/ppermute | solution.py:39
  17.3 2.7 %segment_rows.3.refs_6_.refs_4_ = f32[16,256]{1,0:T(8,128)S(1)} custom-call(bf16[2048,1024]{1,0:T(8,128)(2,1)S(1)} %get-tuple-element.24.refs_0_.refs_5_, f32[1,1024]{1,0:T(1,128)S(1)} %get-tuple-element.25.refs_1_, bf16[32,1024]{1,0:T(8,128)(2,1)S(1)} %get-tuple-element.29.refs_2_.refs_4_), custom_call_target="tpu_custom_call" | custom-call | bytes 4428000 | tf_op jit(solution)/shard_map/segment_rows/pallas_call | solution.py:373
  20.0 0.3 collective-permute-done.2.refs_3_.refs_5_.refs_2_.refs_6_
  20.3 0.4 with_boundaries.1
  20.8 0.0 collective-permute-done.3.refs_2_.refs_4_
  20.8 0.6 %merged.2.refs_6_.refs_1_.refs_3_ = bf16[136,1024]{1,0:T(8,128)(2,1)S(1)} custom-call(f32[128,1024]{1,0:T(8,128)S(1)} %get-tuple-element.32.refs_0_, bf16[136,1024]{1,0:T(8,128)(2,1)S(1)} %get-tuple-element.26.refs_3_.refs_1_, bf16[136,1024]{1,0:T(8,128)(2,1)S(1)} %collective-permute-done.3.refs_2_.refs_4_, f32[1,1024]{1,0:T(1,128)S(1)} %get-tuple-element.33.refs_3_), custom_call_target="tpu_custom_call" | custom-call | bytes 1107000 | tf_op jit(solution)/shard_map/merged/pallas_call | solution.py:373
  21.3 1.6 %collective-permute-start.4 = (bf16[136,1024]{1,0:T(8,128)(2,1)S(1)}, bf16[136,1024]{1,0:T(8,128)(2,1)S(1)}, u32[]{:S(2)}, u32[]{:S(2)}) collective-permute-start(bf16[136,1024]{1,0:T(8,128)(2,1)S(1)} %merged.2.refs_6_.refs_1_.refs_3_), channel_id=1, source_target_pairs={{0,4},{2,6},{4,0},{6,2},{8,12},{10,14},{12,8},{14,10},{1,5},{3,7},... | collective-permute-start | bytes 835592 | tf_op jit(solution)/shard_map/ppermute | solution.py:39
  23.0 3.8 %later_products.3 = (f32[128,1024]{1,0:T(8,128)S(1)}, bf16[128,1024]{1,0:T(8,128)(2,1)S(1)}, f32[128,1024]{1,0:T(8,128)S(1)}, bf16[128,1024]{1,0:T(8,128)(2,1)S(1)}) custom-call(bf16[2048,1024]{1,0:T(8,128)(2,1)S(1)} %get-tuple-element.24.refs_0_.refs_5_, bf16[32,2048]{1,0:T(8,128)(2,1)S(1)} %get-tuple-element.23.after.refs_2_.refs_1_.refs_0_, ...), custom_call_target="tpu_custom_call" | custom-call | bytes 3690000 | tf_op jit(solution)/shard_map/later_products/pallas_call | solution.py:373
  26.8 0.1 collective-permute-start.7
  26.9 0.0 collective-permute-done.5.refs_3_
  26.9 1.6 %collective-permute-done.4.refs_2_.refs_4_ = bf16[136,1024]{1,0:T(8,128)(2,1)S(1)} collective-permute-done((bf16[136,1024]{1,0:T(8,128)(2,1)S(1)}, bf16[136,1024]{1,0:T(8,128)(2,1)S(1)}, u32[]{:S(2)}, u32[]{:S(2)}) %collective-permute-start.4) | collective-permute-done | bytes 278560 | tf_op jit(solution)/shard_map/ppermute | solution.py:39
  28.5 0.8 %merged.3 = (bf16[136,1024]{1,0:T(8,128)(2,1)S(1)}, bf16[136,1024]{1,0:T(8,128)(2,1)S(1)}) custom-call(f32[128,1024]{1,0:T(8,128)S(1)} %get-tuple-element.35.refs_0_, bf16[136,1024]{1,0:T(8,128)(2,1)S(1)} %merged.2.refs_6_.refs_1_.refs_3_, bf16[136,1024]{1,0:T(8,128)(2,1)S(1)} %collective-permute-done.4.refs_2_.refs_4_, ...), custom_call_target="tpu_custom_call" | custom-call | bytes 1107000 | tf_op jit(solution)/shard_map/merged/pallas_call | solution.py:373
  29.2 0.6 %collective-permute-start.6 = (bf16[136,1024]{1,0:T(8,128)(2,1)S(1)}, bf16[136,1024]{1,0:T(8,128)(2,1)S(1)}, u32[]{:S(2)}, u32[]{:S(2)}) collective-permute-start(bf16[136,1024]{1,0:T(8,128)(2,1)S(1)} %get-tuple-element.39), channel_id=1, source_target_pairs={{0,2},{2,0},{4,6},{6,4},{8,10},{10,8},{12,14},{14,12},{1,3},{3,1},... | collective-permute-start | bytes 835592 | tf_op jit(solution)/shard_map/ppermute | solution.py:39
  29.9 2.6 %collective-permute-start.9 = (bf16[136,1024]{1,0:T(8,128)(2,1)S(1)}, bf16[136,1024]{1,0:T(8,128)(2,1)S(1)}, u32[]{:S(2)}, u32[]{:S(2)}) collective-permute-start(bf16[136,1024]{1,0:T(8,128)(2,1)S(1)} %get-tuple-element.41.refs_3_.refs_2_), channel_id=1, source_target_pairs={{0,8},{2,10},{4,12},{6,14},{8,0},{10,2},{12,4},{14,6},{1,9},{3,11}... | collective-permute-start | bytes 835592 | tf_op jit(solution)/shard_map/ppermute | solution.py:39
  32.5 2.7 %segment_rows.4.refs_4_.refs_5_ = f32[16,256]{1,0:T(8,128)S(1)} custom-call(bf16[2048,1024]{1,0:T(8,128)(2,1)S(1)} %get-tuple-element.24.refs_0_.refs_5_, f32[1,1024]{1,0:T(1,128)S(1)} %get-tuple-element.25.refs_1_, bf16[32,1024]{1,0:T(8,128)(2,1)S(1)} %collective-permute-done.2.refs_3_.refs_5_.refs_2_.refs_6_, ...), custom_call_target="tpu_custom_call" | custom-call | bytes 4428000 | tf_op jit(solution)/shard_map/segment_rows/pallas_call | solution.py:373
  35.1 1.0 %collective-permute-done.7.refs_1_ = bf16[128,1024]{1,0:T(8,128)(2,1)S(1)} collective-permute-done((bf16[128,1024]{1,0:T(8,128)(2,1)S(1)}, bf16[128,1024]{1,0:T(8,128)(2,1)S(1)}, u32[]{:S(2)}, u32[]{:S(2)}) %collective-permute-start.7) | collective-permute-done | bytes 262176 | tf_op jit(solution)/shard_map/ppermute | solution.py:39
  36.1 0.5 %resent.1.refs_3_ = bf16[128,1024]{1,0:T(8,128)(2,1)S(1)} custom-call(f32[128,1024]{1,0:T(8,128)S(1)} %get-tuple-element.40.refs_0_, bf16[128,1024]{1,0:T(8,128)(2,1)S(1)} %collective-permute-done.7.refs_1_, bf16[136,1024]{1,0:T(8,128)(2,1)S(1)} %collective-permute-done.3.refs_2_.refs_4_, bf16[136,1024]{1,0:T(8,128)(2,1)S(1)} %merged.2.refs_6_.refs_1_.refs_3_, ...), custom_call_target="tpu_custom_call" | custom-call | bytes 1107000 | tf_op jit(solution)/shard_map/resent/pallas_call | solution.py:373
  36.6 0.8 %collective-permute-start.8 = (bf16[128,1024]{1,0:T(8,128)(2,1)S(1)}, bf16[128,1024]{1,0:T(8,128)(2,1)S(1)}, u32[]{:S(2)}, u32[]{:S(2)}) collective-permute-start(bf16[128,1024]{1,0:T(8,128)(2,1)S(1)} %resent.1.refs_3_), channel_id=1, source_target_pairs={{0,4},{2,6},{4,0},{6,2},{8,12},{10,14},{12,8},{14,10},{1,5},{3,7},... | collective-permute-start | bytes 786440 | tf_op jit(solution)/shard_map/ppermute | solution.py:39
  37.4 5.3 %segment_rows.5.refs_7_.refs_6_ = f32[16,512]{1,0:T(8,128)S(1)} custom-call(bf16[2048,1024]{1,0:T(8,128)(2,1)S(1)} %get-tuple-element.24.refs_0_.refs_5_, f32[1,1024]{1,0:T(1,128)S(1)} %get-tuple-element.25.refs_1_, bf16[32,1024]{1,0:T(8,128)(2,1)S(1)} %collective-permute-done.2.refs_3_.refs_5_.refs_2_.refs_6_, bf16[128,1024]{1,0:T(8,128)(2,1)S(1)} %resent.1.refs_3_), custom_call_target="tpu_custom_call" | custom-call | bytes 4428000 | tf_op jit(solution)/shard_map/segment_rows/pallas_call | solution.py:373
  42.7 3.4 %collective-permute-done.8.refs_3_ = bf16[128,1024]{1,0:T(8,128)(2,1)S(1)} collective-permute-done((bf16[128,1024]{1,0:T(8,128)(2,1)S(1)}, bf16[128,1024]{1,0:T(8,128)(2,1)S(1)}, u32[]{:S(2)}, u32[]{:S(2)}) %collective-permute-start.8) | collective-permute-done | bytes 262176 | tf_op jit(solution)/shard_map/ppermute | solution.py:39
  46.1 0.0 collective-permute-done.6.refs_1_
  46.1 0.6 %added.1 = (f32[128,1024]{1,0:T(8,128)S(1)}, f32[16,256]{1,0:T(8,128)S(1)}) custom-call(f32[128,1024]{1,0:T(8,128)S(1)} %get-tuple-element.34.refs_0_, bf16[136,1024]{1,0:T(8,128)(2,1)S(1)} %collective-permute-done.6.refs_1_, bf16[136,1024]{1,0:T(8,128)(2,1)S(1)} %collective-permute-done.3.refs_2_.refs_4_, ...), custom_call_target="tpu_custom_call" | custom-call | bytes 1107000 | tf_op jit(solution)/shard_map/added/pallas_call | solution.py:373
  46.7 0.0 collective-permute-done.9.refs_3_
  46.8 1.2 %finished.1 = (f32[128,1024]{1,0:T(8,128)}, f32[16,1024]{1,0:T(8,128)}) custom-call(f32[128,1024]{1,0:T(8,128)S(1)} %get-tuple-element.42.refs_0_, f32[16,256]{1,0:T(8,128)S(1)} %get-tuple-element.43.refs_1_, bf16[136,1024]{1,0:T(8,128)(2,1)S(1)} %get-tuple-element.41.refs_3_.refs_2_, bf16[136,1024]{1,0:T(8,128)(2,1)S(1)} %collective-permute-done.9.refs_3_, ...), custom_call_target="tpu_custom_call" | custom-call | bytes 1107000 | tf_op jit(solution)/shard_map/finished/pallas_call | solution.py:373
Async XLA Ops:
  1.9 2.8 %collective-permute-start = (bf16[32,2048]{1,0:T(8,128)(2,1)S(1)}, bf16[32,2048]{1,0:T(8,128)(2,1)S(1)}, u32[]{:S(2)}, u32[]{:S(2)}) collective-permute-start(bf16[32,2048]{1,0:T(8,128)(2,1)S(1)} %get-tuple-element.23.after.refs_2_.refs_1_.refs_0_), channel_id=1, source_target_pairs={{0,1},{1,0},{2,3},{3,2},{4,5},{5,4},{6,7},{7,6},{8,9},{9,8},{10,11... | collective-permute-start | bytes 393224 | tf_op jit(solution)/shard_map/ppermute | solution.py:39
  6.8 14.0 %collective-permute-start.3 = (bf16[136,1024]{1,0:T(8,128)(2,1)S(1)}, bf16[136,1024]{1,0:T(8,128)(2,1)S(1)}, u32[]{:S(2)}, u32[]{:S(2)}) collective-permute-start(bf16[136,1024]{1,0:T(8,128)(2,1)S(1)} %get-tuple-element.26.refs_3_.refs_1_), channel_id=1, source_target_pairs={{0,2},{2,0},{4,6},{6,4},{8,10},{10,8},{12,14},{14,12},{1,3},{3,1},... | collective-permute-start | bytes 835592 | tf_op jit(solution)/shard_map/ppermute | solution.py:39
  9.3 5.8 %collective-permute-start.1 = (bf16[16,1024]{1,0:T(8,128)(2,1)S(1)}, bf16[16,1024]{1,0:T(8,128)(2,1)S(1)}, u32[]{:S(2)}, u32[]{:S(2)}) collective-permute-start(bf16[16,1024]{1,0:T(8,128)(2,1)S(1)} %get-tuple-element.27.refs_0_), channel_id=1, source_target_pairs={{4,0},{8,4},{12,8},{5,1},{9,5},{13,9},{20,16},{24,20},{28,24},{21,... | collective-permute-start | bytes 98312 | tf_op jit(solution)/shard_map/ppermute | solution.py:571
  15.2 5.1 %collective-permute-start.2 = (bf16[32,1024]{1,0:T(8,128)(2,1)S(1)}, bf16[32,1024]{1,0:T(8,128)(2,1)S(1)}, u32[]{:S(2)}, u32[]{:S(2)}) collective-permute-start(bf16[32,1024]{1,0:T(8,128)(2,1)S(1)} %get-tuple-element.29.refs_2_.refs_4_), channel_id=1, source_target_pairs={{0,2},{2,0},{4,6},{6,4},{8,10},{10,8},{12,14},{14,12},{1,3},{3,1},... | collective-permute-start | bytes 196616 | tf_op jit(solution)/shard_map/ppermute | solution.py:39
  15.3 11.6 %collective-permute-start.5 = (bf16[144,1024]{1,0:T(8,128)(2,1)S(1)}, bf16[144,1024]{1,0:T(8,128)(2,1)S(1)}, u32[]{:S(2)}, u32[]{:S(2)}) collective-permute-start(bf16[144,1024]{1,0:T(8,128)(2,1)S(1)} %get-tuple-element.36), channel_id=1, source_target_pairs={{0,2},{2,0},{4,6},{6,4},{8,10},{10,8},{12,14},{14,12},{1,3},{3,1},... | collective-permute-start | bytes 884744 | tf_op jit(solution)/shard_map/ppermute | solution.py:39
  21.3 7.1 %collective-permute-start.4 = (bf16[136,1024]{1,0:T(8,128)(2,1)S(1)}, bf16[136,1024]{1,0:T(8,128)(2,1)S(1)}, u32[]{:S(2)}, u32[]{:S(2)}) collective-permute-start(bf16[136,1024]{1,0:T(8,128)(2,1)S(1)} %merged.2.refs_6_.refs_1_.refs_3_), channel_id=1, source_target_pairs={{0,4},{2,6},{4,0},{6,2},{8,12},{10,14},{12,8},{14,10},{1,5},{3,7},... | collective-permute-start | bytes 835592 | tf_op jit(solution)/shard_map/ppermute | solution.py:39
  26.8 9.3 %collective-permute-start.7 = (bf16[128,1024]{1,0:T(8,128)(2,1)S(1)}, bf16[128,1024]{1,0:T(8,128)(2,1)S(1)}, u32[]{:S(2)}, u32[]{:S(2)}) collective-permute-start(bf16[128,1024]{1,0:T(8,128)(2,1)S(1)} %get-tuple-element.38.refs_6_), channel_id=1, source_target_pairs={{0,2},{2,0},{4,6},{6,4},{8,10},{10,8},{12,14},{14,12},{1,3},{3,1},... | collective-permute-start | bytes 786440 | tf_op jit(solution)/shard_map/ppermute | solution.py:39
  29.2 16.9 %collective-permute-start.6 = (bf16[136,1024]{1,0:T(8,128)(2,1)S(1)}, bf16[136,1024]{1,0:T(8,128)(2,1)S(1)}, u32[]{:S(2)}, u32[]{:S(2)}) collective-permute-start(bf16[136,1024]{1,0:T(8,128)(2,1)S(1)} %get-tuple-element.39), channel_id=1, source_target_pairs={{0,2},{2,0},{4,6},{6,4},{8,10},{10,8},{12,14},{14,12},{1,3},{3,1},... | collective-permute-start | bytes 835592 | tf_op jit(solution)/shard_map/ppermute | solution.py:39
  29.9 16.9 %collective-permute-start.9 = (bf16[136,1024]{1,0:T(8,128)(2,1)S(1)}, bf16[136,1024]{1,0:T(8,128)(2,1)S(1)}, u32[]{:S(2)}, u32[]{:S(2)}) collective-permute-start(bf16[136,1024]{1,0:T(8,128)(2,1)S(1)} %get-tuple-element.41.refs_3_.refs_2_), channel_id=1, source_target_pairs={{0,8},{2,10},{4,12},{6,14},{8,0},{10,2},{12,4},{14,6},{1,9},{3,11}... | collective-permute-start | bytes 835592 | tf_op jit(solution)/shard_map/ppermute | solution.py:39
  36.6 9.5 %collective-permute-start.8 = (bf16[128,1024]{1,0:T(8,128)(2,1)S(1)}, bf16[128,1024]{1,0:T(8,128)(2,1)S(1)}, u32[]{:S(2)}, u32[]{:S(2)}) collective-permute-start(bf16[128,1024]{1,0:T(8,128)(2,1)S(1)} %resent.1.refs_3_), channel_id=1, source_target_pairs={{0,4},{2,6},{4,0},{6,2},{8,12},{10,14},{12,8},{14,10},{1,5},{3,7},... | collective-permute-start | bytes 786440 | tf_op jit(solution)/shard_map/ppermute | solution.py:39

commit v10 on v9

--- a/solution.py
+++ b/solution.py
@@ -225,10 +225,6 @@
 def tails_of(sent, arrived, here):
     zeros = jnp.zeros((LANES - LAGS, here.stop - here.start), jnp.bfloat16)
     return jnp.concatenate([arrived[:LAGS, here], zeros, sent[:LAGS, here], zeros], axis=0)
-
-
-def boundary_of(edges, sent, arrived, here):
-    return jnp.dot(edges[...], tails_of(sent, arrived, here), preferred_element_type=jnp.float32)
 
 
 def first_products_kernel(held, power, own, other, keep, send, shifted):
@@ -255,7 +251,7 @@
     return [pltpu.VMEM((groups * GROUP * REF, rows), jnp.bfloat16)]
 
 
-def first_products(held, power, own, other, chunk):
+def first_products(held, power, own, other, chunk, after):
     rows, width = held.shape
     return call_on_blocks(
         first_products_kernel,
@@ -266,45 +262,41 @@
         other,
         name="first_products",
         micros=PRODUCT_MICROS,
+        after=after,
         scratch=shifted_scratch(rows),
     )
 
 
-def later_products(groups, held, own, other, powers, chunk, tails=(), after=()):
+def later_products(groups, held, own, other, powers, chunk, spare=0, after=()):
     rows, width = held.shape
 
     def kernel(held, own, other, powers, *rest):
-        sides, rest = rest[: len(tails)], rest[len(tails) :]
-        outs, shifted, edges = rest[:-2], rest[-2], rest[-1]
+        outs, shifted = rest[:-1], rest[-1]
         _, ref_powers, bound = sent_powers(powers)
         refs = ref_column(ref_powers)
         for index, bits in enumerate(groups):
             lag_rows(own, other, own_group(bits), shifted.at[pl.ds(index * 2 * chunk, 2 * chunk)])
-            if sides:
-                boundary_rows(own_group(bits), (own, other), ends_of(sides[1]), edges.at[index])
+            if spare:
+                outs[2 * index + 1][chunk:] = jnp.zeros((spare, width), jnp.bfloat16)
         for here in columns(width):
             product = product_of(shifted, held, here)
             for index in range(len(groups)):
                 keep, send = outs[2 * index : 2 * index + 2]
                 first = 2 * index * chunk
-                kept = product[first : first + chunk]
-                if sides:
-                    kept += boundary_of(edges.at[index], *sides, here)
-                keep[:, here] = kept
-                send[:, here] = coded(product[first + chunk : first + 2 * chunk], bound[:, here], refs)
+                keep[:, here] = product[first : first + chunk]
+                send[:chunk, here] = coded(product[first + chunk : first + 2 * chunk], bound[:, here], refs)
 
     return call_on_blocks(
         kernel,
-        [((chunk, width), jnp.float32), ((chunk, width), jnp.bfloat16)] * len(groups),
+        [((chunk, width), jnp.float32), ((chunk + spare, width), jnp.bfloat16)] * len(groups),
         held,
         own,
         other,
         powers,
-        *tails,
         name="later_products",
         micros=PRODUCT_MICROS,
         after=after,
-        scratch=shifted_scratch(rows, len(groups)) + edges_scratch(len(groups), chunk),
+        scratch=shifted_scratch(rows, len(groups)),
     )
 
 
@@ -312,27 +304,23 @@
     return [pltpu.VMEM((count, chunk, 2 * LANES), jnp.bfloat16)]
 
 
-def sides_to_swap(head, after_next, own, other, held_back):
-    def kernel(head, after_next, own, other, held_back, sides, passed):
+def sides_to_swap(head, after_next, own, other):
+    width = head.shape[1]
+
+    def kernel(head, after_next, own, other, sides):
         chan, near = lax.axis_index("chan"), lax.axis_index("tm") & 1
-        passed[...] = widened(held_back[...], LAGS)
         sides[:LAGS] = jnp.where(near == 0, after_next[...], head[...])
-        ours, theirs = [
-            refs[:, refs.shape[1] - LANES :].astype(jnp.float32) for refs in (own, other)
-        ]
+        ours, theirs = [refs[:, refs.shape[1] - LANES :].astype(jnp.float32) for refs in (own, other)]
         first, second = jnp.where(chan == 0, ours, theirs), jnp.where(chan == 0, theirs, ours)
         square = jnp.concatenate([first, second, jnp.zeros((LANES - REF, LANES), jnp.float32)], axis=0)
         sides[LAGS:, :LANES] = square.T[LANES - LAGS :].astype(jnp.bfloat16)
-        sides[LAGS:, LANES:] = jnp.zeros((LAGS, head.shape[1] - LANES), jnp.bfloat16)
-
-    rows, width = held_back.shape
-    outs = [((2 * LAGS, width), jnp.bfloat16), ((rows + LAGS, width), jnp.bfloat16)]
-    return call_on_blocks(
-        kernel, outs, head, after_next, own, other, held_back, name="sides", micros=MERGE_MICROS
-    )
-
-
-def with_boundaries(keeps, groups, own, other, sent, arrived, after):
+        sides[LAGS:, LANES:] = jnp.zeros((LAGS, width - LANES), jnp.bfloat16)
+
+    outs = [((2 * LAGS, width), jnp.bfloat16)]
+    return call_on_blocks(kernel, outs, head, after_next, own, other, name="sides", micros=MERGE_MICROS)[0]
+
+
+def with_boundaries(keeps, groups, own, other, sent, arrived):
     chunk, width = keeps[0].shape
 
     def kernel(own, other, sent, arrived, *rest):
@@ -358,7 +346,6 @@
         *keeps,
         name="with_boundaries",
         micros=MERGE_MICROS,
-        after=after,
         scratch=edges_scratch(len(groups), chunk),
     )
 
@@ -386,10 +373,6 @@
     _, refs, bound = sent_powers(powers)
     chunk = direct.shape[0] // REF * REF
     return expanded(direct[:chunk], bound, ref_column(refs))
-
-
-def widened(code, rows):
-    return jnp.concatenate([code, jnp.zeros((rows, code.shape[1]), code.dtype)], axis=0)
 
 
 def merged(keep, ours, theirs, direct=(), beyond=(), held_back=(), after=()):
@@ -406,12 +389,12 @@
         if beyond:
             sum_bound += inputs[len(direct)][...]
         if held_back:
-            passed[0][...] = widened(inputs[-1][...], EXTRA)
+            passed[0][...] = inputs[-1][...]
         sum_bound = rounded_up(sum_bound)
         out[chunk:] = packed(sums, sum_refs, sum_bound)
         out[:chunk] = coded(total, sum_bound, ref_column(sum_refs))
 
-    outs = [((chunk + EXTRA, width), jnp.bfloat16)] * (1 + len(held_back))
+    outs = [((chunk + EXTRA, width), jnp.bfloat16)] + [(code.shape, code.dtype) for code in held_back]
     arrays = (keep, ours, theirs, *direct, *beyond, *held_back)
     return call_on_blocks(kernel, outs, *arrays, name="merged", micros=MERGE_MICROS, after=after)
 
@@ -426,29 +409,19 @@
     return call_on_blocks(kernel, outs, *arrays, name="resent", micros=MERGE_MICROS, after=after)[0]
 
 
-def added(keep, direct, direct_powers, near, near_powers, held, sides, size, after):
-    rows, width = held.shape
-
-    def kernel(keep, direct, direct_powers, near, near_powers, held, sides, out, edge):
+def added(keep, direct, direct_powers, near, near_powers, after):
+    def kernel(keep, direct, direct_powers, near, near_powers, out):
         out[...] = keep[...] + direct_sums(direct, direct_powers) + direct_sums(near, near_powers)
-        last = held[rows - LAGS :, :size].astype(jnp.float32)
-        beyond = sides[:LAGS, :size].astype(jnp.float32)
-        place = lax.broadcasted_iota(jnp.int32, last.shape, 0)
-        sums = [jnp.zeros((1, size), jnp.float32)]
-        for lag in range(1, LAGS):
-            pairs = jnp.where(place >= LAGS - lag, last * pltpu.roll(beyond, LAGS - lag, 0), 0.0)
-            sums.append(jnp.sum(pairs, axis=0, keepdims=True))
-        edge[...] = jnp.concatenate(sums, axis=0)
-
-    outs = [(keep.shape, jnp.float32), ((LAGS, size), jnp.float32)]
-    arrays = (keep, direct, direct_powers, near, near_powers, held, sides)
-    return call_on_blocks(kernel, outs, *arrays, name="added", micros=MERGE_MICROS, after=after)
-
-
-def finished(slab_rows, segment, partial, edge, ours, theirs, autos):
+
+    outs = [(keep.shape, jnp.float32)]
+    arrays = (keep, direct, direct_powers, near, near_powers)
+    return call_on_blocks(kernel, outs, *arrays, name="added", micros=MERGE_MICROS, after=after)[0]
+
+
+def finished(slab_rows, segment, partial, ours, theirs, autos):
     chunk, width = partial.shape
 
-    def kernel(partial, edge, ours, theirs, *refs):
+    def kernel(partial, ours, theirs, *refs):
         autos, (covariance, segment_auto) = refs[:-2], refs[-2:]
         first_lag = lax.axis_index("tm").astype(jnp.int32) * (chunk // REF)
         lag = lax.broadcasted_iota(jnp.int32, (chunk, 1), 0) // REF + first_lag
@@ -462,8 +435,7 @@
         first = 0
         for auto in autos:
             here = slice(first, first + auto.shape[1])
-            sums = auto[...] + edge[...] if first == 0 else auto[...]
-            segment_auto[:, here] = sums * (scale[:, here] * scale[:, here]) / segment
+            segment_auto[:, here] = auto[...] * (scale[:, here] * scale[:, here]) / segment
             first = here.stop
 
     outs = [(partial.shape, jnp.float32), ((LAGS, width), jnp.float32)]
@@ -471,7 +443,6 @@
         kernel,
         outs,
         partial,
-        edge,
         ours,
         theirs,
         *autos,
@@ -493,8 +464,6 @@
             wide[part * pitch : part * pitch + step, :] = held[end - step : end, here].astype(jnp.float32)
             if part < 7:
                 following = held[end : end + LAGS, here].astype(jnp.float32)
-            elif tail is None:
-                following = jnp.zeros((LAGS, LANES), jnp.float32)
             else:
                 following = tail[:LAGS, here].astype(jnp.float32)
             wide[part * pitch + step : (part + 1) * pitch, :] = following
@@ -516,18 +485,16 @@
 
 def segment_rows(held, power, tail, first, size, after=()):
     rows = held.shape[0]
-    arrays = (held, power) if tail is None else (held, power, tail)
 
     def kernel(*refs):
-        held, power, *rest = refs
-        if tail is None:
-            rest = [None] + rest
-        segment_kernel(first, held, power, *rest)
+        segment_kernel(first, *refs)
 
     return call_on_blocks(
         kernel,
         [((LAGS, size), jnp.float32)],
-        *arrays,
+        held,
+        power,
+        tail,
         name="segment_rows",
         micros=SEGMENT_MICROS,
         after=after,
@@ -580,39 +547,41 @@
     own, head = prepared(strain)
     other = exchanged(own, "chan", 1)
     held, power = loaded(strain, own)
-    size = width // 4
+    size = width // 2
 
     if chunk * 2 == GROUP * REF:
-        keep6, send7 = first_products(held, power, own, other, chunk)
+        after_next = from_pair_ahead(head)
+        keep6, send7 = first_products(held, power, own, other, chunk, after=(after_next,))
         got7 = exchanged(send7, "tm", 1)
-        after_next = from_pair_ahead(head)
-        keep4, send5 = later_products((2,), held, own, other, send7, chunk)
-        sides, send5 = sides_to_swap(head, after_next, own, other, send5)
+        keep4, send5 = later_products((2,), held, own, other, send7, chunk, spare=LAGS)
         got5 = exchanged(send5, "tm", 1)
+        sides = sides_to_swap(head, after_next, own, other)
         tails = (sides, exchanged(sides, "tm", 1))
-        autos = [segment_rows(held, power, None, 0, size, after=(sides,))]
-        keep6, keep4, beyond = with_boundaries((keep6, keep4), (3, 2), own, other, *tails, after=(autos[0],))
-        (send6,) = merged(keep6, send7, got7, beyond=(beyond,))
+        keep2, send3, keep0, send1 = later_products(
+            (1, 0), held, own, other, send7, chunk, after=(send5, sides)
+        )
+        *keeps, beyond = with_boundaries((keep6, keep4, keep2, keep0), (3, 2, 1, 0), own, other, *tails)
+        keep6, keep4, keep2, keep0 = keeps
+        send6, send3 = merged(keep6, send7, got7, beyond=(beyond,), held_back=(send3,))
         got6 = exchanged(send6, "tm", 2)
-        keep2, send3, keep0, send1 = later_products(
-            (1, 0), held, own, other, send7, chunk, tails=tails, after=(send6,)
+        got3 = exchanged(send3, "tm", 1)
+        autos = [segment_rows(held, power, tails[1], 0, size, after=(send6,))]
+        send4, send1 = merged(
+            keep4, send6, got6, direct=(got5, got7), held_back=(send1,), after=(autos[0],)
         )
-        got3 = exchanged(send3, "tm", 1)
-        send4, send1 = merged(keep4, send6, got6, direct=(got5, got7), held_back=(send1,), after=(send3,))
         got4 = exchanged(send4, "tm", 4)
         got1 = exchanged(send1, "tm", 1)
-        autos.append(segment_rows(held, power, tails[1], size, size, after=(send4,)))
-        send2 = resent(keep2, got3, got7, send6, after=(autos[1],))
+        send2 = resent(keep2, got3, got7, send6, after=(send4,))
         got2 = exchanged(send2, "tm", 2)
-        autos.append(segment_rows(held, power, tails[1], 2 * size, 2 * size, after=(send2,)))
-        partial, edge = added(keep0, got1, got7, got2, got6, held, tails[1], size, after=(autos[2],))
-        return tuple(finished(slab_rows, rows, partial, edge, send4, got4, autos))
+        autos.append(segment_rows(held, power, tails[1], size, size, after=(send2,)))
+        partial = added(keep0, got1, got7, got2, got6, after=(autos[1],))
+        return tuple(finished(slab_rows, rows, partial, send4, got4, autos))
 
     tail = passed_along(head, "tm", -1)
     chan = lax.axis_index("chan").astype(jnp.int32)
     time = lax.axis_index("tm").astype(jnp.int32)
     auto = jnp.concatenate(
-        [segment_rows(held, power, tail, size * index, size) for index in range(4)], axis=1
+        [segment_rows(held, power, tail, size * index, size) for index in range(2)], axis=1
     )
     power_other = jnp.sum(jnp.square(other.astype(jnp.float32)), axis=1)
     power = lax.psum(jnp.concatenate([power[0], power_other]), "tm")

time: 48.1 us -> 47.8 us (level)
  starting transfers between devices: 12.4 us -> 11.2 us
  waiting for transfers between devices: 8.66 us -> 9.27 us
    ppermute x9, starting transfers between devices: 10.9 us -> 9.93 us  [exchanged(): lax.ppermute(value, axis, [(source, source ^ bit) for source in range(cou...]
    ppermute x1, waiting for transfers between devices: 2.33 us -> 2.97 us  [from_pair_ahead(): lax.ppermute(value, 'tm', [(time + 2, time) for time in range(0, count -...]
    pallas_call x13 -> x12, Pallas kernels: 22.6 us -> 22.9 us  [call_on_blocks(): pl.pallas_call(body, in_specs=[vmem] * count + [pl.BlockSpec(memory_space...]
  transfers between devices with their start and end apart: 10 -> 10, of which waited for: 5 -> 3; matrix products, arithmetic and copies ran while one was open for 0% -> 0% of each run, Pallas kernels for 45% -> 46%
where the time goes in v10:
time: 47.8 us; the launch traced here: 47.7 us
  Pallas kernels  26.4 us (55%)
  starting transfers between devices  11.2 us (23%)
  waiting for transfers between devices  9.27 us (19%)
  between operations  0.77 us (2%)
    pallas_call x12, Pallas kernels, call_on_blocks(): pl.pallas_call(body, in_specs=[vmem] * count + [pl.BlockSpec(memory_space...  22.9 us
    ppermute x9, starting transfers between devices, exchanged(): lax.ppermute(value, axis, [(source, source ^ bit) for source in range(cou...  9.93 us
    ppermute x9, waiting for transfers between devices, exchanged(): lax.ppermute(value, axis, [(source, source ^ bit) for source in range(cou...  6.3 us
    ppermute x1, waiting for transfers between devices, from_pair_ahead(): lax.ppermute(value, 'tm', [(time + 2, time) for time in range(0, count -...  2.97 us
    pallas_call x1, Pallas kernels, loaded(): pl.pallas_call(kernel, in_specs=[pl.BlockSpec(memory_space=pl.ANY)] * 2,...  2.26 us
    ppermute x1, starting transfers between devices, from_pair_ahead(): lax.ppermute(value, 'tm', [(time + 2, time) for time in range(0, count -...  1.28 us
    pallas_call x1, Pallas kernels, prepared(): pl.pallas_call(prepare_kernel, in_specs=[pl.BlockSpec(memory_space=pl.ANY...  1.28 us
  transfers between devices with their start and end apart: 10, of which 3 were waited for; matrix products, arithmetic and copies ran while one was open for 0% of the time, Pallas kernels for 46%

profile of v10, /device:TPU:0, one launch (start us, length us, event | category | flops | bytes accessed | tf_op | source)
XLA Modules:
  0.0 47.7 jit_solution(15444365104963564363)
XLA Ops:
  0.6 1.3 %prepared.1 = (bf16[32,2048]{1,0:T(8,128)(2,1)S(1)}, bf16[16,1024]{1,0:T(8,128)(2,1)S(1)}) custom-call(bf16[2048,1024]{1,0:T(8,128)(2,1)} %strain.3), custom_call_target="tpu_custom_call" | custom-call | bytes 3690000 | tf_op jit(solution)/shard_map/prepared/pallas_call | solution.py:131
  1.9 0.5 %collective-permute-start = (bf16[32,2048]{1,0:T(8,128)(2,1)S(1)}, bf16[32,2048]{1,0:T(8,128)(2,1)S(1)}, u32[]{:S(2)}, u32[]{:S(2)}) collective-permute-start(bf16[32,2048]{1,0:T(8,128)(2,1)S(1)} %get-tuple-element.23.refs_2_.after.refs_1_.refs_0_), channel_id=1, source_target_pairs={{0,1},{1,0},{2,3},{3,2},{4,5},{5,4},{6,7},{7,6},{8,9},{9,8},{10,11... | collective-permute-start | bytes 393224 | tf_op jit(solution)/shard_map/ppermute | solution.py:39
  2.4 1.3 %collective-permute-start.1 = (bf16[16,1024]{1,0:T(8,128)(2,1)S(1)}, bf16[16,1024]{1,0:T(8,128)(2,1)S(1)}, u32[]{:S(2)}, u32[]{:S(2)}) collective-permute-start(bf16[16,1024]{1,0:T(8,128)(2,1)S(1)} %get-tuple-element.24.refs_0_), channel_id=1, source_target_pairs={{4,0},{8,4},{12,8},{5,1},{9,5},{13,9},{20,16},{24,20},{28,24},{21,... | collective-permute-start | bytes 98312 | tf_op jit(solution)/shard_map/ppermute | solution.py:538
  3.7 2.3 %loaded.1 = (bf16[2048,1024]{1,0:T(8,128)(2,1)S(1)}, f32[1,1024]{1,0:T(1,128)S(1)}) custom-call(bf16[2048,1024]{1,0:T(8,128)(2,1)} %strain.3, bf16[32,2048]{1,0:T(8,128)(2,1)S(1)} %get-tuple-element.23.refs_2_.after.refs_1_.refs_0_), custom_call_target="tpu_custom_call" | custom-call | bytes 3690000 | tf_op jit(solution)/shard_map/loaded/pallas_call | solution.py:185
  6.0 3.0 %collective-permute-done.1.refs_1_.refs_4_ = bf16[16,1024]{1,0:T(8,128)(2,1)S(1)} collective-permute-done((bf16[16,1024]{1,0:T(8,128)(2,1)S(1)}, bf16[16,1024]{1,0:T(8,128)(2,1)S(1)}, u32[]{:S(2)}, u32[]{:S(2)}) %collective-permute-start.1) | collective-permute-done | bytes 32800 | tf_op jit(solution)/shard_map/ppermute | solution.py:538
  9.0 0.0 collective-permute-done.refs_3_.refs_2_.refs_1_
  9.0 2.0 %first_products.1 = (f32[128,1024]{1,0:T(8,128)S(1)}, bf16[136,1024]{1,0:T(8,128)(2,1)S(1)}) custom-call(bf16[2048,1024]{1,0:T(8,128)(2,1)S(1)} %get-tuple-element.25.refs_0_, f32[1,1024]{1,0:T(1,128)S(1)} %get-tuple-element.26.refs_1_, bf16[32,2048]{1,0:T(8,128)(2,1)S(1)} %get-tuple-element.23.refs_2_.after.refs_1_.refs_0_, ...), custom_call_target="tpu_custom_call" | custom-call | bytes 3690000 | tf_op jit(solution)/shard_map/first_products/pallas_call | solution.py:360
  11.0 0.1 collective-permute-start.3
  11.1 0.1 sides.1.refs_5_.refs_2_
  11.2 2.1 %collective-permute-start.2 = (bf16[32,1024]{1,0:T(8,128)(2,1)S(1)}, bf16[32,1024]{1,0:T(8,128)(2,1)S(1)}, u32[]{:S(2)}, u32[]{:S(2)}) collective-permute-start(bf16[32,1024]{1,0:T(8,128)(2,1)S(1)} %sides.1.refs_5_.refs_2_), channel_id=1, source_target_pairs={{0,2},{2,0},{4,6},{6,4},{8,10},{10,8},{12,14},{14,12},{1,3},{3,1},... | collective-permute-start | bytes 196616 | tf_op jit(solution)/shard_map/ppermute | solution.py:39
  13.3 2.0 %later_products.2 = (f32[128,1024]{1,0:T(8,128)S(1)}, bf16[144,1024]{1,0:T(8,128)(2,1)S(1)}) custom-call(bf16[2048,1024]{1,0:T(8,128)(2,1)S(1)} %get-tuple-element.25.refs_0_, bf16[32,2048]{1,0:T(8,128)(2,1)S(1)} %get-tuple-element.23.refs_2_.after.refs_1_.refs_0_, bf16[32,2048]{1,0:T(8,128)(2,1)S(1)} %collective-permute-done.refs_3_.refs_2_.refs_1_, ...), custom_call_target="tpu_custom_call" | custom-call | bytes 3690000 | tf_op jit(solution)/shard_map/later_products/pallas_call | solution.py:360
  15.3 0.1 collective-permute-start.5
  15.3 3.7 %later_products.3 = (f32[128,1024]{1,0:T(8,128)S(1)}, bf16[128,1024]{1,0:T(8,128)(2,1)S(1)}, f32[128,1024]{1,0:T(8,128)S(1)}, bf16[128,1024]{1,0:T(8,128)(2,1)S(1)}) custom-call(bf16[2048,1024]{1,0:T(8,128)(2,1)S(1)} %get-tuple-element.25.refs_0_, bf16[32,2048]{1,0:T(8,128)(2,1)S(1)} %get-tuple-element.23.refs_2_.after.refs_1_.refs_0_, ...), custom_call_target="tpu_custom_call" | custom-call | bytes 3690000 | tf_op jit(solution)/shard_map/later_products/pallas_call | solution.py:360
  19.0 3.0 %collective-permute-done.2.refs_3_.refs_2_ = bf16[32,1024]{1,0:T(8,128)(2,1)S(1)} collective-permute-done((bf16[32,1024]{1,0:T(8,128)(2,1)S(1)}, bf16[32,1024]{1,0:T(8,128)(2,1)S(1)}, u32[]{:S(2)}, u32[]{:S(2)}) %collective-permute-start.2) | collective-permute-done | bytes 65568 | tf_op jit(solution)/shard_map/ppermute | solution.py:39
  22.0 0.7 %with_boundaries.1 = (f32[128,1024]{1,0:T(8,128)S(1)}, f32[128,1024]{1,0:T(8,128)S(1)}, f32[128,1024]{1,0:T(8,128)S(1)}, f32[128,1024]{1,0:T(8,128)S(1)}, f32[1,1024]{1,0:T(1,128)S(1)}) custom-call(bf16[32,2048]{1,0:T(8,128)(2,1)S(1)} %get-tuple-element.23.refs_2_.after.refs_1_.refs_0_, bf16[32,2048]{1,0:T(8,128)(2,1)S(1)} %collective-permute-done.refs_3_.refs_2_.refs_1_, ...), custom_call_target="tpu_custom_call" | custom-call | bytes 1107000 | tf_op jit(solution)/shard_map/with_boundaries/pallas_call | solution.py:360
  22.7 0.0 collective-permute-done.3.refs_2_.refs_4_
  22.7 0.6 %merged.2 = (bf16[136,1024]{1,0:T(8,128)(2,1)S(1)}, bf16[128,1024]{1,0:T(8,128)(2,1)S(1)}) custom-call(f32[128,1024]{1,0:T(8,128)S(1)} %get-tuple-element.35.refs_0_, bf16[136,1024]{1,0:T(8,128)(2,1)S(1)} %get-tuple-element.28.refs_3_.refs_1_, bf16[136,1024]{1,0:T(8,128)(2,1)S(1)} %collective-permute-done.3.refs_2_.refs_4_, ...), custom_call_target="tpu_custom_call" | custom-call | bytes 1107000 | tf_op jit(solution)/shard_map/merged/pallas_call | solution.py:360
  23.3 2.0 %collective-permute-start.4 = (bf16[136,1024]{1,0:T(8,128)(2,1)S(1)}, bf16[136,1024]{1,0:T(8,128)(2,1)S(1)}, u32[]{:S(2)}, u32[]{:S(2)}) collective-permute-start(bf16[136,1024]{1,0:T(8,128)(2,1)S(1)} %get-tuple-element.38.refs_3_.refs_1_), channel_id=1, source_target_pairs={{0,4},{2,6},{4,0},{6,2},{8,12},{10,14},{12,8},{14,10},{1,5},{3,7},... | collective-permute-start | bytes 835592 | tf_op jit(solution)/shard_map/ppermute | solution.py:39
  25.3 0.0 collective-permute-start.7
  25.3 5.5 %segment_rows.2.refs_6_.refs_3_ = f32[16,512]{1,0:T(8,128)S(1)} custom-call(bf16[2048,1024]{1,0:T(8,128)(2,1)S(1)} %get-tuple-element.25.refs_0_, f32[1,1024]{1,0:T(1,128)S(1)} %get-tuple-element.26.refs_1_, bf16[32,1024]{1,0:T(8,128)(2,1)S(1)} %collective-permute-done.2.refs_3_.refs_2_, bf16[136,1024]{1,0:T(8,128)(2,1)S(1)} %get-tuple-element.38.refs_3_.refs_1_), custom_call_target="tpu_custom_call" | custom-call | bytes 4428000 | tf_op jit(solution)/shard_map/segment_rows/pallas_call | solution.py:360
  30.8 0.0 collective-permute-done.5.refs_3_
  30.8 0.0 collective-permute-done.4.refs_2_.refs_4_
  30.8 0.8 %merged.3 = (bf16[136,1024]{1,0:T(8,128)(2,1)S(1)}, bf16[128,1024]{1,0:T(8,128)(2,1)S(1)}) custom-call(f32[128,1024]{1,0:T(8,128)S(1)} %get-tuple-element.34.refs_0_, bf16[136,1024]{1,0:T(8,128)(2,1)S(1)} %get-tuple-element.38.refs_3_.refs_1_, bf16[136,1024]{1,0:T(8,128)(2,1)S(1)} %collective-permute-done.4.refs_2_.refs_4_, ...), custom_call_target="tpu_custom_call" | custom-call | bytes 1107000 | tf_op jit(solution)/shard_map/merged/pallas_call | solution.py:360
  31.6 2.1 %collective-permute-start.9 = (bf16[136,1024]{1,0:T(8,128)(2,1)S(1)}, bf16[136,1024]{1,0:T(8,128)(2,1)S(1)}, u32[]{:S(2)}, u32[]{:S(2)}) collective-permute-start(bf16[136,1024]{1,0:T(8,128)(2,1)S(1)} %get-tuple-element.43.refs_4_.refs_1_), channel_id=1, source_target_pairs={{0,8},{2,10},{4,12},{6,14},{8,0},{10,2},{12,4},{14,6},{1,9},{3,11}... | collective-permute-start | bytes 835592 | tf_op jit(solution)/shard_map/ppermute | solution.py:39
  33.7 0.0 collective-permute-done.7.refs_1_
  33.7 0.5 %resent.1.refs_3_ = bf16[128,1024]{1,0:T(8,128)(2,1)S(1)} custom-call(f32[128,1024]{1,0:T(8,128)S(1)} %get-tuple-element.41.refs_0_, bf16[128,1024]{1,0:T(8,128)(2,1)S(1)} %collective-permute-done.7.refs_1_, bf16[136,1024]{1,0:T(8,128)(2,1)S(1)} %collective-permute-done.3.refs_2_.refs_4_, bf16[136,1024]{1,0:T(8,128)(2,1)S(1)} %get-tuple-element.38.refs_3_.refs_1_, ...), custom_call_target="tpu_custom_call" | custom-call | bytes 1107000 | tf_op jit(solution)/shard_map/resent/pallas_call | solution.py:360
  34.2 1.1 %collective-permute-start.8 = (bf16[128,1024]{1,0:T(8,128)(2,1)S(1)}, bf16[128,1024]{1,0:T(8,128)(2,1)S(1)}, u32[]{:S(2)}, u32[]{:S(2)}) collective-permute-start(bf16[128,1024]{1,0:T(8,128)(2,1)S(1)} %resent.1.refs_3_), channel_id=1, source_target_pairs={{0,4},{2,6},{4,0},{6,2},{8,12},{10,14},{12,8},{14,10},{1,5},{3,7},... | collective-permute-start | bytes 786440 | tf_op jit(solution)/shard_map/ppermute | solution.py:39
  35.3 2.0 %collective-permute-start.6 = (bf16[128,1024]{1,0:T(8,128)(2,1)S(1)}, bf16[128,1024]{1,0:T(8,128)(2,1)S(1)}, u32[]{:S(2)}, u32[]{:S(2)}) collective-permute-start(bf16[128,1024]{1,0:T(8,128)(2,1)S(1)} %get-tuple-element.40), channel_id=1, source_target_pairs={{0,2},{2,0},{4,6},{6,4},{8,10},{10,8},{12,14},{14,12},{1,3},{3,1},... | collective-permute-start | bytes 786440 | tf_op jit(solution)/shard_map/ppermute | solution.py:39
  37.3 5.3 %segment_rows.3.refs_5_.refs_4_ = f32[16,512]{1,0:T(8,128)S(1)} custom-call(bf16[2048,1024]{1,0:T(8,128)(2,1)S(1)} %get-tuple-element.25.refs_0_, f32[1,1024]{1,0:T(1,128)S(1)} %get-tuple-element.26.refs_1_, bf16[32,1024]{1,0:T(8,128)(2,1)S(1)} %collective-permute-done.2.refs_3_.refs_2_, bf16[128,1024]{1,0:T(8,128)(2,1)S(1)} %resent.1.refs_3_), custom_call_target="tpu_custom_call" | custom-call | bytes 4428000 | tf_op jit(solution)/shard_map/segment_rows/pallas_call | solution.py:360
  42.6 3.3 %collective-permute-done.8.refs_3_ = bf16[128,1024]{1,0:T(8,128)(2,1)S(1)} collective-permute-done((bf16[128,1024]{1,0:T(8,128)(2,1)S(1)}, bf16[128,1024]{1,0:T(8,128)(2,1)S(1)}, u32[]{:S(2)}, u32[]{:S(2)}) %collective-permute-start.8) | collective-permute-done | bytes 262176 | tf_op jit(solution)/shard_map/ppermute | solution.py:39
  45.9 0.0 collective-permute-done.6.refs_1_
  45.9 0.5 %added.1.refs_0_ = f32[128,1024]{1,0:T(8,128)S(1)} custom-call(f32[128,1024]{1,0:T(8,128)S(1)} %get-tuple-element.33.refs_0_, bf16[128,1024]{1,0:T(8,128)(2,1)S(1)} %collective-permute-done.6.refs_1_, bf16[136,1024]{1,0:T(8,128)(2,1)S(1)} %collective-permute-done.3.refs_2_.refs_4_, bf16[128,1024]{1,0:T(8,128)(2,1)S(1)} %collective-permute-done.8.refs_3_, ...), custom_call_target="tpu_custom_call" | custom-call | bytes 1107000 | tf_op jit(solution)/shard_map/added/pallas_call | solution.py:360
  46.4 0.0 collective-permute-done.9.refs_2_
  46.5 1.2 %finished.1 = (f32[128,1024]{1,0:T(8,128)}, f32[16,1024]{1,0:T(8,128)}) custom-call(f32[128,1024]{1,0:T(8,128)S(1)} %added.1.refs_0_, bf16[136,1024]{1,0:T(8,128)(2,1)S(1)} %get-tuple-element.43.refs_4_.refs_1_, bf16[136,1024]{1,0:T(8,128)(2,1)S(1)} %collective-permute-done.9.refs_2_, f32[16,512]{1,0:T(8,128)S(1)} %segment_rows.2.refs_6_.refs_3_, ...), custom_call_target="tpu_custom_call" | custom-call | bytes 1107000 | tf_op jit(solution)/shard_map/finished/pallas_call | solution.py:360
Async XLA Ops:
  1.9 7.0 %collective-permute-start = (bf16[32,2048]{1,0:T(8,128)(2,1)S(1)}, bf16[32,2048]{1,0:T(8,128)(2,1)S(1)}, u32[]{:S(2)}, u32[]{:S(2)}) collective-permute-start(bf16[32,2048]{1,0:T(8,128)(2,1)S(1)} %get-tuple-element.23.refs_2_.after.refs_1_.refs_0_), channel_id=1, source_target_pairs={{0,1},{1,0},{2,3},{3,2},{4,5},{5,4},{6,7},{7,6},{8,9},{9,8},{10,11... | collective-permute-start | bytes 393224 | tf_op jit(solution)/shard_map/ppermute | solution.py:39
  2.4 6.5 %collective-permute-start.1 = (bf16[16,1024]{1,0:T(8,128)(2,1)S(1)}, bf16[16,1024]{1,0:T(8,128)(2,1)S(1)}, u32[]{:S(2)}, u32[]{:S(2)}) collective-permute-start(bf16[16,1024]{1,0:T(8,128)(2,1)S(1)} %get-tuple-element.24.refs_0_), channel_id=1, source_target_pairs={{4,0},{8,4},{12,8},{5,1},{9,5},{13,9},{20,16},{24,20},{28,24},{21,... | collective-permute-start | bytes 98312 | tf_op jit(solution)/shard_map/ppermute | solution.py:538
  11.0 11.7 %collective-permute-start.3 = (bf16[136,1024]{1,0:T(8,128)(2,1)S(1)}, bf16[136,1024]{1,0:T(8,128)(2,1)S(1)}, u32[]{:S(2)}, u32[]{:S(2)}) collective-permute-start(bf16[136,1024]{1,0:T(8,128)(2,1)S(1)} %get-tuple-element.28.refs_3_.refs_1_), channel_id=1, source_target_pairs={{0,2},{2,0},{4,6},{6,4},{8,10},{10,8},{12,14},{14,12},{1,3},{3,1},... | collective-permute-start | bytes 835592 | tf_op jit(solution)/shard_map/ppermute | solution.py:39
  11.2 10.8 %collective-permute-start.2 = (bf16[32,1024]{1,0:T(8,128)(2,1)S(1)}, bf16[32,1024]{1,0:T(8,128)(2,1)S(1)}, u32[]{:S(2)}, u32[]{:S(2)}) collective-permute-start(bf16[32,1024]{1,0:T(8,128)(2,1)S(1)} %sides.1.refs_5_.refs_2_), channel_id=1, source_target_pairs={{0,2},{2,0},{4,6},{6,4},{8,10},{10,8},{12,14},{14,12},{1,3},{3,1},... | collective-permute-start | bytes 196616 | tf_op jit(solution)/shard_map/ppermute | solution.py:39
  15.3 15.5 %collective-permute-start.5 = (bf16[144,1024]{1,0:T(8,128)(2,1)S(1)}, bf16[144,1024]{1,0:T(8,128)(2,1)S(1)}, u32[]{:S(2)}, u32[]{:S(2)}) collective-permute-start(bf16[144,1024]{1,0:T(8,128)(2,1)S(1)} %get-tuple-element.30.refs_4_), channel_id=1, source_target_pairs={{0,2},{2,0},{4,6},{6,4},{8,10},{10,8},{12,14},{14,12},{1,3},{3,1},... | collective-permute-start | bytes 884744 | tf_op jit(solution)/shard_map/ppermute | solution.py:39
  23.3 7.5 %collective-permute-start.4 = (bf16[136,1024]{1,0:T(8,128)(2,1)S(1)}, bf16[136,1024]{1,0:T(8,128)(2,1)S(1)}, u32[]{:S(2)}, u32[]{:S(2)}) collective-permute-start(bf16[136,1024]{1,0:T(8,128)(2,1)S(1)} %get-tuple-element.38.refs_3_.refs_1_), channel_id=1, source_target_pairs={{0,4},{2,6},{4,0},{6,2},{8,12},{10,14},{12,8},{14,10},{1,5},{3,7},... | collective-permute-start | bytes 835592 | tf_op jit(solution)/shard_map/ppermute | solution.py:39
  25.3 8.4 %collective-permute-start.7 = (bf16[128,1024]{1,0:T(8,128)(2,1)S(1)}, bf16[128,1024]{1,0:T(8,128)(2,1)S(1)}, u32[]{:S(2)}, u32[]{:S(2)}) collective-permute-start(bf16[128,1024]{1,0:T(8,128)(2,1)S(1)} %get-tuple-element.42), channel_id=1, source_target_pairs={{0,2},{2,0},{4,6},{6,4},{8,10},{10,8},{12,14},{14,12},{1,3},{3,1},... | collective-permute-start | bytes 786440 | tf_op jit(solution)/shard_map/ppermute | solution.py:39
  31.6 14.9 %collective-permute-start.9 = (bf16[136,1024]{1,0:T(8,128)(2,1)S(1)}, bf16[136,1024]{1,0:T(8,128)(2,1)S(1)}, u32[]{:S(2)}, u32[]{:S(2)}) collective-permute-start(bf16[136,1024]{1,0:T(8,128)(2,1)S(1)} %get-tuple-element.43.refs_4_.refs_1_), channel_id=1, source_target_pairs={{0,8},{2,10},{4,12},{6,14},{8,0},{10,2},{12,4},{14,6},{1,9},{3,11}... | collective-permute-start | bytes 835592 | tf_op jit(solution)/shard_map/ppermute | solution.py:39
  34.2 11.7 %collective-permute-start.8 = (bf16[128,1024]{1,0:T(8,128)(2,1)S(1)}, bf16[128,1024]{1,0:T(8,128)(2,1)S(1)}, u32[]{:S(2)}, u32[]{:S(2)}) collective-permute-start(bf16[128,1024]{1,0:T(8,128)(2,1)S(1)} %resent.1.refs_3_), channel_id=1, source_target_pairs={{0,4},{2,6},{4,0},{6,2},{8,12},{10,14},{12,8},{14,10},{1,5},{3,7},... | collective-permute-start | bytes 786440 | tf_op jit(solution)/shard_map/ppermute | solution.py:39
  35.3 10.6 %collective-permute-start.6 = (bf16[128,1024]{1,0:T(8,128)(2,1)S(1)}, bf16[128,1024]{1,0:T(8,128)(2,1)S(1)}, u32[]{:S(2)}, u32[]{:S(2)}) collective-permute-start(bf16[128,1024]{1,0:T(8,128)(2,1)S(1)} %get-tuple-element.40), channel_id=1, source_target_pairs={{0,2},{2,0},{4,6},{6,4},{8,10},{10,8},{12,14},{14,12},{1,3},{3,1},... | collective-permute-start | bytes 786440 | tf_op jit(solution)/shard_map/ppermute | solution.py:39

commit v11 on v10

--- a/solution.py
+++ b/solution.py
@@ -251,7 +251,7 @@
     return [pltpu.VMEM((groups * GROUP * REF, rows), jnp.bfloat16)]
 
 
-def first_products(held, power, own, other, chunk, after):
+def first_products(held, power, own, other, chunk):
     rows, width = held.shape
     return call_on_blocks(
         first_products_kernel,
@@ -262,12 +262,11 @@
         other,
         name="first_products",
         micros=PRODUCT_MICROS,
-        after=after,
         scratch=shifted_scratch(rows),
     )
 
 
-def later_products(groups, held, own, other, powers, chunk, spare=0, after=()):
+def later_products(groups, held, own, other, powers, chunk):
     rows, width = held.shape
 
     def kernel(held, own, other, powers, *rest):
@@ -276,26 +275,23 @@
         refs = ref_column(ref_powers)
         for index, bits in enumerate(groups):
             lag_rows(own, other, own_group(bits), shifted.at[pl.ds(index * 2 * chunk, 2 * chunk)])
-            if spare:
-                outs[2 * index + 1][chunk:] = jnp.zeros((spare, width), jnp.bfloat16)
         for here in columns(width):
             product = product_of(shifted, held, here)
             for index in range(len(groups)):
                 keep, send = outs[2 * index : 2 * index + 2]
                 first = 2 * index * chunk
                 keep[:, here] = product[first : first + chunk]
-                send[:chunk, here] = coded(product[first + chunk : first + 2 * chunk], bound[:, here], refs)
+                send[:, here] = coded(product[first + chunk : first + 2 * chunk], bound[:, here], refs)
 
     return call_on_blocks(
         kernel,
-        [((chunk, width), jnp.float32), ((chunk + spare, width), jnp.bfloat16)] * len(groups),
+        [((chunk, width), jnp.float32), ((chunk, width), jnp.bfloat16)] * len(groups),
         held,
         own,
         other,
         powers,
         name="later_products",
         micros=PRODUCT_MICROS,
-        after=after,
         scratch=shifted_scratch(rows, len(groups)),
     )
 
@@ -304,11 +300,13 @@
     return [pltpu.VMEM((count, chunk, 2 * LANES), jnp.bfloat16)]
 
 
-def sides_to_swap(head, after_next, own, other):
-    width = head.shape[1]
-
-    def kernel(head, after_next, own, other, sides):
+def sides_to_swap(head, after_next, own, other, held_back):
+    rows, width = held_back.shape
+
+    def kernel(head, after_next, own, other, held_back, sides, passed):
         chan, near = lax.axis_index("chan"), lax.axis_index("tm") & 1
+        passed[:rows] = held_back[...]
+        passed[rows:] = jnp.zeros((LAGS, width), jnp.bfloat16)
         sides[:LAGS] = jnp.where(near == 0, after_next[...], head[...])
         ours, theirs = [refs[:, refs.shape[1] - LANES :].astype(jnp.float32) for refs in (own, other)]
         first, second = jnp.where(chan == 0, ours, theirs), jnp.where(chan == 0, theirs, ours)
@@ -316,8 +314,9 @@
         sides[LAGS:, :LANES] = square.T[LANES - LAGS :].astype(jnp.bfloat16)
         sides[LAGS:, LANES:] = jnp.zeros((LAGS, width - LANES), jnp.bfloat16)
 
-    outs = [((2 * LAGS, width), jnp.bfloat16)]
-    return call_on_blocks(kernel, outs, head, after_next, own, other, name="sides", micros=MERGE_MICROS)[0]
+    outs = [((2 * LAGS, width), jnp.bfloat16), ((rows + LAGS, width), jnp.bfloat16)]
+    arrays = (head, after_next, own, other, held_back)
+    return call_on_blocks(kernel, outs, *arrays, name="sides", micros=MERGE_MICROS)
 
 
 def with_boundaries(keeps, groups, own, other, sent, arrived):
@@ -550,16 +549,15 @@
     size = width // 2
 
     if chunk * 2 == GROUP * REF:
+        keep6, send7 = first_products(held, power, own, other, chunk)
+        got7 = exchanged(send7, "tm", 1)
         after_next = from_pair_ahead(head)
-        keep6, send7 = first_products(held, power, own, other, chunk, after=(after_next,))
-        got7 = exchanged(send7, "tm", 1)
-        keep4, send5 = later_products((2,), held, own, other, send7, chunk, spare=LAGS)
+        keep4, send5, keep2, send3, keep0, send1 = later_products(
+            (2, 1, 0), held, own, other, send7, chunk
+        )
+        sides, send5 = sides_to_swap(head, after_next, own, other, send5)
+        tails = (sides, exchanged(sides, "tm", 1))
         got5 = exchanged(send5, "tm", 1)
-        sides = sides_to_swap(head, after_next, own, other)
-        tails = (sides, exchanged(sides, "tm", 1))
-        keep2, send3, keep0, send1 = later_products(
-            (1, 0), held, own, other, send7, chunk, after=(send5, sides)
-        )
         *keeps, beyond = with_boundaries((keep6, keep4, keep2, keep0), (3, 2, 1, 0), own, other, *tails)
         keep6, keep4, keep2, keep0 = keeps
         send6, send3 = merged(keep6, send7, got7, beyond=(beyond,), held_back=(send3,))

time: 47.8 us -> 48.6 us (1.017)
  starting transfers between devices: 11.2 us -> 14.6 us
  waiting for transfers between devices: 9.27 us -> 7.24 us
  Pallas kernels: 26.4 us -> 25.9 us
    ppermute x9, starting transfers between devices: 9.93 us -> 13.1 us  [exchanged(): lax.ppermute(value, axis, [(source, source ^ bit) for source in range(cou...]
    ppermute x1, waiting for transfers between devices: 2.97 us -> 0.01 us  [from_pair_ahead(): lax.ppermute(value, 'tm', [(time + 2, time) for time in range(0, count -...]
    ppermute x9, waiting for transfers between devices: 6.3 us -> 7.24 us  [exchanged(): lax.ppermute(value, axis, [(source, source ^ bit) for source in range(cou...]
    pallas_call x12 -> x11, Pallas kernels: 22.9 us -> 22.3 us  [call_on_blocks(): pl.pallas_call(body, in_specs=[vmem] * count + [pl.BlockSpec(memory_space...]
  transfers between devices with their start and end apart: 10 -> 10, of which waited for: 3 -> 2; matrix products, arithmetic and copies ran while one was open for 0% -> 0% of each run, Pallas kernels for 46% -> 44%
where the time goes in v11:
time: 48.6 us; the launch traced here: 48.5 us
  Pallas kernels  25.9 us (53%)
  starting transfers between devices  14.6 us (30%)
  waiting for transfers between devices  7.24 us (15%)
  between operations  0.78 us (2%)
    pallas_call x11, Pallas kernels, call_on_blocks(): pl.pallas_call(body, in_specs=[vmem] * count + [pl.BlockSpec(memory_space...  22.3 us
    ppermute x9, starting transfers between devices, exchanged(): lax.ppermute(value, axis, [(source, source ^ bit) for source in range(cou...  13.1 us
    ppermute x9, waiting for transfers between devices, exchanged(): lax.ppermute(value, axis, [(source, source ^ bit) for source in range(cou...  7.24 us
    pallas_call x1, Pallas kernels, loaded(): pl.pallas_call(kernel, in_specs=[pl.BlockSpec(memory_space=pl.ANY)] * 2,...  2.25 us
    ppermute x1, starting transfers between devices, from_pair_ahead(): lax.ppermute(value, 'tm', [(time + 2, time) for time in range(0, count -...  1.46 us
    pallas_call x1, Pallas kernels, prepared(): pl.pallas_call(prepare_kernel, in_specs=[pl.BlockSpec(memory_space=pl.ANY...  1.28 us
  transfers between devices with their start and end apart: 10, of which 2 were waited for; matrix products, arithmetic and copies ran while one was open for 0% of the time, Pallas kernels for 44%

profile of v11, /device:TPU:0, one launch (start us, length us, event | category | flops | bytes accessed | tf_op | source)
XLA Modules:
  0.0 48.5 jit_solution(11376991379354934285)
XLA Ops:
  0.6 1.3 %prepared.1 = (bf16[32,2048]{1,0:T(8,128)(2,1)S(1)}, bf16[16,1024]{1,0:T(8,128)(2,1)S(1)}) custom-call(bf16[2048,1024]{1,0:T(8,128)(2,1)} %strain.3), custom_call_target="tpu_custom_call" | custom-call | bytes 3690000 | tf_op jit(solution)/shard_map/prepared/pallas_call | solution.py:131
  1.9 0.5 %collective-permute-start = (bf16[32,2048]{1,0:T(8,128)(2,1)S(1)}, bf16[32,2048]{1,0:T(8,128)(2,1)S(1)}, u32[]{:S(2)}, u32[]{:S(2)}) collective-permute-start(bf16[32,2048]{1,0:T(8,128)(2,1)S(1)} %get-tuple-element.25.after.refs_2_.refs_1_.refs_0_), channel_id=1, source_target_pairs={{0,1},{1,0},{2,3},{3,2},{4,5},{5,4},{6,7},{7,6},{8,9},{9,8},{10,11... | collective-permute-start | bytes 393224 | tf_op jit(solution)/shard_map/ppermute | solution.py:39
  2.4 2.3 %loaded.1 = (bf16[2048,1024]{1,0:T(8,128)(2,1)S(1)}, f32[1,1024]{1,0:T(1,128)S(1)}) custom-call(bf16[2048,1024]{1,0:T(8,128)(2,1)} %strain.3, bf16[32,2048]{1,0:T(8,128)(2,1)S(1)} %get-tuple-element.25.after.refs_2_.refs_1_.refs_0_), custom_call_target="tpu_custom_call" | custom-call | bytes 3690000 | tf_op jit(solution)/shard_map/loaded/pallas_call | solution.py:185
  4.7 0.0 collective-permute-done.refs_3_.refs_2_.refs_1_
  4.7 2.0 %first_products.1 = (f32[128,1024]{1,0:T(8,128)S(1)}, bf16[136,1024]{1,0:T(8,128)(2,1)S(1)}) custom-call(bf16[2048,1024]{1,0:T(8,128)(2,1)S(1)} %get-tuple-element.27.refs_0_, f32[1,1024]{1,0:T(1,128)S(1)} %get-tuple-element.28.refs_1_, bf16[32,2048]{1,0:T(8,128)(2,1)S(1)} %get-tuple-element.25.after.refs_2_.refs_1_.refs_0_, ...), custom_call_target="tpu_custom_call" | custom-call | bytes 3690000 | tf_op jit(solution)/shard_map/first_products/pallas_call | solution.py:359
  6.8 2.6 %collective-permute-start.3 = (bf16[136,1024]{1,0:T(8,128)(2,1)S(1)}, bf16[136,1024]{1,0:T(8,128)(2,1)S(1)}, u32[]{:S(2)}, u32[]{:S(2)}) collective-permute-start(bf16[136,1024]{1,0:T(8,128)(2,1)S(1)} %get-tuple-element.29.refs_3_.refs_1_), channel_id=1, source_target_pairs={{0,2},{2,0},{4,6},{6,4},{8,10},{10,8},{12,14},{14,12},{1,3},{3,1},... | collective-permute-start | bytes 835592 | tf_op jit(solution)/shard_map/ppermute | solution.py:39
  9.3 1.5 %collective-permute-start.1 = (bf16[16,1024]{1,0:T(8,128)(2,1)S(1)}, bf16[16,1024]{1,0:T(8,128)(2,1)S(1)}, u32[]{:S(2)}, u32[]{:S(2)}) collective-permute-start(bf16[16,1024]{1,0:T(8,128)(2,1)S(1)} %get-tuple-element.26.refs_0_), channel_id=1, source_target_pairs={{4,0},{8,4},{12,8},{5,1},{9,5},{13,9},{20,16},{24,20},{28,24},{21,... | collective-permute-start | bytes 98312 | tf_op jit(solution)/shard_map/ppermute | solution.py:537
  10.8 5.3 %later_products.1 = (f32[128,1024]{1,0:T(8,128)S(1)}, bf16[128,1024]{1,0:T(8,128)(2,1)S(1)}, f32[128,1024]{1,0:T(8,128)S(1)}, bf16[128,1024]{1,0:T(8,128)(2,1)S(...) custom-call(bf16[2048,1024]{1,0:T(8,128)(2,1)S(1)} %get-tuple-element.27.refs_0_, ...), custom_call_target="tpu_custom_call" | custom-call | bytes 3690000 | tf_op jit(solution)/shard_map/later_products/pallas_call | solution.py:359
  16.1 0.0 collective-permute-done.1.refs_1_
  16.1 0.1 sides.1
  16.2 0.1 collective-permute-start.2
  16.3 2.0 %collective-permute-start.5 = (bf16[144,1024]{1,0:T(8,128)(2,1)S(1)}, bf16[144,1024]{1,0:T(8,128)(2,1)S(1)}, u32[]{:S(2)}, u32[]{:S(2)}) collective-permute-start(bf16[144,1024]{1,0:T(8,128)(2,1)S(1)} %get-tuple-element.42), channel_id=1, source_target_pairs={{0,2},{2,0},{4,6},{6,4},{8,10},{10,8},{12,14},{14,12},{1,3},{3,1},... | collective-permute-start | bytes 884744 | tf_op jit(solution)/shard_map/ppermute | solution.py:39
  18.3 2.9 %collective-permute-done.2.refs_3_.refs_2_ = bf16[32,1024]{1,0:T(8,128)(2,1)S(1)} collective-permute-done((bf16[32,1024]{1,0:T(8,128)(2,1)S(1)}, bf16[32,1024]{1,0:T(8,128)(2,1)S(1)}, u32[]{:S(2)}, u32[]{:S(2)}) %collective-permute-start.2) | collective-permute-done | bytes 65568 | tf_op jit(solution)/shard_map/ppermute | solution.py:39
  21.2 0.7 %with_boundaries.1 = (f32[128,1024]{1,0:T(8,128)S(1)}, f32[128,1024]{1,0:T(8,128)S(1)}, f32[128,1024]{1,0:T(8,128)S(1)}, f32[128,1024]{1,0:T(8,128)S(1)}, f32[1,1024]{1,0:T(1,128)S(1)}) custom-call(bf16[32,2048]{1,0:T(8,128)(2,1)S(1)} %get-tuple-element.25.after.refs_2_.refs_1_.refs_0_, bf16[32,2048]{1,0:T(8,128)(2,1)S(1)} %collective-permute-done.refs_3_.refs_2_.refs_1_, ...), custom_call_target="tpu_custom_call" | custom-call | bytes 1107000 | tf_op jit(solution)/shard_map/with_boundaries/pallas_call | solution.py:359
  21.9 0.0 collective-permute-done.3.refs_2_.refs_4_
  21.9 0.6 %merged.2 = (bf16[136,1024]{1,0:T(8,128)(2,1)S(1)}, bf16[128,1024]{1,0:T(8,128)(2,1)S(1)}) custom-call(f32[128,1024]{1,0:T(8,128)S(1)} %get-tuple-element.38.refs_0_, bf16[136,1024]{1,0:T(8,128)(2,1)S(1)} %get-tuple-element.29.refs_3_.refs_1_, bf16[136,1024]{1,0:T(8,128)(2,1)S(1)} %collective-permute-done.3.refs_2_.refs_4_, ...), custom_call_target="tpu_custom_call" | custom-call | bytes 1107000 | tf_op jit(solution)/shard_map/merged/pallas_call | solution.py:359
  22.5 2.7 %collective-permute-start.4 = (bf16[136,1024]{1,0:T(8,128)(2,1)S(1)}, bf16[136,1024]{1,0:T(8,128)(2,1)S(1)}, u32[]{:S(2)}, u32[]{:S(2)}) collective-permute-start(bf16[136,1024]{1,0:T(8,128)(2,1)S(1)} %get-tuple-element.41.refs_3_.refs_1_), channel_id=1, source_target_pairs={{0,4},{2,6},{4,0},{6,2},{8,12},{10,14},{12,8},{14,10},{1,5},{3,7},... | collective-permute-start | bytes 835592 | tf_op jit(solution)/shard_map/ppermute | solution.py:39
  25.2 0.0 collective-permute-start.7
  25.2 5.3 %segment_rows.2.refs_6_.refs_3_ = f32[16,512]{1,0:T(8,128)S(1)} custom-call(bf16[2048,1024]{1,0:T(8,128)(2,1)S(1)} %get-tuple-element.27.refs_0_, f32[1,1024]{1,0:T(1,128)S(1)} %get-tuple-element.28.refs_1_, bf16[32,1024]{1,0:T(8,128)(2,1)S(1)} %collective-permute-done.2.refs_3_.refs_2_, bf16[136,1024]{1,0:T(8,128)(2,1)S(1)} %get-tuple-element.41.refs_3_.refs_1_), custom_call_target="tpu_custom_call" | custom-call | bytes 4428000 | tf_op jit(solution)/shard_map/segment_rows/pallas_call | solution.py:359
  30.5 0.0 collective-permute-done.5.refs_3_
  30.5 0.0 collective-permute-done.4.refs_2_.refs_4_
  30.5 0.8 %merged.3 = (bf16[136,1024]{1,0:T(8,128)(2,1)S(1)}, bf16[128,1024]{1,0:T(8,128)(2,1)S(1)}) custom-call(f32[128,1024]{1,0:T(8,128)S(1)} %get-tuple-element.37.refs_0_, bf16[136,1024]{1,0:T(8,128)(2,1)S(1)} %get-tuple-element.41.refs_3_.refs_1_, bf16[136,1024]{1,0:T(8,128)(2,1)S(1)} %collective-permute-done.4.refs_2_.refs_4_, ...), custom_call_target="tpu_custom_call" | custom-call | bytes 1107000 | tf_op jit(solution)/shard_map/merged/pallas_call | solution.py:359
  31.3 2.7 %collective-permute-start.9 = (bf16[136,1024]{1,0:T(8,128)(2,1)S(1)}, bf16[136,1024]{1,0:T(8,128)(2,1)S(1)}, u32[]{:S(2)}, u32[]{:S(2)}) collective-permute-start(bf16[136,1024]{1,0:T(8,128)(2,1)S(1)} %get-tuple-element.47.refs_4_.refs_1_), channel_id=1, source_target_pairs={{0,8},{2,10},{4,12},{6,14},{8,0},{10,2},{12,4},{14,6},{1,9},{3,11}... | collective-permute-start | bytes 835592 | tf_op jit(solution)/shard_map/ppermute | solution.py:39
  34.0 0.0 collective-permute-done.7.refs_1_
  34.0 0.5 %resent.1.refs_3_ = bf16[128,1024]{1,0:T(8,128)(2,1)S(1)} custom-call(f32[128,1024]{1,0:T(8,128)S(1)} %get-tuple-element.45.refs_0_, bf16[128,1024]{1,0:T(8,128)(2,1)S(1)} %collective-permute-done.7.refs_1_, bf16[136,1024]{1,0:T(8,128)(2,1)S(1)} %collective-permute-done.3.refs_2_.refs_4_, bf16[136,1024]{1,0:T(8,128)(2,1)S(1)} %get-tuple-element.41.refs_3_.refs_1_, ...), custom_call_target="tpu_custom_call" | custom-call | bytes 1107000 | tf_op jit(solution)/shard_map/resent/pallas_call | solution.py:359
  34.5 1.4 %collective-permute-start.8 = (bf16[128,1024]{1,0:T(8,128)(2,1)S(1)}, bf16[128,1024]{1,0:T(8,128)(2,1)S(1)}, u32[]{:S(2)}, u32[]{:S(2)}) collective-permute-start(bf16[128,1024]{1,0:T(8,128)(2,1)S(1)} %resent.1.refs_3_), channel_id=1, source_target_pairs={{0,4},{2,6},{4,0},{6,2},{8,12},{10,14},{12,8},{14,10},{1,5},{3,7},... | collective-permute-start | bytes 786440 | tf_op jit(solution)/shard_map/ppermute | solution.py:39
  35.9 1.2 %collective-permute-start.6 = (bf16[128,1024]{1,0:T(8,128)(2,1)S(1)}, bf16[128,1024]{1,0:T(8,128)(2,1)S(1)}, u32[]{:S(2)}, u32[]{:S(2)}) collective-permute-start(bf16[128,1024]{1,0:T(8,128)(2,1)S(1)} %get-tuple-element.44), channel_id=1, source_target_pairs={{0,2},{2,0},{4,6},{6,4},{8,10},{10,8},{12,14},{14,12},{1,3},{3,1},... | collective-permute-start | bytes 786440 | tf_op jit(solution)/shard_map/ppermute | solution.py:39
  37.1 5.3 %segment_rows.3.refs_5_.refs_4_ = f32[16,512]{1,0:T(8,128)S(1)} custom-call(bf16[2048,1024]{1,0:T(8,128)(2,1)S(1)} %get-tuple-element.27.refs_0_, f32[1,1024]{1,0:T(1,128)S(1)} %get-tuple-element.28.refs_1_, bf16[32,1024]{1,0:T(8,128)(2,1)S(1)} %collective-permute-done.2.refs_3_.refs_2_, bf16[128,1024]{1,0:T(8,128)(2,1)S(1)} %resent.1.refs_3_), custom_call_target="tpu_custom_call" | custom-call | bytes 4428000 | tf_op jit(solution)/shard_map/segment_rows/pallas_call | solution.py:359
  42.4 4.3 %collective-permute-done.8.refs_3_ = bf16[128,1024]{1,0:T(8,128)(2,1)S(1)} collective-permute-done((bf16[128,1024]{1,0:T(8,128)(2,1)S(1)}, bf16[128,1024]{1,0:T(8,128)(2,1)S(1)}, u32[]{:S(2)}, u32[]{:S(2)}) %collective-permute-start.8) | collective-permute-done | bytes 262176 | tf_op jit(solution)/shard_map/ppermute | solution.py:39
  46.7 0.0 collective-permute-done.6.refs_1_
  46.7 0.5 %added.1.refs_0_ = f32[128,1024]{1,0:T(8,128)S(1)} custom-call(f32[128,1024]{1,0:T(8,128)S(1)} %get-tuple-element.36.refs_0_, bf16[128,1024]{1,0:T(8,128)(2,1)S(1)} %collective-permute-done.6.refs_1_, bf16[136,1024]{1,0:T(8,128)(2,1)S(1)} %collective-permute-done.3.refs_2_.refs_4_, bf16[128,1024]{1,0:T(8,128)(2,1)S(1)} %collective-permute-done.8.refs_3_, ...), custom_call_target="tpu_custom_call" | custom-call | bytes 1107000 | tf_op jit(solution)/shard_map/added/pallas_call | solution.py:359
  47.3 0.0 collective-permute-done.9.refs_2_
  47.3 1.2 %finished.1 = (f32[128,1024]{1,0:T(8,128)}, f32[16,1024]{1,0:T(8,128)}) custom-call(f32[128,1024]{1,0:T(8,128)S(1)} %added.1.refs_0_, bf16[136,1024]{1,0:T(8,128)(2,1)S(1)} %get-tuple-element.47.refs_4_.refs_1_, bf16[136,1024]{1,0:T(8,128)(2,1)S(1)} %collective-permute-done.9.refs_2_, f32[16,512]{1,0:T(8,128)S(1)} %segment_rows.2.refs_6_.refs_3_, ...), custom_call_target="tpu_custom_call" | custom-call | bytes 1107000 | tf_op jit(solution)/shard_map/finished/pallas_call | solution.py:359
Async XLA Ops:
  1.9 2.8 %collective-permute-start = (bf16[32,2048]{1,0:T(8,128)(2,1)S(1)}, bf16[32,2048]{1,0:T(8,128)(2,1)S(1)}, u32[]{:S(2)}, u32[]{:S(2)}) collective-permute-start(bf16[32,2048]{1,0:T(8,128)(2,1)S(1)} %get-tuple-element.25.after.refs_2_.refs_1_.refs_0_), channel_id=1, source_target_pairs={{0,1},{1,0},{2,3},{3,2},{4,5},{5,4},{6,7},{7,6},{8,9},{9,8},{10,11... | collective-permute-start | bytes 393224 | tf_op jit(solution)/shard_map/ppermute | solution.py:39
  6.8 15.1 %collective-permute-start.3 = (bf16[136,1024]{1,0:T(8,128)(2,1)S(1)}, bf16[136,1024]{1,0:T(8,128)(2,1)S(1)}, u32[]{:S(2)}, u32[]{:S(2)}) collective-permute-start(bf16[136,1024]{1,0:T(8,128)(2,1)S(1)} %get-tuple-element.29.refs_3_.refs_1_), channel_id=1, source_target_pairs={{0,2},{2,0},{4,6},{6,4},{8,10},{10,8},{12,14},{14,12},{1,3},{3,1},... | collective-permute-start | bytes 835592 | tf_op jit(solution)/shard_map/ppermute | solution.py:39
  9.3 6.8 %collective-permute-start.1 = (bf16[16,1024]{1,0:T(8,128)(2,1)S(1)}, bf16[16,1024]{1,0:T(8,128)(2,1)S(1)}, u32[]{:S(2)}, u32[]{:S(2)}) collective-permute-start(bf16[16,1024]{1,0:T(8,128)(2,1)S(1)} %get-tuple-element.26.refs_0_), channel_id=1, source_target_pairs={{4,0},{8,4},{12,8},{5,1},{9,5},{13,9},{20,16},{24,20},{28,24},{21,... | collective-permute-start | bytes 98312 | tf_op jit(solution)/shard_map/ppermute | solution.py:537
  16.2 5.0 %collective-permute-start.2 = (bf16[32,1024]{1,0:T(8,128)(2,1)S(1)}, bf16[32,1024]{1,0:T(8,128)(2,1)S(1)}, u32[]{:S(2)}, u32[]{:S(2)}) collective-permute-start(bf16[32,1024]{1,0:T(8,128)(2,1)S(1)} %get-tuple-element.31.refs_2_), channel_id=1, source_target_pairs={{0,2},{2,0},{4,6},{6,4},{8,10},{10,8},{12,14},{14,12},{1,3},{3,1},... | collective-permute-start | bytes 196616 | tf_op jit(solution)/shard_map/ppermute | solution.py:39
  16.3 14.2 %collective-permute-start.5 = (bf16[144,1024]{1,0:T(8,128)(2,1)S(1)}, bf16[144,1024]{1,0:T(8,128)(2,1)S(1)}, u32[]{:S(2)}, u32[]{:S(2)}) collective-permute-start(bf16[144,1024]{1,0:T(8,128)(2,1)S(1)} %get-tuple-element.42), channel_id=1, source_target_pairs={{0,2},{2,0},{4,6},{6,4},{8,10},{10,8},{12,14},{14,12},{1,3},{3,1},... | collective-permute-start | bytes 884744 | tf_op jit(solution)/shard_map/ppermute | solution.py:39
  22.5 8.1 %collective-permute-start.4 = (bf16[136,1024]{1,0:T(8,128)(2,1)S(1)}, bf16[136,1024]{1,0:T(8,128)(2,1)S(1)}, u32[]{:S(2)}, u32[]{:S(2)}) collective-permute-start(bf16[136,1024]{1,0:T(8,128)(2,1)S(1)} %get-tuple-element.41.refs_3_.refs_1_), channel_id=1, source_target_pairs={{0,4},{2,6},{4,0},{6,2},{8,12},{10,14},{12,8},{14,10},{1,5},{3,7},... | collective-permute-start | bytes 835592 | tf_op jit(solution)/shard_map/ppermute | solution.py:39
  25.2 8.8 %collective-permute-start.7 = (bf16[128,1024]{1,0:T(8,128)(2,1)S(1)}, bf16[128,1024]{1,0:T(8,128)(2,1)S(1)}, u32[]{:S(2)}, u32[]{:S(2)}) collective-permute-start(bf16[128,1024]{1,0:T(8,128)(2,1)S(1)} %get-tuple-element.46), channel_id=1, source_target_pairs={{0,2},{2,0},{4,6},{6,4},{8,10},{10,8},{12,14},{14,12},{1,3},{3,1},... | collective-permute-start | bytes 786440 | tf_op jit(solution)/shard_map/ppermute | solution.py:39
  31.3 15.9 %collective-permute-start.9 = (bf16[136,1024]{1,0:T(8,128)(2,1)S(1)}, bf16[136,1024]{1,0:T(8,128)(2,1)S(1)}, u32[]{:S(2)}, u32[]{:S(2)}) collective-permute-start(bf16[136,1024]{1,0:T(8,128)(2,1)S(1)} %get-tuple-element.47.refs_4_.refs_1_), channel_id=1, source_target_pairs={{0,8},{2,10},{4,12},{6,14},{8,0},{10,2},{12,4},{14,6},{1,9},{3,11}... | collective-permute-start | bytes 835592 | tf_op jit(solution)/shard_map/ppermute | solution.py:39
  34.5 12.2 %collective-permute-start.8 = (bf16[128,1024]{1,0:T(8,128)(2,1)S(1)}, bf16[128,1024]{1,0:T(8,128)(2,1)S(1)}, u32[]{:S(2)}, u32[]{:S(2)}) collective-permute-start(bf16[128,1024]{1,0:T(8,128)(2,1)S(1)} %resent.1.refs_3_), channel_id=1, source_target_pairs={{0,4},{2,6},{4,0},{6,2},{8,12},{10,14},{12,8},{14,10},{1,5},{3,7},... | collective-permute-start | bytes 786440 | tf_op jit(solution)/shard_map/ppermute | solution.py:39
  35.9 10.8 %collective-permute-start.6 = (bf16[128,1024]{1,0:T(8,128)(2,1)S(1)}, bf16[128,1024]{1,0:T(8,128)(2,1)S(1)}, u32[]{:S(2)}, u32[]{:S(2)}) collective-permute-start(bf16[128,1024]{1,0:T(8,128)(2,1)S(1)} %get-tuple-element.44), channel_id=1, source_target_pairs={{0,2},{2,0},{4,6},{6,4},{8,10},{10,8},{12,14},{14,12},{1,3},{3,1},... | collective-permute-start | bytes 786440 | tf_op jit(solution)/shard_map/ppermute | solution.py:39

commit v12 on v11

--- a/solution.py
+++ b/solution.py
@@ -301,12 +301,11 @@
 
 
 def sides_to_swap(head, after_next, own, other, held_back):
-    rows, width = held_back.shape
+    width = head.shape[1]
 
     def kernel(head, after_next, own, other, held_back, sides, passed):
         chan, near = lax.axis_index("chan"), lax.axis_index("tm") & 1
-        passed[:rows] = held_back[...]
-        passed[rows:] = jnp.zeros((LAGS, width), jnp.bfloat16)
+        passed[...] = held_back[...]
         sides[:LAGS] = jnp.where(near == 0, after_next[...], head[...])
         ours, theirs = [refs[:, refs.shape[1] - LANES :].astype(jnp.float32) for refs in (own, other)]
         first, second = jnp.where(chan == 0, ours, theirs), jnp.where(chan == 0, theirs, ours)
@@ -314,17 +313,19 @@
         sides[LAGS:, :LANES] = square.T[LANES - LAGS :].astype(jnp.bfloat16)
         sides[LAGS:, LANES:] = jnp.zeros((LAGS, width - LANES), jnp.bfloat16)
 
-    outs = [((2 * LAGS, width), jnp.bfloat16), ((rows + LAGS, width), jnp.bfloat16)]
+    outs = [((2 * LAGS, width), jnp.bfloat16), (held_back.shape, jnp.bfloat16)]
     arrays = (head, after_next, own, other, held_back)
     return call_on_blocks(kernel, outs, *arrays, name="sides", micros=MERGE_MICROS)
 
 
-def with_boundaries(keeps, groups, own, other, sent, arrived):
+def with_boundaries(keeps, groups, own, other, sent, arrived, held_back):
     chunk, width = keeps[0].shape
 
-    def kernel(own, other, sent, arrived, *rest):
+    def kernel(own, other, sent, arrived, held_back, *rest):
         keeps, rest = rest[: len(groups)], rest[len(groups) :]
-        outs, beyond, edges = rest[: len(groups)], rest[-2], rest[-1]
+        outs, beyond, passed, edges = rest[: len(groups)], rest[-3], rest[-2], rest[-1]
+        passed[:chunk] = held_back[...]
+        passed[chunk:] = jnp.zeros((LAGS, width), jnp.bfloat16)
         for index, bits in enumerate(groups):
             boundary_rows(own_group(bits), (own, other), ends_of(arrived), edges.at[index])
         for here in columns(width):
@@ -334,7 +335,7 @@
                 outs[index][:, here] = keeps[index][:, here] + added
             beyond[:, here] = jnp.sum(jnp.square(tails.astype(jnp.float32)), axis=0, keepdims=True)
 
-    outs = [((chunk, width), jnp.float32)] * len(groups) + [((1, width), jnp.float32)]
+    outs = [((chunk, width), jnp.float32)] * len(groups) + [((1, width), jnp.float32), ((chunk + LAGS, width), jnp.bfloat16)]
     return call_on_blocks(
         kernel,
         outs,
@@ -342,6 +343,7 @@
         other,
         sent,
         arrived,
+        held_back,
         *keeps,
         name="with_boundaries",
         micros=MERGE_MICROS,
@@ -408,26 +410,27 @@
     return call_on_blocks(kernel, outs, *arrays, name="resent", micros=MERGE_MICROS, after=after)[0]
 
 
-def added(keep, direct, direct_powers, near, near_powers, after):
-    def kernel(keep, direct, direct_powers, near, near_powers, out):
-        out[...] = keep[...] + direct_sums(direct, direct_powers) + direct_sums(near, near_powers)
+def added(keep, direct, direct_powers, after):
+    def kernel(keep, direct, direct_powers, out):
+        out[...] = keep[...] + direct_sums(direct, direct_powers)
 
     outs = [(keep.shape, jnp.float32)]
-    arrays = (keep, direct, direct_powers, near, near_powers)
+    arrays = (keep, direct, direct_powers)
     return call_on_blocks(kernel, outs, *arrays, name="added", micros=MERGE_MICROS, after=after)[0]
 
 
-def finished(slab_rows, segment, partial, ours, theirs, autos):
+def finished(slab_rows, segment, partial, near, near_powers, ours, theirs, autos):
     chunk, width = partial.shape
 
-    def kernel(partial, ours, theirs, *refs):
+    def kernel(partial, near, near_powers, ours, theirs, *refs):
         autos, (covariance, segment_auto) = refs[:-2], refs[-2:]
         first_lag = lax.axis_index("tm").astype(jnp.int32) * (chunk // REF)
         lag = lax.broadcasted_iota(jnp.int32, (chunk, 1), 0) // REF + first_lag
         denom = (slab_rows - lag).astype(jnp.float32)
         powers, own_refs, _ = sent_powers(ours)
         their_powers, their_refs, their_bound = sent_powers(theirs)
-        total = partial[...] + expanded(theirs[:chunk], their_bound, ref_column(their_refs))
+        total = partial[...] + direct_sums(near, near_powers)
+        total += expanded(theirs[:chunk], their_bound, ref_column(their_refs))
         scale = 1.0 / jnp.sqrt((powers + their_powers) / slab_rows + 1e-06)
         ref_scale = 1.0 / jnp.sqrt(ref_column(own_refs + their_refs) / slab_rows + 1e-06)
         covariance[...] = total * scale * (for_chunk(ref_scale, chunk) / denom)
@@ -442,6 +445,8 @@
         kernel,
         outs,
         partial,
+        near,
+        near_powers,
         ours,
         theirs,
         *autos,
@@ -550,15 +555,17 @@
 
     if chunk * 2 == GROUP * REF:
         keep6, send7 = first_products(held, power, own, other, chunk)
+        after_next = from_pair_ahead(head)
+        sides, send7 = sides_to_swap(head, after_next, own, other, send7)
         got7 = exchanged(send7, "tm", 1)
-        after_next = from_pair_ahead(head)
+        tails = (sides, exchanged(sides, "tm", 1))
         keep4, send5, keep2, send3, keep0, send1 = later_products(
             (2, 1, 0), held, own, other, send7, chunk
         )
-        sides, send5 = sides_to_swap(head, after_next, own, other, send5)
-        tails = (sides, exchanged(sides, "tm", 1))
+        *keeps, beyond, send5 = with_boundaries(
+            (keep6, keep4, keep2, keep0), (3, 2, 1, 0), own, other, *tails, send5
+        )
         got5 = exchanged(send5, "tm", 1)
-        *keeps, beyond = with_boundaries((keep6, keep4, keep2, keep0), (3, 2, 1, 0), own, other, *tails)
         keep6, keep4, keep2, keep0 = keeps
         send6, send3 = merged(keep6, send7, got7, beyond=(beyond,), held_back=(send3,))
         got6 = exchanged(send6, "tm", 2)
@@ -572,8 +579,8 @@
         send2 = resent(keep2, got3, got7, send6, after=(send4,))
         got2 = exchanged(send2, "tm", 2)
         autos.append(segment_rows(held, power, tails[1], size, size, after=(send2,)))
-        partial = added(keep0, got1, got7, got2, got6, after=(autos[1],))
-        return tuple(finished(slab_rows, rows, partial, send4, got4, autos))
+        partial = added(keep0, got1, got7, after=(autos[1],))
+        return tuple(finished(slab_rows, rows, partial, got2, got6, send4, got4, autos))
 
     tail = passed_along(head, "tm", -1)
     chan = lax.axis_index("chan").astype(jnp.int32)

time: 48.6 us -> 50 us (1.029)
  starting transfers between devices: 14.6 us -> 15.3 us
  waiting for transfers between devices: 7.24 us -> 7.92 us
    ppermute x9, starting transfers between devices: 13.1 us -> 14 us  [exchanged(): lax.ppermute(value, axis, [(source, source ^ bit) for source in range(cou...]
    ppermute x1, waiting for transfers between devices: 0.01 us -> 0.9 us  [from_pair_ahead(): lax.ppermute(value, 'tm', [(time + 2, time) for time in range(0, count -...]
  transfers between devices with their start and end apart: 10 -> 10, of which waited for: 2 -> 3; matrix products, arithmetic and copies ran while one was open for 0% -> 0% of each run, Pallas kernels for 44% -> 46%
where the time goes in v12:
time: 50 us; the launch traced here: 49.9 us
  Pallas kernels  25.9 us (52%)
  starting transfers between devices  15.3 us (31%)
  waiting for transfers between devices  7.92 us (16%)
  between operations  0.76 us (2%)
    pallas_call x11, Pallas kernels, call_on_blocks(): pl.pallas_call(body, in_specs=[vmem] * count + [pl.BlockSpec(memory_space...  22.3 us
    ppermute x9, starting transfers between devices, exchanged(): lax.ppermute(value, axis, [(source, source ^ bit) for source in range(cou...  14 us
    ppermute x9, waiting for transfers between devices, exchanged(): lax.ppermute(value, axis, [(source, source ^ bit) for source in range(cou...  7.03 us
    pallas_call x1, Pallas kernels, loaded(): pl.pallas_call(kernel, in_specs=[pl.BlockSpec(memory_space=pl.ANY)] * 2,...  2.26 us
    ppermute x1, starting transfers between devices, from_pair_ahead(): lax.ppermute(value, 'tm', [(time + 2, time) for time in range(0, count -...  1.28 us
    pallas_call x1, Pallas kernels, prepared(): pl.pallas_call(prepare_kernel, in_specs=[pl.BlockSpec(memory_space=pl.ANY...  1.28 us
  transfers between devices with their start and end apart: 10, of which 3 were waited for; matrix products, arithmetic and copies ran while one was open for 0% of the time, Pallas kernels for 46%

profile of v12, /device:TPU:0, one launch (start us, length us, event | category | flops | bytes accessed | tf_op | source)
XLA Modules:
  0.0 49.9 jit_solution(1564434447185851604)
XLA Ops:
  0.6 1.3 %prepared.1 = (bf16[32,2048]{1,0:T(8,128)(2,1)S(1)}, bf16[16,1024]{1,0:T(8,128)(2,1)S(1)}) custom-call(bf16[2048,1024]{1,0:T(8,128)(2,1)} %strain.3), custom_call_target="tpu_custom_call" | custom-call | bytes 3690000 | tf_op jit(solution)/shard_map/prepared/pallas_call | solution.py:131
  1.9 0.5 %collective-permute-start = (bf16[32,2048]{1,0:T(8,128)(2,1)S(1)}, bf16[32,2048]{1,0:T(8,128)(2,1)S(1)}, u32[]{:S(2)}, u32[]{:S(2)}) collective-permute-start(bf16[32,2048]{1,0:T(8,128)(2,1)S(1)} %get-tuple-element.26.after.refs_2_.refs_1_.refs_0_), channel_id=1, source_target_pairs={{0,1},{1,0},{2,3},{3,2},{4,5},{5,4},{6,7},{7,6},{8,9},{9,8},{10,11... | collective-permute-start | bytes 393224 | tf_op jit(solution)/shard_map/ppermute | solution.py:39
  2.4 1.3 %collective-permute-start.1 = (bf16[16,1024]{1,0:T(8,128)(2,1)S(1)}, bf16[16,1024]{1,0:T(8,128)(2,1)S(1)}, u32[]{:S(2)}, u32[]{:S(2)}) collective-permute-start(bf16[16,1024]{1,0:T(8,128)(2,1)S(1)} %get-tuple-element.27.refs_0_), channel_id=1, source_target_pairs={{4,0},{8,4},{12,8},{5,1},{9,5},{13,9},{20,16},{24,20},{28,24},{21,... | collective-permute-start | bytes 98312 | tf_op jit(solution)/shard_map/ppermute | solution.py:542
  3.7 2.3 %loaded.1 = (bf16[2048,1024]{1,0:T(8,128)(2,1)S(1)}, f32[1,1024]{1,0:T(1,128)S(1)}) custom-call(bf16[2048,1024]{1,0:T(8,128)(2,1)} %strain.3, bf16[32,2048]{1,0:T(8,128)(2,1)S(1)} %get-tuple-element.26.after.refs_2_.refs_1_.refs_0_), custom_call_target="tpu_custom_call" | custom-call | bytes 3690000 | tf_op jit(solution)/shard_map/loaded/pallas_call | solution.py:185
  6.0 0.0 collective-permute-done.refs_3_.refs_2_.refs_1_
  6.0 2.1 %first_products.1 = (f32[128,1024]{1,0:T(8,128)S(1)}, bf16[136,1024]{1,0:T(8,128)(2,1)S(1)}) custom-call(bf16[2048,1024]{1,0:T(8,128)(2,1)S(1)} %get-tuple-element.28.refs_0_, f32[1,1024]{1,0:T(1,128)S(1)} %get-tuple-element.29.refs_1_, bf16[32,2048]{1,0:T(8,128)(2,1)S(1)} %get-tuple-element.26.after.refs_2_.refs_1_.refs_0_, ...), custom_call_target="tpu_custom_call" | custom-call | bytes 3690000 | tf_op jit(solution)/shard_map/first_products/pallas_call | solution.py:361
  8.1 0.9 %collective-permute-done.1.refs_1_ = bf16[16,1024]{1,0:T(8,128)(2,1)S(1)} collective-permute-done((bf16[16,1024]{1,0:T(8,128)(2,1)S(1)}, bf16[16,1024]{1,0:T(8,128)(2,1)S(1)}, u32[]{:S(2)}, u32[]{:S(2)}) %collective-permute-start.1) | collective-permute-done | bytes 32800 | tf_op jit(solution)/shard_map/ppermute | solution.py:542
  9.0 0.1 sides.1
  9.1 1.1 %collective-permute-start.3 = (bf16[136,1024]{1,0:T(8,128)(2,1)S(1)}, bf16[136,1024]{1,0:T(8,128)(2,1)S(1)}, u32[]{:S(2)}, u32[]{:S(2)}) collective-permute-start(bf16[136,1024]{1,0:T(8,128)(2,1)S(1)} %get-tuple-element.32.refs_3_.refs_1_), channel_id=1, source_target_pairs={{0,2},{2,0},{4,6},{6,4},{8,10},{10,8},{12,14},{14,12},{1,3},{3,1},... | collective-permute-start | bytes 835592 | tf_op jit(solution)/shard_map/ppermute | solution.py:39
  10.1 1.0 %collective-permute-start.2 = (bf16[32,1024]{1,0:T(8,128)(2,1)S(1)}, bf16[32,1024]{1,0:T(8,128)(2,1)S(1)}, u32[]{:S(2)}, u32[]{:S(2)}) collective-permute-start(bf16[32,1024]{1,0:T(8,128)(2,1)S(1)} %get-tuple-element.31.refs_2_), channel_id=1, source_target_pairs={{0,2},{2,0},{4,6},{6,4},{8,10},{10,8},{12,14},{14,12},{1,3},{3,1},... | collective-permute-start | bytes 196616 | tf_op jit(solution)/shard_map/ppermute | solution.py:39
  11.1 5.3 %later_products.1 = (f32[128,1024]{1,0:T(8,128)S(1)}, bf16[128,1024]{1,0:T(8,128)(2,1)S(1)}, f32[128,1024]{1,0:T(8,128)S(1)}, bf16[128,1024]{1,0:T(8,128)(2,1)S(...) custom-call(bf16[2048,1024]{1,0:T(8,128)(2,1)S(1)} %get-tuple-element.28.refs_0_, ...), custom_call_target="tpu_custom_call" | custom-call | bytes 3690000 | tf_op jit(solution)/shard_map/later_products/pallas_call | solution.py:361
  16.4 2.5 %collective-permute-done.2.refs_3_.refs_2_ = bf16[32,1024]{1,0:T(8,128)(2,1)S(1)} collective-permute-done((bf16[32,1024]{1,0:T(8,128)(2,1)S(1)}, bf16[32,1024]{1,0:T(8,128)(2,1)S(1)}, u32[]{:S(2)}, u32[]{:S(2)}) %collective-permute-start.2) | collective-permute-done | bytes 65568 | tf_op jit(solution)/shard_map/ppermute | solution.py:39
  19.0 0.7 %with_boundaries.1 = (f32[128,1024]{1,0:T(8,128)S(1)}, f32[128,1024]{1,0:T(8,128)S(1)}, f32[128,1024]{1,0:T(8,128)S(1)}, f32[128,1024]{1,0:T(8,128)S(1)}, f32[1,...) custom-call(bf16[32,2048]{1,0:T(8,128)(2,1)S(1)} %get-tuple-element.26.after.refs_2_.refs_1_.refs_0_, ...), custom_call_target="tpu_custom_call" | custom-call | bytes 1107000 | tf_op jit(solution)/shard_map/with_boundaries/pallas_call | solution.py:361
  19.7 1.6 %collective-permute-start.5 = (bf16[144,1024]{1,0:T(8,128)(2,1)S(1)}, bf16[144,1024]{1,0:T(8,128)(2,1)S(1)}, u32[]{:S(2)}, u32[]{:S(2)}) collective-permute-start(bf16[144,1024]{1,0:T(8,128)(2,1)S(1)} %get-tuple-element.44), channel_id=1, source_target_pairs={{0,2},{2,0},{4,6},{6,4},{8,10},{10,8},{12,14},{14,12},{1,3},{3,1},... | collective-permute-start | bytes 884744 | tf_op jit(solution)/shard_map/ppermute | solution.py:39
  21.3 0.0 collective-permute-done.3.refs_2_.refs_4_
  21.3 0.6 %merged.2 = (bf16[136,1024]{1,0:T(8,128)(2,1)S(1)}, bf16[128,1024]{1,0:T(8,128)(2,1)S(1)}) custom-call(f32[128,1024]{1,0:T(8,128)S(1)} %get-tuple-element.40.refs_0_, bf16[136,1024]{1,0:T(8,128)(2,1)S(1)} %get-tuple-element.32.refs_3_.refs_1_, bf16[136,1024]{1,0:T(8,128)(2,1)S(1)} %collective-permute-done.3.refs_2_.refs_4_, ...), custom_call_target="tpu_custom_call" | custom-call | bytes 1107000 | tf_op jit(solution)/shard_map/merged/pallas_call | solution.py:361
  21.9 1.7 %collective-permute-start.4 = (bf16[136,1024]{1,0:T(8,128)(2,1)S(1)}, bf16[136,1024]{1,0:T(8,128)(2,1)S(1)}, u32[]{:S(2)}, u32[]{:S(2)}) collective-permute-start(bf16[136,1024]{1,0:T(8,128)(2,1)S(1)} %get-tuple-element.43.refs_3_.refs_1_), channel_id=1, source_target_pairs={{0,4},{2,6},{4,0},{6,2},{8,12},{10,14},{12,8},{14,10},{1,5},{3,7},... | collective-permute-start | bytes 835592 | tf_op jit(solution)/shard_map/ppermute | solution.py:39
  23.6 1.7 %collective-permute-start.7 = (bf16[128,1024]{1,0:T(8,128)(2,1)S(1)}, bf16[128,1024]{1,0:T(8,128)(2,1)S(1)}, u32[]{:S(2)}, u32[]{:S(2)}) collective-permute-start(bf16[128,1024]{1,0:T(8,128)(2,1)S(1)} %get-tuple-element.48), channel_id=1, source_target_pairs={{0,2},{2,0},{4,6},{6,4},{8,10},{10,8},{12,14},{14,12},{1,3},{3,1},... | collective-permute-start | bytes 786440 | tf_op jit(solution)/shard_map/ppermute | solution.py:39
  25.3 5.3 %segment_rows.2.refs_6_.refs_5_ = f32[16,512]{1,0:T(8,128)S(1)} custom-call(bf16[2048,1024]{1,0:T(8,128)(2,1)S(1)} %get-tuple-element.28.refs_0_, f32[1,1024]{1,0:T(1,128)S(1)} %get-tuple-element.29.refs_1_, bf16[32,1024]{1,0:T(8,128)(2,1)S(1)} %collective-permute-done.2.refs_3_.refs_2_, bf16[136,1024]{1,0:T(8,128)(2,1)S(1)} %get-tuple-element.43.refs_3_.refs_1_), custom_call_target="tpu_custom_call" | custom-call | bytes 4428000 | tf_op jit(solution)/shard_map/segment_rows/pallas_call | solution.py:361
  30.6 0.0 collective-permute-done.5.refs_3_
  30.6 0.0 collective-permute-done.4.refs_2_
  30.6 0.8 %merged.3 = (bf16[136,1024]{1,0:T(8,128)(2,1)S(1)}, bf16[128,1024]{1,0:T(8,128)(2,1)S(1)}) custom-call(f32[128,1024]{1,0:T(8,128)S(1)} %get-tuple-element.39.refs_0_, bf16[136,1024]{1,0:T(8,128)(2,1)S(1)} %get-tuple-element.43.refs_3_.refs_1_, bf16[136,1024]{1,0:T(8,128)(2,1)S(1)} %collective-permute-done.4.refs_2_, ...), custom_call_target="tpu_custom_call" | custom-call | bytes 1107000 | tf_op jit(solution)/shard_map/merged/pallas_call | solution.py:361
  31.4 3.2 %collective-permute-start.9 = (bf16[136,1024]{1,0:T(8,128)(2,1)S(1)}, bf16[136,1024]{1,0:T(8,128)(2,1)S(1)}, u32[]{:S(2)}, u32[]{:S(2)}) collective-permute-start(bf16[136,1024]{1,0:T(8,128)(2,1)S(1)} %get-tuple-element.49.refs_4_.refs_3_), channel_id=1, source_target_pairs={{0,8},{2,10},{4,12},{6,14},{8,0},{10,2},{12,4},{14,6},{1,9},{3,11}... | collective-permute-start | bytes 835592 | tf_op jit(solution)/shard_map/ppermute | solution.py:39
  34.6 0.4 collective-permute-start.6
  35.0 0.0 collective-permute-done.7.refs_1_
  35.0 0.5 %resent.1.refs_3_ = bf16[128,1024]{1,0:T(8,128)(2,1)S(1)} custom-call(f32[128,1024]{1,0:T(8,128)S(1)} %get-tuple-element.47.refs_0_, bf16[128,1024]{1,0:T(8,128)(2,1)S(1)} %collective-permute-done.7.refs_1_, bf16[136,1024]{1,0:T(8,128)(2,1)S(1)} %collective-permute-done.3.refs_2_.refs_4_, bf16[136,1024]{1,0:T(8,128)(2,1)S(1)} %get-tuple-element.43.refs_3_.refs_1_, ...), custom_call_target="tpu_custom_call" | custom-call | bytes 1107000 | tf_op jit(solution)/shard_map/resent/pallas_call | solution.py:361
  35.5 2.8 %collective-permute-start.8 = (bf16[128,1024]{1,0:T(8,128)(2,1)S(1)}, bf16[128,1024]{1,0:T(8,128)(2,1)S(1)}, u32[]{:S(2)}, u32[]{:S(2)}) collective-permute-start(bf16[128,1024]{1,0:T(8,128)(2,1)S(1)} %resent.1.refs_3_), channel_id=1, source_target_pairs={{0,4},{2,6},{4,0},{6,2},{8,12},{10,14},{12,8},{14,10},{1,5},{3,7},... | collective-permute-start | bytes 786440 | tf_op jit(solution)/shard_map/ppermute | solution.py:39
  38.3 5.3 %segment_rows.3.refs_3_.refs_6_ = f32[16,512]{1,0:T(8,128)S(1)} custom-call(bf16[2048,1024]{1,0:T(8,128)(2,1)S(1)} %get-tuple-element.28.refs_0_, f32[1,1024]{1,0:T(1,128)S(1)} %get-tuple-element.29.refs_1_, bf16[32,1024]{1,0:T(8,128)(2,1)S(1)} %collective-permute-done.2.refs_3_.refs_2_, bf16[128,1024]{1,0:T(8,128)(2,1)S(1)} %resent.1.refs_3_), custom_call_target="tpu_custom_call" | custom-call | bytes 4428000 | tf_op jit(solution)/shard_map/segment_rows/pallas_call | solution.py:361
  43.6 0.0 collective-permute-done.6.refs_1_
  43.6 0.3 added.1.refs_0_
  44.0 4.5 %collective-permute-done.8.refs_1_ = bf16[128,1024]{1,0:T(8,128)(2,1)S(1)} collective-permute-done((bf16[128,1024]{1,0:T(8,128)(2,1)S(1)}, bf16[128,1024]{1,0:T(8,128)(2,1)S(1)}, u32[]{:S(2)}, u32[]{:S(2)}) %collective-permute-start.8) | collective-permute-done | bytes 262176 | tf_op jit(solution)/shard_map/ppermute | solution.py:39
  48.4 0.0 collective-permute-done.9.refs_4_
  48.4 1.4 %finished.1 = (f32[128,1024]{1,0:T(8,128)}, f32[16,1024]{1,0:T(8,128)}) custom-call(f32[128,1024]{1,0:T(8,128)S(1)} %added.1.refs_0_, bf16[128,1024]{1,0:T(8,128)(2,1)S(1)} %collective-permute-done.8.refs_1_, bf16[136,1024]{1,0:T(8,128)(2,1)S(1)} %collective-permute-done.4.refs_2_, bf16[136,1024]{1,0:T(8,128)(2,1)S(1)} %get-tuple-element.49.refs_4_.refs_3_, ...), custom_call_target="tpu_custom_call" | custom-call | bytes 1107000 | tf_op jit(solution)/shard_map/finished/pallas_call | solution.py:361
Async XLA Ops:
  1.9 4.1 %collective-permute-start = (bf16[32,2048]{1,0:T(8,128)(2,1)S(1)}, bf16[32,2048]{1,0:T(8,128)(2,1)S(1)}, u32[]{:S(2)}, u32[]{:S(2)}) collective-permute-start(bf16[32,2048]{1,0:T(8,128)(2,1)S(1)} %get-tuple-element.26.after.refs_2_.refs_1_.refs_0_), channel_id=1, source_target_pairs={{0,1},{1,0},{2,3},{3,2},{4,5},{5,4},{6,7},{7,6},{8,9},{9,8},{10,11... | collective-permute-start | bytes 393224 | tf_op jit(solution)/shard_map/ppermute | solution.py:39
  2.4 6.5 %collective-permute-start.1 = (bf16[16,1024]{1,0:T(8,128)(2,1)S(1)}, bf16[16,1024]{1,0:T(8,128)(2,1)S(1)}, u32[]{:S(2)}, u32[]{:S(2)}) collective-permute-start(bf16[16,1024]{1,0:T(8,128)(2,1)S(1)} %get-tuple-element.27.refs_0_), channel_id=1, source_target_pairs={{4,0},{8,4},{12,8},{5,1},{9,5},{13,9},{20,16},{24,20},{28,24},{21,... | collective-permute-start | bytes 98312 | tf_op jit(solution)/shard_map/ppermute | solution.py:542
  9.1 12.2 %collective-permute-start.3 = (bf16[136,1024]{1,0:T(8,128)(2,1)S(1)}, bf16[136,1024]{1,0:T(8,128)(2,1)S(1)}, u32[]{:S(2)}, u32[]{:S(2)}) collective-permute-start(bf16[136,1024]{1,0:T(8,128)(2,1)S(1)} %get-tuple-element.32.refs_3_.refs_1_), channel_id=1, source_target_pairs={{0,2},{2,0},{4,6},{6,4},{8,10},{10,8},{12,14},{14,12},{1,3},{3,1},... | collective-permute-start | bytes 835592 | tf_op jit(solution)/shard_map/ppermute | solution.py:39
  10.1 8.9 %collective-permute-start.2 = (bf16[32,1024]{1,0:T(8,128)(2,1)S(1)}, bf16[32,1024]{1,0:T(8,128)(2,1)S(1)}, u32[]{:S(2)}, u32[]{:S(2)}) collective-permute-start(bf16[32,1024]{1,0:T(8,128)(2,1)S(1)} %get-tuple-element.31.refs_2_), channel_id=1, source_target_pairs={{0,2},{2,0},{4,6},{6,4},{8,10},{10,8},{12,14},{14,12},{1,3},{3,1},... | collective-permute-start | bytes 196616 | tf_op jit(solution)/shard_map/ppermute | solution.py:39
  19.7 11.0 %collective-permute-start.5 = (bf16[144,1024]{1,0:T(8,128)(2,1)S(1)}, bf16[144,1024]{1,0:T(8,128)(2,1)S(1)}, u32[]{:S(2)}, u32[]{:S(2)}) collective-permute-start(bf16[144,1024]{1,0:T(8,128)(2,1)S(1)} %get-tuple-element.44), channel_id=1, source_target_pairs={{0,2},{2,0},{4,6},{6,4},{8,10},{10,8},{12,14},{14,12},{1,3},{3,1},... | collective-permute-start | bytes 884744 | tf_op jit(solution)/shard_map/ppermute | solution.py:39
  21.9 8.8 %collective-permute-start.4 = (bf16[136,1024]{1,0:T(8,128)(2,1)S(1)}, bf16[136,1024]{1,0:T(8,128)(2,1)S(1)}, u32[]{:S(2)}, u32[]{:S(2)}) collective-permute-start(bf16[136,1024]{1,0:T(8,128)(2,1)S(1)} %get-tuple-element.43.refs_3_.refs_1_), channel_id=1, source_target_pairs={{0,4},{2,6},{4,0},{6,2},{8,12},{10,14},{12,8},{14,10},{1,5},{3,7},... | collective-permute-start | bytes 835592 | tf_op jit(solution)/shard_map/ppermute | solution.py:39
  23.6 11.4 %collective-permute-start.7 = (bf16[128,1024]{1,0:T(8,128)(2,1)S(1)}, bf16[128,1024]{1,0:T(8,128)(2,1)S(1)}, u32[]{:S(2)}, u32[]{:S(2)}) collective-permute-start(bf16[128,1024]{1,0:T(8,128)(2,1)S(1)} %get-tuple-element.48), channel_id=1, source_target_pairs={{0,2},{2,0},{4,6},{6,4},{8,10},{10,8},{12,14},{14,12},{1,3},{3,1},... | collective-permute-start | bytes 786440 | tf_op jit(solution)/shard_map/ppermute | solution.py:39
  31.4 17.0 %collective-permute-start.9 = (bf16[136,1024]{1,0:T(8,128)(2,1)S(1)}, bf16[136,1024]{1,0:T(8,128)(2,1)S(1)}, u32[]{:S(2)}, u32[]{:S(2)}) collective-permute-start(bf16[136,1024]{1,0:T(8,128)(2,1)S(1)} %get-tuple-element.49.refs_4_.refs_3_), channel_id=1, source_target_pairs={{0,8},{2,10},{4,12},{6,14},{8,0},{10,2},{12,4},{14,6},{1,9},{3,11}... | collective-permute-start | bytes 835592 | tf_op jit(solution)/shard_map/ppermute | solution.py:39
  34.6 9.0 %collective-permute-start.6 = (bf16[128,1024]{1,0:T(8,128)(2,1)S(1)}, bf16[128,1024]{1,0:T(8,128)(2,1)S(1)}, u32[]{:S(2)}, u32[]{:S(2)}) collective-permute-start(bf16[128,1024]{1,0:T(8,128)(2,1)S(1)} %get-tuple-element.46), channel_id=1, source_target_pairs={{0,2},{2,0},{4,6},{6,4},{8,10},{10,8},{12,14},{14,12},{1,3},{3,1},... | collective-permute-start | bytes 786440 | tf_op jit(solution)/shard_map/ppermute | solution.py:39
  35.5 12.9 %collective-permute-start.8 = (bf16[128,1024]{1,0:T(8,128)(2,1)S(1)}, bf16[128,1024]{1,0:T(8,128)(2,1)S(1)}, u32[]{:S(2)}, u32[]{:S(2)}) collective-permute-start(bf16[128,1024]{1,0:T(8,128)(2,1)S(1)} %resent.1.refs_3_), channel_id=1, source_target_pairs={{0,4},{2,6},{4,0},{6,2},{8,12},{10,14},{12,8},{14,10},{1,5},{3,7},... | collective-permute-start | bytes 786440 | tf_op jit(solution)/shard_map/ppermute | solution.py:39

commit v13 on v12

--- a/solution.py
+++ b/solution.py
@@ -61,11 +61,11 @@
     return high, middle, value - high - middle
 
 
-def packed(powers, ref_powers, channel_bound):
+def packed(powers, ref_powers, channel_bound, *more):
     rows = list(bf16_pieces(powers))
     refs = jnp.concatenate(bf16_pieces(ref_powers), axis=1)
     pad = jnp.zeros((1, powers.shape[1] - refs.shape[1]), jnp.float32)
-    rows += [jnp.concatenate([refs, pad], axis=1), channel_bound]
+    rows += [jnp.concatenate([refs, pad], axis=1), channel_bound] + list(more)
     rows += [jnp.zeros_like(powers)] * (EXTRA - len(rows))
     return jnp.concatenate(rows, axis=0).astype(jnp.bfloat16)
 
@@ -217,14 +217,30 @@
                 edges[pl.ds(start, HALF), side * LANES : (side + 1) * LANES] = moved.astype(jnp.bfloat16)
 
 
+def last_samples(own, other):
+    chan = lax.axis_index("chan")
+    ours, theirs = [refs[:, refs.shape[1] - LANES :].astype(jnp.float32) for refs in (own, other)]
+    first, second = jnp.where(chan == 0, ours, theirs), jnp.where(chan == 0, theirs, ours)
+    square = jnp.concatenate([first, second, jnp.zeros((LANES - REF, LANES), jnp.float32)], axis=0)
+    rows = square.T[LANES - LAGS :, :REF]
+    return jnp.concatenate([rows[index : index + 1] for index in range(LAGS)], axis=1)
+
+
 def ends_of(code):
-    rows = code[LAGS : 2 * LAGS, :LANES].astype(jnp.float32)
+    row = code[-EXTRA:].astype(jnp.float32)[5:6]
+    rows = jnp.concatenate([row[:, index * REF : (index + 1) * REF] for index in range(LAGS)], axis=0)
+    rows = jnp.concatenate([rows, jnp.zeros((LAGS, LANES - REF), jnp.float32)], axis=1)
     return jnp.concatenate([jnp.zeros((LANES - LAGS, LANES), jnp.float32), rows], axis=0).T[:REF]
+
+
+def tail_of(code, here):
+    first = code.shape[0] // REF * REF
+    return code[first : first + LAGS, here]
 
 
 def tails_of(sent, arrived, here):
     zeros = jnp.zeros((LANES - LAGS, here.stop - here.start), jnp.bfloat16)
-    return jnp.concatenate([arrived[:LAGS, here], zeros, sent[:LAGS, here], zeros], axis=0)
+    return jnp.concatenate([tail_of(arrived, here), zeros, tail_of(sent, here), zeros], axis=0)
 
 
 def first_products_kernel(held, power, own, other, keep, send, shifted):
@@ -240,7 +256,8 @@
     bound = rounded_up(power[...])
     pad = jnp.zeros((1, LANES - REF), jnp.float32)
     chunk = keep.shape[0]
-    send[chunk:] = packed(power[...], jnp.concatenate([as_row(refs), pad], axis=1), bound)
+    refs_row = jnp.concatenate([as_row(refs), pad], axis=1)
+    send[chunk:] = packed(power[...], refs_row, bound, last_samples(own, other))
     for here in columns(held.shape[1]):
         product = product_of(shifted, held, here)
         keep[:, here] = product[:chunk]
@@ -266,7 +283,7 @@
     )
 
 
-def later_products(groups, held, own, other, powers, chunk):
+def later_products(groups, held, own, other, powers, chunk, spare=0, after=()):
     rows, width = held.shape
 
     def kernel(held, own, other, powers, *rest):
@@ -275,80 +292,32 @@
         refs = ref_column(ref_powers)
         for index, bits in enumerate(groups):
             lag_rows(own, other, own_group(bits), shifted.at[pl.ds(index * 2 * chunk, 2 * chunk)])
+            if spare:
+                outs[2 * index + 1][chunk:] = jnp.zeros((spare, width), jnp.bfloat16)
         for here in columns(width):
             product = product_of(shifted, held, here)
             for index in range(len(groups)):
                 keep, send = outs[2 * index : 2 * index + 2]
                 first = 2 * index * chunk
                 keep[:, here] = product[first : first + chunk]
-                send[:, here] = coded(product[first + chunk : first + 2 * chunk], bound[:, here], refs)
+                send[:chunk, here] = coded(product[first + chunk : first + 2 * chunk], bound[:, here], refs)
 
     return call_on_blocks(
         kernel,
-        [((chunk, width), jnp.float32), ((chunk, width), jnp.bfloat16)] * len(groups),
+        [((chunk, width), jnp.float32), ((chunk + spare, width), jnp.bfloat16)] * len(groups),
         held,
         own,
         other,
         powers,
         name="later_products",
         micros=PRODUCT_MICROS,
+        after=after,
         scratch=shifted_scratch(rows, len(groups)),
     )
 
 
 def edges_scratch(count, chunk):
     return [pltpu.VMEM((count, chunk, 2 * LANES), jnp.bfloat16)]
-
-
-def sides_to_swap(head, after_next, own, other, held_back):
-    width = head.shape[1]
-
-    def kernel(head, after_next, own, other, held_back, sides, passed):
-        chan, near = lax.axis_index("chan"), lax.axis_index("tm") & 1
-        passed[...] = held_back[...]
-        sides[:LAGS] = jnp.where(near == 0, after_next[...], head[...])
-        ours, theirs = [refs[:, refs.shape[1] - LANES :].astype(jnp.float32) for refs in (own, other)]
-        first, second = jnp.where(chan == 0, ours, theirs), jnp.where(chan == 0, theirs, ours)
-        square = jnp.concatenate([first, second, jnp.zeros((LANES - REF, LANES), jnp.float32)], axis=0)
-        sides[LAGS:, :LANES] = square.T[LANES - LAGS :].astype(jnp.bfloat16)
-        sides[LAGS:, LANES:] = jnp.zeros((LAGS, width - LANES), jnp.bfloat16)
-
-    outs = [((2 * LAGS, width), jnp.bfloat16), (held_back.shape, jnp.bfloat16)]
-    arrays = (head, after_next, own, other, held_back)
-    return call_on_blocks(kernel, outs, *arrays, name="sides", micros=MERGE_MICROS)
-
-
-def with_boundaries(keeps, groups, own, other, sent, arrived, held_back):
-    chunk, width = keeps[0].shape
-
-    def kernel(own, other, sent, arrived, held_back, *rest):
-        keeps, rest = rest[: len(groups)], rest[len(groups) :]
-        outs, beyond, passed, edges = rest[: len(groups)], rest[-3], rest[-2], rest[-1]
-        passed[:chunk] = held_back[...]
-        passed[chunk:] = jnp.zeros((LAGS, width), jnp.bfloat16)
-        for index, bits in enumerate(groups):
-            boundary_rows(own_group(bits), (own, other), ends_of(arrived), edges.at[index])
-        for here in columns(width):
-            tails = tails_of(sent, arrived, here)
-            for index in range(len(groups)):
-                added = jnp.dot(edges[index], tails, preferred_element_type=jnp.float32)
-                outs[index][:, here] = keeps[index][:, here] + added
-            beyond[:, here] = jnp.sum(jnp.square(tails.astype(jnp.float32)), axis=0, keepdims=True)
-
-    outs = [((chunk, width), jnp.float32)] * len(groups) + [((1, width), jnp.float32), ((chunk + LAGS, width), jnp.bfloat16)]
-    return call_on_blocks(
-        kernel,
-        outs,
-        own,
-        other,
-        sent,
-        arrived,
-        held_back,
-        *keeps,
-        name="with_boundaries",
-        micros=MERGE_MICROS,
-        scratch=edges_scratch(len(groups), chunk),
-    )
 
 
 def call_on_blocks(kernel, outs, *arrays, name, micros, after=(), scratch=(), space=pltpu.VMEM):
@@ -370,33 +339,104 @@
     )(*arrays, *after)
 
 
+def with_tails(head, after_next, send):
+    rows, width = send.shape
+    chunk = rows - EXTRA
+
+    def kernel(head, after_next, send, out):
+        near = lax.axis_index("tm") & 1
+        out[:chunk] = send[:chunk]
+        out[chunk : chunk + LAGS] = jnp.where(near == 0, after_next[...], head[...])
+        out[chunk + LAGS :] = send[chunk:]
+
+    outs = [((rows + LAGS, width), jnp.bfloat16)]
+    return call_on_blocks(kernel, outs, head, after_next, send, name="with_tails", micros=MERGE_MICROS)[0]
+
+
+def with_boundaries(keeps, groups, own, other, sent, arrived, after):
+    chunk, width = keeps[0].shape
+
+    def kernel(own, other, sent, arrived, *rest):
+        keeps, outs, edges = rest[: len(groups)], rest[len(groups) : -1], rest[-1]
+        for index, bits in enumerate(groups):
+            boundary_rows(own_group(bits), (own, other), ends_of(arrived), edges.at[index])
+        for here in columns(width):
+            tails = tails_of(sent, arrived, here)
+            for index in range(len(groups)):
+                added = jnp.dot(edges[index], tails, preferred_element_type=jnp.float32)
+                outs[index][:, here] = keeps[index][:, here] + added
+
+    return call_on_blocks(
+        kernel,
+        [((chunk, width), jnp.float32)] * len(groups),
+        own,
+        other,
+        sent,
+        arrived,
+        *keeps,
+        name="with_boundaries",
+        micros=MERGE_MICROS,
+        after=after,
+        scratch=edges_scratch(len(groups), chunk),
+    )
+
+
+def merged_near(keep, group, own, other, ours, theirs, held_back):
+    chunk, width = keep.shape
+
+    def kernel(keep, own, other, ours, theirs, held_back, out, passed, edges):
+        passed[...] = held_back[...]
+        boundary_rows(own_group(group), (own, other), ends_of(theirs), edges.at[0])
+        powers, refs, bound = sent_powers(ours)
+        their_powers, their_refs, their_bound = sent_powers(theirs)
+        their_refs_column, sum_refs = ref_column(their_refs), refs + their_refs
+        sum_refs_column = ref_column(sum_refs)
+        bounds = []
+        for here in columns(width):
+            tails = tails_of(ours, theirs, here)
+            total = keep[:, here] + jnp.dot(edges[0], tails, preferred_element_type=jnp.float32)
+            total += expanded(theirs[:chunk, here], their_bound[:, here], their_refs_column)
+            beyond = jnp.sum(jnp.square(tails.astype(jnp.float32)), axis=0, keepdims=True)
+            bounds.append(rounded_up(bound[:, here] + their_bound[:, here] + beyond))
+            out[:chunk, here] = coded(total, bounds[-1], sum_refs_column)
+        out[chunk:] = packed(powers + their_powers, sum_refs, jnp.concatenate(bounds, axis=1))
+
+    return call_on_blocks(
+        kernel,
+        [((chunk + EXTRA, width), jnp.bfloat16), (held_back.shape, jnp.bfloat16)],
+        keep,
+        own,
+        other,
+        ours,
+        theirs,
+        held_back,
+        name="merged_near",
+        micros=MERGE_MICROS,
+        scratch=edges_scratch(1, chunk),
+    )
+
+
 def direct_sums(direct, powers):
     _, refs, bound = sent_powers(powers)
     chunk = direct.shape[0] // REF * REF
     return expanded(direct[:chunk], bound, ref_column(refs))
 
 
-def merged(keep, ours, theirs, direct=(), beyond=(), held_back=(), after=()):
+def merged(keep, ours, theirs, direct, direct_powers, held_back, after):
     chunk, width = keep.shape
 
-    def kernel(keep, ours, theirs, *refs):
-        inputs, out, passed = refs[: -1 - len(held_back)], refs[len(arrays) - 3], refs[len(arrays) - 2 :]
+    def kernel(keep, ours, theirs, direct, direct_powers, held_back, out, passed):
+        passed[...] = held_back[...]
         powers, refs, bound = sent_powers(ours)
         their_powers, their_refs, their_bound = sent_powers(theirs)
-        sums, sum_refs, sum_bound = powers + their_powers, refs + their_refs, bound + their_bound
+        sum_refs, sum_bound = refs + their_refs, rounded_up(bound + their_bound)
         total = keep[...] + expanded(theirs[:chunk], their_bound, ref_column(their_refs))
-        if direct:
-            total += direct_sums(inputs[0], inputs[1])
-        if beyond:
-            sum_bound += inputs[len(direct)][...]
-        if held_back:
-            passed[0][...] = inputs[-1][...]
-        sum_bound = rounded_up(sum_bound)
-        out[chunk:] = packed(sums, sum_refs, sum_bound)
+        total += direct_sums(direct, direct_powers)
+        out[chunk:] = packed(powers + their_powers, sum_refs, sum_bound)
         out[:chunk] = coded(total, sum_bound, ref_column(sum_refs))
 
-    outs = [((chunk + EXTRA, width), jnp.bfloat16)] + [(code.shape, code.dtype) for code in held_back]
-    arrays = (keep, ours, theirs, *direct, *beyond, *held_back)
+    outs = [((chunk + EXTRA, width), jnp.bfloat16), (held_back.shape, jnp.bfloat16)]
+    arrays = (keep, ours, theirs, direct, direct_powers, held_back)
     return call_on_blocks(kernel, outs, *arrays, name="merged", micros=MERGE_MICROS, after=after)
 
 
@@ -469,7 +509,7 @@
             if part < 7:
                 following = held[end : end + LAGS, here].astype(jnp.float32)
             else:
-                following = tail[:LAGS, here].astype(jnp.float32)
+                following = tail_of(tail, here).astype(jnp.float32)
             wide[part * pitch + step : (part + 1) * pitch, :] = following
         taken = lambda first: wide[pl.ds(first, 8, stride=pitch), :]
 
@@ -556,29 +596,26 @@
     if chunk * 2 == GROUP * REF:
         keep6, send7 = first_products(held, power, own, other, chunk)
         after_next = from_pair_ahead(head)
-        sides, send7 = sides_to_swap(head, after_next, own, other, send7)
+        send7 = with_tails(head, after_next, send7)
         got7 = exchanged(send7, "tm", 1)
-        tails = (sides, exchanged(sides, "tm", 1))
-        keep4, send5, keep2, send3, keep0, send1 = later_products(
-            (2, 1, 0), held, own, other, send7, chunk
+        keep4, send5 = later_products((2,), held, own, other, send7, chunk, spare=LAGS)
+        got5 = exchanged(send5, "tm", 1)
+        keep2, send3, keep0, send1 = later_products(
+            (1, 0), held, own, other, send7, chunk, after=(send5,)
         )
-        *keeps, beyond, send5 = with_boundaries(
-            (keep6, keep4, keep2, keep0), (3, 2, 1, 0), own, other, *tails, send5
-        )
-        got5 = exchanged(send5, "tm", 1)
-        keep6, keep4, keep2, keep0 = keeps
-        send6, send3 = merged(keep6, send7, got7, beyond=(beyond,), held_back=(send3,))
+        send6, send3 = merged_near(keep6, 3, own, other, send7, got7, send3)
         got6 = exchanged(send6, "tm", 2)
         got3 = exchanged(send3, "tm", 1)
-        autos = [segment_rows(held, power, tails[1], 0, size, after=(send6,))]
-        send4, send1 = merged(
-            keep4, send6, got6, direct=(got5, got7), held_back=(send1,), after=(autos[0],)
+        keep4, keep2, keep0 = with_boundaries(
+            (keep4, keep2, keep0), (2, 1, 0), own, other, send7, got7, after=(send6,)
         )
+        autos = [segment_rows(held, power, got7, 0, size, after=(keep4,))]
+        send4, send1 = merged(keep4, send6, got6, got5, got7, send1, after=(autos[0],))
         got4 = exchanged(send4, "tm", 4)
         got1 = exchanged(send1, "tm", 1)
         send2 = resent(keep2, got3, got7, send6, after=(send4,))
         got2 = exchanged(send2, "tm", 2)
-        autos.append(segment_rows(held, power, tails[1], size, size, after=(send2,)))
+        autos.append(segment_rows(held, power, got7, size, size, after=(send2,)))
         partial = added(keep0, got1, got7, after=(autos[1],))
         return tuple(finished(slab_rows, rows, partial, got2, got6, send4, got4, autos))
 

time: 50 us -> 48 us (0.960)
  starting transfers between devices: 15.3 us -> 12 us
  Pallas kernels: 25.9 us -> 26.5 us
  waiting for transfers between devices: 7.92 us -> 8.52 us
    ppermute x9 -> x8, starting transfers between devices: 14 us -> 10.7 us  [exchanged(): lax.ppermute(value, axis, [(source, source ^ bit) for source in range(cou...]
    pallas_call x11 -> x12, Pallas kernels: 22.3 us -> 23 us  [call_on_blocks(): pl.pallas_call(body, in_specs=[vmem] * count + [pl.BlockSpec(memory_space...]
    ppermute x9 -> x8, waiting for transfers between devices: 7.03 us -> 7.65 us  [exchanged(): lax.ppermute(value, axis, [(source, source ^ bit) for source in range(cou...]
  transfers between devices with their start and end apart: 10 -> 9, of which waited for: 3 -> 3; matrix products, arithmetic and copies ran while one was open for 0% -> 0% of each run, Pallas kernels for 46% -> 50%
where the time goes in v13:
time: 48 us; the launch traced here: 47.8 us
  Pallas kernels  26.5 us (55%)
  starting transfers between devices  12 us (25%)
  waiting for transfers between devices  8.52 us (18%)
  between operations  0.76 us (2%)
    pallas_call x12, Pallas kernels, call_on_blocks(): pl.pallas_call(body, in_specs=[vmem] * count + [pl.BlockSpec(memory_space...  23 us
    ppermute x8, starting transfers between devices, exchanged(): lax.ppermute(value, axis, [(source, source ^ bit) for source in range(cou...  10.7 us
    ppermute x8, waiting for transfers between devices, exchanged(): lax.ppermute(value, axis, [(source, source ^ bit) for source in range(cou...  7.65 us
    pallas_call x1, Pallas kernels, loaded(): pl.pallas_call(kernel, in_specs=[pl.BlockSpec(memory_space=pl.ANY)] * 2,...  2.26 us
    ppermute x1, starting transfers between devices, from_pair_ahead(): lax.ppermute(value, 'tm', [(time + 2, time) for time in range(0, count -...  1.28 us
    pallas_call x1, Pallas kernels, prepared(): pl.pallas_call(prepare_kernel, in_specs=[pl.BlockSpec(memory_space=pl.ANY...  1.28 us
  transfers between devices with their start and end apart: 9, of which 3 were waited for; matrix products, arithmetic and copies ran while one was open for 0% of the time, Pallas kernels for 50%

profile of v13, /device:TPU:0, one launch (start us, length us, event | category | flops | bytes accessed | tf_op | source)
XLA Modules:
  0.0 47.8 jit_solution(3229227538966392056)
XLA Ops:
  0.6 1.3 %prepared.1 = (bf16[32,2048]{1,0:T(8,128)(2,1)S(1)}, bf16[16,1024]{1,0:T(8,128)(2,1)S(1)}) custom-call(bf16[2048,1024]{1,0:T(8,128)(2,1)} %strain.3), custom_call_target="tpu_custom_call" | custom-call | bytes 3690000 | tf_op jit(solution)/shard_map/prepared/pallas_call | solution.py:131
  1.9 0.5 %collective-permute-start = (bf16[32,2048]{1,0:T(8,128)(2,1)S(1)}, bf16[32,2048]{1,0:T(8,128)(2,1)S(1)}, u32[]{:S(2)}, u32[]{:S(2)}) collective-permute-start(bf16[32,2048]{1,0:T(8,128)(2,1)S(1)} %get-tuple-element.21.after.refs_2_.refs_1_.refs_0_), channel_id=1, source_target_pairs={{0,1},{1,0},{2,3},{3,2},{4,5},{5,4},{6,7},{7,6},{8,9},{9,8},{10,11... | collective-permute-start | bytes 393224 | tf_op jit(solution)/shard_map/ppermute | solution.py:39
  2.4 1.3 %collective-permute-start.1 = (bf16[16,1024]{1,0:T(8,128)(2,1)S(1)}, bf16[16,1024]{1,0:T(8,128)(2,1)S(1)}, u32[]{:S(2)}, u32[]{:S(2)}) collective-permute-start(bf16[16,1024]{1,0:T(8,128)(2,1)S(1)} %get-tuple-element.22.refs_0_), channel_id=1, source_target_pairs={{4,0},{8,4},{12,8},{5,1},{9,5},{13,9},{20,16},{24,20},{28,24},{21,... | collective-permute-start | bytes 98312 | tf_op jit(solution)/shard_map/ppermute | solution.py:582
  3.7 2.3 %loaded.1 = (bf16[2048,1024]{1,0:T(8,128)(2,1)S(1)}, f32[1,1024]{1,0:T(1,128)S(1)}) custom-call(bf16[2048,1024]{1,0:T(8,128)(2,1)} %strain.3, bf16[32,2048]{1,0:T(8,128)(2,1)S(1)} %get-tuple-element.21.after.refs_2_.refs_1_.refs_0_), custom_call_target="tpu_custom_call" | custom-call | bytes 3690000 | tf_op jit(solution)/shard_map/loaded/pallas_call | solution.py:185
  6.0 0.0 collective-permute-done.refs_3_.refs_2_.refs_1_
  6.0 2.1 %first_products.1 = (f32[128,1024]{1,0:T(8,128)S(1)}, bf16[136,1024]{1,0:T(8,128)(2,1)S(1)}) custom-call(bf16[2048,1024]{1,0:T(8,128)(2,1)S(1)} %get-tuple-element.23.refs_0_, f32[1,1024]{1,0:T(1,128)S(1)} %get-tuple-element.24.refs_1_, bf16[32,2048]{1,0:T(8,128)(2,1)S(1)} %get-tuple-element.21.after.refs_2_.refs_1_.refs_0_, ...), custom_call_target="tpu_custom_call" | custom-call | bytes 3690000 | tf_op jit(solution)/shard_map/first_products/pallas_call | solution.py:330
  8.1 0.9 %collective-permute-done.1.refs_1_ = bf16[16,1024]{1,0:T(8,128)(2,1)S(1)} collective-permute-done((bf16[16,1024]{1,0:T(8,128)(2,1)S(1)}, bf16[16,1024]{1,0:T(8,128)(2,1)S(1)}, u32[]{:S(2)}, u32[]{:S(2)}) %collective-permute-start.1) | collective-permute-done | bytes 32800 | tf_op jit(solution)/shard_map/ppermute | solution.py:582
  9.0 1.1 %collective-permute-start.2 = (bf16[152,1024]{1,0:T(8,128)(2,1)S(1)}, bf16[152,1024]{1,0:T(8,128)(2,1)S(1)}, u32[]{:S(2)}, u32[]{:S(2)}) collective-permute-start(bf16[152,1024]{1,0:T(8,128)(2,1)S(1)} %with_tails.1.refs_3_.refs_2_), channel_id=1, source_target_pairs={{0,2},{2,0},{4,6},{6,4},{8,10},{10,8},{12,14},{14,12},{1,3},{3,1},... | collective-permute-start | bytes 933896 | tf_op jit(solution)/shard_map/ppermute | solution.py:39
  10.1 2.0 %later_products.2 = (f32[128,1024]{1,0:T(8,128)S(1)}, bf16[144,1024]{1,0:T(8,128)(2,1)S(1)}) custom-call(bf16[2048,1024]{1,0:T(8,128)(2,1)S(1)} %get-tuple-element.23.refs_0_, bf16[32,2048]{1,0:T(8,128)(2,1)S(1)} %get-tuple-element.21.after.refs_2_.refs_1_.refs_0_, bf16[32,2048]{1,0:T(8,128)(2,1)S(1)} %collective-permute-done.refs_3_.refs_2_.refs_1_, ...), custom_call_target="tpu_custom_call" | custom-call | bytes 3690000 | tf_op jit(solution)/shard_map/later_products/pallas_call | solution.py:330
  12.1 1.1 %collective-permute-start.4 = (bf16[144,1024]{1,0:T(8,128)(2,1)S(1)}, bf16[144,1024]{1,0:T(8,128)(2,1)S(1)}, u32[]{:S(2)}, u32[]{:S(2)}) collective-permute-start(bf16[144,1024]{1,0:T(8,128)(2,1)S(1)} %get-tuple-element.27.refs_4_), channel_id=1, source_target_pairs={{0,2},{2,0},{4,6},{6,4},{8,10},{10,8},{12,14},{14,12},{1,3},{3,1},... | collective-permute-start | bytes 884744 | tf_op jit(solution)/shard_map/ppermute | solution.py:39
  13.1 3.7 %later_products.3 = (f32[128,1024]{1,0:T(8,128)S(1)}, bf16[128,1024]{1,0:T(8,128)(2,1)S(1)}, f32[128,1024]{1,0:T(8,128)S(1)}, bf16[128,1024]{1,0:T(8,128)(2,1)S(1)}) custom-call(bf16[2048,1024]{1,0:T(8,128)(2,1)S(1)} %get-tuple-element.23.refs_0_, bf16[32,2048]{1,0:T(8,128)(2,1)S(1)} %get-tuple-element.21.after.refs_2_.refs_1_.refs_0_, ...), custom_call_target="tpu_custom_call" | custom-call | bytes 3690000 | tf_op jit(solution)/shard_map/later_products/pallas_call | solution.py:330
  16.8 2.5 %collective-permute-done.2.refs_4_.refs_3_.refs_2_ = bf16[152,1024]{1,0:T(8,128)(2,1)S(1)} collective-permute-done((bf16[152,1024]{1,0:T(8,128)(2,1)S(1)}, bf16[152,1024]{1,0:T(8,128)(2,1)S(1)}, u32[]{:S(2)}, u32[]{:S(2)}) %collective-permute-start.2) | collective-permute-done | bytes 311328 | tf_op jit(solution)/shard_map/ppermute | solution.py:39
  19.3 0.7 %merged_near.1 = (bf16[136,1024]{1,0:T(8,128)(2,1)S(1)}, bf16[128,1024]{1,0:T(8,128)(2,1)S(1)}) custom-call(f32[128,1024]{1,0:T(8,128)S(1)} %get-tuple-element.30.refs_0_, bf16[32,2048]{1,0:T(8,128)(2,1)S(1)} %get-tuple-element.21.after.refs_2_.refs_1_.refs_0_, bf16[32,2048]{1,0:T(8,128)(2,1)S(1)} %collective-permute-done.refs_3_.refs_2_.refs_1_, ...), custom_call_target="tpu_custom_call" | custom-call | bytes 1107000 | tf_op jit(solution)/shard_map/merged_near/pallas_call | solution.py:330
  20.0 2.4 %collective-permute-start.3 = (bf16[136,1024]{1,0:T(8,128)(2,1)S(1)}, bf16[136,1024]{1,0:T(8,128)(2,1)S(1)}, u32[]{:S(2)}, u32[]{:S(2)}) collective-permute-start(bf16[136,1024]{1,0:T(8,128)(2,1)S(1)} %get-tuple-element.32.refs_7_.refs_1_.refs_3_), channel_id=1, source_target_pairs={{0,4},{2,6},{4,0},{6,2},{8,12},{10,14},{12,8},{14,10},{1,5},{3,7},... | collective-permute-start | bytes 835592 | tf_op jit(solution)/shard_map/ppermute | solution.py:39
  22.4 0.2 collective-permute-start.6
  22.6 0.6 %with_boundaries.1 = (f32[128,1024]{1,0:T(8,128)S(1)}, f32[128,1024]{1,0:T(8,128)S(1)}, f32[128,1024]{1,0:T(8,128)S(1)}) custom-call(bf16[32,2048]{1,0:T(8,128)(2,1)S(1)} %get-tuple-element.21.after.refs_2_.refs_1_.refs_0_, bf16[32,2048]{1,0:T(8,128)(2,1)S(1)} %collective-permute-done.refs_3_.refs_2_.refs_1_, ...), custom_call_target="tpu_custom_call" | custom-call | bytes 1107000 | tf_op jit(solution)/shard_map/with_boundaries/pallas_call | solution.py:330
  23.2 5.5 %segment_rows.2.refs_6_.refs_5_ = f32[16,512]{1,0:T(8,128)S(1)} custom-call(bf16[2048,1024]{1,0:T(8,128)(2,1)S(1)} %get-tuple-element.23.refs_0_, f32[1,1024]{1,0:T(1,128)S(1)} %get-tuple-element.24.refs_1_, bf16[152,1024]{1,0:T(8,128)(2,1)S(1)} %collective-permute-done.2.refs_4_.refs_3_.refs_2_, f32[128,1024]{1,0:T(8,128)S(1)} %get-tuple-element.34.refs_3_.refs_0_), custom_call_target="tpu_custom_call" | custom-call | bytes 4428000 | tf_op jit(solution)/shard_map/segment_rows/pallas_call | solution.py:330
  28.7 0.0 collective-permute-done.4.refs_3_
  28.8 0.0 collective-permute-done.3.refs_2_
  28.8 0.8 %merged.1 = (bf16[136,1024]{1,0:T(8,128)(2,1)S(1)}, bf16[128,1024]{1,0:T(8,128)(2,1)S(1)}) custom-call(f32[128,1024]{1,0:T(8,128)S(1)} %get-tuple-element.34.refs_3_.refs_0_, bf16[136,1024]{1,0:T(8,128)(2,1)S(1)} %get-tuple-element.32.refs_7_.refs_1_.refs_3_, bf16[136,1024]{1,0:T(8,128)(2,1)S(1)} %collective-permute-done.3.refs_2_, ...), custom_call_target="tpu_custom_call" | custom-call | bytes 1107000 | tf_op jit(solution)/shard_map/merged/pallas_call | solution.py:330
  29.6 2.9 %collective-permute-start.8 = (bf16[136,1024]{1,0:T(8,128)(2,1)S(1)}, bf16[136,1024]{1,0:T(8,128)(2,1)S(1)}, u32[]{:S(2)}, u32[]{:S(2)}) collective-permute-start(bf16[136,1024]{1,0:T(8,128)(2,1)S(1)} %get-tuple-element.39.refs_4_.refs_3_), channel_id=1, source_target_pairs={{0,8},{2,10},{4,12},{6,14},{8,0},{10,2},{12,4},{14,6},{1,9},{3,11}... | collective-permute-start | bytes 835592 | tf_op jit(solution)/shard_map/ppermute | solution.py:39
  32.5 2.0 %collective-permute-start.5 = (bf16[128,1024]{1,0:T(8,128)(2,1)S(1)}, bf16[128,1024]{1,0:T(8,128)(2,1)S(1)}, u32[]{:S(2)}, u32[]{:S(2)}) collective-permute-start(bf16[128,1024]{1,0:T(8,128)(2,1)S(1)} %get-tuple-element.36), channel_id=1, source_target_pairs={{0,2},{2,0},{4,6},{6,4},{8,10},{10,8},{12,14},{14,12},{1,3},{3,1},... | collective-permute-start | bytes 786440 | tf_op jit(solution)/shard_map/ppermute | solution.py:39
  34.5 0.0 collective-permute-done.6.refs_1_
  34.5 0.5 %resent.1.refs_3_ = bf16[128,1024]{1,0:T(8,128)(2,1)S(1)} custom-call(f32[128,1024]{1,0:T(8,128)S(1)} %get-tuple-element.37.refs_0_, bf16[128,1024]{1,0:T(8,128)(2,1)S(1)} %collective-permute-done.6.refs_1_, bf16[152,1024]{1,0:T(8,128)(2,1)S(1)} %collective-permute-done.2.refs_4_.refs_3_.refs_2_, ...), custom_call_target="tpu_custom_call" | custom-call | bytes 1107000 | tf_op jit(solution)/shard_map/resent/pallas_call | solution.py:330
  35.0 0.5 %collective-permute-start.7 = (bf16[128,1024]{1,0:T(8,128)(2,1)S(1)}, bf16[128,1024]{1,0:T(8,128)(2,1)S(1)}, u32[]{:S(2)}, u32[]{:S(2)}) collective-permute-start(bf16[128,1024]{1,0:T(8,128)(2,1)S(1)} %resent.1.refs_3_), channel_id=1, source_target_pairs={{0,4},{2,6},{4,0},{6,2},{8,12},{10,14},{12,8},{14,10},{1,5},{3,7},... | collective-permute-start | bytes 786440 | tf_op jit(solution)/shard_map/ppermute | solution.py:39
  35.5 5.3 %segment_rows.3.refs_3_.refs_6_ = f32[16,512]{1,0:T(8,128)S(1)} custom-call(bf16[2048,1024]{1,0:T(8,128)(2,1)S(1)} %get-tuple-element.23.refs_0_, f32[1,1024]{1,0:T(1,128)S(1)} %get-tuple-element.24.refs_1_, bf16[152,1024]{1,0:T(8,128)(2,1)S(1)} %collective-permute-done.2.refs_4_.refs_3_.refs_2_, bf16[128,1024]{1,0:T(8,128)(2,1)S(1)} %resent.1.refs_3_), custom_call_target="tpu_custom_call" | custom-call | bytes 4428000 | tf_op jit(solution)/shard_map/segment_rows/pallas_call | solution.py:330
  40.9 0.0 collective-permute-done.5.refs_1_
  40.9 0.3 added.1.refs_0_
  41.2 5.2 %collective-permute-done.7.refs_1_ = bf16[128,1024]{1,0:T(8,128)(2,1)S(1)} collective-permute-done((bf16[128,1024]{1,0:T(8,128)(2,1)S(1)}, bf16[128,1024]{1,0:T(8,128)(2,1)S(1)}, u32[]{:S(2)}, u32[]{:S(2)}) %collective-permute-start.7) | collective-permute-done | bytes 262176 | tf_op jit(solution)/shard_map/ppermute | solution.py:39
  46.4 0.0 collective-permute-done.8.refs_4_
  46.4 1.4 %finished.1 = (f32[128,1024]{1,0:T(8,128)}, f32[16,1024]{1,0:T(8,128)}) custom-call(f32[128,1024]{1,0:T(8,128)S(1)} %added.1.refs_0_, bf16[128,1024]{1,0:T(8,128)(2,1)S(1)} %collective-permute-done.7.refs_1_, bf16[136,1024]{1,0:T(8,128)(2,1)S(1)} %collective-permute-done.3.refs_2_, bf16[136,1024]{1,0:T(8,128)(2,1)S(1)} %get-tuple-element.39.refs_4_.refs_3_, ...), custom_call_target="tpu_custom_call" | custom-call | bytes 1107000 | tf_op jit(solution)/shard_map/finished/pallas_call | solution.py:330
  (1 shorter events, 0.0 us)
Async XLA Ops:
  1.9 4.1 %collective-permute-start = (bf16[32,2048]{1,0:T(8,128)(2,1)S(1)}, bf16[32,2048]{1,0:T(8,128)(2,1)S(1)}, u32[]{:S(2)}, u32[]{:S(2)}) collective-permute-start(bf16[32,2048]{1,0:T(8,128)(2,1)S(1)} %get-tuple-element.21.after.refs_2_.refs_1_.refs_0_), channel_id=1, source_target_pairs={{0,1},{1,0},{2,3},{3,2},{4,5},{5,4},{6,7},{7,6},{8,9},{9,8},{10,11... | collective-permute-start | bytes 393224 | tf_op jit(solution)/shard_map/ppermute | solution.py:39
  2.4 6.5 %collective-permute-start.1 = (bf16[16,1024]{1,0:T(8,128)(2,1)S(1)}, bf16[16,1024]{1,0:T(8,128)(2,1)S(1)}, u32[]{:S(2)}, u32[]{:S(2)}) collective-permute-start(bf16[16,1024]{1,0:T(8,128)(2,1)S(1)} %get-tuple-element.22.refs_0_), channel_id=1, source_target_pairs={{4,0},{8,4},{12,8},{5,1},{9,5},{13,9},{20,16},{24,20},{28,24},{21,... | collective-permute-start | bytes 98312 | tf_op jit(solution)/shard_map/ppermute | solution.py:582
  9.0 10.3 %collective-permute-start.2 = (bf16[152,1024]{1,0:T(8,128)(2,1)S(1)}, bf16[152,1024]{1,0:T(8,128)(2,1)S(1)}, u32[]{:S(2)}, u32[]{:S(2)}) collective-permute-start(bf16[152,1024]{1,0:T(8,128)(2,1)S(1)} %with_tails.1.refs_3_.refs_2_), channel_id=1, source_target_pairs={{0,2},{2,0},{4,6},{6,4},{8,10},{10,8},{12,14},{14,12},{1,3},{3,1},... | collective-permute-start | bytes 933896 | tf_op jit(solution)/shard_map/ppermute | solution.py:39
  12.1 16.7 %collective-permute-start.4 = (bf16[144,1024]{1,0:T(8,128)(2,1)S(1)}, bf16[144,1024]{1,0:T(8,128)(2,1)S(1)}, u32[]{:S(2)}, u32[]{:S(2)}) collective-permute-start(bf16[144,1024]{1,0:T(8,128)(2,1)S(1)} %get-tuple-element.27.refs_4_), channel_id=1, source_target_pairs={{0,2},{2,0},{4,6},{6,4},{8,10},{10,8},{12,14},{14,12},{1,3},{3,1},... | collective-permute-start | bytes 884744 | tf_op jit(solution)/shard_map/ppermute | solution.py:39
  20.0 8.8 %collective-permute-start.3 = (bf16[136,1024]{1,0:T(8,128)(2,1)S(1)}, bf16[136,1024]{1,0:T(8,128)(2,1)S(1)}, u32[]{:S(2)}, u32[]{:S(2)}) collective-permute-start(bf16[136,1024]{1,0:T(8,128)(2,1)S(1)} %get-tuple-element.32.refs_7_.refs_1_.refs_3_), channel_id=1, source_target_pairs={{0,4},{2,6},{4,0},{6,2},{8,12},{10,14},{12,8},{14,10},{1,5},{3,7},... | collective-permute-start | bytes 835592 | tf_op jit(solution)/shard_map/ppermute | solution.py:39
  22.4 12.2 %collective-permute-start.6 = (bf16[128,1024]{1,0:T(8,128)(2,1)S(1)}, bf16[128,1024]{1,0:T(8,128)(2,1)S(1)}, u32[]{:S(2)}, u32[]{:S(2)}) collective-permute-start(bf16[128,1024]{1,0:T(8,128)(2,1)S(1)} %get-tuple-element.38), channel_id=1, source_target_pairs={{0,2},{2,0},{4,6},{6,4},{8,10},{10,8},{12,14},{14,12},{1,3},{3,1},... | collective-permute-start | bytes 786440 | tf_op jit(solution)/shard_map/ppermute | solution.py:39
  29.6 16.8 %collective-permute-start.8 = (bf16[136,1024]{1,0:T(8,128)(2,1)S(1)}, bf16[136,1024]{1,0:T(8,128)(2,1)S(1)}, u32[]{:S(2)}, u32[]{:S(2)}) collective-permute-start(bf16[136,1024]{1,0:T(8,128)(2,1)S(1)} %get-tuple-element.39.refs_4_.refs_3_), channel_id=1, source_target_pairs={{0,8},{2,10},{4,12},{6,14},{8,0},{10,2},{12,4},{14,6},{1,9},{3,11}... | collective-permute-start | bytes 835592 | tf_op jit(solution)/shard_map/ppermute | solution.py:39
  32.5 8.4 %collective-permute-start.5 = (bf16[128,1024]{1,0:T(8,128)(2,1)S(1)}, bf16[128,1024]{1,0:T(8,128)(2,1)S(1)}, u32[]{:S(2)}, u32[]{:S(2)}) collective-permute-start(bf16[128,1024]{1,0:T(8,128)(2,1)S(1)} %get-tuple-element.36), channel_id=1, source_target_pairs={{0,2},{2,0},{4,6},{6,4},{8,10},{10,8},{12,14},{14,12},{1,3},{3,1},... | collective-permute-start | bytes 786440 | tf_op jit(solution)/shard_map/ppermute | solution.py:39
  35.0 11.3 %collective-permute-start.7 = (bf16[128,1024]{1,0:T(8,128)(2,1)S(1)}, bf16[128,1024]{1,0:T(8,128)(2,1)S(1)}, u32[]{:S(2)}, u32[]{:S(2)}) collective-permute-start(bf16[128,1024]{1,0:T(8,128)(2,1)S(1)} %resent.1.refs_3_), channel_id=1, source_target_pairs={{0,4},{2,6},{4,0},{6,2},{8,12},{10,14},{12,8},{14,10},{1,5},{3,7},... | collective-permute-start | bytes 786440 | tf_op jit(solution)/shard_map/ppermute | solution.py:39

commit v14 on v13

--- a/solution.py
+++ b/solution.py
@@ -422,11 +422,10 @@
     return expanded(direct[:chunk], bound, ref_column(refs))
 
 
-def merged(keep, ours, theirs, direct, direct_powers, held_back, after):
+def merged(keep, ours, theirs, direct, direct_powers, after):
     chunk, width = keep.shape
 
-    def kernel(keep, ours, theirs, direct, direct_powers, held_back, out, passed):
-        passed[...] = held_back[...]
+    def kernel(keep, ours, theirs, direct, direct_powers, out):
         powers, refs, bound = sent_powers(ours)
         their_powers, their_refs, their_bound = sent_powers(theirs)
         sum_refs, sum_bound = refs + their_refs, rounded_up(bound + their_bound)
@@ -435,9 +434,9 @@
         out[chunk:] = packed(powers + their_powers, sum_refs, sum_bound)
         out[:chunk] = coded(total, sum_bound, ref_column(sum_refs))
 
-    outs = [((chunk + EXTRA, width), jnp.bfloat16), (held_back.shape, jnp.bfloat16)]
-    arrays = (keep, ours, theirs, direct, direct_powers, held_back)
-    return call_on_blocks(kernel, outs, *arrays, name="merged", micros=MERGE_MICROS, after=after)
+    outs = [((chunk + EXTRA, width), jnp.bfloat16)]
+    arrays = (keep, ours, theirs, direct, direct_powers)
+    return call_on_blocks(kernel, outs, *arrays, name="merged", micros=MERGE_MICROS, after=after)[0]
 
 
 def resent(keep, direct, direct_powers, ours, after):
@@ -527,23 +526,27 @@
         )
 
 
-def segment_rows(held, power, tail, first, size, after=()):
+def segment_rows(held, power, tail, first, size, held_back=(), after=()):
     rows = held.shape[0]
 
-    def kernel(*refs):
-        segment_kernel(first, *refs)
+    def kernel(held, power, tail, *refs):
+        codes, out, passed, wide = refs[: len(held_back)], refs[len(held_back)], refs[len(held_back) + 1 : -1], refs[-1]
+        for code, to in zip(codes, passed):
+            to[...] = code[...]
+        segment_kernel(first, held, power, tail, out, wide)
 
     return call_on_blocks(
         kernel,
-        [((LAGS, size), jnp.float32)],
+        [((LAGS, size), jnp.float32)] + [(code.shape, code.dtype) for code in held_back],
         held,
         power,
         tail,
+        *held_back,
         name="segment_rows",
         micros=SEGMENT_MICROS,
         after=after,
         scratch=[pltpu.VMEM((rows + 8 * LAGS, LANES), jnp.float32)],
-    )[0]
+    )
 
 
 def all_products_kernel(held, own, other, tail, out, shifted):
@@ -591,8 +594,6 @@
     own, head = prepared(strain)
     other = exchanged(own, "chan", 1)
     held, power = loaded(strain, own)
-    size = width // 2
-
     if chunk * 2 == GROUP * REF:
         keep6, send7 = first_products(held, power, own, other, chunk)
         after_next = from_pair_ahead(head)
@@ -609,22 +610,21 @@
         keep4, keep2, keep0 = with_boundaries(
             (keep4, keep2, keep0), (2, 1, 0), own, other, send7, got7, after=(send6,)
         )
-        autos = [segment_rows(held, power, got7, 0, size, after=(keep4,))]
-        send4, send1 = merged(keep4, send6, got6, got5, got7, send1, after=(autos[0],))
+        size = width // 4
+        auto, send1 = segment_rows(held, power, got7, 0, size, held_back=(send1,), after=(keep4,))
+        got1 = exchanged(send1, "tm", 1)
+        send4 = merged(keep4, send6, got6, got5, got7, after=(auto,))
         got4 = exchanged(send4, "tm", 4)
-        got1 = exchanged(send1, "tm", 1)
         send2 = resent(keep2, got3, got7, send6, after=(send4,))
         got2 = exchanged(send2, "tm", 2)
-        autos.append(segment_rows(held, power, got7, size, size, after=(send2,)))
+        autos = [auto, *segment_rows(held, power, got7, size, width - size, after=(send2,))]
         partial = added(keep0, got1, got7, after=(autos[1],))
         return tuple(finished(slab_rows, rows, partial, got2, got6, send4, got4, autos))
 
     tail = passed_along(head, "tm", -1)
     chan = lax.axis_index("chan").astype(jnp.int32)
     time = lax.axis_index("tm").astype(jnp.int32)
-    auto = jnp.concatenate(
-        [segment_rows(held, power, tail, size * index, size) for index in range(2)], axis=1
-    )
+    (auto,) = segment_rows(held, power, tail, 0, width)
     power_other = jnp.sum(jnp.square(other.astype(jnp.float32)), axis=1)
     power = lax.psum(jnp.concatenate([power[0], power_other]), "tm")
     inv = 1.0 / jnp.sqrt(power / slab_rows + 1e-06)

time: 48 us -> 46.4 us (0.967)
  waiting for transfers between devices: 8.52 us -> 7.55 us
  starting transfers between devices: 12 us -> 11.4 us
    ppermute x8, waiting for transfers between devices: 7.65 us -> 6.68 us  [exchanged(): lax.ppermute(value, axis, [(source, source ^ bit) for source in range(cou...]
    ppermute x8, starting transfers between devices: 10.7 us -> 10.2 us  [exchanged(): lax.ppermute(value, axis, [(source, source ^ bit) for source in range(cou...]
  transfers between devices with their start and end apart: 9 -> 9, of which waited for: 3 -> 4; matrix products, arithmetic and copies ran while one was open for 0% -> 0% of each run, Pallas kernels for 50% -> 51%
where the time goes in v14:
time: 46.4 us; the launch traced here: 46.3 us
  Pallas kernels  26.5 us (57%)
  starting transfers between devices  11.4 us (25%)
  waiting for transfers between devices  7.55 us (16%)
  between operations  0.75 us (2%)
    pallas_call x12, Pallas kernels, call_on_blocks(): pl.pallas_call(body, in_specs=[vmem] * count + [pl.BlockSpec(memory_space...  23 us
    ppermute x8, starting transfers between devices, exchanged(): lax.ppermute(value, axis, [(source, source ^ bit) for source in range(cou...  10.2 us
    ppermute x8, waiting for transfers between devices, exchanged(): lax.ppermute(value, axis, [(source, source ^ bit) for source in range(cou...  6.68 us
    pallas_call x1, Pallas kernels, loaded(): pl.pallas_call(kernel, in_specs=[pl.BlockSpec(memory_space=pl.ANY)] * 2,...  2.26 us
    ppermute x1, starting transfers between devices, from_pair_ahead(): lax.ppermute(value, 'tm', [(time + 2, time) for time in range(0, count -...  1.28 us
    pallas_call x1, Pallas kernels, prepared(): pl.pallas_call(prepare_kernel, in_specs=[pl.BlockSpec(memory_space=pl.ANY...  1.28 us
  transfers between devices with their start and end apart: 9, of which 4 were waited for; matrix products, arithmetic and copies ran while one was open for 0% of the time, Pallas kernels for 51%

profile of v14, /device:TPU:0, one launch (start us, length us, event | category | flops | bytes accessed | tf_op | source)
XLA Modules:
  0.0 46.3 jit_solution(5301935222201060379)
XLA Ops:
  0.6 1.3 %prepared.1 = (bf16[32,2048]{1,0:T(8,128)(2,1)S(1)}, bf16[16,1024]{1,0:T(8,128)(2,1)S(1)}) custom-call(bf16[2048,1024]{1,0:T(8,128)(2,1)} %strain.3), custom_call_target="tpu_custom_call" | custom-call | bytes 3690000 | tf_op jit(solution)/shard_map/prepared/pallas_call | solution.py:131
  1.9 0.5 %collective-permute-start = (bf16[32,2048]{1,0:T(8,128)(2,1)S(1)}, bf16[32,2048]{1,0:T(8,128)(2,1)S(1)}, u32[]{:S(2)}, u32[]{:S(2)}) collective-permute-start(bf16[32,2048]{1,0:T(8,128)(2,1)S(1)} %get-tuple-element.21.after.refs_2_.refs_1_.refs_0_), channel_id=1, source_target_pairs={{0,1},{1,0},{2,3},{3,2},{4,5},{5,4},{6,7},{7,6},{8,9},{9,8},{10,11... | collective-permute-start | bytes 393224 | tf_op jit(solution)/shard_map/ppermute | solution.py:39
  2.4 1.3 %collective-permute-start.1 = (bf16[16,1024]{1,0:T(8,128)(2,1)S(1)}, bf16[16,1024]{1,0:T(8,128)(2,1)S(1)}, u32[]{:S(2)}, u32[]{:S(2)}) collective-permute-start(bf16[16,1024]{1,0:T(8,128)(2,1)S(1)} %get-tuple-element.22.refs_0_), channel_id=1, source_target_pairs={{4,0},{8,4},{12,8},{5,1},{9,5},{13,9},{20,16},{24,20},{28,24},{21,... | collective-permute-start | bytes 98312 | tf_op jit(solution)/shard_map/ppermute | solution.py:585
  3.7 2.3 %loaded.1 = (bf16[2048,1024]{1,0:T(8,128)(2,1)S(1)}, f32[1,1024]{1,0:T(1,128)S(1)}) custom-call(bf16[2048,1024]{1,0:T(8,128)(2,1)} %strain.3, bf16[32,2048]{1,0:T(8,128)(2,1)S(1)} %get-tuple-element.21.after.refs_2_.refs_1_.refs_0_), custom_call_target="tpu_custom_call" | custom-call | bytes 3690000 | tf_op jit(solution)/shard_map/loaded/pallas_call | solution.py:185
  6.0 0.0 collective-permute-done.refs_3_.refs_2_.refs_1_
  6.0 2.1 %first_products.1 = (f32[128,1024]{1,0:T(8,128)S(1)}, bf16[136,1024]{1,0:T(8,128)(2,1)S(1)}) custom-call(bf16[2048,1024]{1,0:T(8,128)(2,1)S(1)} %get-tuple-element.23.refs_0_, f32[1,1024]{1,0:T(1,128)S(1)} %get-tuple-element.24.refs_1_, bf16[32,2048]{1,0:T(8,128)(2,1)S(1)} %get-tuple-element.21.after.refs_2_.refs_1_.refs_0_, ...), custom_call_target="tpu_custom_call" | custom-call | bytes 3690000 | tf_op jit(solution)/shard_map/first_products/pallas_call | solution.py:330
  8.1 0.9 %collective-permute-done.1.refs_1_ = bf16[16,1024]{1,0:T(8,128)(2,1)S(1)} collective-permute-done((bf16[16,1024]{1,0:T(8,128)(2,1)S(1)}, bf16[16,1024]{1,0:T(8,128)(2,1)S(1)}, u32[]{:S(2)}, u32[]{:S(2)}) %collective-permute-start.1) | collective-permute-done | bytes 32800 | tf_op jit(solution)/shard_map/ppermute | solution.py:585
  9.0 1.1 %collective-permute-start.2 = (bf16[152,1024]{1,0:T(8,128)(2,1)S(1)}, bf16[152,1024]{1,0:T(8,128)(2,1)S(1)}, u32[]{:S(2)}, u32[]{:S(2)}) collective-permute-start(bf16[152,1024]{1,0:T(8,128)(2,1)S(1)} %with_tails.1.refs_3_.refs_2_), channel_id=1, source_target_pairs={{0,2},{2,0},{4,6},{6,4},{8,10},{10,8},{12,14},{14,12},{1,3},{3,1},... | collective-permute-start | bytes 933896 | tf_op jit(solution)/shard_map/ppermute | solution.py:39
  10.1 2.0 %later_products.2 = (f32[128,1024]{1,0:T(8,128)S(1)}, bf16[144,1024]{1,0:T(8,128)(2,1)S(1)}) custom-call(bf16[2048,1024]{1,0:T(8,128)(2,1)S(1)} %get-tuple-element.23.refs_0_, bf16[32,2048]{1,0:T(8,128)(2,1)S(1)} %get-tuple-element.21.after.refs_2_.refs_1_.refs_0_, bf16[32,2048]{1,0:T(8,128)(2,1)S(1)} %collective-permute-done.refs_3_.refs_2_.refs_1_, ...), custom_call_target="tpu_custom_call" | custom-call | bytes 3690000 | tf_op jit(solution)/shard_map/later_products/pallas_call | solution.py:330
  12.1 1.1 %collective-permute-start.6 = (bf16[144,1024]{1,0:T(8,128)(2,1)S(1)}, bf16[144,1024]{1,0:T(8,128)(2,1)S(1)}, u32[]{:S(2)}, u32[]{:S(2)}) collective-permute-start(bf16[144,1024]{1,0:T(8,128)(2,1)S(1)} %get-tuple-element.27.refs_4_), channel_id=1, source_target_pairs={{0,2},{2,0},{4,6},{6,4},{8,10},{10,8},{12,14},{14,12},{1,3},{3,1},... | collective-permute-start | bytes 884744 | tf_op jit(solution)/shard_map/ppermute | solution.py:39
  13.1 3.7 %later_products.3 = (f32[128,1024]{1,0:T(8,128)S(1)}, bf16[128,1024]{1,0:T(8,128)(2,1)S(1)}, f32[128,1024]{1,0:T(8,128)S(1)}, bf16[128,1024]{1,0:T(8,128)(2,1)S(1)}) custom-call(bf16[2048,1024]{1,0:T(8,128)(2,1)S(1)} %get-tuple-element.23.refs_0_, bf16[32,2048]{1,0:T(8,128)(2,1)S(1)} %get-tuple-element.21.after.refs_2_.refs_1_.refs_0_, ...), custom_call_target="tpu_custom_call" | custom-call | bytes 3690000 | tf_op jit(solution)/shard_map/later_products/pallas_call | solution.py:330
  16.8 2.5 %collective-permute-done.2.refs_4_.refs_3_.refs_2_ = bf16[152,1024]{1,0:T(8,128)(2,1)S(1)} collective-permute-done((bf16[152,1024]{1,0:T(8,128)(2,1)S(1)}, bf16[152,1024]{1,0:T(8,128)(2,1)S(1)}, u32[]{:S(2)}, u32[]{:S(2)}) %collective-permute-start.2) | collective-permute-done | bytes 311328 | tf_op jit(solution)/shard_map/ppermute | solution.py:39
  19.3 0.7 %merged_near.1 = (bf16[136,1024]{1,0:T(8,128)(2,1)S(1)}, bf16[128,1024]{1,0:T(8,128)(2,1)S(1)}) custom-call(f32[128,1024]{1,0:T(8,128)S(1)} %get-tuple-element.30.refs_0_, bf16[32,2048]{1,0:T(8,128)(2,1)S(1)} %get-tuple-element.21.after.refs_2_.refs_1_.refs_0_, bf16[32,2048]{1,0:T(8,128)(2,1)S(1)} %collective-permute-done.refs_3_.refs_2_.refs_1_, ...), custom_call_target="tpu_custom_call" | custom-call | bytes 1107000 | tf_op jit(solution)/shard_map/merged_near/pallas_call | solution.py:330
  20.0 2.4 %collective-permute-start.5 = (bf16[136,1024]{1,0:T(8,128)(2,1)S(1)}, bf16[136,1024]{1,0:T(8,128)(2,1)S(1)}, u32[]{:S(2)}, u32[]{:S(2)}) collective-permute-start(bf16[136,1024]{1,0:T(8,128)(2,1)S(1)} %get-tuple-element.32.refs_7_.refs_1_.refs_3_), channel_id=1, source_target_pairs={{0,4},{2,6},{4,0},{6,2},{8,12},{10,14},{12,8},{14,10},{1,5},{3,7},... | collective-permute-start | bytes 835592 | tf_op jit(solution)/shard_map/ppermute | solution.py:39
  22.4 0.2 collective-permute-start.4
  22.6 0.6 %with_boundaries.1 = (f32[128,1024]{1,0:T(8,128)S(1)}, f32[128,1024]{1,0:T(8,128)S(1)}, f32[128,1024]{1,0:T(8,128)S(1)}) custom-call(bf16[32,2048]{1,0:T(8,128)(2,1)S(1)} %get-tuple-element.21.after.refs_2_.refs_1_.refs_0_, bf16[32,2048]{1,0:T(8,128)(2,1)S(1)} %collective-permute-done.refs_3_.refs_2_.refs_1_, ...), custom_call_target="tpu_custom_call" | custom-call | bytes 1107000 | tf_op jit(solution)/shard_map/with_boundaries/pallas_call | solution.py:330
  23.2 2.9 %segment_rows.2 = (f32[16,256]{1,0:T(8,128)S(1)}, bf16[128,1024]{1,0:T(8,128)(2,1)S(1)}) custom-call(bf16[2048,1024]{1,0:T(8,128)(2,1)S(1)} %get-tuple-element.23.refs_0_, f32[1,1024]{1,0:T(1,128)S(1)} %get-tuple-element.24.refs_1_, bf16[152,1024]{1,0:T(8,128)(2,1)S(1)} %collective-permute-done.2.refs_4_.refs_3_.refs_2_, ...), custom_call_target="tpu_custom_call" | custom-call | bytes 4428000 | tf_op jit(solution)/shard_map/segment_rows/pallas_call | solution.py:330
  26.1 0.0 collective-permute-done.6.refs_3_
  26.1 2.4 %collective-permute-done.5.refs_2_ = bf16[136,1024]{1,0:T(8,128)(2,1)S(1)} collective-permute-done((bf16[136,1024]{1,0:T(8,128)(2,1)S(1)}, bf16[136,1024]{1,0:T(8,128)(2,1)S(1)}, u32[]{:S(2)}, u32[]{:S(2)}) %collective-permute-start.5) | collective-permute-done | bytes 278560 | tf_op jit(solution)/shard_map/ppermute | solution.py:39
  28.5 0.8 %merged.1.refs_4_.refs_3_ = bf16[136,1024]{1,0:T(8,128)(2,1)S(1)} custom-call(f32[128,1024]{1,0:T(8,128)S(1)} %get-tuple-element.35.refs_4_.refs_0_, bf16[136,1024]{1,0:T(8,128)(2,1)S(1)} %get-tuple-element.32.refs_7_.refs_1_.refs_3_, bf16[136,1024]{1,0:T(8,128)(2,1)S(1)} %collective-permute-done.5.refs_2_, ...), custom_call_target="tpu_custom_call" | custom-call | bytes 1107000 | tf_op jit(solution)/shard_map/merged/pallas_call | solution.py:330
  29.3 2.7 %collective-permute-start.8 = (bf16[136,1024]{1,0:T(8,128)(2,1)S(1)}, bf16[136,1024]{1,0:T(8,128)(2,1)S(1)}, u32[]{:S(2)}, u32[]{:S(2)}) collective-permute-start(bf16[136,1024]{1,0:T(8,128)(2,1)S(1)} %merged.1.refs_4_.refs_3_), channel_id=1, source_target_pairs={{0,8},{2,10},{4,12},{6,14},{8,0},{10,2},{12,4},{14,6},{1,9},{3,11}... | collective-permute-start | bytes 835592 | tf_op jit(solution)/shard_map/ppermute | solution.py:39
  31.9 0.6 %collective-permute-start.3 = (bf16[128,1024]{1,0:T(8,128)(2,1)S(1)}, bf16[128,1024]{1,0:T(8,128)(2,1)S(1)}, u32[]{:S(2)}, u32[]{:S(2)}) collective-permute-start(bf16[128,1024]{1,0:T(8,128)(2,1)S(1)} %get-tuple-element.36), channel_id=1, source_target_pairs={{0,2},{2,0},{4,6},{6,4},{8,10},{10,8},{12,14},{14,12},{1,3},{3,1},... | collective-permute-start | bytes 786440 | tf_op jit(solution)/shard_map/ppermute | solution.py:39
  32.5 0.0 collective-permute-done.4.refs_1_
  32.5 0.5 %resent.1.refs_3_ = bf16[128,1024]{1,0:T(8,128)(2,1)S(1)} custom-call(f32[128,1024]{1,0:T(8,128)S(1)} %get-tuple-element.37.refs_0_, bf16[128,1024]{1,0:T(8,128)(2,1)S(1)} %collective-permute-done.4.refs_1_, bf16[152,1024]{1,0:T(8,128)(2,1)S(1)} %collective-permute-done.2.refs_4_.refs_3_.refs_2_, ...), custom_call_target="tpu_custom_call" | custom-call | bytes 1107000 | tf_op jit(solution)/shard_map/resent/pallas_call | solution.py:330
  33.1 1.6 %collective-permute-start.7 = (bf16[128,1024]{1,0:T(8,128)(2,1)S(1)}, bf16[128,1024]{1,0:T(8,128)(2,1)S(1)}, u32[]{:S(2)}, u32[]{:S(2)}) collective-permute-start(bf16[128,1024]{1,0:T(8,128)(2,1)S(1)} %resent.1.refs_3_), channel_id=1, source_target_pairs={{0,4},{2,6},{4,0},{6,2},{8,12},{10,14},{12,8},{14,10},{1,5},{3,7},... | collective-permute-start | bytes 786440 | tf_op jit(solution)/shard_map/ppermute | solution.py:39
  34.7 8.0 %segment_rows.3.refs_3_.refs_6_ = f32[16,768]{1,0:T(8,128)S(1)} custom-call(bf16[2048,1024]{1,0:T(8,128)(2,1)S(1)} %get-tuple-element.23.refs_0_, f32[1,1024]{1,0:T(1,128)S(1)} %get-tuple-element.24.refs_1_, bf16[152,1024]{1,0:T(8,128)(2,1)S(1)} %collective-permute-done.2.refs_4_.refs_3_.refs_2_, bf16[128,1024]{1,0:T(8,128)(2,1)S(1)} %resent.1.refs_3_), custom_call_target="tpu_custom_call" | custom-call | bytes 4428000 | tf_op jit(solution)/shard_map/segment_rows/pallas_call | solution.py:330
  42.7 0.0 collective-permute-done.3.refs_1_
  42.7 0.3 added.1.refs_0_
  43.0 1.8 %collective-permute-done.7.refs_1_ = bf16[128,1024]{1,0:T(8,128)(2,1)S(1)} collective-permute-done((bf16[128,1024]{1,0:T(8,128)(2,1)S(1)}, bf16[128,1024]{1,0:T(8,128)(2,1)S(1)}, u32[]{:S(2)}, u32[]{:S(2)}) %collective-permute-start.7) | collective-permute-done | bytes 262176 | tf_op jit(solution)/shard_map/ppermute | solution.py:39
  44.8 0.0 collective-permute-done.8.refs_4_
  44.8 1.4 %finished.1 = (f32[128,1024]{1,0:T(8,128)}, f32[16,1024]{1,0:T(8,128)}) custom-call(f32[128,1024]{1,0:T(8,128)S(1)} %added.1.refs_0_, bf16[128,1024]{1,0:T(8,128)(2,1)S(1)} %collective-permute-done.7.refs_1_, bf16[136,1024]{1,0:T(8,128)(2,1)S(1)} %collective-permute-done.5.refs_2_, bf16[136,1024]{1,0:T(8,128)(2,1)S(1)} %merged.1.refs_4_.refs_3_, ...), custom_call_target="tpu_custom_call" | custom-call | bytes 1107000 | tf_op jit(solution)/shard_map/finished/pallas_call | solution.py:330
  (1 shorter events, 0.0 us)
Async XLA Ops:
  1.9 4.1 %collective-permute-start = (bf16[32,2048]{1,0:T(8,128)(2,1)S(1)}, bf16[32,2048]{1,0:T(8,128)(2,1)S(1)}, u32[]{:S(2)}, u32[]{:S(2)}) collective-permute-start(bf16[32,2048]{1,0:T(8,128)(2,1)S(1)} %get-tuple-element.21.after.refs_2_.refs_1_.refs_0_), channel_id=1, source_target_pairs={{0,1},{1,0},{2,3},{3,2},{4,5},{5,4},{6,7},{7,6},{8,9},{9,8},{10,11... | collective-permute-start | bytes 393224 | tf_op jit(solution)/shard_map/ppermute | solution.py:39
  2.4 6.5 %collective-permute-start.1 = (bf16[16,1024]{1,0:T(8,128)(2,1)S(1)}, bf16[16,1024]{1,0:T(8,128)(2,1)S(1)}, u32[]{:S(2)}, u32[]{:S(2)}) collective-permute-start(bf16[16,1024]{1,0:T(8,128)(2,1)S(1)} %get-tuple-element.22.refs_0_), channel_id=1, source_target_pairs={{4,0},{8,4},{12,8},{5,1},{9,5},{13,9},{20,16},{24,20},{28,24},{21,... | collective-permute-start | bytes 98312 | tf_op jit(solution)/shard_map/ppermute | solution.py:585
  9.0 10.3 %collective-permute-start.2 = (bf16[152,1024]{1,0:T(8,128)(2,1)S(1)}, bf16[152,1024]{1,0:T(8,128)(2,1)S(1)}, u32[]{:S(2)}, u32[]{:S(2)}) collective-permute-start(bf16[152,1024]{1,0:T(8,128)(2,1)S(1)} %with_tails.1.refs_3_.refs_2_), channel_id=1, source_target_pairs={{0,2},{2,0},{4,6},{6,4},{8,10},{10,8},{12,14},{14,12},{1,3},{3,1},... | collective-permute-start | bytes 933896 | tf_op jit(solution)/shard_map/ppermute | solution.py:39
  12.1 14.0 %collective-permute-start.6 = (bf16[144,1024]{1,0:T(8,128)(2,1)S(1)}, bf16[144,1024]{1,0:T(8,128)(2,1)S(1)}, u32[]{:S(2)}, u32[]{:S(2)}) collective-permute-start(bf16[144,1024]{1,0:T(8,128)(2,1)S(1)} %get-tuple-element.27.refs_4_), channel_id=1, source_target_pairs={{0,2},{2,0},{4,6},{6,4},{8,10},{10,8},{12,14},{14,12},{1,3},{3,1},... | collective-permute-start | bytes 884744 | tf_op jit(solution)/shard_map/ppermute | solution.py:39
  20.0 8.5 %collective-permute-start.5 = (bf16[136,1024]{1,0:T(8,128)(2,1)S(1)}, bf16[136,1024]{1,0:T(8,128)(2,1)S(1)}, u32[]{:S(2)}, u32[]{:S(2)}) collective-permute-start(bf16[136,1024]{1,0:T(8,128)(2,1)S(1)} %get-tuple-element.32.refs_7_.refs_1_.refs_3_), channel_id=1, source_target_pairs={{0,4},{2,6},{4,0},{6,2},{8,12},{10,14},{12,8},{14,10},{1,5},{3,7},... | collective-permute-start | bytes 835592 | tf_op jit(solution)/shard_map/ppermute | solution.py:39
  22.4 10.2 %collective-permute-start.4 = (bf16[128,1024]{1,0:T(8,128)(2,1)S(1)}, bf16[128,1024]{1,0:T(8,128)(2,1)S(1)}, u32[]{:S(2)}, u32[]{:S(2)}) collective-permute-start(bf16[128,1024]{1,0:T(8,128)(2,1)S(1)} %get-tuple-element.38), channel_id=1, source_target_pairs={{0,2},{2,0},{4,6},{6,4},{8,10},{10,8},{12,14},{14,12},{1,3},{3,1},... | collective-permute-start | bytes 786440 | tf_op jit(solution)/shard_map/ppermute | solution.py:39
  29.3 15.6 %collective-permute-start.8 = (bf16[136,1024]{1,0:T(8,128)(2,1)S(1)}, bf16[136,1024]{1,0:T(8,128)(2,1)S(1)}, u32[]{:S(2)}, u32[]{:S(2)}) collective-permute-start(bf16[136,1024]{1,0:T(8,128)(2,1)S(1)} %merged.1.refs_4_.refs_3_), channel_id=1, source_target_pairs={{0,8},{2,10},{4,12},{6,14},{8,0},{10,2},{12,4},{14,6},{1,9},{3,11}... | collective-permute-start | bytes 835592 | tf_op jit(solution)/shard_map/ppermute | solution.py:39
  31.9 10.7 %collective-permute-start.3 = (bf16[128,1024]{1,0:T(8,128)(2,1)S(1)}, bf16[128,1024]{1,0:T(8,128)(2,1)S(1)}, u32[]{:S(2)}, u32[]{:S(2)}) collective-permute-start(bf16[128,1024]{1,0:T(8,128)(2,1)S(1)} %get-tuple-element.36), channel_id=1, source_target_pairs={{0,2},{2,0},{4,6},{6,4},{8,10},{10,8},{12,14},{14,12},{1,3},{3,1},... | collective-permute-start | bytes 786440 | tf_op jit(solution)/shard_map/ppermute | solution.py:39
  33.1 11.8 %collective-permute-start.7 = (bf16[128,1024]{1,0:T(8,128)(2,1)S(1)}, bf16[128,1024]{1,0:T(8,128)(2,1)S(1)}, u32[]{:S(2)}, u32[]{:S(2)}) collective-permute-start(bf16[128,1024]{1,0:T(8,128)(2,1)S(1)} %resent.1.refs_3_), channel_id=1, source_target_pairs={{0,4},{2,6},{4,0},{6,2},{8,12},{10,14},{12,8},{14,10},{1,5},{3,7},... | collective-permute-start | bytes 786440 | tf_op jit(solution)/shard_map/ppermute | solution.py:39

commit v15 on v14

--- a/solution.py
+++ b/solution.py
@@ -439,14 +439,15 @@
     return call_on_blocks(kernel, outs, *arrays, name="merged", micros=MERGE_MICROS, after=after)[0]
 
 
-def resent(keep, direct, direct_powers, ours, after):
-    def kernel(keep, direct, direct_powers, ours, out):
+def resent(keep, direct, direct_powers, ours, held_back, after):
+    def kernel(keep, direct, direct_powers, ours, held_back, out, passed):
+        passed[...] = held_back[...]
         _, refs, bound = sent_powers(ours)
         out[...] = coded(keep[...] + direct_sums(direct, direct_powers), bound, ref_column(refs))
 
-    outs = [(keep.shape, jnp.bfloat16)]
-    arrays = (keep, direct, direct_powers, ours)
-    return call_on_blocks(kernel, outs, *arrays, name="resent", micros=MERGE_MICROS, after=after)[0]
+    outs = [(keep.shape, jnp.bfloat16), (held_back.shape, jnp.bfloat16)]
+    arrays = (keep, direct, direct_powers, ours, held_back)
+    return call_on_blocks(kernel, outs, *arrays, name="resent", micros=MERGE_MICROS, after=after)
 
 
 def added(keep, direct, direct_powers, after):
@@ -611,15 +612,15 @@
             (keep4, keep2, keep0), (2, 1, 0), own, other, send7, got7, after=(send6,)
         )
         size = width // 4
-        auto, send1 = segment_rows(held, power, got7, 0, size, held_back=(send1,), after=(keep4,))
-        got1 = exchanged(send1, "tm", 1)
+        (auto,) = segment_rows(held, power, got7, 0, size, after=(keep4,))
         send4 = merged(keep4, send6, got6, got5, got7, after=(auto,))
         got4 = exchanged(send4, "tm", 4)
-        send2 = resent(keep2, got3, got7, send6, after=(send4,))
+        send2, send1 = resent(keep2, got3, got7, send6, send1, after=(send4,))
         got2 = exchanged(send2, "tm", 2)
+        got1 = exchanged(send1, "tm", 1)
         autos = [auto, *segment_rows(held, power, got7, size, width - size, after=(send2,))]
-        partial = added(keep0, got1, got7, after=(autos[1],))
-        return tuple(finished(slab_rows, rows, partial, got2, got6, send4, got4, autos))
+        partial = added(keep0, got2, got6, after=(autos[1],))
+        return tuple(finished(slab_rows, rows, partial, got1, got7, send4, got4, autos))
 
     tail = passed_along(head, "tm", -1)
     chan = lax.axis_index("chan").astype(jnp.int32)

time: 46.4 us -> 46.8 us (level)
  no operation moved by 1% of the time
where the time goes in v15:
time: 46.8 us; the launch traced here: 46.6 us
  Pallas kernels  26.5 us (57%)
  starting transfers between devices  11.4 us (24%)
  waiting for transfers between devices  7.89 us (17%)
  between operations  0.76 us (2%)
    pallas_call x12, Pallas kernels, call_on_blocks(): pl.pallas_call(body, in_specs=[vmem] * count + [pl.BlockSpec(memory_space...  23 us
    ppermute x8, starting transfers between devices, exchanged(): lax.ppermute(value, axis, [(source, source ^ bit) for source in range(cou...  10.2 us
    ppermute x8, waiting for transfers between devices, exchanged(): lax.ppermute(value, axis, [(source, source ^ bit) for source in range(cou...  7.02 us
    pallas_call x1, Pallas kernels, loaded(): pl.pallas_call(kernel, in_specs=[pl.BlockSpec(memory_space=pl.ANY)] * 2,...  2.26 us
    ppermute x1, starting transfers between devices, from_pair_ahead(): lax.ppermute(value, 'tm', [(time + 2, time) for time in range(0, count -...  1.28 us
    pallas_call x1, Pallas kernels, prepared(): pl.pallas_call(prepare_kernel, in_specs=[pl.BlockSpec(memory_space=pl.ANY...  1.28 us
  transfers between devices with their start and end apart: 9, of which 4 were waited for; matrix products, arithmetic and copies ran while one was open for 0% of the time, Pallas kernels for 51%

profile of v15, /device:TPU:0, one launch (start us, length us, event | category | flops | bytes accessed | tf_op | source)
XLA Modules:
  0.0 46.6 jit_solution(12415268030587319887)
XLA Ops:
  0.6 1.3 %prepared.1 = (bf16[32,2048]{1,0:T(8,128)(2,1)S(1)}, bf16[16,1024]{1,0:T(8,128)(2,1)S(1)}) custom-call(bf16[2048,1024]{1,0:T(8,128)(2,1)} %strain.3), custom_call_target="tpu_custom_call" | custom-call | bytes 3690000 | tf_op jit(solution)/shard_map/prepared/pallas_call | solution.py:131
  1.9 0.5 %collective-permute-start = (bf16[32,2048]{1,0:T(8,128)(2,1)S(1)}, bf16[32,2048]{1,0:T(8,128)(2,1)S(1)}, u32[]{:S(2)}, u32[]{:S(2)}) collective-permute-start(bf16[32,2048]{1,0:T(8,128)(2,1)S(1)} %get-tuple-element.21.after.refs_2_.refs_1_.refs_0_), channel_id=1, source_target_pairs={{0,1},{1,0},{2,3},{3,2},{4,5},{5,4},{6,7},{7,6},{8,9},{9,8},{10,11... | collective-permute-start | bytes 393224 | tf_op jit(solution)/shard_map/ppermute | solution.py:39
  2.4 1.3 %collective-permute-start.1 = (bf16[16,1024]{1,0:T(8,128)(2,1)S(1)}, bf16[16,1024]{1,0:T(8,128)(2,1)S(1)}, u32[]{:S(2)}, u32[]{:S(2)}) collective-permute-start(bf16[16,1024]{1,0:T(8,128)(2,1)S(1)} %get-tuple-element.22.refs_0_), channel_id=1, source_target_pairs={{4,0},{8,4},{12,8},{5,1},{9,5},{13,9},{20,16},{24,20},{28,24},{21,... | collective-permute-start | bytes 98312 | tf_op jit(solution)/shard_map/ppermute | solution.py:586
  3.7 2.3 %loaded.1 = (bf16[2048,1024]{1,0:T(8,128)(2,1)S(1)}, f32[1,1024]{1,0:T(1,128)S(1)}) custom-call(bf16[2048,1024]{1,0:T(8,128)(2,1)} %strain.3, bf16[32,2048]{1,0:T(8,128)(2,1)S(1)} %get-tuple-element.21.after.refs_2_.refs_1_.refs_0_), custom_call_target="tpu_custom_call" | custom-call | bytes 3690000 | tf_op jit(solution)/shard_map/loaded/pallas_call | solution.py:185
  6.0 0.0 collective-permute-done.refs_3_.refs_2_.refs_1_
  6.0 2.1 %first_products.1 = (f32[128,1024]{1,0:T(8,128)S(1)}, bf16[136,1024]{1,0:T(8,128)(2,1)S(1)}) custom-call(bf16[2048,1024]{1,0:T(8,128)(2,1)S(1)} %get-tuple-element.23.refs_0_, f32[1,1024]{1,0:T(1,128)S(1)} %get-tuple-element.24.refs_1_, bf16[32,2048]{1,0:T(8,128)(2,1)S(1)} %get-tuple-element.21.after.refs_2_.refs_1_.refs_0_, ...), custom_call_target="tpu_custom_call" | custom-call | bytes 3690000 | tf_op jit(solution)/shard_map/first_products/pallas_call | solution.py:330
  8.1 0.9 %collective-permute-done.1.refs_1_ = bf16[16,1024]{1,0:T(8,128)(2,1)S(1)} collective-permute-done((bf16[16,1024]{1,0:T(8,128)(2,1)S(1)}, bf16[16,1024]{1,0:T(8,128)(2,1)S(1)}, u32[]{:S(2)}, u32[]{:S(2)}) %collective-permute-start.1) | collective-permute-done | bytes 32800 | tf_op jit(solution)/shard_map/ppermute | solution.py:586
  9.0 1.1 %collective-permute-start.2 = (bf16[152,1024]{1,0:T(8,128)(2,1)S(1)}, bf16[152,1024]{1,0:T(8,128)(2,1)S(1)}, u32[]{:S(2)}, u32[]{:S(2)}) collective-permute-start(bf16[152,1024]{1,0:T(8,128)(2,1)S(1)} %with_tails.1.refs_3_.refs_2_), channel_id=1, source_target_pairs={{0,2},{2,0},{4,6},{6,4},{8,10},{10,8},{12,14},{14,12},{1,3},{3,1},... | collective-permute-start | bytes 933896 | tf_op jit(solution)/shard_map/ppermute | solution.py:39
  10.1 2.0 %later_products.2 = (f32[128,1024]{1,0:T(8,128)S(1)}, bf16[144,1024]{1,0:T(8,128)(2,1)S(1)}) custom-call(bf16[2048,1024]{1,0:T(8,128)(2,1)S(1)} %get-tuple-element.23.refs_0_, bf16[32,2048]{1,0:T(8,128)(2,1)S(1)} %get-tuple-element.21.after.refs_2_.refs_1_.refs_0_, bf16[32,2048]{1,0:T(8,128)(2,1)S(1)} %collective-permute-done.refs_3_.refs_2_.refs_1_, ...), custom_call_target="tpu_custom_call" | custom-call | bytes 3690000 | tf_op jit(solution)/shard_map/later_products/pallas_call | solution.py:330
  12.1 1.1 %collective-permute-start.5 = (bf16[144,1024]{1,0:T(8,128)(2,1)S(1)}, bf16[144,1024]{1,0:T(8,128)(2,1)S(1)}, u32[]{:S(2)}, u32[]{:S(2)}) collective-permute-start(bf16[144,1024]{1,0:T(8,128)(2,1)S(1)} %get-tuple-element.27.refs_4_), channel_id=1, source_target_pairs={{0,2},{2,0},{4,6},{6,4},{8,10},{10,8},{12,14},{14,12},{1,3},{3,1},... | collective-permute-start | bytes 884744 | tf_op jit(solution)/shard_map/ppermute | solution.py:39
  13.1 3.7 %later_products.3 = (f32[128,1024]{1,0:T(8,128)S(1)}, bf16[128,1024]{1,0:T(8,128)(2,1)S(1)}, f32[128,1024]{1,0:T(8,128)S(1)}, bf16[128,1024]{1,0:T(8,128)(2,1)S(1)}) custom-call(bf16[2048,1024]{1,0:T(8,128)(2,1)S(1)} %get-tuple-element.23.refs_0_, bf16[32,2048]{1,0:T(8,128)(2,1)S(1)} %get-tuple-element.21.after.refs_2_.refs_1_.refs_0_, ...), custom_call_target="tpu_custom_call" | custom-call | bytes 3690000 | tf_op jit(solution)/shard_map/later_products/pallas_call | solution.py:330
  16.8 2.5 %collective-permute-done.2.refs_4_.refs_3_.refs_2_ = bf16[152,1024]{1,0:T(8,128)(2,1)S(1)} collective-permute-done((bf16[152,1024]{1,0:T(8,128)(2,1)S(1)}, bf16[152,1024]{1,0:T(8,128)(2,1)S(1)}, u32[]{:S(2)}, u32[]{:S(2)}) %collective-permute-start.2) | collective-permute-done | bytes 311328 | tf_op jit(solution)/shard_map/ppermute | solution.py:39
  19.3 0.7 %merged_near.1 = (bf16[136,1024]{1,0:T(8,128)(2,1)S(1)}, bf16[128,1024]{1,0:T(8,128)(2,1)S(1)}) custom-call(f32[128,1024]{1,0:T(8,128)S(1)} %get-tuple-element.30.refs_0_, bf16[32,2048]{1,0:T(8,128)(2,1)S(1)} %get-tuple-element.21.after.refs_2_.refs_1_.refs_0_, bf16[32,2048]{1,0:T(8,128)(2,1)S(1)} %collective-permute-done.refs_3_.refs_2_.refs_1_, ...), custom_call_target="tpu_custom_call" | custom-call | bytes 1107000 | tf_op jit(solution)/shard_map/merged_near/pallas_call | solution.py:330
  20.0 2.4 %collective-permute-start.4 = (bf16[136,1024]{1,0:T(8,128)(2,1)S(1)}, bf16[136,1024]{1,0:T(8,128)(2,1)S(1)}, u32[]{:S(2)}, u32[]{:S(2)}) collective-permute-start(bf16[136,1024]{1,0:T(8,128)(2,1)S(1)} %get-tuple-element.32.refs_7_.refs_1_.refs_3_), channel_id=1, source_target_pairs={{0,4},{2,6},{4,0},{6,2},{8,12},{10,14},{12,8},{14,10},{1,5},{3,7},... | collective-permute-start | bytes 835592 | tf_op jit(solution)/shard_map/ppermute | solution.py:39
  22.4 0.2 collective-permute-start.3
  22.6 0.6 %with_boundaries.1 = (f32[128,1024]{1,0:T(8,128)S(1)}, f32[128,1024]{1,0:T(8,128)S(1)}, f32[128,1024]{1,0:T(8,128)S(1)}) custom-call(bf16[32,2048]{1,0:T(8,128)(2,1)S(1)} %get-tuple-element.21.after.refs_2_.refs_1_.refs_0_, bf16[32,2048]{1,0:T(8,128)(2,1)S(1)} %collective-permute-done.refs_3_.refs_2_.refs_1_, ...), custom_call_target="tpu_custom_call" | custom-call | bytes 1107000 | tf_op jit(solution)/shard_map/with_boundaries/pallas_call | solution.py:330
  23.2 2.8 %segment_rows.2.refs_5_ = f32[16,256]{1,0:T(8,128)S(1)} custom-call(bf16[2048,1024]{1,0:T(8,128)(2,1)S(1)} %get-tuple-element.23.refs_0_, f32[1,1024]{1,0:T(1,128)S(1)} %get-tuple-element.24.refs_1_, bf16[152,1024]{1,0:T(8,128)(2,1)S(1)} %collective-permute-done.2.refs_4_.refs_3_.refs_2_, f32[128,1024]{1,0:T(8,128)S(1)} %get-tuple-element.37.refs_3_.refs_0_), custom_call_target="tpu_custom_call" | custom-call | bytes 4428000 | tf_op jit(solution)/shard_map/segment_rows/pallas_call | solution.py:330
  26.1 0.0 collective-permute-done.5.refs_3_
  26.1 2.4 %collective-permute-done.4.refs_2_ = bf16[136,1024]{1,0:T(8,128)(2,1)S(1)} collective-permute-done((bf16[136,1024]{1,0:T(8,128)(2,1)S(1)}, bf16[136,1024]{1,0:T(8,128)(2,1)S(1)}, u32[]{:S(2)}, u32[]{:S(2)}) %collective-permute-start.4) | collective-permute-done | bytes 278560 | tf_op jit(solution)/shard_map/ppermute | solution.py:39
  28.5 0.8 %merged.1.refs_5_.refs_3_ = bf16[136,1024]{1,0:T(8,128)(2,1)S(1)} custom-call(f32[128,1024]{1,0:T(8,128)S(1)} %get-tuple-element.37.refs_3_.refs_0_, bf16[136,1024]{1,0:T(8,128)(2,1)S(1)} %get-tuple-element.32.refs_7_.refs_1_.refs_3_, bf16[136,1024]{1,0:T(8,128)(2,1)S(1)} %collective-permute-done.4.refs_2_, ...), custom_call_target="tpu_custom_call" | custom-call | bytes 1107000 | tf_op jit(solution)/shard_map/merged/pallas_call | solution.py:330
  29.3 2.7 %collective-permute-start.8 = (bf16[136,1024]{1,0:T(8,128)(2,1)S(1)}, bf16[136,1024]{1,0:T(8,128)(2,1)S(1)}, u32[]{:S(2)}, u32[]{:S(2)}) collective-permute-start(bf16[136,1024]{1,0:T(8,128)(2,1)S(1)} %merged.1.refs_5_.refs_3_), channel_id=1, source_target_pairs={{0,8},{2,10},{4,12},{6,14},{8,0},{10,2},{12,4},{14,6},{1,9},{3,11}... | collective-permute-start | bytes 835592 | tf_op jit(solution)/shard_map/ppermute | solution.py:39
  31.9 0.0 collective-permute-done.3.refs_1_
  31.9 0.5 %resent.1 = (bf16[128,1024]{1,0:T(8,128)(2,1)S(1)}, bf16[128,1024]{1,0:T(8,128)(2,1)S(1)}) custom-call(f32[128,1024]{1,0:T(8,128)S(1)} %get-tuple-element.34.refs_0_, bf16[128,1024]{1,0:T(8,128)(2,1)S(1)} %collective-permute-done.3.refs_1_, bf16[152,1024]{1,0:T(8,128)(2,1)S(1)} %collective-permute-done.2.refs_4_.refs_3_.refs_2_, ...), custom_call_target="tpu_custom_call" | custom-call | bytes 1107000 | tf_op jit(solution)/shard_map/resent/pallas_call | solution.py:330
  32.5 1.6 %collective-permute-start.6 = (bf16[128,1024]{1,0:T(8,128)(2,1)S(1)}, bf16[128,1024]{1,0:T(8,128)(2,1)S(1)}, u32[]{:S(2)}, u32[]{:S(2)}) collective-permute-start(bf16[128,1024]{1,0:T(8,128)(2,1)S(1)} %get-tuple-element.38.refs_3_), channel_id=1, source_target_pairs={{0,4},{2,6},{4,0},{6,2},{8,12},{10,14},{12,8},{14,10},{1,5},{3,7},... | collective-permute-start | bytes 786440 | tf_op jit(solution)/shard_map/ppermute | solution.py:39
  34.1 0.6 %collective-permute-start.7 = (bf16[128,1024]{1,0:T(8,128)(2,1)S(1)}, bf16[128,1024]{1,0:T(8,128)(2,1)S(1)}, u32[]{:S(2)}, u32[]{:S(2)}) collective-permute-start(bf16[128,1024]{1,0:T(8,128)(2,1)S(1)} %get-tuple-element.39), channel_id=1, source_target_pairs={{0,2},{2,0},{4,6},{6,4},{8,10},{10,8},{12,14},{14,12},{1,3},{3,1},... | collective-permute-start | bytes 786440 | tf_op jit(solution)/shard_map/ppermute | solution.py:39
  34.7 8.0 %segment_rows.3.refs_3_.refs_6_ = f32[16,768]{1,0:T(8,128)S(1)} custom-call(bf16[2048,1024]{1,0:T(8,128)(2,1)S(1)} %get-tuple-element.23.refs_0_, f32[1,1024]{1,0:T(1,128)S(1)} %get-tuple-element.24.refs_1_, bf16[152,1024]{1,0:T(8,128)(2,1)S(1)} %collective-permute-done.2.refs_4_.refs_3_.refs_2_, bf16[128,1024]{1,0:T(8,128)(2,1)S(1)} %get-tuple-element.38.refs_3_), custom_call_target="tpu_custom_call" | custom-call | bytes 4428000 | tf_op jit(solution)/shard_map/segment_rows/pallas_call | solution.py:330
  42.7 2.2 %collective-permute-done.6.refs_1_ = bf16[128,1024]{1,0:T(8,128)(2,1)S(1)} collective-permute-done((bf16[128,1024]{1,0:T(8,128)(2,1)S(1)}, bf16[128,1024]{1,0:T(8,128)(2,1)S(1)}, u32[]{:S(2)}, u32[]{:S(2)}) %collective-permute-start.6) | collective-permute-done | bytes 262176 | tf_op jit(solution)/shard_map/ppermute | solution.py:39
  44.8 0.3 added.1.refs_0_
  45.2 0.0 collective-permute-done.7.refs_1_
  45.2 0.0 collective-permute-done.8.refs_4_
  45.2 1.4 %finished.1 = (f32[128,1024]{1,0:T(8,128)}, f32[16,1024]{1,0:T(8,128)}) custom-call(f32[128,1024]{1,0:T(8,128)S(1)} %added.1.refs_0_, bf16[128,1024]{1,0:T(8,128)(2,1)S(1)} %collective-permute-done.7.refs_1_, bf16[152,1024]{1,0:T(8,128)(2,1)S(1)} %collective-permute-done.2.refs_4_.refs_3_.refs_2_, bf16[136,1024]{1,0:T(8,128)(2,1)S(1)} %merged.1.refs_5_.refs_3_, ...), custom_call_target="tpu_custom_call" | custom-call | bytes 1107000 | tf_op jit(solution)/shard_map/finished/pallas_call | solution.py:330
  (1 shorter events, 0.0 us)
Async XLA Ops:
  1.9 4.1 %collective-permute-start = (bf16[32,2048]{1,0:T(8,128)(2,1)S(1)}, bf16[32,2048]{1,0:T(8,128)(2,1)S(1)}, u32[]{:S(2)}, u32[]{:S(2)}) collective-permute-start(bf16[32,2048]{1,0:T(8,128)(2,1)S(1)} %get-tuple-element.21.after.refs_2_.refs_1_.refs_0_), channel_id=1, source_target_pairs={{0,1},{1,0},{2,3},{3,2},{4,5},{5,4},{6,7},{7,6},{8,9},{9,8},{10,11... | collective-permute-start | bytes 393224 | tf_op jit(solution)/shard_map/ppermute | solution.py:39
  2.4 6.5 %collective-permute-start.1 = (bf16[16,1024]{1,0:T(8,128)(2,1)S(1)}, bf16[16,1024]{1,0:T(8,128)(2,1)S(1)}, u32[]{:S(2)}, u32[]{:S(2)}) collective-permute-start(bf16[16,1024]{1,0:T(8,128)(2,1)S(1)} %get-tuple-element.22.refs_0_), channel_id=1, source_target_pairs={{4,0},{8,4},{12,8},{5,1},{9,5},{13,9},{20,16},{24,20},{28,24},{21,... | collective-permute-start | bytes 98312 | tf_op jit(solution)/shard_map/ppermute | solution.py:586
  9.0 10.3 %collective-permute-start.2 = (bf16[152,1024]{1,0:T(8,128)(2,1)S(1)}, bf16[152,1024]{1,0:T(8,128)(2,1)S(1)}, u32[]{:S(2)}, u32[]{:S(2)}) collective-permute-start(bf16[152,1024]{1,0:T(8,128)(2,1)S(1)} %with_tails.1.refs_3_.refs_2_), channel_id=1, source_target_pairs={{0,2},{2,0},{4,6},{6,4},{8,10},{10,8},{12,14},{14,12},{1,3},{3,1},... | collective-permute-start | bytes 933896 | tf_op jit(solution)/shard_map/ppermute | solution.py:39
  12.1 14.0 %collective-permute-start.5 = (bf16[144,1024]{1,0:T(8,128)(2,1)S(1)}, bf16[144,1024]{1,0:T(8,128)(2,1)S(1)}, u32[]{:S(2)}, u32[]{:S(2)}) collective-permute-start(bf16[144,1024]{1,0:T(8,128)(2,1)S(1)} %get-tuple-element.27.refs_4_), channel_id=1, source_target_pairs={{0,2},{2,0},{4,6},{6,4},{8,10},{10,8},{12,14},{14,12},{1,3},{3,1},... | collective-permute-start | bytes 884744 | tf_op jit(solution)/shard_map/ppermute | solution.py:39
  20.0 8.5 %collective-permute-start.4 = (bf16[136,1024]{1,0:T(8,128)(2,1)S(1)}, bf16[136,1024]{1,0:T(8,128)(2,1)S(1)}, u32[]{:S(2)}, u32[]{:S(2)}) collective-permute-start(bf16[136,1024]{1,0:T(8,128)(2,1)S(1)} %get-tuple-element.32.refs_7_.refs_1_.refs_3_), channel_id=1, source_target_pairs={{0,4},{2,6},{4,0},{6,2},{8,12},{10,14},{12,8},{14,10},{1,5},{3,7},... | collective-permute-start | bytes 835592 | tf_op jit(solution)/shard_map/ppermute | solution.py:39
  22.4 9.6 %collective-permute-start.3 = (bf16[128,1024]{1,0:T(8,128)(2,1)S(1)}, bf16[128,1024]{1,0:T(8,128)(2,1)S(1)}, u32[]{:S(2)}, u32[]{:S(2)}) collective-permute-start(bf16[128,1024]{1,0:T(8,128)(2,1)S(1)} %get-tuple-element.35), channel_id=1, source_target_pairs={{0,2},{2,0},{4,6},{6,4},{8,10},{10,8},{12,14},{14,12},{1,3},{3,1},... | collective-permute-start | bytes 786440 | tf_op jit(solution)/shard_map/ppermute | solution.py:39
  29.3 15.9 %collective-permute-start.8 = (bf16[136,1024]{1,0:T(8,128)(2,1)S(1)}, bf16[136,1024]{1,0:T(8,128)(2,1)S(1)}, u32[]{:S(2)}, u32[]{:S(2)}) collective-permute-start(bf16[136,1024]{1,0:T(8,128)(2,1)S(1)} %merged.1.refs_5_.refs_3_), channel_id=1, source_target_pairs={{0,8},{2,10},{4,12},{6,14},{8,0},{10,2},{12,4},{14,6},{1,9},{3,11}... | collective-permute-start | bytes 835592 | tf_op jit(solution)/shard_map/ppermute | solution.py:39
  32.5 12.4 %collective-permute-start.6 = (bf16[128,1024]{1,0:T(8,128)(2,1)S(1)}, bf16[128,1024]{1,0:T(8,128)(2,1)S(1)}, u32[]{:S(2)}, u32[]{:S(2)}) collective-permute-start(bf16[128,1024]{1,0:T(8,128)(2,1)S(1)} %get-tuple-element.38.refs_3_), channel_id=1, source_target_pairs={{0,4},{2,6},{4,0},{6,2},{8,12},{10,14},{12,8},{14,10},{1,5},{3,7},... | collective-permute-start | bytes 786440 | tf_op jit(solution)/shard_map/ppermute | solution.py:39
  34.1 11.1 %collective-permute-start.7 = (bf16[128,1024]{1,0:T(8,128)(2,1)S(1)}, bf16[128,1024]{1,0:T(8,128)(2,1)S(1)}, u32[]{:S(2)}, u32[]{:S(2)}) collective-permute-start(bf16[128,1024]{1,0:T(8,128)(2,1)S(1)} %get-tuple-element.39), channel_id=1, source_target_pairs={{0,2},{2,0},{4,6},{6,4},{8,10},{10,8},{12,14},{14,12},{1,3},{3,1},... | collective-permute-start | bytes 786440 | tf_op jit(solution)/shard_map/ppermute | solution.py:39

commit v16 on v15

--- a/solution.py
+++ b/solution.py
@@ -292,8 +292,8 @@
         refs = ref_column(ref_powers)
         for index, bits in enumerate(groups):
             lag_rows(own, other, own_group(bits), shifted.at[pl.ds(index * 2 * chunk, 2 * chunk)])
-            if spare:
-                outs[2 * index + 1][chunk:] = jnp.zeros((spare, width), jnp.bfloat16)
+            if spare and index == 0:
+                outs[1][chunk:] = jnp.zeros((spare, width), jnp.bfloat16)
         for here in columns(width):
             product = product_of(shifted, held, here)
             for index in range(len(groups)):
@@ -304,7 +304,14 @@
 
     return call_on_blocks(
         kernel,
-        [((chunk, width), jnp.float32), ((chunk + spare, width), jnp.bfloat16)] * len(groups),
+        [
+            (shape, dtype)
+            for index in range(len(groups))
+            for shape, dtype in (
+                ((chunk, width), jnp.float32),
+                ((chunk + (0 if index else spare), width), jnp.bfloat16),
+            )
+        ],
         held,
         own,
         other,
@@ -600,11 +607,10 @@
         after_next = from_pair_ahead(head)
         send7 = with_tails(head, after_next, send7)
         got7 = exchanged(send7, "tm", 1)
-        keep4, send5 = later_products((2,), held, own, other, send7, chunk, spare=LAGS)
+        keep4, send5, keep2, send3, keep0, send1 = later_products(
+            (2, 1, 0), held, own, other, send7, chunk, spare=LAGS
+        )
         got5 = exchanged(send5, "tm", 1)
-        keep2, send3, keep0, send1 = later_products(
-            (1, 0), held, own, other, send7, chunk, after=(send5,)
-        )
         send6, send3 = merged_near(keep6, 3, own, other, send7, got7, send3)
         got6 = exchanged(send6, "tm", 2)
         got3 = exchanged(send3, "tm", 1)

time: 46.8 us -> 46.8 us (level)
  starting transfers between devices: 11.4 us -> 12.3 us
  Pallas kernels: 26.5 us -> 26 us
    ppermute x8, starting transfers between devices: 10.2 us -> 11 us  [exchanged(): lax.ppermute(value, axis, [(source, source ^ bit) for source in range(cou...]
    pallas_call x12 -> x11, Pallas kernels: 23 us -> 22.4 us  [call_on_blocks(): pl.pallas_call(body, in_specs=[vmem] * count + [pl.BlockSpec(memory_space...]
  transfers between devices with their start and end apart: 9 -> 9, of which waited for: 4 -> 4; matrix products, arithmetic and copies ran while one was open for 0% -> 0% of each run, Pallas kernels for 51% -> 50%
where the time goes in v16:
time: 46.8 us; the launch traced here: 46.6 us
  Pallas kernels  26 us (56%)
  starting transfers between devices  12.3 us (26%)
  waiting for transfers between devices  7.61 us (16%)
  between operations  0.76 us (2%)
    pallas_call x11, Pallas kernels, call_on_blocks(): pl.pallas_call(body, in_specs=[vmem] * count + [pl.BlockSpec(memory_space...  22.4 us
    ppermute x8, starting transfers between devices, exchanged(): lax.ppermute(value, axis, [(source, source ^ bit) for source in range(cou...  11 us
    ppermute x8, waiting for transfers between devices, exchanged(): lax.ppermute(value, axis, [(source, source ^ bit) for source in range(cou...  6.72 us
    pallas_call x1, Pallas kernels, loaded(): pl.pallas_call(kernel, in_specs=[pl.BlockSpec(memory_space=pl.ANY)] * 2,...  2.26 us
    ppermute x1, starting transfers between devices, from_pair_ahead(): lax.ppermute(value, 'tm', [(time + 2, time) for time in range(0, count -...  1.28 us
    pallas_call x1, Pallas kernels, prepared(): pl.pallas_call(prepare_kernel, in_specs=[pl.BlockSpec(memory_space=pl.ANY...  1.28 us
  transfers between devices with their start and end apart: 9, of which 4 were waited for; matrix products, arithmetic and copies ran while one was open for 0% of the time, Pallas kernels for 50%

profile of v16, /device:TPU:0, one launch (start us, length us, event | category | flops | bytes accessed | tf_op | source)
XLA Modules:
  0.0 46.6 jit_solution(5100460094290005333)
XLA Ops:
  0.6 1.3 %prepared.1 = (bf16[32,2048]{1,0:T(8,128)(2,1)S(1)}, bf16[16,1024]{1,0:T(8,128)(2,1)S(1)}) custom-call(bf16[2048,1024]{1,0:T(8,128)(2,1)} %strain.3), custom_call_target="tpu_custom_call" | custom-call | bytes 3690000 | tf_op jit(solution)/shard_map/prepared/pallas_call | solution.py:131
  1.9 0.5 %collective-permute-start = (bf16[32,2048]{1,0:T(8,128)(2,1)S(1)}, bf16[32,2048]{1,0:T(8,128)(2,1)S(1)}, u32[]{:S(2)}, u32[]{:S(2)}) collective-permute-start(bf16[32,2048]{1,0:T(8,128)(2,1)S(1)} %get-tuple-element.21.after.refs_2_.refs_1_.refs_0_), channel_id=1, source_target_pairs={{0,1},{1,0},{2,3},{3,2},{4,5},{5,4},{6,7},{7,6},{8,9},{9,8},{10,11... | collective-permute-start | bytes 393224 | tf_op jit(solution)/shard_map/ppermute | solution.py:39
  2.4 1.3 %collective-permute-start.1 = (bf16[16,1024]{1,0:T(8,128)(2,1)S(1)}, bf16[16,1024]{1,0:T(8,128)(2,1)S(1)}, u32[]{:S(2)}, u32[]{:S(2)}) collective-permute-start(bf16[16,1024]{1,0:T(8,128)(2,1)S(1)} %get-tuple-element.22.refs_0_), channel_id=1, source_target_pairs={{4,0},{8,4},{12,8},{5,1},{9,5},{13,9},{20,16},{24,20},{28,24},{21,... | collective-permute-start | bytes 98312 | tf_op jit(solution)/shard_map/ppermute | solution.py:593
  3.7 2.3 %loaded.1 = (bf16[2048,1024]{1,0:T(8,128)(2,1)S(1)}, f32[1,1024]{1,0:T(1,128)S(1)}) custom-call(bf16[2048,1024]{1,0:T(8,128)(2,1)} %strain.3, bf16[32,2048]{1,0:T(8,128)(2,1)S(1)} %get-tuple-element.21.after.refs_2_.refs_1_.refs_0_), custom_call_target="tpu_custom_call" | custom-call | bytes 3690000 | tf_op jit(solution)/shard_map/loaded/pallas_call | solution.py:185
  6.0 0.0 collective-permute-done.refs_3_.refs_2_.refs_1_
  6.0 2.1 %first_products.1 = (f32[128,1024]{1,0:T(8,128)S(1)}, bf16[136,1024]{1,0:T(8,128)(2,1)S(1)}) custom-call(bf16[2048,1024]{1,0:T(8,128)(2,1)S(1)} %get-tuple-element.23.refs_0_, f32[1,1024]{1,0:T(1,128)S(1)} %get-tuple-element.24.refs_1_, bf16[32,2048]{1,0:T(8,128)(2,1)S(1)} %get-tuple-element.21.after.refs_2_.refs_1_.refs_0_, ...), custom_call_target="tpu_custom_call" | custom-call | bytes 3690000 | tf_op jit(solution)/shard_map/first_products/pallas_call | solution.py:337
  8.1 0.9 %collective-permute-done.1.refs_1_ = bf16[16,1024]{1,0:T(8,128)(2,1)S(1)} collective-permute-done((bf16[16,1024]{1,0:T(8,128)(2,1)S(1)}, bf16[16,1024]{1,0:T(8,128)(2,1)S(1)}, u32[]{:S(2)}, u32[]{:S(2)}) %collective-permute-start.1) | collective-permute-done | bytes 32800 | tf_op jit(solution)/shard_map/ppermute | solution.py:593
  9.0 1.1 %collective-permute-start.2 = (bf16[152,1024]{1,0:T(8,128)(2,1)S(1)}, bf16[152,1024]{1,0:T(8,128)(2,1)S(1)}, u32[]{:S(2)}, u32[]{:S(2)}) collective-permute-start(bf16[152,1024]{1,0:T(8,128)(2,1)S(1)} %with_tails.1.refs_3_.refs_2_), channel_id=1, source_target_pairs={{0,2},{2,0},{4,6},{6,4},{8,10},{10,8},{12,14},{14,12},{1,3},{3,1},... | collective-permute-start | bytes 933896 | tf_op jit(solution)/shard_map/ppermute | solution.py:39
  10.1 5.3 %later_products.1 = (f32[128,1024]{1,0:T(8,128)S(1)}, bf16[144,1024]{1,0:T(8,128)(2,1)S(1)}, f32[128,1024]{1,0:T(8,128)S(1)}, bf16[128,1024]{1,0:T(8,128)(2,1)S(...) custom-call(bf16[2048,1024]{1,0:T(8,128)(2,1)S(1)} %get-tuple-element.23.refs_0_, ...), custom_call_target="tpu_custom_call" | custom-call | bytes 3690000 | tf_op jit(solution)/shard_map/later_products/pallas_call | solution.py:337
  15.4 1.1 %collective-permute-start.5 = (bf16[144,1024]{1,0:T(8,128)(2,1)S(1)}, bf16[144,1024]{1,0:T(8,128)(2,1)S(1)}, u32[]{:S(2)}, u32[]{:S(2)}) collective-permute-start(bf16[144,1024]{1,0:T(8,128)(2,1)S(1)} %get-tuple-element.37), channel_id=1, source_target_pairs={{0,2},{2,0},{4,6},{6,4},{8,10},{10,8},{12,14},{14,12},{1,3},{3,1},... | collective-permute-start | bytes 884744 | tf_op jit(solution)/shard_map/ppermute | solution.py:39
  16.4 1.8 %collective-permute-done.2.refs_4_.refs_3_.refs_2_ = bf16[152,1024]{1,0:T(8,128)(2,1)S(1)} collective-permute-done((bf16[152,1024]{1,0:T(8,128)(2,1)S(1)}, bf16[152,1024]{1,0:T(8,128)(2,1)S(1)}, u32[]{:S(2)}, u32[]{:S(2)}) %collective-permute-start.2) | collective-permute-done | bytes 311328 | tf_op jit(solution)/shard_map/ppermute | solution.py:39
  18.2 0.7 %merged_near.1 = (bf16[136,1024]{1,0:T(8,128)(2,1)S(1)}, bf16[128,1024]{1,0:T(8,128)(2,1)S(1)}) custom-call(f32[128,1024]{1,0:T(8,128)S(1)} %get-tuple-element.29.refs_0_, bf16[32,2048]{1,0:T(8,128)(2,1)S(1)} %get-tuple-element.21.after.refs_2_.refs_1_.refs_0_, bf16[32,2048]{1,0:T(8,128)(2,1)S(1)} %collective-permute-done.refs_3_.refs_2_.refs_1_, ...), custom_call_target="tpu_custom_call" | custom-call | bytes 1107000 | tf_op jit(solution)/shard_map/merged_near/pallas_call | solution.py:337
  18.9 3.4 %collective-permute-start.4 = (bf16[136,1024]{1,0:T(8,128)(2,1)S(1)}, bf16[136,1024]{1,0:T(8,128)(2,1)S(1)}, u32[]{:S(2)}, u32[]{:S(2)}) collective-permute-start(bf16[136,1024]{1,0:T(8,128)(2,1)S(1)} %get-tuple-element.31.refs_7_.refs_1_.refs_3_), channel_id=1, source_target_pairs={{0,4},{2,6},{4,0},{6,2},{8,12},{10,14},{12,8},{14,10},{1,5},{3,7},... | collective-permute-start | bytes 835592 | tf_op jit(solution)/shard_map/ppermute | solution.py:39
  22.4 0.0 collective-permute-start.3
  22.4 0.6 %with_boundaries.1 = (f32[128,1024]{1,0:T(8,128)S(1)}, f32[128,1024]{1,0:T(8,128)S(1)}, f32[128,1024]{1,0:T(8,128)S(1)}) custom-call(bf16[32,2048]{1,0:T(8,128)(2,1)S(1)} %get-tuple-element.21.after.refs_2_.refs_1_.refs_0_, bf16[32,2048]{1,0:T(8,128)(2,1)S(1)} %collective-permute-done.refs_3_.refs_2_.refs_1_, ...), custom_call_target="tpu_custom_call" | custom-call | bytes 1107000 | tf_op jit(solution)/shard_map/with_boundaries/pallas_call | solution.py:337
  23.0 2.7 %segment_rows.2.refs_5_ = f32[16,256]{1,0:T(8,128)S(1)} custom-call(bf16[2048,1024]{1,0:T(8,128)(2,1)S(1)} %get-tuple-element.23.refs_0_, f32[1,1024]{1,0:T(1,128)S(1)} %get-tuple-element.24.refs_1_, bf16[152,1024]{1,0:T(8,128)(2,1)S(1)} %collective-permute-done.2.refs_4_.refs_3_.refs_2_, f32[128,1024]{1,0:T(8,128)S(1)} %get-tuple-element.36.refs_3_.refs_0_), custom_call_target="tpu_custom_call" | custom-call | bytes 4428000 | tf_op jit(solution)/shard_map/segment_rows/pallas_call | solution.py:337
  25.7 0.0 collective-permute-done.5.refs_3_
  25.7 2.8 %collective-permute-done.4.refs_2_ = bf16[136,1024]{1,0:T(8,128)(2,1)S(1)} collective-permute-done((bf16[136,1024]{1,0:T(8,128)(2,1)S(1)}, bf16[136,1024]{1,0:T(8,128)(2,1)S(1)}, u32[]{:S(2)}, u32[]{:S(2)}) %collective-permute-start.4) | collective-permute-done | bytes 278560 | tf_op jit(solution)/shard_map/ppermute | solution.py:39
  28.5 0.8 %merged.1.refs_5_.refs_3_ = bf16[136,1024]{1,0:T(8,128)(2,1)S(1)} custom-call(f32[128,1024]{1,0:T(8,128)S(1)} %get-tuple-element.36.refs_3_.refs_0_, bf16[136,1024]{1,0:T(8,128)(2,1)S(1)} %get-tuple-element.31.refs_7_.refs_1_.refs_3_, bf16[136,1024]{1,0:T(8,128)(2,1)S(1)} %collective-permute-done.4.refs_2_, ...), custom_call_target="tpu_custom_call" | custom-call | bytes 1107000 | tf_op jit(solution)/shard_map/merged/pallas_call | solution.py:337
  29.3 2.6 %collective-permute-start.8 = (bf16[136,1024]{1,0:T(8,128)(2,1)S(1)}, bf16[136,1024]{1,0:T(8,128)(2,1)S(1)}, u32[]{:S(2)}, u32[]{:S(2)}) collective-permute-start(bf16[136,1024]{1,0:T(8,128)(2,1)S(1)} %merged.1.refs_5_.refs_3_), channel_id=1, source_target_pairs={{0,8},{2,10},{4,12},{6,14},{8,0},{10,2},{12,4},{14,6},{1,9},{3,11}... | collective-permute-start | bytes 835592 | tf_op jit(solution)/shard_map/ppermute | solution.py:39
  31.9 0.0 collective-permute-done.3.refs_1_
  31.9 0.5 %resent.1 = (bf16[128,1024]{1,0:T(8,128)(2,1)S(1)}, bf16[128,1024]{1,0:T(8,128)(2,1)S(1)}) custom-call(f32[128,1024]{1,0:T(8,128)S(1)} %get-tuple-element.33.refs_0_, bf16[128,1024]{1,0:T(8,128)(2,1)S(1)} %collective-permute-done.3.refs_1_, bf16[152,1024]{1,0:T(8,128)(2,1)S(1)} %collective-permute-done.2.refs_4_.refs_3_.refs_2_, ...), custom_call_target="tpu_custom_call" | custom-call | bytes 1107000 | tf_op jit(solution)/shard_map/resent/pallas_call | solution.py:337
  32.4 1.7 %collective-permute-start.6 = (bf16[128,1024]{1,0:T(8,128)(2,1)S(1)}, bf16[128,1024]{1,0:T(8,128)(2,1)S(1)}, u32[]{:S(2)}, u32[]{:S(2)}) collective-permute-start(bf16[128,1024]{1,0:T(8,128)(2,1)S(1)} %get-tuple-element.38.refs_3_), channel_id=1, source_target_pairs={{0,4},{2,6},{4,0},{6,2},{8,12},{10,14},{12,8},{14,10},{1,5},{3,7},... | collective-permute-start | bytes 786440 | tf_op jit(solution)/shard_map/ppermute | solution.py:39
  34.1 0.6 %collective-permute-start.7 = (bf16[128,1024]{1,0:T(8,128)(2,1)S(1)}, bf16[128,1024]{1,0:T(8,128)(2,1)S(1)}, u32[]{:S(2)}, u32[]{:S(2)}) collective-permute-start(bf16[128,1024]{1,0:T(8,128)(2,1)S(1)} %get-tuple-element.39), channel_id=1, source_target_pairs={{0,2},{2,0},{4,6},{6,4},{8,10},{10,8},{12,14},{14,12},{1,3},{3,1},... | collective-permute-start | bytes 786440 | tf_op jit(solution)/shard_map/ppermute | solution.py:39
  34.7 8.0 %segment_rows.3.refs_3_.refs_6_ = f32[16,768]{1,0:T(8,128)S(1)} custom-call(bf16[2048,1024]{1,0:T(8,128)(2,1)S(1)} %get-tuple-element.23.refs_0_, f32[1,1024]{1,0:T(1,128)S(1)} %get-tuple-element.24.refs_1_, bf16[152,1024]{1,0:T(8,128)(2,1)S(1)} %collective-permute-done.2.refs_4_.refs_3_.refs_2_, bf16[128,1024]{1,0:T(8,128)(2,1)S(1)} %get-tuple-element.38.refs_3_), custom_call_target="tpu_custom_call" | custom-call | bytes 4428000 | tf_op jit(solution)/shard_map/segment_rows/pallas_call | solution.py:337
  42.7 2.1 %collective-permute-done.6.refs_1_ = bf16[128,1024]{1,0:T(8,128)(2,1)S(1)} collective-permute-done((bf16[128,1024]{1,0:T(8,128)(2,1)S(1)}, bf16[128,1024]{1,0:T(8,128)(2,1)S(1)}, u32[]{:S(2)}, u32[]{:S(2)}) %collective-permute-start.6) | collective-permute-done | bytes 262176 | tf_op jit(solution)/shard_map/ppermute | solution.py:39
  44.9 0.3 added.1.refs_0_
  45.2 0.0 collective-permute-done.7.refs_1_
  45.2 0.0 collective-permute-done.8.refs_4_
  45.2 1.4 %finished.1 = (f32[128,1024]{1,0:T(8,128)}, f32[16,1024]{1,0:T(8,128)}) custom-call(f32[128,1024]{1,0:T(8,128)S(1)} %added.1.refs_0_, bf16[128,1024]{1,0:T(8,128)(2,1)S(1)} %collective-permute-done.7.refs_1_, bf16[152,1024]{1,0:T(8,128)(2,1)S(1)} %collective-permute-done.2.refs_4_.refs_3_.refs_2_, bf16[136,1024]{1,0:T(8,128)(2,1)S(1)} %merged.1.refs_5_.refs_3_, ...), custom_call_target="tpu_custom_call" | custom-call | bytes 1107000 | tf_op jit(solution)/shard_map/finished/pallas_call | solution.py:337
  (1 shorter events, 0.0 us)
Async XLA Ops:
  1.9 4.1 %collective-permute-start = (bf16[32,2048]{1,0:T(8,128)(2,1)S(1)}, bf16[32,2048]{1,0:T(8,128)(2,1)S(1)}, u32[]{:S(2)}, u32[]{:S(2)}) collective-permute-start(bf16[32,2048]{1,0:T(8,128)(2,1)S(1)} %get-tuple-element.21.after.refs_2_.refs_1_.refs_0_), channel_id=1, source_target_pairs={{0,1},{1,0},{2,3},{3,2},{4,5},{5,4},{6,7},{7,6},{8,9},{9,8},{10,11... | collective-permute-start | bytes 393224 | tf_op jit(solution)/shard_map/ppermute | solution.py:39
  2.4 6.5 %collective-permute-start.1 = (bf16[16,1024]{1,0:T(8,128)(2,1)S(1)}, bf16[16,1024]{1,0:T(8,128)(2,1)S(1)}, u32[]{:S(2)}, u32[]{:S(2)}) collective-permute-start(bf16[16,1024]{1,0:T(8,128)(2,1)S(1)} %get-tuple-element.22.refs_0_), channel_id=1, source_target_pairs={{4,0},{8,4},{12,8},{5,1},{9,5},{13,9},{20,16},{24,20},{28,24},{21,... | collective-permute-start | bytes 98312 | tf_op jit(solution)/shard_map/ppermute | solution.py:593
  9.0 9.2 %collective-permute-start.2 = (bf16[152,1024]{1,0:T(8,128)(2,1)S(1)}, bf16[152,1024]{1,0:T(8,128)(2,1)S(1)}, u32[]{:S(2)}, u32[]{:S(2)}) collective-permute-start(bf16[152,1024]{1,0:T(8,128)(2,1)S(1)} %with_tails.1.refs_3_.refs_2_), channel_id=1, source_target_pairs={{0,2},{2,0},{4,6},{6,4},{8,10},{10,8},{12,14},{14,12},{1,3},{3,1},... | collective-permute-start | bytes 933896 | tf_op jit(solution)/shard_map/ppermute | solution.py:39
  15.4 10.3 %collective-permute-start.5 = (bf16[144,1024]{1,0:T(8,128)(2,1)S(1)}, bf16[144,1024]{1,0:T(8,128)(2,1)S(1)}, u32[]{:S(2)}, u32[]{:S(2)}) collective-permute-start(bf16[144,1024]{1,0:T(8,128)(2,1)S(1)} %get-tuple-element.37), channel_id=1, source_target_pairs={{0,2},{2,0},{4,6},{6,4},{8,10},{10,8},{12,14},{14,12},{1,3},{3,1},... | collective-permute-start | bytes 884744 | tf_op jit(solution)/shard_map/ppermute | solution.py:39
  18.9 9.5 %collective-permute-start.4 = (bf16[136,1024]{1,0:T(8,128)(2,1)S(1)}, bf16[136,1024]{1,0:T(8,128)(2,1)S(1)}, u32[]{:S(2)}, u32[]{:S(2)}) collective-permute-start(bf16[136,1024]{1,0:T(8,128)(2,1)S(1)} %get-tuple-element.31.refs_7_.refs_1_.refs_3_), channel_id=1, source_target_pairs={{0,4},{2,6},{4,0},{6,2},{8,12},{10,14},{12,8},{14,10},{1,5},{3,7},... | collective-permute-start | bytes 835592 | tf_op jit(solution)/shard_map/ppermute | solution.py:39
  22.4 9.6 %collective-permute-start.3 = (bf16[128,1024]{1,0:T(8,128)(2,1)S(1)}, bf16[128,1024]{1,0:T(8,128)(2,1)S(1)}, u32[]{:S(2)}, u32[]{:S(2)}) collective-permute-start(bf16[128,1024]{1,0:T(8,128)(2,1)S(1)} %get-tuple-element.34), channel_id=1, source_target_pairs={{0,2},{2,0},{4,6},{6,4},{8,10},{10,8},{12,14},{14,12},{1,3},{3,1},... | collective-permute-start | bytes 786440 | tf_op jit(solution)/shard_map/ppermute | solution.py:39
  29.3 15.9 %collective-permute-start.8 = (bf16[136,1024]{1,0:T(8,128)(2,1)S(1)}, bf16[136,1024]{1,0:T(8,128)(2,1)S(1)}, u32[]{:S(2)}, u32[]{:S(2)}) collective-permute-start(bf16[136,1024]{1,0:T(8,128)(2,1)S(1)} %merged.1.refs_5_.refs_3_), channel_id=1, source_target_pairs={{0,8},{2,10},{4,12},{6,14},{8,0},{10,2},{12,4},{14,6},{1,9},{3,11}... | collective-permute-start | bytes 835592 | tf_op jit(solution)/shard_map/ppermute | solution.py:39
  32.4 12.4 %collective-permute-start.6 = (bf16[128,1024]{1,0:T(8,128)(2,1)S(1)}, bf16[128,1024]{1,0:T(8,128)(2,1)S(1)}, u32[]{:S(2)}, u32[]{:S(2)}) collective-permute-start(bf16[128,1024]{1,0:T(8,128)(2,1)S(1)} %get-tuple-element.38.refs_3_), channel_id=1, source_target_pairs={{0,4},{2,6},{4,0},{6,2},{8,12},{10,14},{12,8},{14,10},{1,5},{3,7},... | collective-permute-start | bytes 786440 | tf_op jit(solution)/shard_map/ppermute | solution.py:39
  34.1 11.1 %collective-permute-start.7 = (bf16[128,1024]{1,0:T(8,128)(2,1)S(1)}, bf16[128,1024]{1,0:T(8,128)(2,1)S(1)}, u32[]{:S(2)}, u32[]{:S(2)}) collective-permute-start(bf16[128,1024]{1,0:T(8,128)(2,1)S(1)} %get-tuple-element.39), channel_id=1, source_target_pairs={{0,2},{2,0},{4,6},{6,4},{8,10},{10,8},{12,14},{14,12},{1,3},{3,1},... | collective-permute-start | bytes 786440 | tf_op jit(solution)/shard_map/ppermute | solution.py:39

commit v17 on v16

--- a/solution.py
+++ b/solution.py
@@ -11,7 +11,7 @@
 LANES = 128
 EXTRA = 8
 FETCHES = 8
-STEP = 256
+STEP = 512
 GROUP = 4
 POWER = 16
 CODE_SCALE = 2.0 ** (126 / POWER)

time: 46.8 us -> 46.8 us (level)
  no operation moved by 1% of the time
where the time goes in v17:
time: 46.8 us; the launch traced here: 46.6 us
  Pallas kernels  25.9 us (55%)
  starting transfers between devices  12.3 us (26%)
  waiting for transfers between devices  7.69 us (16%)
  between operations  0.76 us (2%)
    pallas_call x11, Pallas kernels, call_on_blocks(): pl.pallas_call(body, in_specs=[vmem] * count + [pl.BlockSpec(memory_space...  22.3 us
    ppermute x8, starting transfers between devices, exchanged(): lax.ppermute(value, axis, [(source, source ^ bit) for source in range(cou...  11 us
    ppermute x8, waiting for transfers between devices, exchanged(): lax.ppermute(value, axis, [(source, source ^ bit) for source in range(cou...  6.81 us
    pallas_call x1, Pallas kernels, loaded(): pl.pallas_call(kernel, in_specs=[pl.BlockSpec(memory_space=pl.ANY)] * 2,...  2.26 us
    ppermute x1, starting transfers between devices, from_pair_ahead(): lax.ppermute(value, 'tm', [(time + 2, time) for time in range(0, count -...  1.28 us
    pallas_call x1, Pallas kernels, prepared(): pl.pallas_call(prepare_kernel, in_specs=[pl.BlockSpec(memory_space=pl.ANY...  1.28 us
  transfers between devices with their start and end apart: 9, of which 4 were waited for; matrix products, arithmetic and copies ran while one was open for 0% of the time, Pallas kernels for 50%

profile of v17, /device:TPU:0, one launch (start us, length us, event | category | flops | bytes accessed | tf_op | source)
XLA Modules:
  0.0 46.6 jit_solution(815079904817157559)
XLA Ops:
  0.6 1.3 %prepared.1 = (bf16[32,2048]{1,0:T(8,128)(2,1)S(1)}, bf16[16,1024]{1,0:T(8,128)(2,1)S(1)}) custom-call(bf16[2048,1024]{1,0:T(8,128)(2,1)} %strain.3), custom_call_target="tpu_custom_call" | custom-call | bytes 3690000 | tf_op jit(solution)/shard_map/prepared/pallas_call | solution.py:131
  1.9 0.5 %collective-permute-start = (bf16[32,2048]{1,0:T(8,128)(2,1)S(1)}, bf16[32,2048]{1,0:T(8,128)(2,1)S(1)}, u32[]{:S(2)}, u32[]{:S(2)}) collective-permute-start(bf16[32,2048]{1,0:T(8,128)(2,1)S(1)} %get-tuple-element.21.after.refs_2_.refs_1_.refs_0_), channel_id=1, source_target_pairs={{0,1},{1,0},{2,3},{3,2},{4,5},{5,4},{6,7},{7,6},{8,9},{9,8},{10,11... | collective-permute-start | bytes 393224 | tf_op jit(solution)/shard_map/ppermute | solution.py:39
  2.4 1.3 %collective-permute-start.1 = (bf16[16,1024]{1,0:T(8,128)(2,1)S(1)}, bf16[16,1024]{1,0:T(8,128)(2,1)S(1)}, u32[]{:S(2)}, u32[]{:S(2)}) collective-permute-start(bf16[16,1024]{1,0:T(8,128)(2,1)S(1)} %get-tuple-element.22.refs_0_), channel_id=1, source_target_pairs={{4,0},{8,4},{12,8},{5,1},{9,5},{13,9},{20,16},{24,20},{28,24},{21,... | collective-permute-start | bytes 98312 | tf_op jit(solution)/shard_map/ppermute | solution.py:593
  3.7 2.3 %loaded.1 = (bf16[2048,1024]{1,0:T(8,128)(2,1)S(1)}, f32[1,1024]{1,0:T(1,128)S(1)}) custom-call(bf16[2048,1024]{1,0:T(8,128)(2,1)} %strain.3, bf16[32,2048]{1,0:T(8,128)(2,1)S(1)} %get-tuple-element.21.after.refs_2_.refs_1_.refs_0_), custom_call_target="tpu_custom_call" | custom-call | bytes 3690000 | tf_op jit(solution)/shard_map/loaded/pallas_call | solution.py:185
  6.0 0.0 collective-permute-done.refs_3_.refs_2_.refs_1_
  6.0 2.1 %first_products.1 = (f32[128,1024]{1,0:T(8,128)S(1)}, bf16[136,1024]{1,0:T(8,128)(2,1)S(1)}) custom-call(bf16[2048,1024]{1,0:T(8,128)(2,1)S(1)} %get-tuple-element.23.refs_0_, f32[1,1024]{1,0:T(1,128)S(1)} %get-tuple-element.24.refs_1_, bf16[32,2048]{1,0:T(8,128)(2,1)S(1)} %get-tuple-element.21.after.refs_2_.refs_1_.refs_0_, ...), custom_call_target="tpu_custom_call" | custom-call | bytes 3690000 | tf_op jit(solution)/shard_map/first_products/pallas_call | solution.py:337
  8.1 0.9 %collective-permute-done.1.refs_1_ = bf16[16,1024]{1,0:T(8,128)(2,1)S(1)} collective-permute-done((bf16[16,1024]{1,0:T(8,128)(2,1)S(1)}, bf16[16,1024]{1,0:T(8,128)(2,1)S(1)}, u32[]{:S(2)}, u32[]{:S(2)}) %collective-permute-start.1) | collective-permute-done | bytes 32800 | tf_op jit(solution)/shard_map/ppermute | solution.py:593
  9.0 1.1 %collective-permute-start.2 = (bf16[152,1024]{1,0:T(8,128)(2,1)S(1)}, bf16[152,1024]{1,0:T(8,128)(2,1)S(1)}, u32[]{:S(2)}, u32[]{:S(2)}) collective-permute-start(bf16[152,1024]{1,0:T(8,128)(2,1)S(1)} %with_tails.1.refs_3_.refs_2_), channel_id=1, source_target_pairs={{0,2},{2,0},{4,6},{6,4},{8,10},{10,8},{12,14},{14,12},{1,3},{3,1},... | collective-permute-start | bytes 933896 | tf_op jit(solution)/shard_map/ppermute | solution.py:39
  10.1 5.3 %later_products.1 = (f32[128,1024]{1,0:T(8,128)S(1)}, bf16[144,1024]{1,0:T(8,128)(2,1)S(1)}, f32[128,1024]{1,0:T(8,128)S(1)}, bf16[128,1024]{1,0:T(8,128)(2,1)S(...) custom-call(bf16[2048,1024]{1,0:T(8,128)(2,1)S(1)} %get-tuple-element.23.refs_0_, ...), custom_call_target="tpu_custom_call" | custom-call | bytes 3690000 | tf_op jit(solution)/shard_map/later_products/pallas_call | solution.py:337
  15.4 1.1 %collective-permute-start.5 = (bf16[144,1024]{1,0:T(8,128)(2,1)S(1)}, bf16[144,1024]{1,0:T(8,128)(2,1)S(1)}, u32[]{:S(2)}, u32[]{:S(2)}) collective-permute-start(bf16[144,1024]{1,0:T(8,128)(2,1)S(1)} %get-tuple-element.37), channel_id=1, source_target_pairs={{0,2},{2,0},{4,6},{6,4},{8,10},{10,8},{12,14},{14,12},{1,3},{3,1},... | collective-permute-start | bytes 884744 | tf_op jit(solution)/shard_map/ppermute | solution.py:39
  16.4 1.8 %collective-permute-done.2.refs_4_.refs_3_.refs_2_ = bf16[152,1024]{1,0:T(8,128)(2,1)S(1)} collective-permute-done((bf16[152,1024]{1,0:T(8,128)(2,1)S(1)}, bf16[152,1024]{1,0:T(8,128)(2,1)S(1)}, u32[]{:S(2)}, u32[]{:S(2)}) %collective-permute-start.2) | collective-permute-done | bytes 311328 | tf_op jit(solution)/shard_map/ppermute | solution.py:39
  18.2 0.7 %merged_near.1 = (bf16[136,1024]{1,0:T(8,128)(2,1)S(1)}, bf16[128,1024]{1,0:T(8,128)(2,1)S(1)}) custom-call(f32[128,1024]{1,0:T(8,128)S(1)} %get-tuple-element.29.refs_0_, bf16[32,2048]{1,0:T(8,128)(2,1)S(1)} %get-tuple-element.21.after.refs_2_.refs_1_.refs_0_, bf16[32,2048]{1,0:T(8,128)(2,1)S(1)} %collective-permute-done.refs_3_.refs_2_.refs_1_, ...), custom_call_target="tpu_custom_call" | custom-call | bytes 1107000 | tf_op jit(solution)/shard_map/merged_near/pallas_call | solution.py:337
  18.9 3.4 %collective-permute-start.4 = (bf16[136,1024]{1,0:T(8,128)(2,1)S(1)}, bf16[136,1024]{1,0:T(8,128)(2,1)S(1)}, u32[]{:S(2)}, u32[]{:S(2)}) collective-permute-start(bf16[136,1024]{1,0:T(8,128)(2,1)S(1)} %get-tuple-element.31.refs_7_.refs_1_.refs_3_), channel_id=1, source_target_pairs={{0,4},{2,6},{4,0},{6,2},{8,12},{10,14},{12,8},{14,10},{1,5},{3,7},... | collective-permute-start | bytes 835592 | tf_op jit(solution)/shard_map/ppermute | solution.py:39
  22.4 0.0 collective-permute-start.3
  22.4 0.6 %with_boundaries.1 = (f32[128,1024]{1,0:T(8,128)S(1)}, f32[128,1024]{1,0:T(8,128)S(1)}, f32[128,1024]{1,0:T(8,128)S(1)}) custom-call(bf16[32,2048]{1,0:T(8,128)(2,1)S(1)} %get-tuple-element.21.after.refs_2_.refs_1_.refs_0_, bf16[32,2048]{1,0:T(8,128)(2,1)S(1)} %collective-permute-done.refs_3_.refs_2_.refs_1_, ...), custom_call_target="tpu_custom_call" | custom-call | bytes 1107000 | tf_op jit(solution)/shard_map/with_boundaries/pallas_call | solution.py:337
  22.9 2.7 %segment_rows.2.refs_5_ = f32[16,256]{1,0:T(8,128)S(1)} custom-call(bf16[2048,1024]{1,0:T(8,128)(2,1)S(1)} %get-tuple-element.23.refs_0_, f32[1,1024]{1,0:T(1,128)S(1)} %get-tuple-element.24.refs_1_, bf16[152,1024]{1,0:T(8,128)(2,1)S(1)} %collective-permute-done.2.refs_4_.refs_3_.refs_2_, f32[128,1024]{1,0:T(8,128)S(1)} %get-tuple-element.36.refs_3_.refs_0_), custom_call_target="tpu_custom_call" | custom-call | bytes 4428000 | tf_op jit(solution)/shard_map/segment_rows/pallas_call | solution.py:337
  25.6 0.0 collective-permute-done.5.refs_3_
  25.6 2.8 %collective-permute-done.4.refs_2_ = bf16[136,1024]{1,0:T(8,128)(2,1)S(1)} collective-permute-done((bf16[136,1024]{1,0:T(8,128)(2,1)S(1)}, bf16[136,1024]{1,0:T(8,128)(2,1)S(1)}, u32[]{:S(2)}, u32[]{:S(2)}) %collective-permute-start.4) | collective-permute-done | bytes 278560 | tf_op jit(solution)/shard_map/ppermute | solution.py:39
  28.5 0.8 %merged.1.refs_5_.refs_3_ = bf16[136,1024]{1,0:T(8,128)(2,1)S(1)} custom-call(f32[128,1024]{1,0:T(8,128)S(1)} %get-tuple-element.36.refs_3_.refs_0_, bf16[136,1024]{1,0:T(8,128)(2,1)S(1)} %get-tuple-element.31.refs_7_.refs_1_.refs_3_, bf16[136,1024]{1,0:T(8,128)(2,1)S(1)} %collective-permute-done.4.refs_2_, ...), custom_call_target="tpu_custom_call" | custom-call | bytes 1107000 | tf_op jit(solution)/shard_map/merged/pallas_call | solution.py:337
  29.3 2.6 %collective-permute-start.8 = (bf16[136,1024]{1,0:T(8,128)(2,1)S(1)}, bf16[136,1024]{1,0:T(8,128)(2,1)S(1)}, u32[]{:S(2)}, u32[]{:S(2)}) collective-permute-start(bf16[136,1024]{1,0:T(8,128)(2,1)S(1)} %merged.1.refs_5_.refs_3_), channel_id=1, source_target_pairs={{0,8},{2,10},{4,12},{6,14},{8,0},{10,2},{12,4},{14,6},{1,9},{3,11}... | collective-permute-start | bytes 835592 | tf_op jit(solution)/shard_map/ppermute | solution.py:39
  31.9 0.0 collective-permute-done.3.refs_1_
  31.9 0.5 %resent.1 = (bf16[128,1024]{1,0:T(8,128)(2,1)S(1)}, bf16[128,1024]{1,0:T(8,128)(2,1)S(1)}) custom-call(f32[128,1024]{1,0:T(8,128)S(1)} %get-tuple-element.33.refs_0_, bf16[128,1024]{1,0:T(8,128)(2,1)S(1)} %collective-permute-done.3.refs_1_, bf16[152,1024]{1,0:T(8,128)(2,1)S(1)} %collective-permute-done.2.refs_4_.refs_3_.refs_2_, ...), custom_call_target="tpu_custom_call" | custom-call | bytes 1107000 | tf_op jit(solution)/shard_map/resent/pallas_call | solution.py:337
  32.4 1.7 %collective-permute-start.6 = (bf16[128,1024]{1,0:T(8,128)(2,1)S(1)}, bf16[128,1024]{1,0:T(8,128)(2,1)S(1)}, u32[]{:S(2)}, u32[]{:S(2)}) collective-permute-start(bf16[128,1024]{1,0:T(8,128)(2,1)S(1)} %get-tuple-element.38.refs_3_), channel_id=1, source_target_pairs={{0,4},{2,6},{4,0},{6,2},{8,12},{10,14},{12,8},{14,10},{1,5},{3,7},... | collective-permute-start | bytes 786440 | tf_op jit(solution)/shard_map/ppermute | solution.py:39
  34.1 0.6 %collective-permute-start.7 = (bf16[128,1024]{1,0:T(8,128)(2,1)S(1)}, bf16[128,1024]{1,0:T(8,128)(2,1)S(1)}, u32[]{:S(2)}, u32[]{:S(2)}) collective-permute-start(bf16[128,1024]{1,0:T(8,128)(2,1)S(1)} %get-tuple-element.39), channel_id=1, source_target_pairs={{0,2},{2,0},{4,6},{6,4},{8,10},{10,8},{12,14},{14,12},{1,3},{3,1},... | collective-permute-start | bytes 786440 | tf_op jit(solution)/shard_map/ppermute | solution.py:39
  34.7 8.0 %segment_rows.3.refs_3_.refs_6_ = f32[16,768]{1,0:T(8,128)S(1)} custom-call(bf16[2048,1024]{1,0:T(8,128)(2,1)S(1)} %get-tuple-element.23.refs_0_, f32[1,1024]{1,0:T(1,128)S(1)} %get-tuple-element.24.refs_1_, bf16[152,1024]{1,0:T(8,128)(2,1)S(1)} %collective-permute-done.2.refs_4_.refs_3_.refs_2_, bf16[128,1024]{1,0:T(8,128)(2,1)S(1)} %get-tuple-element.38.refs_3_), custom_call_target="tpu_custom_call" | custom-call | bytes 4428000 | tf_op jit(solution)/shard_map/segment_rows/pallas_call | solution.py:337
  42.7 2.2 %collective-permute-done.6.refs_1_ = bf16[128,1024]{1,0:T(8,128)(2,1)S(1)} collective-permute-done((bf16[128,1024]{1,0:T(8,128)(2,1)S(1)}, bf16[128,1024]{1,0:T(8,128)(2,1)S(1)}, u32[]{:S(2)}, u32[]{:S(2)}) %collective-permute-start.6) | collective-permute-done | bytes 262176 | tf_op jit(solution)/shard_map/ppermute | solution.py:39
  44.9 0.3 added.1.refs_0_
  45.2 0.0 collective-permute-done.7.refs_1_
  45.2 0.0 collective-permute-done.8.refs_4_
  45.2 1.4 %finished.1 = (f32[128,1024]{1,0:T(8,128)}, f32[16,1024]{1,0:T(8,128)}) custom-call(f32[128,1024]{1,0:T(8,128)S(1)} %added.1.refs_0_, bf16[128,1024]{1,0:T(8,128)(2,1)S(1)} %collective-permute-done.7.refs_1_, bf16[152,1024]{1,0:T(8,128)(2,1)S(1)} %collective-permute-done.2.refs_4_.refs_3_.refs_2_, bf16[136,1024]{1,0:T(8,128)(2,1)S(1)} %merged.1.refs_5_.refs_3_, ...), custom_call_target="tpu_custom_call" | custom-call | bytes 1107000 | tf_op jit(solution)/shard_map/finished/pallas_call | solution.py:337
  (1 shorter events, 0.0 us)
Async XLA Ops:
  1.9 4.1 %collective-permute-start = (bf16[32,2048]{1,0:T(8,128)(2,1)S(1)}, bf16[32,2048]{1,0:T(8,128)(2,1)S(1)}, u32[]{:S(2)}, u32[]{:S(2)}) collective-permute-start(bf16[32,2048]{1,0:T(8,128)(2,1)S(1)} %get-tuple-element.21.after.refs_2_.refs_1_.refs_0_), channel_id=1, source_target_pairs={{0,1},{1,0},{2,3},{3,2},{4,5},{5,4},{6,7},{7,6},{8,9},{9,8},{10,11... | collective-permute-start | bytes 393224 | tf_op jit(solution)/shard_map/ppermute | solution.py:39
  2.4 6.5 %collective-permute-start.1 = (bf16[16,1024]{1,0:T(8,128)(2,1)S(1)}, bf16[16,1024]{1,0:T(8,128)(2,1)S(1)}, u32[]{:S(2)}, u32[]{:S(2)}) collective-permute-start(bf16[16,1024]{1,0:T(8,128)(2,1)S(1)} %get-tuple-element.22.refs_0_), channel_id=1, source_target_pairs={{4,0},{8,4},{12,8},{5,1},{9,5},{13,9},{20,16},{24,20},{28,24},{21,... | collective-permute-start | bytes 98312 | tf_op jit(solution)/shard_map/ppermute | solution.py:593
  9.0 9.2 %collective-permute-start.2 = (bf16[152,1024]{1,0:T(8,128)(2,1)S(1)}, bf16[152,1024]{1,0:T(8,128)(2,1)S(1)}, u32[]{:S(2)}, u32[]{:S(2)}) collective-permute-start(bf16[152,1024]{1,0:T(8,128)(2,1)S(1)} %with_tails.1.refs_3_.refs_2_), channel_id=1, source_target_pairs={{0,2},{2,0},{4,6},{6,4},{8,10},{10,8},{12,14},{14,12},{1,3},{3,1},... | collective-permute-start | bytes 933896 | tf_op jit(solution)/shard_map/ppermute | solution.py:39
  15.4 10.2 %collective-permute-start.5 = (bf16[144,1024]{1,0:T(8,128)(2,1)S(1)}, bf16[144,1024]{1,0:T(8,128)(2,1)S(1)}, u32[]{:S(2)}, u32[]{:S(2)}) collective-permute-start(bf16[144,1024]{1,0:T(8,128)(2,1)S(1)} %get-tuple-element.37), channel_id=1, source_target_pairs={{0,2},{2,0},{4,6},{6,4},{8,10},{10,8},{12,14},{14,12},{1,3},{3,1},... | collective-permute-start | bytes 884744 | tf_op jit(solution)/shard_map/ppermute | solution.py:39
  18.9 9.5 %collective-permute-start.4 = (bf16[136,1024]{1,0:T(8,128)(2,1)S(1)}, bf16[136,1024]{1,0:T(8,128)(2,1)S(1)}, u32[]{:S(2)}, u32[]{:S(2)}) collective-permute-start(bf16[136,1024]{1,0:T(8,128)(2,1)S(1)} %get-tuple-element.31.refs_7_.refs_1_.refs_3_), channel_id=1, source_target_pairs={{0,4},{2,6},{4,0},{6,2},{8,12},{10,14},{12,8},{14,10},{1,5},{3,7},... | collective-permute-start | bytes 835592 | tf_op jit(solution)/shard_map/ppermute | solution.py:39
  22.4 9.5 %collective-permute-start.3 = (bf16[128,1024]{1,0:T(8,128)(2,1)S(1)}, bf16[128,1024]{1,0:T(8,128)(2,1)S(1)}, u32[]{:S(2)}, u32[]{:S(2)}) collective-permute-start(bf16[128,1024]{1,0:T(8,128)(2,1)S(1)} %get-tuple-element.34), channel_id=1, source_target_pairs={{0,2},{2,0},{4,6},{6,4},{8,10},{10,8},{12,14},{14,12},{1,3},{3,1},... | collective-permute-start | bytes 786440 | tf_op jit(solution)/shard_map/ppermute | solution.py:39
  29.3 15.9 %collective-permute-start.8 = (bf16[136,1024]{1,0:T(8,128)(2,1)S(1)}, bf16[136,1024]{1,0:T(8,128)(2,1)S(1)}, u32[]{:S(2)}, u32[]{:S(2)}) collective-permute-start(bf16[136,1024]{1,0:T(8,128)(2,1)S(1)} %merged.1.refs_5_.refs_3_), channel_id=1, source_target_pairs={{0,8},{2,10},{4,12},{6,14},{8,0},{10,2},{12,4},{14,6},{1,9},{3,11}... | collective-permute-start | bytes 835592 | tf_op jit(solution)/shard_map/ppermute | solution.py:39
  32.4 12.4 %collective-permute-start.6 = (bf16[128,1024]{1,0:T(8,128)(2,1)S(1)}, bf16[128,1024]{1,0:T(8,128)(2,1)S(1)}, u32[]{:S(2)}, u32[]{:S(2)}) collective-permute-start(bf16[128,1024]{1,0:T(8,128)(2,1)S(1)} %get-tuple-element.38.refs_3_), channel_id=1, source_target_pairs={{0,4},{2,6},{4,0},{6,2},{8,12},{10,14},{12,8},{14,10},{1,5},{3,7},... | collective-permute-start | bytes 786440 | tf_op jit(solution)/shard_map/ppermute | solution.py:39
  34.1 11.1 %collective-permute-start.7 = (bf16[128,1024]{1,0:T(8,128)(2,1)S(1)}, bf16[128,1024]{1,0:T(8,128)(2,1)S(1)}, u32[]{:S(2)}, u32[]{:S(2)}) collective-permute-start(bf16[128,1024]{1,0:T(8,128)(2,1)S(1)} %get-tuple-element.39), channel_id=1, source_target_pairs={{0,2},{2,0},{4,6},{6,4},{8,10},{10,8},{12,14},{14,12},{1,3},{3,1},... | collective-permute-start | bytes 786440 | tf_op jit(solution)/shard_map/ppermute | solution.py:39
